TPU v7x, 32 devices: a whole 2x2x4 slice. The times are simulated.
32 devices in a mesh: space: 8 (over y, x, core), scan: 4 (over z).
Axes of the slice: x: 2, y: 2, z: 4, core: 2. Of those that a mesh axis runs over, the one named last changes fastest.
Arguments:
- act_zero: bfloat16 [4, 8, 512, 96], P('scan', 'space'), may hold values from -6 to 6
- pre_act: bfloat16 [4, 8, 512, 96], P('scan', 'space'), may hold values from -6 to 6
- cot_out: bfloat16 [4, 8, 512, 96], P('scan', 'space'), may hold values from -0.59765625 to 0.59765625
- weight_one: bfloat16 [27, 96, 96], replicated, may hold values from -0.625 to 0.625
- weight_two: bfloat16 [27, 96, 96], replicated, may hold values from -0.625 to 0.625
- in_map: int32 [4, 8, 27, 256], P('scan', 'space'), may hold values from 0 to 640, as said below
- out_map: int32 [4, 8, 27, 256], P('scan', 'space'), may hold values from 0 to 512, as said below
- send_lo: int32 [4, 8, 64], P('scan', 'space'), may hold values from 0 to 511, as said below
- send_hi: int32 [4, 8, 64], P('scan', 'space'), may hold values from 0 to 511, as said below
Outputs:
- grad_act: bfloat16 [4, 8, 512, 96], P('scan', 'space')
- grad_w_one: float32 [27, 96, 96], replicated
- grad_w_two: float32 [27, 96, 96], replicated
Inputs may be any that keep to these rules, and one draw needn't show every extreme that they name: Per brick and offset the live slots come first and number a multiple of 32; the input rows of one offset differ, and so do its output rows; empty slots hold in_map 512 + 2 * 64 and out_map 512; in every draw some brick has every slot live. `out_map`: see in_map. send_lo and send_hi of one brick hold 128 different rows. `send_hi`: see send_lo.
All inputs are finite; a program needn't handle non-finite values.
Results may differ from a plain program's by a relative error of at most 0.0049.
Values may be sent and summed in bfloat16 or wider, within the bound.
No kernel may reach another device: no remote copies, remote signals or barrier semaphores. Data moves between devices by JAX's collectives and lax.ppermute only.
A program may use at most 64 MiB of HBM per device.

v0:
```python
import jax
import jax.numpy as jnp
from jax import lax
from jax.sharding import PartitionSpec as P


def passed_along(block, axis, distance):
    devices = range(lax.axis_size(axis))
    route = [(i - distance, i) for i in devices if i - distance in devices]
    return lax.ppermute(block, axis, route)


def pass_rim(stacked, offset):
    return passed_along(stacked, "space", offset)


def send_back(piece, offset):
    return passed_along(piece, "space", offset)


def layer_grads(ext_feats, cot, weight, ins, outs):
    padded = jnp.concatenate([cot, jnp.zeros((1, cot.shape[1]), cot.dtype)], 0)
    gathered = ext_feats[ins]
    cot_rows = padded[outs]
    delta_w = jnp.einsum("kpc,kpd->kcd", gathered, cot_rows, preferred_element_type=jnp.float32)
    back = jnp.einsum("kpd,kcd->kpc", cot_rows, weight, preferred_element_type=jnp.float32)
    delta_x = (
        jnp.zeros(ext_feats.shape, jnp.float32)
        .at[ins.reshape(-1)]
        .add(back.reshape(-1, back.shape[2]))
    )
    return (delta_w, delta_x)


def settle(delta_x, lo_rows, hi_rows):
    rows = delta_x.shape[0] // 1
    span = lo_rows.shape[0]
    rows = rows - 2 * span - 1
    local = delta_x[:rows]
    from_above = send_back(delta_x[rows : rows + span], -1)
    from_below = send_back(delta_x[rows + span : rows + 2 * span], 1)
    return local.at[hi_rows].add(from_above).at[lo_rows].add(from_below)


def total_weights(grads):
    return lax.psum((grads[0],), ("space", "scan"))


def shards(act_zero, pre_act, cot_out, weight_one, weight_two, in_map, out_map, send_lo, send_hi):
    feats_zero = act_zero[0, 0]
    pre = pre_act[0, 0]
    feats_one = jnp.maximum(pre, jnp.zeros_like(pre))
    lo_rows = send_lo[0, 0]
    hi_rows = send_hi[0, 0]
    ins = in_map[0, 0]
    outs = out_map[0, 0]
    chans = feats_zero.shape[1]
    scenes = lax.axis_size("scan")
    from_left = pass_rim(jnp.stack([feats_zero[hi_rows], feats_one[hi_rows]]), 1)
    from_right = pass_rim(jnp.stack([feats_zero[lo_rows], feats_one[lo_rows]]), -1)
    zero_row = jnp.zeros((1, chans), feats_zero.dtype)
    ext_zero = jnp.concatenate([feats_zero, from_left[0], from_right[0], zero_row], 0)
    ext_one = jnp.concatenate([feats_one, from_left[1], from_right[1], zero_row], 0)
    delta_two, delta_x = layer_grads(ext_one, cot_out[0, 0], weight_two, ins, outs)
    summed_two = total_weights((delta_two,))[0]
    back_two = settle(delta_x, lo_rows, hi_rows)
    cot_one = jnp.where(pre > 0, back_two, 0.0).astype(jnp.bfloat16)
    delta_one, delta_x = layer_grads(ext_zero, cot_one, weight_one, ins, outs)
    summed_one = total_weights((delta_one,))[0]
    back_one = settle(delta_x, lo_rows, hi_rows)
    grad_act = back_one.astype(jnp.bfloat16)[None, None]
    return (grad_act, summed_one / scenes, summed_two / scenes)


def solution(mesh):
    return jax.shard_map(
        shards,
        mesh=mesh,
        in_specs=(
            P("scan", "space", None, None),
            P("scan", "space", None, None),
            P("scan", "space", None, None),
            P(),
            P(),
            P("scan", "space", None, None),
            P("scan", "space", None, None),
            P("scan", "space", None),
            P("scan", "space", None),
        ),
        out_specs=(P("scan", "space", None, None), P(), P()),
        check_vma=False,
    )
```

profile of v0, /device:TPU:0, one launch (start us, length us, event | category | flops | bytes accessed | tf_op | source)
XLA Modules:
  0.0 289.8 jit_solution(2920923015324140642)
XLA Ops:
  7.2 0.9 fusion.6
  8.1 1.0 copy.24
  9.2 0.8 fusion.4
  10.1 13.0 %gather_fusion = bf16[6912,96]{1,0:T(8,128)(2,1)S(1)} fusion(bf16[513,96]{1,0:T(8,128)(2,1)S(1)} %concatenate.12, s32[7168]{0:T(1024)S(1)} %pad_clamp_fusion.1), kind=kCustom, calls=%fused_computation | custom fusion | bytes 2681856 | tf_op jit(solution)/shard_map/gather | solution.py:24
  23.2 2.4 fusion.11
  25.6 46.6 %scatter_custom_fusion = f32[641,96]{1,0:T(8,128)S(1)} fusion(s32[6912]{0:T(1024)S(1)} %fusion.6, f32[6912,96]{1,0:T(8,128)} %bitcast.55, f32[]{:T(128)} %constant.7.clone.1), kind=kCustom, calls=%fused_computation.21 | custom fusion | flops 663552 | bytes 246656 | tf_op jit(solution)/shard_map/scatter-add | solution.py:30
  72.8 1.3 collective-permute-start
  74.1 3.0 %collective-permute-start.1 = (f32[64,96]{1,0:T(8,128)}, f32[64,96]{1,0:T(8,128)S(1)}, u32[]{:S(2)}, u32[]{:S(2)}) collective-permute-start(f32[64,96]{1,0:T(8,128)} %get-tuple-element.13), channel_id=1, source_target_pairs={{0,4},{4,8},{8,12},{12,16},{16,20},{20,24},{24,28},{1,5},{5,9},{9,... | collective-permute-start | bytes 73736 | tf_op jit(solution)/shard_map/ppermute | solution.py:10
  77.5 0.6 gather_fusion.5
  78.1 0.6 gather_fusion.4
  79.4 1.3 collective-permute-start.5
  80.7 0.6 gather_fusion.3
  82.6 4.9 %collective-permute-start.4 = (bf16[2,64,96]{2,1,0:T(8,128)(2,1)}, bf16[2,64,96]{2,1,0:T(8,128)(2,1)}, u32[]{:S(2)}, u32[]{:S(2)}) collective-permute-start(bf16[2,64,96]{2,1,0:T(8,128)(2,1)} %pad_maximum_fusion), channel_id=1, source_target_pairs={{0,4},{4,8},{8,12},{12,16},{16,20},{20,24},{24,28},{1,5},{5,9},{9,... | collective-permute-start | bytes 73736 | tf_op jit(solution)/shard_map/ppermute | solution.py:10
  87.7 1.3 scatter_fusion
  88.9 1.0 scatter_fusion.1
  90.0 0.7 slice_bitcast_fusion
  90.8 14.7 %gather_fusion.1 = bf16[6912,96]{1,0:T(8,128)(2,1)} fusion(bf16[513,96]{1,0:T(8,128)(2,1)S(1)} %concatenate.13, s32[7168]{0:T(1024)S(1)} %pad_clamp_fusion.1), kind=kCustom, calls=%fused_computation.1 | custom fusion | bytes 2681856 | tf_op jit(solution)/shard_map/gather | solution.py:24
  105.5 0.7 slice_bitcast_fusion.1
  106.4 14.7 %gather_fusion.6 = bf16[6912,96]{1,0:T(8,128)(2,1)} fusion(bf16[641,96]{1,0:T(8,128)(2,1)S(1)} %get-tuple-element.20, s32[7168]{0:T(1024)S(1)} %pad_clamp_fusion), kind=kCustom, calls=%fused_computation.6 | custom fusion | bytes 2681856 | tf_op jit(solution)/shard_map/gather | solution.py:23
  121.2 14.7 %gather_fusion.7 = bf16[6912,96]{1,0:T(8,128)(2,1)} fusion(bf16[641,96]{1,0:T(8,128)(2,1)S(1)} %get-tuple-element.19, s32[7168]{0:T(1024)S(1)} %pad_clamp_fusion), kind=kCustom, calls=%fused_computation.7 | custom fusion | bytes 2681856 | tf_op jit(solution)/shard_map/gather | solution.py:23
  135.9 3.4 %fusion.14 = f32[27,96,96]{2,1,0:T(8,128)} fusion(bf16[27,256,96]{2,1,0:T(8,128)(2,1)} %bitcast.53, bf16[27,256,96]{2,1,0:T(8,128)(2,1)S(1)} %bitcast.49), kind=kOutput, calls=%fused_computation.50 | convolution fusion | flops 127401984 | bytes 3649536 | tf_op jit(solution)/shard_map/kpc,kpd->kcd/dot_general | solution.py:25
  139.4 1.8 fusion.13
  141.2 1.4 copy-done.2
  142.8 2.4 fusion.12
  145.2 46.6 %scatter_custom_fusion.3 = f32[641,96]{1,0:T(8,128)S(1)} fusion(s32[6912]{0:T(1024)} %copy-done.8, f32[6912,96]{1,0:T(8,128)} %bitcast.54, f32[]{:T(128)} %constant.7.clone.1), kind=kCustom, calls=%fused_computation.19 | custom fusion | flops 663552 | bytes 246656 | tf_op jit(solution)/shard_map/scatter-add | solution.py:30
  191.8 1.3 collective-permute-start.2
  193.1 3.0 %collective-permute-start.3 = (f32[64,96]{1,0:T(8,128)S(1)}, f32[64,96]{1,0:T(8,128)S(1)}, u32[]{:S(2)}, u32[]{:S(2)}) collective-permute-start(f32[64,96]{1,0:T(8,128)S(1)} %get-tuple-element.11), channel_id=1, source_target_pairs={{0,4},{4,8},{8,12},{12,16},{16,20},{20,24},{24,28},{1,5},{5,9},{9,... | collective-permute-start | bytes 73736 | tf_op jit(solution)/shard_map/ppermute | solution.py:10
  196.2 1.0 scatter_fusion.2
  197.2 1.0 scatter_fusion.3
  198.3 0.7 copy.37
  199.0 80.5 %all-reduce.5.cloned.1.call-done = (f32[27,96,96]{2,1,0:T(8,128)}, f32[27,96,96]{2,1,0:T(8,128)}) async-done(((f32[27,96,96]{2,1,0:T(8,128)}, f32[27,96,96]{2,1,0:T(8,128)}), (f32[27,96,96]{2,1,0:T(8,128)}, f32[27,96,96]{2,1,0:T(8,128)})) %all-reduce.5.cloned.1.call-update) | async-done | bytes 1990672 | tf_op jit(solution)/shard_map/psum | solution.py:46
  279.5 3.4 %broadcast_multiply_fusion = (f32[27,96,96]{2,1,0:T(8,128)}, f32[27,96,96]{2,1,0:T(8,128)}) fusion(f32[27,96,96]{2,1,0:T(8,128)} %get-tuple-element.10, f32[27,96,96]{2,1,0:T(8,128)} %get-tuple-element.9), kind=kLoop, calls=%fused_computation.14 | loop fusion | flops 497664 | bytes 3981312 | tf_op jit(solution)/shard_map/div | solution.py:72
  (62 shorter events, 3.5 us)
Async XLA Ops:
  7.2 15.9 %copy-start = (bf16[27,96,96]{2,1,0:T(8,128)(2,1)S(1)}, bf16[27,96,96]{2,1,0:T(8,128)(2,1)}, u32[]{:S(2)}) copy-start(bf16[27,96,96]{2,1,0:T(8,128)(2,1)} %param.13) | copy-start | bytes 1492996
  7.2 272.3 %all-reduce.5.cloned.1.call-start = ((), (), s32[]{:S(2)}) async-start(), calls=%async_computation | async-start | bytes 5308416 | tf_op jit(solution)/shard_map/psum | solution.py:46
  8.1 17.4 %copy-start.8 = (s32[6912]{0:T(1024)}, s32[6912]{0:T(1024)S(1)}, u32[]{:S(2)}) copy-start(s32[6912]{0:T(1024)S(1)} %fusion.6) | copy-start | bytes 82948
  23.1 54.0 %copy-start.13 = (s32[1,1,64]{2,1,0:T(1,128)S(1)}, s32[1,1,64]{2,1,0:T(1,128)}, u32[]{:S(2)}) copy-start(s32[1,1,64]{2,1,0:T(1,128)} %param.16) | copy-start | bytes 772
  23.1 54.0 %copy-start.6 = (bf16[1,1,512,96]{2,3,1,0:T(8,128)(2,1)S(1)}, bf16[1,1,512,96]{2,3,1,0:T(8,128)(2,1)}, u32[]{:S(2)}) copy-start(bf16[1,1,512,96]{2,3,1,0:T(8,128)(2,1)} %param.10) | copy-start | bytes 294916
  23.1 54.2 %copy-start.7 = (bf16[1,1,512,96]{2,3,1,0:T(8,128)(2,1)S(1)}, bf16[1,1,512,96]{2,3,1,0:T(8,128)(2,1)}, u32[]{:S(2)}) copy-start(bf16[1,1,512,96]{2,3,1,0:T(8,128)(2,1)} %param.9) | copy-start | bytes 294916
  23.2 57.5 %copy-start.14 = (s32[1,1,64]{2,1,0:T(1,128)S(1)}, s32[1,1,64]{2,1,0:T(1,128)}, u32[]{:S(2)}) copy-start(s32[1,1,64]{2,1,0:T(1,128)} %param.17) | copy-start | bytes 772
  25.6 61.9 %copy-start.5 = (s32[1,1,27,256]{3,1,2,0:T(1,128)S(1)}, s32[1,1,27,256]{3,1,2,0:T(1,128)}, u32[]{:S(2)}) copy-start(s32[1,1,27,256]{3,1,2,0:T(1,128)} %param.14) | copy-start | bytes 82948
  72.8 14.8 %collective-permute-start = (f32[64,96]{1,0:T(8,128)}, f32[64,96]{1,0:T(8,128)}, u32[]{:S(2)}, u32[]{:S(2)}) collective-permute-start(f32[64,96]{1,0:T(8,128)} %get-tuple-element.14), channel_id=1, source_target_pairs={{4,0},{8,4},{12,8},{16,12},{20,16},{24,20},{28,24},{5,1},{9,5},{13... | collective-permute-start | bytes 73736 | tf_op jit(solution)/shard_map/ppermute | solution.py:10
  74.1 14.8 %collective-permute-start.1 = (f32[64,96]{1,0:T(8,128)}, f32[64,96]{1,0:T(8,128)S(1)}, u32[]{:S(2)}, u32[]{:S(2)}) collective-permute-start(f32[64,96]{1,0:T(8,128)} %get-tuple-element.13), channel_id=1, source_target_pairs={{0,4},{4,8},{8,12},{12,16},{16,20},{20,24},{24,28},{1,5},{5,9},{9,... | collective-permute-start | bytes 73736 | tf_op jit(solution)/shard_map/ppermute | solution.py:10
  77.2 12.9 %copy-start.9 = (s32[64]{0:T(128)}, s32[64]{0:T(128)S(1)}, u32[]{:S(2)}) copy-start(s32[64]{0:T(128)S(1)} %fusion.8) | copy-start | bytes 772
  79.4 10.7 %collective-permute-start.5 = (bf16[2,64,96]{2,1,0:T(8,128)(2,1)}, bf16[2,64,96]{2,1,0:T(8,128)(2,1)}, u32[]{:S(2)}, u32[]{:S(2)}) collective-permute-start(bf16[2,64,96]{2,1,0:T(8,128)(2,1)} %pad_maximum_fusion.1), channel_id=1, source_target_pairs={{4,0},{8,4},{12,8},{16,12},{20,16},{24,20},{28,24},{5,1},{9,5},{13... | collective-permute-start | bytes 73736 | tf_op jit(solution)/shard_map/ppermute | solution.py:10
  80.7 24.9 %copy-start.11 = (s32[64]{0:T(128)}, s32[64]{0:T(128)S(1)}, u32[]{:S(2)}) copy-start(s32[64]{0:T(128)S(1)} %fusion.7) | copy-start | bytes 772
  82.6 22.9 %collective-permute-start.4 = (bf16[2,64,96]{2,1,0:T(8,128)(2,1)}, bf16[2,64,96]{2,1,0:T(8,128)(2,1)}, u32[]{:S(2)}, u32[]{:S(2)}) collective-permute-start(bf16[2,64,96]{2,1,0:T(8,128)(2,1)} %pad_maximum_fusion), channel_id=1, source_target_pairs={{0,4},{4,8},{8,12},{12,16},{16,20},{20,24},{24,28},{1,5},{5,9},{9,... | collective-permute-start | bytes 73736 | tf_op jit(solution)/shard_map/ppermute | solution.py:10
  135.9 3.4 %copy-start.1 = (bf16[6912,96]{1,0:T(8,128)(2,1)S(1)}, bf16[6912,96]{1,0:T(8,128)(2,1)}, u32[]{:S(2)}) copy-start(bf16[6912,96]{1,0:T(8,128)(2,1)} %gather_fusion.1) | copy-start | bytes 3981316
  135.9 3.4 %copy-start.3 = (bf16[6912,96]{1,0:T(8,128)(2,1)S(1)}, bf16[6912,96]{1,0:T(8,128)(2,1)}, u32[]{:S(2)}) copy-start(bf16[6912,96]{1,0:T(8,128)(2,1)} %gather_fusion.6) | copy-start | bytes 3981316
  141.2 1.5 copy-start.2
  141.2 1.6 copy-start.4
  142.8 53.4 %copy-start.12 = (s32[64]{0:T(128)S(1)}, s32[64]{0:T(128)}, u32[]{:S(2)}) copy-start(s32[64]{0:T(128)} %copy-done.11) | copy-start | bytes 772
  142.8 54.4 %copy-start.10 = (s32[64]{0:T(128)S(1)}, s32[64]{0:T(128)}, u32[]{:S(2)}) copy-start(s32[64]{0:T(128)} %copy-done.9) | copy-start | bytes 772
  191.8 4.4 %collective-permute-start.2 = (f32[64,96]{1,0:T(8,128)S(1)}, f32[64,96]{1,0:T(8,128)S(1)}, u32[]{:S(2)}, u32[]{:S(2)}) collective-permute-start(f32[64,96]{1,0:T(8,128)S(1)} %get-tuple-element.12), channel_id=1, source_target_pairs={{4,0},{8,4},{12,8},{16,12},{20,16},{24,20},{28,24},{5,1},{9,5},{13... | collective-permute-start | bytes 73736 | tf_op jit(solution)/shard_map/ppermute | solution.py:10
  193.1 4.1 %collective-permute-start.3 = (f32[64,96]{1,0:T(8,128)S(1)}, f32[64,96]{1,0:T(8,128)S(1)}, u32[]{:S(2)}, u32[]{:S(2)}) collective-permute-start(f32[64,96]{1,0:T(8,128)S(1)} %get-tuple-element.11), channel_id=1, source_target_pairs={{0,4},{4,8},{8,12},{12,16},{16,20},{20,24},{24,28},{1,5},{5,9},{9,... | collective-permute-start | bytes 73736 | tf_op jit(solution)/shard_map/ppermute | solution.py:10
Sparse Core Ops, SparseCore 0:
  141.3 138.1 all-reduce.4
where the time goes:
time: 291 us; the launch traced here: 290 us
  other arithmetic  104 us (36%)
  waiting for transfers between devices  80.5 us (28%)
  local copies, waits for them, and re-layouts  65.7 us (23%)
  starting transfers between devices  14.8 us (5%)
  between operations  14.5 us (5%)
  matrix products  9.99 us (3%)
    scatter-add x2, other arithmetic, layer_grads(): delta_x = jnp.zeros(ext_feats.shape, jnp.float32).at[ins.reshape(-1)].add...  93.2 us
    psum x1, waiting for transfers between devices, total_weights(): return lax.psum((grads[0],), ('space', 'scan'))  80.5 us
    gather x2, local copies, waits for them, and re-layouts, layer_grads(): gathered = ext_feats[ins]  29.5 us
    gather x2, local copies, waits for them, and re-layouts, layer_grads(): cot_rows = padded[outs]  27.8 us
    ppermute x6, starting transfers between devices, passed_along(): return lax.ppermute(block, axis, route)  14.8 us
  transfers between devices with their start and end apart: 7, of which 1 were waited for; matrix products, arithmetic and copies ran while one was open for 25% of the time, Pallas kernels for 0%

commit v1 on v0

v1 whole, which is shorter than its diff:
```python
import functools

import jax
import jax.numpy as jnp
from jax import lax
from jax.experimental import pallas as pl
from jax.experimental.pallas import tpu as pltpu
from jax.sharding import PartitionSpec as P

F32, BF16, I32 = jnp.float32, jnp.bfloat16, jnp.int32
VMEM = pl.BlockSpec(memory_space=pltpu.VMEM)
LANES = 128
GROUP = 256
UNROLL = 9
NT = (((1,), (1,)), ((), ()))


def call(body, outs, args, scratch=(), flops=0, moved=0):
    single = not isinstance(outs, (list, tuple))
    return pl.pallas_call(
        body,
        out_shape=outs if single else tuple(outs),
        in_specs=[VMEM] * len(args),
        out_specs=VMEM if single else (VMEM,) * len(outs),
        scratch_shapes=scratch,
        compiler_params=pltpu.CompilerParams(vmem_limit_bytes=40 << 20),
        cost_estimate=pl.CostEstimate(flops=flops, bytes_accessed=moved, transcendentals=0),
    )(*args)


def shape(dims, dtype):
    return jax.ShapeDtypeStruct(dims, dtype)


def loop(steps, body):
    unroll = next(u for u in range(UNROLL, 0, -1) if steps % u == 0)

    def step(i, carry):
        body(i)
        return carry

    lax.fori_loop(0, steps, step, 0, unroll=unroll)


def one_hot(rows, index):
    return (lax.broadcasted_iota(I32, (rows, index.shape[1]), 0) == index).astype(F32).astype(BF16)


def dot(a, b):
    return jnp.dot(a, b, preferred_element_type=F32)


def dot_nt(a, b):
    return lax.dot_general(a, b, NT, preferred_element_type=F32)


def offset_rows(k, chans):
    return pl.ds(pl.multiple_of(k * chans, chans), chans)


def rim_index(hi_ref, lo_ref):
    return jnp.concatenate([hi_ref[...], lo_ref[...]], 1)


def first_half(dims, own_parity):
    lane = lax.broadcasted_iota(I32, dims, 1)
    return (lane < dims[1] // 2) == own_parity


def is_even():
    return lax.rem(lax.axis_index("space"), 2) == 0


def rim_body(zero_ref, pre_ref, hi_ref, lo_ref, rim_ref):
    pick = one_hot(zero_ref.shape[1], rim_index(hi_ref, lo_ref))
    one = jnp.maximum(pre_ref[...], jnp.zeros_like(pre_ref))
    chans = zero_ref.shape[0]
    rim_ref[:chans] = dot(zero_ref[...], pick).astype(BF16)
    rim_ref[chans:] = dot(one, pick).astype(BF16)


def add_back(weight_ref, t_ref, total_ref):
    count, chans = weight_ref.shape[0], weight_ref.shape[1]
    total_ref[...] = jnp.zeros_like(total_ref)

    def body(g):
        part = None
        for j in range(3):
            k = g * 3 + j
            term = dot(weight_ref[k], t_ref[offset_rows(k, chans), :])
            part = term if part is None else part + term
        total_ref[...] += part

    assert count % 3 == 0
    loop(count // 3, body)


def split_back(total_ref, own_ref, rim_ref):
    rows = own_ref.shape[1]
    own_ref[...] = total_ref[:, :rows]
    rim_ref[...] = total_ref[:, rows:]


def two_body(ins_ref, outs_ref, cot_ref, weight_ref, t_ref, inv_ref, own_ref, rim_ref, c_ref, total_ref):
    count, pairs = ins_ref.shape[0], ins_ref.shape[2]
    chans, rows = cot_ref.shape
    ext = t_ref.shape[1]
    tall = chans + 16
    row = lax.broadcasted_iota(I32, (16, pairs), 0)

    def pick_outs(k):
        index = outs_ref[k]
        base = pl.multiple_of(k * tall, 16)
        c_ref[pl.ds(base, chans), :] = dot(cot_ref[...], one_hot(rows, index)).astype(BF16)
        left = rows - index
        code = jnp.where(row == 0, left // 16, jnp.where(row == 1, left % 16, 0))
        c_ref[pl.ds(base + chans, 16), :] = code.astype(F32).astype(BF16)

    loop(count, pick_outs)

    def put_ins(k):
        picked = c_ref[pl.ds(pl.multiple_of(k * tall, 16), tall), :]
        placed = dot_nt(picked, one_hot(ext, ins_ref[k]))
        t_ref[offset_rows(k, chans), :] = placed[:chans].astype(BF16)
        code = placed[chans : chans + 1] * 16.0 + placed[chans + 1 : chans + 2]
        inv_ref[k] = rows - code.astype(I32)

    loop(count, put_ins)
    t_ref[count * chans :, :] = jnp.zeros((t_ref.shape[0] - count * chans, ext), BF16)
    add_back(weight_ref, t_ref, total_ref)
    split_back(total_ref, own_ref, rim_ref)


def weight_sums(ext, t_ref, sum_ref, keep_ref, send_ref):
    chans = ext.shape[0]
    tiles = t_ref.shape[0] // LANES
    for start in range(0, tiles, 2):
        width = min(2, tiles - start)
        grad = dot_nt(ext, t_ref[start * LANES : (start + width) * LANES, :])
        for j in range(width):
            sum_ref[(start + j) * chans : (start + j + 1) * chans, :] = grad[:, j * LANES : (j + 1) * LANES]
    sum_ref[tiles * chans :, :] = jnp.zeros((sum_ref.shape[0] - tiles * chans, LANES), F32)
    me = lax.axis_index("space")
    slots = lax.axis_size("space") // 2
    rows = keep_ref.shape[0] // slots
    for slot in range(slots):
        for out_ref, bit in ((keep_ref, 0), (send_ref, 1)):
            piece = jnp.bitwise_xor(me, 2 * slot + bit)
            block = sum_ref[pl.ds(pl.multiple_of(piece * rows, rows), rows), :]
            out_ref[slot * rows : (slot + 1) * rows, :] = block.astype(out_ref.dtype)


def two_weights_body(pre_ref, near_ref, far_ref, t_ref, keep_ref, send_ref, sum_ref):
    chans = pre_ref.shape[0]
    one = jnp.maximum(pre_ref[...], jnp.zeros_like(pre_ref))
    ext = extended(one, near_ref[chans:].astype(F32), far_ref[chans:].astype(F32))
    weight_sums(ext, t_ref, sum_ref, keep_ref, send_ref)


def extended(feats, near, far):
    rim = jnp.where(first_half(near.shape, is_even()), far, near).astype(feats.dtype)
    return jnp.concatenate([feats, rim], 1)


def settled(own, near, far, hi_ref, lo_ref):
    part = jnp.where(first_half(near.shape, is_even()), near, far)
    place = one_hot(own.shape[1], rim_index(hi_ref, lo_ref))
    high = part.astype(BF16)
    low = (part - high.astype(F32)).astype(BF16)
    return own + dot_nt(high, place) + dot_nt(low, place)


def one_body(
    own_ref, near_ref, far_ref, hi_ref, lo_ref, pre_ref, zero_ref, rnear_ref, rfar_ref, inv_ref, t_ref, keep_ref, send_ref, cot_ref, sum_ref
):
    chans, rows = pre_ref.shape
    count, ext = inv_ref.shape[0], inv_ref.shape[2]
    back = settled(own_ref[...], near_ref[...], far_ref[...], hi_ref, lo_ref)
    cot_ref[...] = jnp.where(pre_ref[...].astype(F32) > 0, back, 0.0).astype(BF16)

    def place(k):
        t_ref[offset_rows(k, chans), :] = dot(cot_ref[...], one_hot(rows, inv_ref[k])).astype(BF16)

    loop(count, place)
    t_ref[count * chans :, :] = jnp.zeros((t_ref.shape[0] - count * chans, ext), BF16)
    feats = extended(zero_ref[...], rnear_ref[:chans].astype(F32), rfar_ref[:chans].astype(F32))
    weight_sums(feats, t_ref, sum_ref, keep_ref, send_ref)


def back_body(weight_ref, t_ref, own_ref, rim_ref, total_ref):
    add_back(weight_ref, t_ref, total_ref)
    split_back(total_ref, own_ref, rim_ref)


def settle_body(own_ref, near_ref, far_ref, hi_ref, lo_ref, out_ref):
    out_ref[...] = settled(own_ref[...], near_ref[...], far_ref[...], hi_ref, lo_ref).astype(BF16)


def core_sum_body(keep_ref, got_ref, own_ref, *send_refs):
    rows = own_ref.shape[0]
    own_ref[...] = keep_ref[:rows] + got_ref[:rows].astype(F32)
    for slot, send_ref in enumerate(send_refs, 1):
        part = slice(slot * rows, (slot + 1) * rows)
        send_ref[...] = (keep_ref[part] + got_ref[part].astype(F32)).astype(BF16)


def chip_sum_body(own_ref, *refs):
    total = own_ref[...]
    for got_ref in refs[:-1]:
        total = total + got_ref[...].astype(F32)
    refs[-1][...] = total.astype(BF16)


def scan_sum_body(*refs):
    terms = [ref[...].astype(F32) for ref in refs[:-1]]
    while len(terms) > 1:
        terms = [a + b for a, b in zip(terms[::2], terms[1::2], strict=True)]
    refs[-1][...] = terms[0].astype(BF16)


def unpack_body(scale, *refs):
    *piece_refs, out_ref, all_ref = refs
    me = lax.axis_index("space")
    rows = piece_refs[0].shape[0]
    for slot, piece_ref in enumerate(piece_refs):
        piece = jnp.bitwise_xor(me, slot)
        all_ref[pl.ds(pl.multiple_of(piece * rows, rows), rows), :] = piece_ref[...].astype(F32)
    count, chans = out_ref.shape[0], out_ref.shape[1]
    lane = lax.broadcasted_iota(I32, (chans, LANES), 1)
    for k in range(count):
        tile, shift = divmod(k * chans, LANES)
        block = all_ref[tile * chans : (tile + 1) * chans, :]
        if shift:
            block = pltpu.roll(block, LANES - shift, 1)
        if shift + chans > LANES:
            after = pltpu.roll(all_ref[(tile + 1) * chans : (tile + 2) * chans, :], LANES - shift, 1)
            block = jnp.where(lane < LANES - shift, block, after)
        out_ref[k] = block[:, :chans] * scale


def swap(block, axis, bit):
    return lax.ppermute(block, axis, [(i, i ^ bit) for i in range(lax.axis_size(axis))])


def swap_neighbours(block):
    bricks = lax.axis_size("space")
    near = swap(block, "space", 1)
    inner = range(1, bricks - 1)
    far = lax.ppermute(block, "space", [(i, i + 1 if i % 2 else i - 1) for i in inner])
    return near, far


def summed(keep, send, weight_shape, scale):
    slots = lax.axis_size("space") // 2
    scans = lax.axis_size("scan")
    rows = keep.shape[0] // slots
    got = swap(send, "space", 1)
    outs = [shape((rows, LANES), F32)] + [shape((rows, LANES), BF16)] * (slots - 1)
    own, *sends = call(core_sum_body, outs, [keep, got])
    gots = [swap(block, "space", 2 * slot) for slot, block in enumerate(sends, 1)]
    part = call(chip_sum_body, shape((rows, LANES), BF16), [own, *gots])
    if scans & (scans - 1):
        total = lax.psum(part, "scan")
    else:
        terms = [part] + [swap(part, "scan", bit) for bit in range(1, scans)]
        total = call(scan_sum_body, shape((rows, LANES), BF16), terms)
    pieces = []
    for slot in range(slots):
        piece = swap(total, "space", 2 * slot) if slot else total
        pieces += [piece, swap(piece, "space", 1)]
    packed = 2 * keep.shape[0]
    return call(
        functools.partial(unpack_body, scale), shape(weight_shape, F32), pieces, scratch=[pltpu.VMEM((packed, LANES), F32)]
    )


def shards(act_zero, pre_act, cot_out, weight_one, weight_two, in_map, out_map, send_lo, send_hi):
    zero, pre, cot = (x[0, 0].T for x in (act_zero, pre_act, cot_out))
    ins, outs = (x[0, 0][:, None, :] for x in (in_map, out_map))
    lo, hi = send_lo[0], send_hi[0]
    chans, rows = zero.shape
    count, _, pairs = ins.shape
    rim = 2 * lo.shape[1]
    ext = rows + rim
    scenes = lax.axis_size("scan")
    bricks = lax.axis_size("space")
    tiles = -(-count * chans // LANES)
    tall = tiles * LANES
    unit = 16 * bricks
    packed = -(-tiles * chans // unit) * unit
    halves = [shape((packed // 2, LANES), F32), shape((packed // 2, LANES), BF16)]
    packed_sum = pltpu.VMEM((packed, LANES), F32)
    gather_flops = 2 * count * chans * ext * rows
    back_flops = 2 * count * chans * chans * ext

    rims = call(rim_body, shape((2 * chans, rim), BF16), [zero, pre, hi, lo])
    rims_near, rims_far = swap_neighbours(rims)

    t_two, inv, own, delta = call(
        two_body,
        [shape((tall, ext), BF16), shape((count, 1, ext), I32), shape((chans, rows), F32), shape((chans, rim), F32)],
        [ins, outs, cot, weight_two],
        scratch=[pltpu.VMEM((count * (chans + 16), pairs), BF16), pltpu.VMEM((chans, ext), F32)],
        flops=gather_flops + back_flops,
        moved=8 << 20,
    )
    near, far = swap_neighbours(delta)
    keep_two, send_two = call(
        two_weights_body, halves, [pre, rims_near, rims_far, t_two], scratch=[packed_sum], flops=back_flops, moved=6 << 20
    )
    t_one, keep_one, send_one = call(
        one_body,
        [shape((tall, ext), BF16), *halves],
        [own, near, far, hi, lo, pre, zero, rims_near, rims_far, inv],
        scratch=[pltpu.VMEM((chans, rows), BF16), packed_sum],
        flops=gather_flops + back_flops,
        moved=8 << 20,
    )
    grad_two = summed(keep_two, send_two, weight_two.shape, 1.0 / scenes)
    grad_one = summed(keep_one, send_one, weight_one.shape, 1.0 / scenes)
    own, delta = call(
        back_body,
        [shape((chans, rows), F32), shape((chans, rim), F32)],
        [weight_one, t_one],
        scratch=[pltpu.VMEM((chans, ext), F32)],
        flops=back_flops,
        moved=6 << 20,
    )
    near, far = swap_neighbours(delta)
    grad_act = call(settle_body, shape((chans, rows), BF16), [own, near, far, hi, lo])
    return grad_act.T[None, None], grad_one, grad_two


def solution(mesh):
    return jax.shard_map(
        shards,
        mesh=mesh,
        in_specs=(
            P("scan", "space", None, None),
            P("scan", "space", None, None),
            P("scan", "space", None, None),
            P(),
            P(),
            P("scan", "space", None, None),
            P("scan", "space", None, None),
            P("scan", "space", None),
            P("scan", "space", None),
        ),
        out_specs=(P("scan", "space", None, None), P(), P()),
        check_vma=False,
    )
```

time: 291 us -> 72.6 us (0.25)
  other arithmetic: 104 us -> 0 us
  waiting for transfers between devices: 80.5 us -> 7.11 us
  local copies, waits for them, and re-layouts: 65.7 us -> 6.59 us
  starting transfers between devices: 14.8 us -> 39.4 us
  Pallas kernels: 0 us -> 18.2 us
  between operations: 14.5 us -> 0.87 us
  matrix products: 9.99 us -> 0 us
    scatter-add x6 -> x0, other arithmetic: 97.5 us -> none  [the longest x2 93.2 us: layer_grads(): delta_x = jnp.zeros(ext_feats.shape, jnp.float32).at[ins.reshape(-1)].add...]
    psum x1 -> x0, waiting for transfers between devices: 80.5 us -> none  [total_weights(): return lax.psum((grads[0],), ('space', 'scan'))]
    gather x8 -> x0, local copies, waits for them, and re-layouts: 59.8 us -> none  [the longest x2 29.5 us: layer_grads(): gathered = ext_feats[ins]]
    ppermute x6 -> x34, starting transfers between devices: 14.8 us -> 39.4 us  [the longest x31 37.3 us: swap(): lax.ppermute(block, axis, [(i, i ^ bit) for i in range(lax.axis_size(axis...]
    pallas_call x0 -> x14, Pallas kernels: none -> 18.2 us  [call(): pl.pallas_call(body, out_shape=outs if single else tuple(outs), in_specs=...]
    ppermute x6 -> x34, waiting for transfers between devices: 0.02 us -> 7.11 us  [the longest x31 7.1 us: swap(): lax.ppermute(block, axis, [(i, i ^ bit) for i in range(lax.axis_size(axis...]
    dot_general x2 -> x0, matrix products: 5.24 us -> none  [layer_grads(): jnp.einsum('kpc,kpd->kcd', gathered, cot_rows, preferred_element_type=jnp...]
    reshape x2 -> x0, matrix products: 4.75 us -> none  [layer_grads(): back.reshape(-1, back.shape[2])]
  transfers between devices with their start and end apart: 7 -> 34, of which waited for: 1 -> 6; matrix products, arithmetic and copies ran while one was open for 25% -> 0% of each run, Pallas kernels for 0% -> 23%
where the time goes in v1:
time: 72.6 us; the launch traced here: 72.2 us
  starting transfers between devices  39.4 us (54%)
  Pallas kernels  18.2 us (25%)
  waiting for transfers between devices  7.11 us (10%)
  local copies, waits for them, and re-layouts  6.59 us (9%)
  between operations  0.87 us (1%)
    ppermute x31, starting transfers between devices, swap(): lax.ppermute(block, axis, [(i, i ^ bit) for i in range(lax.axis_size(axis...  37.3 us
    pallas_call x14, Pallas kernels, call(): pl.pallas_call(body, out_shape=outs if single else tuple(outs), in_specs=...  18.2 us
    ppermute x31, waiting for transfers between devices, swap(): lax.ppermute(block, axis, [(i, i ^ bit) for i in range(lax.axis_size(axis...  7.1 us
    unnamed x26, local copies, waits for them, and re-layouts  6.59 us
    ppermute x3, starting transfers between devices, swap_neighbours(): lax.ppermute(block, 'space', [(i, i + 1 if i % 2 else i - 1) for i in inn...  2.11 us
  transfers between devices with their start and end apart: 34, of which 6 were waited for; matrix products, arithmetic and copies ran while one was open for 0% of the time, Pallas kernels for 23%

profile of v1, /device:TPU:0, one launch (start us, length us, event | category | flops | bytes accessed | tf_op | source)
XLA Modules:
  0.0 72.2 jit_solution(8564515486153779650)
XLA Ops:
  0.6 0.9 %copy-done.1 = bf16[1,1,512,96]{2,3,1,0:T(8,128)(2,1)S(1)} copy-done((bf16[1,1,512,96]{2,3,1,0:T(8,128)(2,1)S(1)}, bf16[1,1,512,96]{2,3,1,0:T(8,128)(2,1)}, u32[]{:S(2)}) %copy-start.1) | copy-done | bytes 98328
  1.5 0.9 %copy-done.3 = bf16[1,1,512,96]{2,3,1,0:T(8,128)(2,1)S(1)} copy-done((bf16[1,1,512,96]{2,3,1,0:T(8,128)(2,1)S(1)}, bf16[1,1,512,96]{2,3,1,0:T(8,128)(2,1)}, u32[]{:S(2)}) %copy-start.3) | copy-done | bytes 98328
  4.7 4.4 %collective-permute-start.2 = (bf16[192,128]{1,0:T(8,128)(2,1)S(1)}, bf16[192,128]{1,0:T(8,128)(2,1)S(1)}, u32[]{:S(2)}, u32[]{:S(2)}) collective-permute-start(bf16[192,128]{1,0:T(8,128)(2,1)S(1)} %shard_map.113), channel_id=1, source_target_pairs={{0,4},{4,0},{8,12},{12,8},{16,20},{20,16},{24,28},{28,24},{1,5},{5... | collective-permute-start | bytes 147464 | tf_op jit(solution)/shard_map/ppermute | solution.py:242
  9.0 1.1 %copy-done.9 = bf16[27,96,96]{2,1,0:T(8,128)(2,1)S(1)} copy-done((bf16[27,96,96]{2,1,0:T(8,128)(2,1)S(1)}, bf16[27,96,96]{2,1,0:T(8,128)(2,1)}, u32[]{:S(2)}) %copy-start.9) | copy-done | bytes 497688
  10.1 0.9 %copy-done.10 = bf16[1,1,512,96]{2,3,1,0:T(8,128)(2,1)S(1)} copy-done((bf16[1,1,512,96]{2,3,1,0:T(8,128)(2,1)S(1)}, bf16[1,1,512,96]{2,3,1,0:T(8,128)(2,1)}, u32[]{:S(2)}) %copy-start.10) | copy-done | bytes 98328
  11.0 0.7 %copy-done.11 = s32[1,1,27,256]{3,1,2,0:T(1,128)S(1)} copy-done((s32[1,1,27,256]{3,1,2,0:T(1,128)S(1)}, s32[1,1,27,256]{3,1,2,0:T(1,128)}, u32[]{:S(2)}) %copy-start.11) | copy-done | bytes 27672
  12.5 5.7 %shard_map.112 = (bf16[2688,640]{1,0:T(8,128)(2,1)S(1)}, s32[27,1,640]{2,1,0:T(1,128)S(1)}, f32[96,512]{1,0:T(8,128)S(1)}, f32[96,128]{1,0:T(8,128)S(1)}) custom-call(s32[27,1,256]{2,1,0:T(1,128)S(1)} %bitcast.28, s32[27,1,256]{2,1,0:T(1,128)S(1)} %bitcast.29, bf16[96,512]{1,0:T(8,128)(2,1)S(1)} %bitcast.27, bf16[27,96,96]{2,1,0:T(8,128)(2,1)S(1)} %copy-done.9), custom_call_target="tpu_custom_call" | custom-call | flops 2017198080 | bytes 8388608 | tf_op jit(solution)/shard_map/pallas_call | solution.py:20
  18.3 0.8 %collective-permute-start.1 = (f32[96,128]{1,0:T(8,128)S(1)}, f32[96,128]{1,0:T(8,128)S(1)}, u32[]{:S(2)}, u32[]{:S(2)}) collective-permute-start(f32[96,128]{1,0:T(8,128)S(1)} %get-tuple-element.23), channel_id=1, source_target_pairs={{4,8},{8,4},{12,16},{16,12},{20,24},{24,20},{5,9},{9,5},{13,17},{1... | collective-permute-start | bytes 147464 | tf_op jit(solution)/shard_map/ppermute | solution.py:249
  19.1 2.9 %collective-permute-start = (f32[96,128]{1,0:T(8,128)S(1)}, f32[96,128]{1,0:T(8,128)S(1)}, u32[]{:S(2)}, u32[]{:S(2)}) collective-permute-start(f32[96,128]{1,0:T(8,128)S(1)} %get-tuple-element.23), channel_id=1, source_target_pairs={{0,4},{4,0},{8,12},{12,8},{16,20},{20,16},{24,28},{28,24},{1,5},{5... | collective-permute-start | bytes 147464 | tf_op jit(solution)/shard_map/ppermute | solution.py:242
  22.0 1.2 %shard_map.121 = (f32[1024,128]{1,0:T(8,128)S(1)}, bf16[1024,128]{1,0:T(8,128)(2,1)S(1)}) custom-call(bf16[96,512]{1,0:T(8,128)(2,1)S(1)} %bitcast.17, bf16[192,128]{1,0:T(8,128)(2,1)S(1)} %collective-permute-done.2.rnear_ref.near_ref, bf16[192,128]{1,0:T(8,128)(2,1)S(1)} %collective-permute-done.3.rfar_ref.far_ref, ...), custom_call_target="tpu_custom_call" | custom-call | flops 318504960 | bytes 6291456 | tf_op jit(solution)/shard_map/pallas_call | solution.py:20
  23.4 5.6 %shard_map.114 = (bf16[2688,640]{1,0:T(8,128)(2,1)S(1)}, f32[1024,128]{1,0:T(8,128)S(1)}, bf16[1024,128]{1,0:T(8,128)(2,1)S(1)}) custom-call(f32[96,512]{1,0:T(8,128)S(1)} %get-tuple-element.22.own_ref, f32[96,128]{1,0:T(8,128)S(1)} %collective-permute-done.near_ref, f32[96,128]{1,0:T(8,128)S(1)} %collective-permute-done.1.far_ref, s32[1,64]{1,0:T(1,128)S(1)} %bitcast.22, ...), custom_call_target="tpu_custom_call" | custom-call | flops 2017198080 | bytes 8388608 | tf_op jit(solution)/shard_map/pallas_call | solution.py:20
  29.6 2.5 %collective-permute-start.21 = (bf16[256,128]{1,0:T(8,128)(2,1)S(1)}, bf16[256,128]{1,0:T(8,128)(2,1)S(1)}, u32[]{:S(2)}, u32[]{:S(2)}) collective-permute-start(bf16[256,128]{1,0:T(8,128)(2,1)S(1)} %get-tuple-element.38), channel_id=1, source_target_pairs={{0,8},{4,12},{8,0},{12,4},{16,24},{20,28},{24,16},{28,20},{1,9},{5... | collective-permute-start | bytes 196616 | tf_op jit(solution)/shard_map/ppermute | solution.py:242
  32.2 1.4 %collective-permute-start.23 = (bf16[256,128]{1,0:T(8,128)(2,1)S(1)}, bf16[256,128]{1,0:T(8,128)(2,1)S(1)}, u32[]{:S(2)}, u32[]{:S(2)}) collective-permute-start(bf16[256,128]{1,0:T(8,128)(2,1)S(1)} %get-tuple-element.40), channel_id=1, source_target_pairs={{0,24},{4,28},{8,16},{12,20},{16,8},{20,12},{24,0},{28,4},{1,25},{... | collective-permute-start | bytes 196616 | tf_op jit(solution)/shard_map/ppermute | solution.py:242
  33.7 2.0 %collective-permute-start.7 = (bf16[256,128]{1,0:T(8,128)(2,1)S(1)}, bf16[256,128]{1,0:T(8,128)(2,1)S(1)}, u32[]{:S(2)}, u32[]{:S(2)}) collective-permute-start(bf16[256,128]{1,0:T(8,128)(2,1)S(1)} %get-tuple-element.31), channel_id=1, source_target_pairs={{0,8},{4,12},{8,0},{12,4},{16,24},{20,28},{24,16},{28,20},{1,9},{5... | collective-permute-start | bytes 196616 | tf_op jit(solution)/shard_map/ppermute | solution.py:242
  35.8 1.4 %collective-permute-start.9 = (bf16[256,128]{1,0:T(8,128)(2,1)S(1)}, bf16[256,128]{1,0:T(8,128)(2,1)S(1)}, u32[]{:S(2)}, u32[]{:S(2)}) collective-permute-start(bf16[256,128]{1,0:T(8,128)(2,1)S(1)} %get-tuple-element.33), channel_id=1, source_target_pairs={{0,24},{4,28},{8,16},{12,20},{16,8},{20,12},{24,0},{28,4},{1,25},{... | collective-permute-start | bytes 196616 | tf_op jit(solution)/shard_map/ppermute | solution.py:242
  38.0 3.7 %collective-permute-start.26 = (bf16[256,128]{1,0:T(8,128)(2,1)S(1)}, bf16[256,128]{1,0:T(8,128)(2,1)S(1)}, u32[]{:S(2)}, u32[]{:S(2)}) collective-permute-start(bf16[256,128]{1,0:T(8,128)(2,1)S(1)} %shard_map.123.refs_0_), channel_id=1, source_target_pairs={{0,3},{1,2},{2,1},{3,0},{4,7},{5,6},{6,5},{7,4},{8,11},{9,10},{10,... | collective-permute-start | bytes 196616 | tf_op jit(solution)/shard_map/ppermute | solution.py:242
  41.6 0.8 %collective-permute-start.24 = (bf16[256,128]{1,0:T(8,128)(2,1)S(1)}, bf16[256,128]{1,0:T(8,128)(2,1)S(1)}, u32[]{:S(2)}, u32[]{:S(2)}) collective-permute-start(bf16[256,128]{1,0:T(8,128)(2,1)S(1)} %shard_map.123.refs_0_), channel_id=1, source_target_pairs={{0,1},{1,0},{2,3},{3,2},{4,5},{5,4},{6,7},{7,6},{8,9},{9,8},{10,11... | collective-permute-start | bytes 196616 | tf_op jit(solution)/shard_map/ppermute | solution.py:242
  42.5 3.7 %collective-permute-start.12 = (bf16[256,128]{1,0:T(8,128)(2,1)S(1)}, bf16[256,128]{1,0:T(8,128)(2,1)S(1)}, u32[]{:S(2)}, u32[]{:S(2)}) collective-permute-start(bf16[256,128]{1,0:T(8,128)(2,1)S(1)} %shard_map.118.refs_0_), channel_id=1, source_target_pairs={{0,3},{1,2},{2,1},{3,0},{4,7},{5,6},{6,5},{7,4},{8,11},{9,10},{10,... | collective-permute-start | bytes 196616 | tf_op jit(solution)/shard_map/ppermute | solution.py:242
  46.1 0.8 %collective-permute-start.10 = (bf16[256,128]{1,0:T(8,128)(2,1)S(1)}, bf16[256,128]{1,0:T(8,128)(2,1)S(1)}, u32[]{:S(2)}, u32[]{:S(2)}) collective-permute-start(bf16[256,128]{1,0:T(8,128)(2,1)S(1)} %shard_map.118.refs_0_), channel_id=1, source_target_pairs={{0,1},{1,0},{2,3},{3,2},{4,5},{5,4},{6,7},{7,6},{8,9},{9,8},{10,11... | collective-permute-start | bytes 196616 | tf_op jit(solution)/shard_map/ppermute | solution.py:242
  46.9 1.0 %shard_map.115 = (f32[96,512]{1,0:T(8,128)S(1)}, f32[96,128]{1,0:T(8,128)S(1)}) custom-call(bf16[27,96,96]{2,1,0:T(8,128)(2,1)S(1)} %copy-done, bf16[2688,640]{1,0:T(8,128)(2,1)S(1)} %get-tuple-element.25.t_ref), custom_call_target="tpu_custom_call" | custom-call | flops 318504960 | bytes 6291456 | tf_op jit(solution)/shard_map/pallas_call | solution.py:20
  48.0 1.9 %collective-permute-done.25.refs_2_ = bf16[256,128]{1,0:T(8,128)(2,1)S(1)} collective-permute-done((bf16[256,128]{1,0:T(8,128)(2,1)S(1)}, bf16[256,128]{1,0:T(8,128)(2,1)S(1)}, u32[]{:S(2)}, u32[]{:S(2)}) %collective-permute-start.25) | collective-permute-done | bytes 65568 | tf_op jit(solution)/shard_map/ppermute | solution.py:242
  50.5 3.2 %collective-permute-start.32 = (bf16[256,128]{1,0:T(8,128)(2,1)S(1)}, bf16[256,128]{1,0:T(8,128)(2,1)S(1)}, u32[]{:S(2)}, u32[]{:S(2)}) collective-permute-start(bf16[256,128]{1,0:T(8,128)(2,1)S(1)} %shard_map.124.refs_0_), channel_id=1, source_target_pairs={{0,24},{4,28},{8,16},{12,20},{16,8},{20,12},{24,0},{28,4},{1,25},{... | collective-permute-start | bytes 196616 | tf_op jit(solution)/shard_map/ppermute | solution.py:242
  53.8 4.4 %collective-permute-start.30 = (bf16[256,128]{1,0:T(8,128)(2,1)S(1)}, bf16[256,128]{1,0:T(8,128)(2,1)S(1)}, u32[]{:S(2)}, u32[]{:S(2)}) collective-permute-start(bf16[256,128]{1,0:T(8,128)(2,1)S(1)} %shard_map.124.refs_0_), channel_id=1, source_target_pairs={{0,16},{4,20},{8,24},{12,28},{16,0},{20,4},{24,8},{28,12},{1,17},{... | collective-permute-start | bytes 196616 | tf_op jit(solution)/shard_map/ppermute | solution.py:242
  58.8 0.8 %collective-permute-done.4.near_ref = f32[96,128]{1,0:T(8,128)S(1)} collective-permute-done((f32[96,128]{1,0:T(8,128)S(1)}, f32[96,128]{1,0:T(8,128)S(1)}, u32[]{:S(2)}, u32[]{:S(2)}) %collective-permute-start.4) | collective-permute-done | bytes 49184 | tf_op jit(solution)/shard_map/ppermute | solution.py:242
  59.7 1.4 %collective-permute-start.18 = (bf16[256,128]{1,0:T(8,128)(2,1)S(1)}, bf16[256,128]{1,0:T(8,128)(2,1)S(1)}, u32[]{:S(2)}, u32[]{:S(2)}) collective-permute-start(bf16[256,128]{1,0:T(8,128)(2,1)S(1)} %shard_map.119.refs_0_), channel_id=1, source_target_pairs={{0,24},{4,28},{8,16},{12,20},{16,8},{20,12},{24,0},{28,4},{1,25},{... | collective-permute-start | bytes 196616 | tf_op jit(solution)/shard_map/ppermute | solution.py:242
  61.1 2.0 %collective-permute-start.16 = (bf16[256,128]{1,0:T(8,128)(2,1)S(1)}, bf16[256,128]{1,0:T(8,128)(2,1)S(1)}, u32[]{:S(2)}, u32[]{:S(2)}) collective-permute-start(bf16[256,128]{1,0:T(8,128)(2,1)S(1)} %shard_map.119.refs_0_), channel_id=1, source_target_pairs={{0,16},{4,20},{8,24},{12,28},{16,0},{20,4},{24,8},{28,12},{1,17},{... | collective-permute-start | bytes 196616 | tf_op jit(solution)/shard_map/ppermute | solution.py:242
  63.7 1.3 %collective-permute-done.18.refs_6_ = bf16[256,128]{1,0:T(8,128)(2,1)S(1)} collective-permute-done((bf16[256,128]{1,0:T(8,128)(2,1)S(1)}, bf16[256,128]{1,0:T(8,128)(2,1)S(1)}, u32[]{:S(2)}, u32[]{:S(2)}) %collective-permute-start.18) | collective-permute-done | bytes 65568 | tf_op jit(solution)/shard_map/ppermute | solution.py:242
  65.0 1.3 %collective-permute-done.16.refs_4_ = bf16[256,128]{1,0:T(8,128)(2,1)S(1)} collective-permute-done((bf16[256,128]{1,0:T(8,128)(2,1)S(1)}, bf16[256,128]{1,0:T(8,128)(2,1)S(1)}, u32[]{:S(2)}, u32[]{:S(2)}) %collective-permute-start.16) | collective-permute-done | bytes 65568 | tf_op jit(solution)/shard_map/ppermute | solution.py:242
  66.4 1.0 %collective-permute-done.14.refs_2_ = bf16[256,128]{1,0:T(8,128)(2,1)S(1)} collective-permute-done((bf16[256,128]{1,0:T(8,128)(2,1)S(1)}, bf16[256,128]{1,0:T(8,128)(2,1)S(1)}, u32[]{:S(2)}, u32[]{:S(2)}) %collective-permute-start.14) | collective-permute-done | bytes 65568 | tf_op jit(solution)/shard_map/ppermute | solution.py:242
  67.9 0.9 %shard_map.116 = bf16[96,512]{1,0:T(8,128)(2,1)} custom-call(f32[96,512]{1,0:T(8,128)S(1)} %get-tuple-element.26.own_ref, f32[96,128]{1,0:T(8,128)S(1)} %collective-permute-done.4.near_ref, f32[96,128]{1,0:T(8,128)S(1)} %collective-permute-done.5.far_ref, s32[1,64]{1,0:T(1,128)S(1)} %bitcast.23, s32[1,64]{1,0:T(1,128)S(1)} %bitcast.26), custom_call_target="tpu_custom_call" | custom-call | tf_op jit(solution)/shard_map/pallas_call | solution.py:20
  68.9 1.6 %shard_map.125 = f32[27,96,96]{2,1,0:T(8,128)} custom-call(bf16[256,128]{1,0:T(8,128)(2,1)S(1)} %shard_map.124.refs_0_, bf16[256,128]{1,0:T(8,128)(2,1)S(1)} %collective-permute-done.27.refs_1_, bf16[256,128]{1,0:T(8,128)(2,1)S(1)} %collective-permute-done.28.refs_2_, bf16[256,128]{1,0:T(8,128)(2,1)S(1)} %collective-permute-done.29.refs_3_, ...), custom_call_target="tpu_custom_call" | custom-call | tf_op jit(solution)/shard_map/pallas_call | solution.py:20
  70.5 1.6 %shard_map.120 = f32[27,96,96]{2,1,0:T(8,128)} custom-call(bf16[256,128]{1,0:T(8,128)(2,1)S(1)} %shard_map.119.refs_0_, bf16[256,128]{1,0:T(8,128)(2,1)S(1)} %collective-permute-done.13.refs_1_, bf16[256,128]{1,0:T(8,128)(2,1)S(1)} %collective-permute-done.14.refs_2_, bf16[256,128]{1,0:T(8,128)(2,1)S(1)} %collective-permute-done.15.refs_3_, ...), custom_call_target="tpu_custom_call" | custom-call | tf_op jit(solution)/shard_map/pallas_call | solution.py:20
  (76 shorter events, 7.4 us)
Async XLA Ops:
  4.0 18.0 %collective-permute-start.3 = (bf16[192,128]{1,0:T(8,128)(2,1)S(1)}, bf16[192,128]{1,0:T(8,128)(2,1)S(1)}, u32[]{:S(2)}, u32[]{:S(2)}) collective-permute-start(bf16[192,128]{1,0:T(8,128)(2,1)S(1)} %shard_map.113), channel_id=1, source_target_pairs={{4,8},{8,4},{12,16},{16,12},{20,24},{24,20},{5,9},{9,5},{13,17},{1... | collective-permute-start | bytes 147464 | tf_op jit(solution)/shard_map/ppermute | solution.py:249
  4.7 17.4 %collective-permute-start.2 = (bf16[192,128]{1,0:T(8,128)(2,1)S(1)}, bf16[192,128]{1,0:T(8,128)(2,1)S(1)}, u32[]{:S(2)}, u32[]{:S(2)}) collective-permute-start(bf16[192,128]{1,0:T(8,128)(2,1)S(1)} %shard_map.113), channel_id=1, source_target_pairs={{0,4},{4,0},{8,12},{12,8},{16,20},{20,16},{24,28},{28,24},{1,5},{5... | collective-permute-start | bytes 147464 | tf_op jit(solution)/shard_map/ppermute | solution.py:242
  18.3 5.0 %collective-permute-start.1 = (f32[96,128]{1,0:T(8,128)S(1)}, f32[96,128]{1,0:T(8,128)S(1)}, u32[]{:S(2)}, u32[]{:S(2)}) collective-permute-start(f32[96,128]{1,0:T(8,128)S(1)} %get-tuple-element.23), channel_id=1, source_target_pairs={{4,8},{8,4},{12,16},{16,12},{20,24},{24,20},{5,9},{9,5},{13,17},{1... | collective-permute-start | bytes 147464 | tf_op jit(solution)/shard_map/ppermute | solution.py:249
  19.1 4.2 %collective-permute-start = (f32[96,128]{1,0:T(8,128)S(1)}, f32[96,128]{1,0:T(8,128)S(1)}, u32[]{:S(2)}, u32[]{:S(2)}) collective-permute-start(f32[96,128]{1,0:T(8,128)S(1)} %get-tuple-element.23), channel_id=1, source_target_pairs={{0,4},{4,0},{8,12},{12,8},{16,20},{20,16},{24,28},{28,24},{1,5},{5... | collective-permute-start | bytes 147464 | tf_op jit(solution)/shard_map/ppermute | solution.py:242
  23.2 6.3 %collective-permute-start.20 = (bf16[1024,128]{1,0:T(8,128)(2,1)S(1)}, bf16[1024,128]{1,0:T(8,128)(2,1)S(1)}, u32[]{:S(2)}, u32[]{:S(2)}) collective-permute-start(bf16[1024,128]{1,0:T(8,128)(2,1)S(1)} %get-tuple-element.36), channel_id=1, source_target_pairs={{0,4},{4,0},{8,12},{12,8},{16,20},{20,16},{24,28},{28,24},{1,5},{5... | collective-permute-start | bytes 786440 | tf_op jit(solution)/shard_map/ppermute | solution.py:242
  28.9 4.7 %collective-permute-start.6 = (bf16[1024,128]{1,0:T(8,128)(2,1)S(1)}, bf16[1024,128]{1,0:T(8,128)(2,1)S(1)}, u32[]{:S(2)}, u32[]{:S(2)}) collective-permute-start(bf16[1024,128]{1,0:T(8,128)(2,1)S(1)} %get-tuple-element.29), channel_id=1, source_target_pairs={{0,4},{4,0},{8,12},{12,8},{16,20},{20,16},{24,28},{28,24},{1,5},{5... | collective-permute-start | bytes 786440 | tf_op jit(solution)/shard_map/ppermute | solution.py:242
  29.6 6.2 %collective-permute-start.21 = (bf16[256,128]{1,0:T(8,128)(2,1)S(1)}, bf16[256,128]{1,0:T(8,128)(2,1)S(1)}, u32[]{:S(2)}, u32[]{:S(2)}) collective-permute-start(bf16[256,128]{1,0:T(8,128)(2,1)S(1)} %get-tuple-element.38), channel_id=1, source_target_pairs={{0,8},{4,12},{8,0},{12,4},{16,24},{20,28},{24,16},{28,20},{1,9},{5... | collective-permute-start | bytes 196616 | tf_op jit(solution)/shard_map/ppermute | solution.py:242
  32.1 5.9 %collective-permute-start.22 = (bf16[256,128]{1,0:T(8,128)(2,1)S(1)}, bf16[256,128]{1,0:T(8,128)(2,1)S(1)}, u32[]{:S(2)}, u32[]{:S(2)}) collective-permute-start(bf16[256,128]{1,0:T(8,128)(2,1)S(1)} %get-tuple-element.39), channel_id=1, source_target_pairs={{0,16},{4,20},{8,24},{12,28},{16,0},{20,4},{24,8},{28,12},{1,17},{... | collective-permute-start | bytes 196616 | tf_op jit(solution)/shard_map/ppermute | solution.py:242
  32.2 5.8 %collective-permute-start.23 = (bf16[256,128]{1,0:T(8,128)(2,1)S(1)}, bf16[256,128]{1,0:T(8,128)(2,1)S(1)}, u32[]{:S(2)}, u32[]{:S(2)}) collective-permute-start(bf16[256,128]{1,0:T(8,128)(2,1)S(1)} %get-tuple-element.40), channel_id=1, source_target_pairs={{0,24},{4,28},{8,16},{12,20},{16,8},{20,12},{24,0},{28,4},{1,25},{... | collective-permute-start | bytes 196616 | tf_op jit(solution)/shard_map/ppermute | solution.py:242
  33.7 8.0 %collective-permute-start.7 = (bf16[256,128]{1,0:T(8,128)(2,1)S(1)}, bf16[256,128]{1,0:T(8,128)(2,1)S(1)}, u32[]{:S(2)}, u32[]{:S(2)}) collective-permute-start(bf16[256,128]{1,0:T(8,128)(2,1)S(1)} %get-tuple-element.31), channel_id=1, source_target_pairs={{0,8},{4,12},{8,0},{12,4},{16,24},{20,28},{24,16},{28,20},{1,9},{5... | collective-permute-start | bytes 196616 | tf_op jit(solution)/shard_map/ppermute | solution.py:242
  35.7 6.7 %collective-permute-start.8 = (bf16[256,128]{1,0:T(8,128)(2,1)S(1)}, bf16[256,128]{1,0:T(8,128)(2,1)S(1)}, u32[]{:S(2)}, u32[]{:S(2)}) collective-permute-start(bf16[256,128]{1,0:T(8,128)(2,1)S(1)} %get-tuple-element.32), channel_id=1, source_target_pairs={{0,16},{4,20},{8,24},{12,28},{16,0},{20,4},{24,8},{28,12},{1,17},{... | collective-permute-start | bytes 196616 | tf_op jit(solution)/shard_map/ppermute | solution.py:242
  35.8 6.6 %collective-permute-start.9 = (bf16[256,128]{1,0:T(8,128)(2,1)S(1)}, bf16[256,128]{1,0:T(8,128)(2,1)S(1)}, u32[]{:S(2)}, u32[]{:S(2)}) collective-permute-start(bf16[256,128]{1,0:T(8,128)(2,1)S(1)} %get-tuple-element.33), channel_id=1, source_target_pairs={{0,24},{4,28},{8,16},{12,20},{16,8},{20,12},{24,0},{28,4},{1,25},{... | collective-permute-start | bytes 196616 | tf_op jit(solution)/shard_map/ppermute | solution.py:242
  38.0 8.2 %collective-permute-start.26 = (bf16[256,128]{1,0:T(8,128)(2,1)S(1)}, bf16[256,128]{1,0:T(8,128)(2,1)S(1)}, u32[]{:S(2)}, u32[]{:S(2)}) collective-permute-start(bf16[256,128]{1,0:T(8,128)(2,1)S(1)} %shard_map.123.refs_0_), channel_id=1, source_target_pairs={{0,3},{1,2},{2,1},{3,0},{4,7},{5,6},{6,5},{7,4},{8,11},{9,10},{10,... | collective-permute-start | bytes 196616 | tf_op jit(solution)/shard_map/ppermute | solution.py:242
  41.6 8.2 %collective-permute-start.25 = (bf16[256,128]{1,0:T(8,128)(2,1)S(1)}, bf16[256,128]{1,0:T(8,128)(2,1)S(1)}, u32[]{:S(2)}, u32[]{:S(2)}) collective-permute-start(bf16[256,128]{1,0:T(8,128)(2,1)S(1)} %shard_map.123.refs_0_), channel_id=1, source_target_pairs={{0,2},{1,3},{2,0},{3,1},{4,6},{5,7},{6,4},{7,5},{8,10},{9,11},{10,... | collective-permute-start | bytes 196616 | tf_op jit(solution)/shard_map/ppermute | solution.py:242
  41.6 8.9 %collective-permute-start.24 = (bf16[256,128]{1,0:T(8,128)(2,1)S(1)}, bf16[256,128]{1,0:T(8,128)(2,1)S(1)}, u32[]{:S(2)}, u32[]{:S(2)}) collective-permute-start(bf16[256,128]{1,0:T(8,128)(2,1)S(1)} %shard_map.123.refs_0_), channel_id=1, source_target_pairs={{0,1},{1,0},{2,3},{3,2},{4,5},{5,4},{6,7},{7,6},{8,9},{9,8},{10,11... | collective-permute-start | bytes 196616 | tf_op jit(solution)/shard_map/ppermute | solution.py:242
  42.5 15.7 %collective-permute-start.12 = (bf16[256,128]{1,0:T(8,128)(2,1)S(1)}, bf16[256,128]{1,0:T(8,128)(2,1)S(1)}, u32[]{:S(2)}, u32[]{:S(2)}) collective-permute-start(bf16[256,128]{1,0:T(8,128)(2,1)S(1)} %shard_map.118.refs_0_), channel_id=1, source_target_pairs={{0,3},{1,2},{2,1},{3,0},{4,7},{5,6},{6,5},{7,4},{8,11},{9,10},{10,... | collective-permute-start | bytes 196616 | tf_op jit(solution)/shard_map/ppermute | solution.py:242
  46.1 12.1 %collective-permute-start.11 = (bf16[256,128]{1,0:T(8,128)(2,1)S(1)}, bf16[256,128]{1,0:T(8,128)(2,1)S(1)}, u32[]{:S(2)}, u32[]{:S(2)}) collective-permute-start(bf16[256,128]{1,0:T(8,128)(2,1)S(1)} %shard_map.118.refs_0_), channel_id=1, source_target_pairs={{0,2},{1,3},{2,0},{3,1},{4,6},{5,7},{6,4},{7,5},{8,10},{9,11},{10,... | collective-permute-start | bytes 196616 | tf_op jit(solution)/shard_map/ppermute | solution.py:242
  46.1 12.2 %collective-permute-start.10 = (bf16[256,128]{1,0:T(8,128)(2,1)S(1)}, bf16[256,128]{1,0:T(8,128)(2,1)S(1)}, u32[]{:S(2)}, u32[]{:S(2)}) collective-permute-start(bf16[256,128]{1,0:T(8,128)(2,1)S(1)} %shard_map.118.refs_0_), channel_id=1, source_target_pairs={{0,1},{1,0},{2,3},{3,2},{4,5},{5,4},{6,7},{7,6},{8,9},{9,8},{10,11... | collective-permute-start | bytes 196616 | tf_op jit(solution)/shard_map/ppermute | solution.py:242
  49.8 3.9 %collective-permute-start.5 = (f32[96,128]{1,0:T(8,128)S(1)}, f32[96,128]{1,0:T(8,128)S(1)}, u32[]{:S(2)}, u32[]{:S(2)}) collective-permute-start(f32[96,128]{1,0:T(8,128)S(1)} %get-tuple-element.27), channel_id=1, source_target_pairs={{4,8},{8,4},{12,16},{16,12},{20,24},{24,20},{5,9},{9,5},{13,17},{1... | collective-permute-start | bytes 147464 | tf_op jit(solution)/shard_map/ppermute | solution.py:249
  50.5 10.5 %collective-permute-start.32 = (bf16[256,128]{1,0:T(8,128)(2,1)S(1)}, bf16[256,128]{1,0:T(8,128)(2,1)S(1)}, u32[]{:S(2)}, u32[]{:S(2)}) collective-permute-start(bf16[256,128]{1,0:T(8,128)(2,1)S(1)} %shard_map.124.refs_0_), channel_id=1, source_target_pairs={{0,24},{4,28},{8,16},{12,20},{16,8},{20,12},{24,0},{28,4},{1,25},{... | collective-permute-start | bytes 196616 | tf_op jit(solution)/shard_map/ppermute | solution.py:242
  53.8 9.3 %collective-permute-start.30 = (bf16[256,128]{1,0:T(8,128)(2,1)S(1)}, bf16[256,128]{1,0:T(8,128)(2,1)S(1)}, u32[]{:S(2)}, u32[]{:S(2)}) collective-permute-start(bf16[256,128]{1,0:T(8,128)(2,1)S(1)} %shard_map.124.refs_0_), channel_id=1, source_target_pairs={{0,16},{4,20},{8,24},{12,28},{16,0},{20,4},{24,8},{28,12},{1,17},{... | collective-permute-start | bytes 196616 | tf_op jit(solution)/shard_map/ppermute | solution.py:242
  58.2 5.0 %collective-permute-start.28 = (bf16[256,128]{1,0:T(8,128)(2,1)S(1)}, bf16[256,128]{1,0:T(8,128)(2,1)S(1)}, u32[]{:S(2)}, u32[]{:S(2)}) collective-permute-start(bf16[256,128]{1,0:T(8,128)(2,1)S(1)} %shard_map.124.refs_0_), channel_id=1, source_target_pairs={{0,8},{4,12},{8,0},{12,4},{16,24},{20,28},{24,16},{28,20},{1,9},{5... | collective-permute-start | bytes 196616 | tf_op jit(solution)/shard_map/ppermute | solution.py:242
  58.2 5.0 %collective-permute-start.27 = (bf16[256,128]{1,0:T(8,128)(2,1)S(1)}, bf16[256,128]{1,0:T(8,128)(2,1)S(1)}, u32[]{:S(2)}, u32[]{:S(2)}) collective-permute-start(bf16[256,128]{1,0:T(8,128)(2,1)S(1)} %shard_map.124.refs_0_), channel_id=1, source_target_pairs={{0,4},{4,0},{8,12},{12,8},{16,20},{20,16},{24,28},{28,24},{1,5},{5... | collective-permute-start | bytes 196616 | tf_op jit(solution)/shard_map/ppermute | solution.py:242
  59.7 5.3 %collective-permute-start.18 = (bf16[256,128]{1,0:T(8,128)(2,1)S(1)}, bf16[256,128]{1,0:T(8,128)(2,1)S(1)}, u32[]{:S(2)}, u32[]{:S(2)}) collective-permute-start(bf16[256,128]{1,0:T(8,128)(2,1)S(1)} %shard_map.119.refs_0_), channel_id=1, source_target_pairs={{0,24},{4,28},{8,16},{12,20},{16,8},{20,12},{24,0},{28,4},{1,25},{... | collective-permute-start | bytes 196616 | tf_op jit(solution)/shard_map/ppermute | solution.py:242
  61.1 5.3 %collective-permute-start.16 = (bf16[256,128]{1,0:T(8,128)(2,1)S(1)}, bf16[256,128]{1,0:T(8,128)(2,1)S(1)}, u32[]{:S(2)}, u32[]{:S(2)}) collective-permute-start(bf16[256,128]{1,0:T(8,128)(2,1)S(1)} %shard_map.119.refs_0_), channel_id=1, source_target_pairs={{0,16},{4,20},{8,24},{12,28},{16,0},{20,4},{24,8},{28,12},{1,17},{... | collective-permute-start | bytes 196616 | tf_op jit(solution)/shard_map/ppermute | solution.py:242
  63.1 4.3 %collective-permute-start.14 = (bf16[256,128]{1,0:T(8,128)(2,1)S(1)}, bf16[256,128]{1,0:T(8,128)(2,1)S(1)}, u32[]{:S(2)}, u32[]{:S(2)}) collective-permute-start(bf16[256,128]{1,0:T(8,128)(2,1)S(1)} %shard_map.119.refs_0_), channel_id=1, source_target_pairs={{0,8},{4,12},{8,0},{12,4},{16,24},{20,28},{24,16},{28,20},{1,9},{5... | collective-permute-start | bytes 196616 | tf_op jit(solution)/shard_map/ppermute | solution.py:242
  63.2 4.2 %collective-permute-start.33 = (bf16[256,128]{1,0:T(8,128)(2,1)S(1)}, bf16[256,128]{1,0:T(8,128)(2,1)S(1)}, u32[]{:S(2)}, u32[]{:S(2)}) collective-permute-start(bf16[256,128]{1,0:T(8,128)(2,1)S(1)} %collective-permute-done.32.refs_6_), channel_id=1, source_target_pairs={{0,4},{4,0},{8,12},{12,8},{16,20},{20,16},{24,28},{28,24},{1,5},{5... | collective-permute-start | bytes 196616 | tf_op jit(solution)/shard_map/ppermute | solution.py:242
  63.2 4.7 %collective-permute-start.31 = (bf16[256,128]{1,0:T(8,128)(2,1)S(1)}, bf16[256,128]{1,0:T(8,128)(2,1)S(1)}, u32[]{:S(2)}, u32[]{:S(2)}) collective-permute-start(bf16[256,128]{1,0:T(8,128)(2,1)S(1)} %collective-permute-done.30.refs_4_), channel_id=1, source_target_pairs={{0,4},{4,0},{8,12},{12,8},{16,20},{20,16},{24,28},{28,24},{1,5},{5... | collective-permute-start | bytes 196616 | tf_op jit(solution)/shard_map/ppermute | solution.py:242
  65.0 5.5 %collective-permute-start.13 = (bf16[256,128]{1,0:T(8,128)(2,1)S(1)}, bf16[256,128]{1,0:T(8,128)(2,1)S(1)}, u32[]{:S(2)}, u32[]{:S(2)}) collective-permute-start(bf16[256,128]{1,0:T(8,128)(2,1)S(1)} %shard_map.119.refs_0_), channel_id=1, source_target_pairs={{0,4},{4,0},{8,12},{12,8},{16,20},{20,16},{24,28},{28,24},{1,5},{5... | collective-permute-start | bytes 196616 | tf_op jit(solution)/shard_map/ppermute | solution.py:242
  67.4 3.2 %collective-permute-start.19 = (bf16[256,128]{1,0:T(8,128)(2,1)S(1)}, bf16[256,128]{1,0:T(8,128)(2,1)S(1)}, u32[]{:S(2)}, u32[]{:S(2)}) collective-permute-start(bf16[256,128]{1,0:T(8,128)(2,1)S(1)} %collective-permute-done.18.refs_6_), channel_id=1, source_target_pairs={{0,4},{4,0},{8,12},{12,8},{16,20},{20,16},{24,28},{28,24},{1,5},{5... | collective-permute-start | bytes 196616 | tf_op jit(solution)/shard_map/ppermute | solution.py:242
  67.4 3.2 %collective-permute-start.17 = (bf16[256,128]{1,0:T(8,128)(2,1)S(1)}, bf16[256,128]{1,0:T(8,128)(2,1)S(1)}, u32[]{:S(2)}, u32[]{:S(2)}) collective-permute-start(bf16[256,128]{1,0:T(8,128)(2,1)S(1)} %collective-permute-done.16.refs_4_), channel_id=1, source_target_pairs={{0,4},{4,0},{8,12},{12,8},{16,20},{20,16},{24,28},{28,24},{1,5},{5... | collective-permute-start | bytes 196616 | tf_op jit(solution)/shard_map/ppermute | solution.py:242
  67.9 2.7 %collective-permute-start.15 = (bf16[256,128]{1,0:T(8,128)(2,1)S(1)}, bf16[256,128]{1,0:T(8,128)(2,1)S(1)}, u32[]{:S(2)}, u32[]{:S(2)}) collective-permute-start(bf16[256,128]{1,0:T(8,128)(2,1)S(1)} %collective-permute-done.14.refs_2_), channel_id=1, source_target_pairs={{0,4},{4,0},{8,12},{12,8},{16,20},{20,16},{24,28},{28,24},{1,5},{5... | collective-permute-start | bytes 196616 | tf_op jit(solution)/shard_map/ppermute | solution.py:242
  (15 other events, 58.8 us)

commit v2 on v1

v2 whole, which is shorter than its diff:
```python
import functools

import jax
import jax.numpy as jnp
from jax import lax
from jax.experimental import pallas as pl
from jax.experimental.pallas import tpu as pltpu
from jax.sharding import PartitionSpec as P

F32, BF16, I32 = jnp.float32, jnp.bfloat16, jnp.int32
VMEM = pl.BlockSpec(memory_space=pltpu.VMEM)
HBM = pl.BlockSpec(memory_space=pltpu.HBM)
LANES = 128
BLOCK = 256
WHOLE = 62 << 20
UNROLL = 9
NT = (((1,), (1,)), ((), ()))


def call(body, outs, args, scratch=(), flops=0, moved=0, args_in=VMEM, outs_in=VMEM, room=40 << 20):
    single = not isinstance(outs, (list, tuple))
    return pl.pallas_call(
        body,
        out_shape=outs if single else tuple(outs),
        in_specs=[args_in] * len(args),
        out_specs=outs_in if single or isinstance(outs_in, tuple) else (outs_in,) * len(outs),
        scratch_shapes=scratch,
        compiler_params=pltpu.CompilerParams(vmem_limit_bytes=room),
        cost_estimate=pl.CostEstimate(flops=flops, bytes_accessed=moved, transcendentals=0),
    )(*args)


def shape(dims, dtype):
    return jax.ShapeDtypeStruct(dims, dtype)


def loop(steps, body):
    unroll = next(u for u in range(UNROLL, 0, -1) if steps % u == 0)

    def step(i, carry):
        body(i)
        return carry

    lax.fori_loop(0, steps, step, 0, unroll=unroll)


def one_hot(rows, index):
    count = lax.broadcasted_iota(I32, (min(rows, BLOCK), index.shape[1]), 0).astype(F32).astype(BF16)
    blocks = []
    for start in range(0, rows, BLOCK):
        wanted = (index - start).astype(F32).astype(BF16)
        hit = count[: min(BLOCK, rows - start)] == wanted
        blocks.append(jnp.where(hit, jnp.ones((), BF16), jnp.zeros((), BF16)))
    return jnp.concatenate(blocks, 0)


def dot(a, b):
    return jnp.dot(a, b, preferred_element_type=F32)


def dot_nt(a, b):
    return lax.dot_general(a, b, NT, preferred_element_type=F32)


def offset_rows(k, chans):
    return pl.ds(pl.multiple_of(k * chans, chans), chans)


def rim_index(hi_ref, lo_ref):
    return jnp.concatenate([hi_ref[...], lo_ref[...]], 1)


def first_half(dims, own_parity):
    lane = lax.broadcasted_iota(I32, dims, 1)
    return (lane < dims[1] // 2) == own_parity


def is_even():
    return lax.rem(lax.axis_index("space"), 2) == 0


def add_back(weight_ref, t_ref, total_ref):
    count, chans = weight_ref.shape[0], weight_ref.shape[1]
    total_ref[...] = jnp.zeros_like(total_ref)

    def body(g):
        part = None
        for j in range(3):
            k = g * 3 + j
            term = dot(weight_ref[k], t_ref[offset_rows(k, chans), :])
            part = term if part is None else part + term
        total_ref[...] += part

    assert count % 3 == 0
    loop(count // 3, body)


def split_parts(value):
    high = value.astype(BF16)
    return high, (value - high.astype(F32)).astype(BF16)


def two_body(*refs):
    operands, (t_out, own_ref, edge_ref), scratch = refs[:8], refs[8:11], refs[11:]
    locals_, (t_ref, c_ref, total_ref, sems) = scratch[:8], scratch[8:]
    copies = [
        pltpu.make_async_copy(operand, local, sems.at[i]) for i, (operand, local) in enumerate(zip(operands, locals_, strict=True))
    ]
    for copy in copies:
        copy.start()
    outs_ref, cot_ref, ins_ref, weight_ref, hi_ref, lo_ref, zero_ref, pre_ref = locals_
    count, pairs = ins_ref.shape[0], ins_ref.shape[2]
    chans, rows = cot_ref.shape
    ext = t_ref.shape[1]
    tall = chans + 16
    row = lax.broadcasted_iota(I32, (16, pairs), 0)
    t_ref[count * chans :, :] = jnp.zeros((t_ref.shape[0] - count * chans, ext), BF16)

    def pick_outs(k):
        index = outs_ref[k]
        base = pl.multiple_of(k * tall, 16)
        c_ref[pl.ds(base, chans), :] = dot(cot_ref[...], one_hot(rows, index)).astype(BF16)
        left = rows - index
        code = jnp.where(row == 0, left // 16, jnp.where(row == 1, left % 16, 0))
        c_ref[pl.ds(base + chans, 16), :] = code.astype(F32).astype(BF16)

    copies[0].wait()
    copies[1].wait()
    loop(count, pick_outs)

    def put_ins(k):
        picked = c_ref[pl.ds(pl.multiple_of(k * tall, 16), tall), :]
        placed = dot_nt(picked, one_hot(ext, ins_ref[k]))
        t_ref[offset_rows(k, chans), :] = placed[:chans].astype(BF16)
        code = placed[chans : chans + 1] * 16.0 + placed[chans + 1 : chans + 2]
        own_ref[pl.ds(chans + k, 1), :] = rows - code

    copies[2].wait()
    loop(count, put_ins)
    stored = pltpu.make_async_copy(t_ref, t_out, sems.at[len(operands)])
    stored.start()
    copies[3].wait()
    add_back(weight_ref, t_ref, total_ref)
    own_ref[:chans] = total_ref[...]
    for i, part in enumerate(split_parts(total_ref[:, rows:])):
        edge_ref[i * chans : (i + 1) * chans] = part
    for copy in copies[4:]:
        copy.wait()
    pick = one_hot(rows, rim_index(hi_ref, lo_ref))
    one = jnp.maximum(pre_ref[...], jnp.zeros_like(pre_ref))
    edge_ref[2 * chans : 3 * chans] = dot(zero_ref[...], pick).astype(BF16)
    edge_ref[3 * chans :] = dot(one, pick).astype(BF16)
    stored.wait()


def weight_sums(ext, t_ref, sum_ref, keep_ref, send_ref):
    chans = ext.shape[0]
    tiles = t_ref.shape[0] // LANES
    for start in range(0, tiles, 2):
        width = min(2, tiles - start)
        grad = dot_nt(ext, t_ref[start * LANES : (start + width) * LANES, :])
        for j in range(width):
            sum_ref[(start + j) * chans : (start + j + 1) * chans, :] = grad[:, j * LANES : (j + 1) * LANES]
    sum_ref[tiles * chans :, :] = jnp.zeros((sum_ref.shape[0] - tiles * chans, LANES), F32)
    me = lax.axis_index("space")
    slots = lax.axis_size("space") // 2
    rows = keep_ref.shape[0] // slots
    for slot in range(slots):
        for out_ref, bit in ((keep_ref, 0), (send_ref, 1)):
            piece = jnp.bitwise_xor(me, 2 * slot + bit)
            block = sum_ref[pl.ds(pl.multiple_of(piece * rows, rows), rows), :]
            out_ref[slot * rows : (slot + 1) * rows, :] = block.astype(out_ref.dtype)


def two_weights_body(pre_ref, near_ref, far_ref, t_ref, keep_ref, send_ref, sum_ref):
    chans = pre_ref.shape[0]
    one = jnp.maximum(pre_ref[...], jnp.zeros_like(pre_ref))
    ext = extended(one, near_ref[3 * chans :].astype(F32), far_ref[3 * chans :].astype(F32))
    weight_sums(ext, t_ref, sum_ref, keep_ref, send_ref)


def extended(feats, near, far):
    rim = jnp.where(first_half(near.shape, is_even()), far, near).astype(feats.dtype)
    return jnp.concatenate([feats, rim], 1)


def settled(own, near, far, hi_ref, lo_ref):
    chans = own.shape[0]
    part = jnp.where(first_half(near.shape, is_even()), near.astype(F32), far.astype(F32)).astype(BF16)
    place = one_hot(own.shape[1], rim_index(hi_ref, lo_ref))
    moved = dot_nt(part, place)
    return own + moved[:chans] + moved[chans:]


def one_body(count, own_ref, near_ref, far_ref, hi_ref, lo_ref, pre_ref, zero_ref, t_ref, keep_ref, send_ref, cot_ref, sum_ref):
    chans, rows = pre_ref.shape
    ext = own_ref.shape[1]
    back = settled(own_ref[:chans, :rows], near_ref[: 2 * chans], far_ref[: 2 * chans], hi_ref, lo_ref)
    cot_ref[...] = jnp.where(pre_ref[...].astype(F32) > 0, back, 0.0).astype(BF16)

    def place(k):
        t_ref[offset_rows(k, chans), :] = dot(cot_ref[...], one_hot(rows, own_ref[pl.ds(chans + k, 1), :])).astype(BF16)

    loop(count, place)
    t_ref[count * chans :, :] = jnp.zeros((t_ref.shape[0] - count * chans, ext), BF16)
    rim = slice(2 * chans, 3 * chans)
    feats = extended(zero_ref[...], near_ref[rim].astype(F32), far_ref[rim].astype(F32))
    weight_sums(feats, t_ref, sum_ref, keep_ref, send_ref)


def back_body(weight_ref, t_ref, own_ref, edge_ref, total_ref):
    chans, rows = own_ref.shape
    add_back(weight_ref, t_ref, total_ref)
    own_ref[...] = total_ref[:, :rows]
    for i, part in enumerate(split_parts(total_ref[:, rows:])):
        edge_ref[i * chans : (i + 1) * chans] = part


def settle_body(own_ref, near_ref, far_ref, hi_ref, lo_ref, out_ref):
    out_ref[...] = settled(own_ref[...], near_ref[...], far_ref[...], hi_ref, lo_ref).astype(BF16)


def core_sum_body(layers, *refs):
    ins, (own_ref, *send_refs) = refs[: 2 * layers], refs[2 * layers :]
    rows = own_ref.shape[0] // layers
    for layer in range(layers):
        keep_ref, got_ref = ins[2 * layer : 2 * layer + 2]
        there = slice(layer * rows, (layer + 1) * rows)
        own_ref[there] = keep_ref[:rows] + got_ref[:rows].astype(F32)
        for slot, send_ref in enumerate(send_refs, 1):
            part = slice(slot * rows, (slot + 1) * rows)
            send_ref[there] = (keep_ref[part] + got_ref[part].astype(F32)).astype(BF16)


def chip_sum_body(own_ref, *refs):
    total = own_ref[...]
    for got_ref in refs[:-1]:
        total = total + got_ref[...].astype(F32)
    refs[-1][...] = total.astype(BF16)


def scan_sum_body(*refs):
    terms = [ref[...].astype(F32) for ref in refs[:-1]]
    while len(terms) > 1:
        terms = [a + b for a, b in zip(terms[::2], terms[1::2], strict=True)]
    refs[-1][...] = terms[0].astype(BF16)


def unpack_body(scale, layers, *refs):
    *refs, all_ref, sems = refs
    piece_refs, outs, locals_ = refs[: -2 * layers], refs[-2 * layers : -layers], refs[-layers:]
    me = lax.axis_index("space")
    rows = piece_refs[0].shape[0] // layers
    count, chans = locals_[0].shape[0], locals_[0].shape[1]
    lane = lax.broadcasted_iota(I32, (chans, LANES), 1)
    copies = []
    for layer in range(layers):
        for slot, piece_ref in enumerate(piece_refs):
            piece = jnp.bitwise_xor(me, slot)
            block = piece_ref[layer * rows : (layer + 1) * rows].astype(F32)
            all_ref[pl.ds(pl.multiple_of(piece * rows, rows), rows), :] = block
        for k in range(count):
            tile, shift = divmod(k * chans, LANES)
            block = all_ref[tile * chans : (tile + 1) * chans, :]
            if shift:
                block = pltpu.roll(block, LANES - shift, 1)
            if shift + chans > LANES:
                after = pltpu.roll(all_ref[(tile + 1) * chans : (tile + 2) * chans, :], LANES - shift, 1)
                block = jnp.where(lane < LANES - shift, block, after)
            locals_[layer][k] = block[:, :chans] * scale
        copies.append(pltpu.make_async_copy(locals_[layer], outs[layer], sems.at[layer]))
        copies[-1].start()
    for copy in copies:
        copy.wait()


def swap(block, axis, bit):
    return lax.ppermute(block, axis, [(i, i ^ bit) for i in range(lax.axis_size(axis))])


def swap_neighbours(block):
    bricks = lax.axis_size("space")
    near = swap(block, "space", 1)
    inner = range(1, bricks - 1)
    far = lax.ppermute(block, "space", [(i, i + 1 if i % 2 else i - 1) for i in inner])
    return near, far


def summed(parts, weight_shape, scale, beside):
    layers = len(parts)
    slots = lax.axis_size("space") // 2
    scans = lax.axis_size("scan")
    packed = 2 * parts[0][0].shape[0]
    rows = layers * packed // (2 * slots)
    outs = [shape((rows, LANES), F32)] + [shape((rows, LANES), BF16)] * (slots - 1)
    own, *sends = call(functools.partial(core_sum_body, layers), outs, [x for part in parts for x in part])
    gots = [swap(block, "space", 2 * slot) for slot, block in enumerate(sends, 1)]
    own, step = beside[0](own)
    part = call(chip_sum_body, shape((rows, LANES), BF16), [own, *gots])
    if scans & (scans - 1):
        part, result = beside[1](part, step)
        total = lax.psum(part, "scan")
    else:
        terms = [part] + [swap(part, "scan", bit) for bit in range(1, scans)]
        terms[0], result = beside[1](terms[0], step)
        total = call(scan_sum_body, shape((rows, LANES), BF16), terms)
    pieces = []
    for slot in range(slots):
        piece = swap(total, "space", 2 * slot) if slot else total
        pieces += [piece, swap(piece, "space", 1)]
    return result, call(
        functools.partial(unpack_body, scale, layers),
        [shape(weight_shape, F32)] * layers,
        pieces,
        scratch=[pltpu.VMEM(weight_shape, F32)] * layers + [pltpu.VMEM((packed, LANES), F32), pltpu.SemaphoreType.DMA((layers,))],
        outs_in=HBM,
    )


def shards(act_zero, pre_act, cot_out, weight_one, weight_two, in_map, out_map, send_lo, send_hi):
    zero, pre, cot = (x[0, 0].T for x in (act_zero, pre_act, cot_out))
    ins, outs = (x[0, 0][:, None, :] for x in (in_map, out_map))
    lo, hi = send_lo[0], send_hi[0]
    chans, rows = zero.shape
    count, _, pairs = ins.shape
    rim = 2 * lo.shape[1]
    ext = rows + rim
    scenes = lax.axis_size("scan")
    bricks = lax.axis_size("space")
    tiles = -(-count * chans // LANES)
    tall = tiles * LANES
    unit = 16 * bricks
    packed = -(-tiles * chans // unit) * unit
    halves = [shape((packed // 2, LANES), F32), shape((packed // 2, LANES), BF16)]
    packed_sum = pltpu.VMEM((packed, LANES), F32)
    gather_flops = 2 * count * chans * ext * rows
    back_flops = 2 * count * chans * chans * ext

    operands = [outs, cot, ins, weight_two, hi, lo, zero, pre]
    t_two, own, edge = call(
        two_body,
        [shape((tall, ext), BF16), shape((chans + -(-count // 8) * 8, ext), F32), shape((4 * chans, rim), BF16)],
        operands,
        scratch=[pltpu.VMEM(x.shape, x.dtype) for x in operands]
        + [
            pltpu.VMEM((tall, ext), BF16),
            pltpu.VMEM((count * (chans + 16), pairs), BF16),
            pltpu.VMEM((chans, ext), F32),
            pltpu.SemaphoreType.DMA((len(operands) + 1,)),
        ],
        flops=gather_flops + back_flops,
        moved=8 << 20,
        args_in=HBM,
        outs_in=(HBM, VMEM, VMEM),
        room=WHOLE,
    )
    near, far = swap_neighbours(edge)
    t_one, keep_one, send_one = call(
        functools.partial(one_body, count),
        [shape((tall, ext), BF16), *halves],
        [own, near, far, hi, lo, pre, zero],
        scratch=[pltpu.VMEM((chans, rows), BF16), packed_sum],
        flops=gather_flops + back_flops,
        moved=8 << 20,
    )
    got_one = swap(send_one, "space", 1)
    near, far, t_one = lax.optimization_barrier((near, far, t_one))
    keep_two, send_two = call(two_weights_body, halves, [pre, near, far, t_two], scratch=[packed_sum], flops=back_flops, moved=6 << 20)
    got_two = swap(send_two, "space", 1)
    t_one, keep_two = lax.optimization_barrier((t_one, keep_two))
    own, edge = call(
        back_body,
        [shape((chans, rows), F32), shape((2 * chans, rim), BF16)],
        [weight_one, t_one],
        scratch=[pltpu.VMEM((chans, ext), F32)],
        flops=back_flops,
        moved=6 << 20,
    )
    keep_one, edge = lax.optimization_barrier((keep_one, edge))
    def swap_edges(held):
        held, block = lax.optimization_barrier((held, edge))
        near, far = swap_neighbours(block)
        held, near, far = lax.optimization_barrier((held, near, far))
        return held, (near, far)

    def settle(held, edges):
        held, own_rows, near, far = lax.optimization_barrier((held, own, *edges))
        grad_act = call(settle_body, shape((chans, rows), BF16), [own_rows, near, far, hi, lo])
        return lax.optimization_barrier((held, grad_act))

    grad_act, (grad_one, grad_two) = summed(
        [(keep_one, got_one), (keep_two, got_two)], weight_one.shape, 1.0 / scenes, (swap_edges, settle)
    )
    return grad_act.T[None, None], grad_one, grad_two


def solution(mesh):
    return jax.shard_map(
        shards,
        mesh=mesh,
        in_specs=(
            P("scan", "space", None, None),
            P("scan", "space", None, None),
            P("scan", "space", None, None),
            P(),
            P(),
            P("scan", "space", None, None),
            P("scan", "space", None, None),
            P("scan", "space", None),
            P("scan", "space", None),
        ),
        out_specs=(P("scan", "space", None, None), P(), P()),
        check_vma=False,
    )
```

time: 72.6 us -> 64.1 us (0.88)
  starting transfers between devices: 39.4 us -> 23.9 us
  waiting for transfers between devices: 7.11 us -> 19.2 us
  local copies, waits for them, and re-layouts: 6.59 us -> 0.99 us
  Pallas kernels: 18.2 us -> 19.1 us
    ppermute x31 -> x17, starting transfers between devices: 37.3 us -> 22.6 us  [swap(): lax.ppermute(block, axis, [(i, i ^ bit) for i in range(lax.axis_size(axis...]
    ppermute x31 -> x17, waiting for transfers between devices: 7.1 us -> 19.2 us  [swap(): lax.ppermute(block, axis, [(i, i ^ bit) for i in range(lax.axis_size(axis...]
    unnamed x26 -> x14, local copies, waits for them, and re-layouts: 6.59 us -> 0.99 us
    pallas_call x14 -> x9, Pallas kernels: 18.2 us -> 19.1 us  [call(): pl.pallas_call(body, out_shape=outs if single else tuple(outs), in_specs=...]
    ppermute x3 -> x2, starting transfers between devices: 2.11 us -> 1.32 us  [swap_neighbours(): lax.ppermute(block, 'space', [(i, i + 1 if i % 2 else i - 1) for i in inn...]
  transfers between devices with their start and end apart: 34 -> 19, of which waited for: 6 -> 12; matrix products, arithmetic and copies ran while one was open for 0% -> 0% of each run, Pallas kernels for 23% -> 3%
where the time goes in v2:
time: 64.1 us; the launch traced here: 63.9 us
  starting transfers between devices  23.9 us (37%)
  waiting for transfers between devices  19.2 us (30%)
  Pallas kernels  19.1 us (30%)
  local copies, waits for them, and re-layouts  0.99 us (2%)
  between operations  0.77 us (1%)
    ppermute x17, starting transfers between devices, swap(): lax.ppermute(block, axis, [(i, i ^ bit) for i in range(lax.axis_size(axis...  22.6 us
    ppermute x17, waiting for transfers between devices, swap(): lax.ppermute(block, axis, [(i, i ^ bit) for i in range(lax.axis_size(axis...  19.2 us
    pallas_call x9, Pallas kernels, call(): pl.pallas_call(body, out_shape=outs if single else tuple(outs), in_specs=...  19.1 us
    ppermute x2, starting transfers between devices, swap_neighbours(): lax.ppermute(block, 'space', [(i, i + 1 if i % 2 else i - 1) for i in inn...  1.32 us
  transfers between devices with their start and end apart: 19, of which 12 were waited for; matrix products, arithmetic and copies ran while one was open for 0% of the time, Pallas kernels for 3%

profile of v2, /device:TPU:0, one launch (start us, length us, event | category | flops | bytes accessed | tf_op | source)
XLA Modules:
  0.0 63.9 jit_solution(11509401586338471521)
XLA Ops:
  0.7 8.2 %shard_map.112 = (bf16[2688,640]{1,0:T(8,128)(2,1)}, f32[128,640]{1,0:T(8,128)}, bf16[384,128]{1,0:T(8,128)(2,1)}) custom-call(s32[27,1,256]{2,1,0:T(1,128)} %bitcast.29, bf16[96,512]{1,0:T(8,128)(2,1)} %bitcast.28, s32[27,1,256]{2,1,0:T(1,128)} %bitcast.30, bf16[27,96,96]{2,1,0:T(8,128)(2,1)} %refs_3_.1, s32[1,64]{1,0:T(1,128)} %bitcast.19, ...), custom_call_target="tpu_custom_call" | custom-call | flops 2017198080 | bytes 8388608 | tf_op jit(solution)/shard_map/pallas_call | solution.py:22
  8.9 0.7 %collective-permute-start.1 = (bf16[384,128]{1,0:T(8,128)(2,1)}, bf16[384,128]{1,0:T(8,128)(2,1)S(1)}, u32[]{:S(2)}, u32[]{:S(2)}) collective-permute-start(bf16[384,128]{1,0:T(8,128)(2,1)} %get-tuple-element.38), channel_id=1, source_target_pairs={{4,8},{8,4},{12,16},{16,12},{20,24},{24,20},{5,9},{9,5},{13,17},{1... | collective-permute-start | bytes 294920 | tf_op jit(solution)/shard_map/ppermute | solution.py:285
  9.5 4.4 %collective-permute-start = (bf16[384,128]{1,0:T(8,128)(2,1)}, bf16[384,128]{1,0:T(8,128)(2,1)S(1)}, u32[]{:S(2)}, u32[]{:S(2)}) collective-permute-start(bf16[384,128]{1,0:T(8,128)(2,1)} %get-tuple-element.38), channel_id=1, source_target_pairs={{0,4},{4,0},{8,12},{12,8},{16,20},{20,16},{24,28},{28,24},{1,5},{5... | collective-permute-start | bytes 294920 | tf_op jit(solution)/shard_map/ppermute | solution.py:278
  13.9 1.2 %collective-permute-done.near_ref = bf16[384,128]{1,0:T(8,128)(2,1)S(1)} collective-permute-done((bf16[384,128]{1,0:T(8,128)(2,1)}, bf16[384,128]{1,0:T(8,128)(2,1)S(1)}, u32[]{:S(2)}, u32[]{:S(2)}) %collective-permute-start) | collective-permute-done | bytes 98336 | tf_op jit(solution)/shard_map/ppermute | solution.py:278
  15.1 1.0 %copy-done.6 = f32[128,640]{1,0:T(8,128)S(1)} copy-done((f32[128,640]{1,0:T(8,128)S(1)}, f32[128,640]{1,0:T(8,128)}, u32[]{:S(2)}) %copy-start.6) | copy-done | bytes 327704
  16.0 5.0 %shard_map.113 = (bf16[2688,640]{1,0:T(8,128)(2,1)S(1)}, f32[1024,128]{1,0:T(8,128)S(1)}, bf16[1024,128]{1,0:T(8,128)(2,1)S(1)}) custom-call(f32[128,640]{1,0:T(8,128)S(1)} %copy-done.6, bf16[384,128]{1,0:T(8,128)(2,1)S(1)} %collective-permute-done.near_ref, bf16[384,128]{1,0:T(8,128)(2,1)S(1)} %collective-permute-done.1.far_ref, s32[1,64]{1,0:T(1,128)S(1)} %bitcast.20, ...), custom_call_target="tpu_custom_call" | custom-call | flops 2017198080 | bytes 8388608 | tf_op jit(solution)/shard_map/pallas_call | solution.py:22
  21.1 1.2 %shard_map.114 = (f32[1024,128]{1,0:T(8,128)S(1)}, bf16[1024,128]{1,0:T(8,128)(2,1)S(1)}) custom-call(bf16[96,512]{1,0:T(8,128)(2,1)S(1)} %bitcast.18, bf16[384,128]{1,0:T(8,128)(2,1)S(1)} %collective-permute-done.near_ref, bf16[384,128]{1,0:T(8,128)(2,1)S(1)} %collective-permute-done.1.far_ref, bf16[2688,640]{1,0:T(8,128)(2,1)S(1)} %copy-done), custom_call_target="tpu_custom_call" | custom-call | flops 318504960 | bytes 6291456 | tf_op jit(solution)/shard_map/pallas_call | solution.py:22
  22.3 1.5 %collective-permute-start.3 = (bf16[1024,128]{1,0:T(8,128)(2,1)S(1)}, bf16[1024,128]{1,0:T(8,128)(2,1)S(1)}, u32[]{:S(2)}, u32[]{:S(2)}) collective-permute-start(bf16[1024,128]{1,0:T(8,128)(2,1)S(1)} %get-tuple-element.51), channel_id=1, source_target_pairs={{0,4},{4,0},{8,12},{12,8},{16,20},{20,16},{24,28},{28,24},{1,5},{5... | collective-permute-start | bytes 786440 | tf_op jit(solution)/shard_map/ppermute | solution.py:278
  23.9 1.0 %shard_map.115 = (f32[96,512]{1,0:T(8,128)S(1)}, bf16[192,128]{1,0:T(8,128)(2,1)S(1)}) custom-call(bf16[27,96,96]{2,1,0:T(8,128)(2,1)S(1)} %copy-done.1, bf16[2688,640]{1,0:T(8,128)(2,1)S(1)} %get-tuple-element.46.t_ref), custom_call_target="tpu_custom_call" | custom-call | flops 318504960 | bytes 6291456 | tf_op jit(solution)/shard_map/pallas_call | solution.py:22
  25.0 0.4 collective-permute-done.2.refs_1_
  25.4 0.1 shard_map.116
  25.4 3.3 %collective-permute-start.6 = (bf16[512,128]{1,0:T(8,128)(2,1)S(1)}, bf16[512,128]{1,0:T(8,128)(2,1)S(1)}, u32[]{:S(2)}, u32[]{:S(2)}) collective-permute-start(bf16[512,128]{1,0:T(8,128)(2,1)S(1)} %get-tuple-element.57), channel_id=1, source_target_pairs={{0,8},{4,12},{8,0},{12,4},{16,24},{20,28},{24,16},{28,20},{1,9},{5... | collective-permute-start | bytes 393224 | tf_op jit(solution)/shard_map/ppermute | solution.py:278
  28.7 1.1 %collective-permute-start.7 = (bf16[512,128]{1,0:T(8,128)(2,1)S(1)}, bf16[512,128]{1,0:T(8,128)(2,1)S(1)}, u32[]{:S(2)}, u32[]{:S(2)}) collective-permute-start(bf16[512,128]{1,0:T(8,128)(2,1)S(1)} %get-tuple-element.58), channel_id=1, source_target_pairs={{0,16},{4,20},{8,24},{12,28},{16,0},{20,4},{24,8},{28,12},{1,17},{... | collective-permute-start | bytes 393224 | tf_op jit(solution)/shard_map/ppermute | solution.py:278
  29.8 0.4 collective-permute-start.8
  30.3 0.7 %collective-permute-start.5 = (bf16[192,128]{1,0:T(8,128)(2,1)S(1)}, bf16[192,128]{1,0:T(8,128)(2,1)S(1)}, u32[]{:S(2)}, u32[]{:S(2)}) collective-permute-start(bf16[192,128]{1,0:T(8,128)(2,1)S(1)} %get-tuple-element.55), channel_id=1, source_target_pairs={{4,8},{8,4},{12,16},{16,12},{20,24},{24,20},{5,9},{9,5},{13,17},{1... | collective-permute-start | bytes 147464 | tf_op jit(solution)/shard_map/ppermute | solution.py:285
  30.9 3.4 %collective-permute-start.4 = (bf16[192,128]{1,0:T(8,128)(2,1)S(1)}, bf16[192,128]{1,0:T(8,128)(2,1)S(1)}, u32[]{:S(2)}, u32[]{:S(2)}) collective-permute-start(bf16[192,128]{1,0:T(8,128)(2,1)S(1)} %get-tuple-element.55), channel_id=1, source_target_pairs={{0,4},{4,0},{8,12},{12,8},{16,20},{20,16},{24,28},{28,24},{1,5},{5... | collective-permute-start | bytes 147464 | tf_op jit(solution)/shard_map/ppermute | solution.py:278
  34.3 0.9 %collective-permute-done.4.near_ref = bf16[192,128]{1,0:T(8,128)(2,1)S(1)} collective-permute-done((bf16[192,128]{1,0:T(8,128)(2,1)S(1)}, bf16[192,128]{1,0:T(8,128)(2,1)S(1)}, u32[]{:S(2)}, u32[]{:S(2)}) %collective-permute-start.4) | collective-permute-done | bytes 49184 | tf_op jit(solution)/shard_map/ppermute | solution.py:278
  35.2 1.8 %collective-permute-done.7.refs_1_ = bf16[512,128]{1,0:T(8,128)(2,1)S(1)} collective-permute-done((bf16[512,128]{1,0:T(8,128)(2,1)S(1)}, bf16[512,128]{1,0:T(8,128)(2,1)S(1)}, u32[]{:S(2)}, u32[]{:S(2)}) %collective-permute-start.7) | collective-permute-done | bytes 131104 | tf_op jit(solution)/shard_map/ppermute | solution.py:278
  37.1 3.7 %collective-permute-start.11 = (bf16[512,128]{1,0:T(8,128)(2,1)S(1)}, bf16[512,128]{1,0:T(8,128)(2,1)S(1)}, u32[]{:S(2)}, u32[]{:S(2)}) collective-permute-start(bf16[512,128]{1,0:T(8,128)(2,1)S(1)} %shard_map.117.refs_0_), channel_id=1, source_target_pairs={{0,3},{1,2},{2,1},{3,0},{4,7},{5,6},{6,5},{7,4},{8,11},{9,10},{10,... | collective-permute-start | bytes 393224 | tf_op jit(solution)/shard_map/ppermute | solution.py:278
  40.7 0.8 %collective-permute-start.9 = (bf16[512,128]{1,0:T(8,128)(2,1)S(1)}, bf16[512,128]{1,0:T(8,128)(2,1)S(1)}, u32[]{:S(2)}, u32[]{:S(2)}) collective-permute-start(bf16[512,128]{1,0:T(8,128)(2,1)S(1)} %shard_map.117.refs_0_), channel_id=1, source_target_pairs={{0,1},{1,0},{2,3},{3,2},{4,5},{5,4},{6,7},{7,6},{8,9},{9,8},{10,11... | collective-permute-start | bytes 393224 | tf_op jit(solution)/shard_map/ppermute | solution.py:278
  41.5 0.9 %shard_map.118 = bf16[96,512]{1,0:T(8,128)(2,1)} custom-call(f32[96,512]{1,0:T(8,128)S(1)} %get-tuple-element.64.own_ref, bf16[192,128]{1,0:T(8,128)(2,1)S(1)} %collective-permute-done.4.near_ref, bf16[192,128]{1,0:T(8,128)(2,1)S(1)} %collective-permute-done.5.far_ref, s32[1,64]{1,0:T(1,128)S(1)} %bitcast.21, s32[1,64]{1,0:T(1,128)S(1)} %bitcast.24), custom_call_target="tpu_custom_call" | custom-call | tf_op jit(solution)/shard_map/pallas_call | solution.py:22
  42.4 2.9 %collective-permute-done.11.refs_3_ = bf16[512,128]{1,0:T(8,128)(2,1)S(1)} collective-permute-done((bf16[512,128]{1,0:T(8,128)(2,1)S(1)}, bf16[512,128]{1,0:T(8,128)(2,1)S(1)}, u32[]{:S(2)}, u32[]{:S(2)}) %collective-permute-start.11) | collective-permute-done | bytes 131104 | tf_op jit(solution)/shard_map/ppermute | solution.py:278
  45.4 5.9 %collective-permute-done.10.refs_2_ = bf16[512,128]{1,0:T(8,128)(2,1)S(1)} collective-permute-done((bf16[512,128]{1,0:T(8,128)(2,1)S(1)}, bf16[512,128]{1,0:T(8,128)(2,1)S(1)}, u32[]{:S(2)}, u32[]{:S(2)}) %collective-permute-start.10) | collective-permute-done | bytes 131104 | tf_op jit(solution)/shard_map/ppermute | solution.py:278
  51.3 1.5 %collective-permute-start.17 = (bf16[512,128]{1,0:T(8,128)(2,1)S(1)}, bf16[512,128]{1,0:T(8,128)(2,1)S(1)}, u32[]{:S(2)}, u32[]{:S(2)}) collective-permute-start(bf16[512,128]{1,0:T(8,128)(2,1)S(1)} %shard_map.119.refs_0_), channel_id=1, source_target_pairs={{0,24},{4,28},{8,16},{12,20},{16,8},{20,12},{24,0},{28,4},{1,25},{... | collective-permute-start | bytes 393224 | tf_op jit(solution)/shard_map/ppermute | solution.py:278
  52.8 2.3 %collective-permute-start.15 = (bf16[512,128]{1,0:T(8,128)(2,1)S(1)}, bf16[512,128]{1,0:T(8,128)(2,1)S(1)}, u32[]{:S(2)}, u32[]{:S(2)}) collective-permute-start(bf16[512,128]{1,0:T(8,128)(2,1)S(1)} %shard_map.119.refs_0_), channel_id=1, source_target_pairs={{0,16},{4,20},{8,24},{12,28},{16,0},{20,4},{24,8},{28,12},{1,17},{... | collective-permute-start | bytes 393224 | tf_op jit(solution)/shard_map/ppermute | solution.py:278
  55.1 2.7 %collective-permute-done.17.refs_6_ = bf16[512,128]{1,0:T(8,128)(2,1)S(1)} collective-permute-done((bf16[512,128]{1,0:T(8,128)(2,1)S(1)}, bf16[512,128]{1,0:T(8,128)(2,1)S(1)}, u32[]{:S(2)}, u32[]{:S(2)}) %collective-permute-start.17) | collective-permute-done | bytes 131104 | tf_op jit(solution)/shard_map/ppermute | solution.py:278
  57.8 2.0 %collective-permute-done.15.refs_4_ = bf16[512,128]{1,0:T(8,128)(2,1)S(1)} collective-permute-done((bf16[512,128]{1,0:T(8,128)(2,1)S(1)}, bf16[512,128]{1,0:T(8,128)(2,1)S(1)}, u32[]{:S(2)}, u32[]{:S(2)}) %collective-permute-start.15) | collective-permute-done | bytes 131104 | tf_op jit(solution)/shard_map/ppermute | solution.py:278
  59.8 0.3 collective-permute-done.13.refs_2_
  60.1 0.2 collective-permute-start.14
  60.3 0.8 %collective-permute-done.16.refs_5_ = bf16[512,128]{1,0:T(8,128)(2,1)S(1)} collective-permute-done((bf16[512,128]{1,0:T(8,128)(2,1)S(1)}, bf16[512,128]{1,0:T(8,128)(2,1)S(1)}, u32[]{:S(2)}, u32[]{:S(2)}) %collective-permute-start.16) | collective-permute-done | bytes 131104 | tf_op jit(solution)/shard_map/ppermute | solution.py:278
  61.1 0.3 collective-permute-done.14.refs_3_
  61.4 2.5 %shard_map.120 = (f32[27,96,96]{2,1,0:T(8,128)}, f32[27,96,96]{2,1,0:T(8,128)}) custom-call(bf16[512,128]{1,0:T(8,128)(2,1)S(1)} %shard_map.119.refs_0_, bf16[512,128]{1,0:T(8,128)(2,1)S(1)} %collective-permute-done.12.refs_1_, bf16[512,128]{1,0:T(8,128)(2,1)S(1)} %collective-permute-done.13.refs_2_, bf16[512,128]{1,0:T(8,128)(2,1)S(1)} %collective-permute-done.14.refs_3_, ...), custom_call_target="tpu_custom_call" | custom-call | tf_op jit(solution)/shard_map/pallas_call | solution.py:22
  (29 shorter events, 0.3 us)
Async XLA Ops:
  0.6 14.4 %copy-start.2 = (bf16[1,1,512,96]{2,3,1,0:T(8,128)(2,1)S(1)}, bf16[1,1,512,96]{2,3,1,0:T(8,128)(2,1)}, u32[]{:S(2)}) copy-start(bf16[1,1,512,96]{2,3,1,0:T(8,128)(2,1)} %param.10) | copy-start | bytes 294916
  0.6 14.4 %copy-start.3 = (s32[1,1,64]{2,1,0:T(1,128)S(1)}, s32[1,1,64]{2,1,0:T(1,128)}, u32[]{:S(2)}) copy-start(s32[1,1,64]{2,1,0:T(1,128)} %param.17) | copy-start | bytes 772
  0.7 14.4 %copy-start.4 = (s32[1,1,64]{2,1,0:T(1,128)S(1)}, s32[1,1,64]{2,1,0:T(1,128)}, u32[]{:S(2)}) copy-start(s32[1,1,64]{2,1,0:T(1,128)} %param.16) | copy-start | bytes 772
  0.7 14.4 %copy-start.5 = (bf16[1,1,512,96]{2,3,1,0:T(8,128)(2,1)S(1)}, bf16[1,1,512,96]{2,3,1,0:T(8,128)(2,1)}, u32[]{:S(2)}) copy-start(bf16[1,1,512,96]{2,3,1,0:T(8,128)(2,1)} %param.9) | copy-start | bytes 294916
  8.9 5.0 %collective-permute-start.1 = (bf16[384,128]{1,0:T(8,128)(2,1)}, bf16[384,128]{1,0:T(8,128)(2,1)S(1)}, u32[]{:S(2)}, u32[]{:S(2)}) collective-permute-start(bf16[384,128]{1,0:T(8,128)(2,1)} %get-tuple-element.38), channel_id=1, source_target_pairs={{4,8},{8,4},{12,16},{16,12},{20,24},{24,20},{5,9},{9,5},{13,17},{1... | collective-permute-start | bytes 294920 | tf_op jit(solution)/shard_map/ppermute | solution.py:285
  9.5 5.5 %collective-permute-start = (bf16[384,128]{1,0:T(8,128)(2,1)}, bf16[384,128]{1,0:T(8,128)(2,1)S(1)}, u32[]{:S(2)}, u32[]{:S(2)}) collective-permute-start(bf16[384,128]{1,0:T(8,128)(2,1)} %get-tuple-element.38), channel_id=1, source_target_pairs={{0,4},{4,0},{8,12},{12,8},{16,20},{20,16},{24,28},{28,24},{1,5},{5... | collective-permute-start | bytes 294920 | tf_op jit(solution)/shard_map/ppermute | solution.py:278
  15.1 1.0 %copy-start.6 = (f32[128,640]{1,0:T(8,128)S(1)}, f32[128,640]{1,0:T(8,128)}, u32[]{:S(2)}) copy-start(f32[128,640]{1,0:T(8,128)} %get-tuple-element.37.own_ref) | copy-start | bytes 983044
  16.0 5.1 %copy-start = (bf16[2688,640]{1,0:T(8,128)(2,1)S(1)}, bf16[2688,640]{1,0:T(8,128)(2,1)}, u32[]{:S(2)}) copy-start(bf16[2688,640]{1,0:T(8,128)(2,1)} %get-tuple-element.44.t_ref) | copy-start | bytes 10321924
  21.1 2.8 %copy-start.1 = (bf16[27,96,96]{2,1,0:T(8,128)(2,1)S(1)}, bf16[27,96,96]{2,1,0:T(8,128)(2,1)}, u32[]{:S(2)}) copy-start(bf16[27,96,96]{2,1,0:T(8,128)(2,1)} %weight_ref.1) | copy-start | bytes 1492996
  22.3 2.7 %collective-permute-start.3 = (bf16[1024,128]{1,0:T(8,128)(2,1)S(1)}, bf16[1024,128]{1,0:T(8,128)(2,1)S(1)}, u32[]{:S(2)}, u32[]{:S(2)}) collective-permute-start(bf16[1024,128]{1,0:T(8,128)(2,1)S(1)} %get-tuple-element.51), channel_id=1, source_target_pairs={{0,4},{4,0},{8,12},{12,8},{16,20},{20,16},{24,28},{28,24},{1,5},{5... | collective-permute-start | bytes 786440 | tf_op jit(solution)/shard_map/ppermute | solution.py:278
  23.8 1.5 %collective-permute-start.2 = (bf16[1024,128]{1,0:T(8,128)(2,1)S(1)}, bf16[1024,128]{1,0:T(8,128)(2,1)S(1)}, u32[]{:S(2)}, u32[]{:S(2)}) collective-permute-start(bf16[1024,128]{1,0:T(8,128)(2,1)S(1)} %get-tuple-element.49), channel_id=1, source_target_pairs={{0,4},{4,0},{8,12},{12,8},{16,20},{20,16},{24,28},{28,24},{1,5},{5... | collective-permute-start | bytes 786440 | tf_op jit(solution)/shard_map/ppermute | solution.py:278
  25.4 9.7 %collective-permute-start.6 = (bf16[512,128]{1,0:T(8,128)(2,1)S(1)}, bf16[512,128]{1,0:T(8,128)(2,1)S(1)}, u32[]{:S(2)}, u32[]{:S(2)}) collective-permute-start(bf16[512,128]{1,0:T(8,128)(2,1)S(1)} %get-tuple-element.57), channel_id=1, source_target_pairs={{0,8},{4,12},{8,0},{12,4},{16,24},{20,28},{24,16},{28,20},{1,9},{5... | collective-permute-start | bytes 393224 | tf_op jit(solution)/shard_map/ppermute | solution.py:278
  28.7 8.3 %collective-permute-start.7 = (bf16[512,128]{1,0:T(8,128)(2,1)S(1)}, bf16[512,128]{1,0:T(8,128)(2,1)S(1)}, u32[]{:S(2)}, u32[]{:S(2)}) collective-permute-start(bf16[512,128]{1,0:T(8,128)(2,1)S(1)} %get-tuple-element.58), channel_id=1, source_target_pairs={{0,16},{4,20},{8,24},{12,28},{16,0},{20,4},{24,8},{28,12},{1,17},{... | collective-permute-start | bytes 393224 | tf_op jit(solution)/shard_map/ppermute | solution.py:278
  29.8 7.2 %collective-permute-start.8 = (bf16[512,128]{1,0:T(8,128)(2,1)S(1)}, bf16[512,128]{1,0:T(8,128)(2,1)S(1)}, u32[]{:S(2)}, u32[]{:S(2)}) collective-permute-start(bf16[512,128]{1,0:T(8,128)(2,1)S(1)} %get-tuple-element.59), channel_id=1, source_target_pairs={{0,24},{4,28},{8,16},{12,20},{16,8},{20,12},{24,0},{28,4},{1,25},{... | collective-permute-start | bytes 393224 | tf_op jit(solution)/shard_map/ppermute | solution.py:278
  30.3 4.0 %collective-permute-start.5 = (bf16[192,128]{1,0:T(8,128)(2,1)S(1)}, bf16[192,128]{1,0:T(8,128)(2,1)S(1)}, u32[]{:S(2)}, u32[]{:S(2)}) collective-permute-start(bf16[192,128]{1,0:T(8,128)(2,1)S(1)} %get-tuple-element.55), channel_id=1, source_target_pairs={{4,8},{8,4},{12,16},{16,12},{20,24},{24,20},{5,9},{9,5},{13,17},{1... | collective-permute-start | bytes 147464 | tf_op jit(solution)/shard_map/ppermute | solution.py:285
  30.9 4.3 %collective-permute-start.4 = (bf16[192,128]{1,0:T(8,128)(2,1)S(1)}, bf16[192,128]{1,0:T(8,128)(2,1)S(1)}, u32[]{:S(2)}, u32[]{:S(2)}) collective-permute-start(bf16[192,128]{1,0:T(8,128)(2,1)S(1)} %get-tuple-element.55), channel_id=1, source_target_pairs={{0,4},{4,0},{8,12},{12,8},{16,20},{20,16},{24,28},{28,24},{1,5},{5... | collective-permute-start | bytes 147464 | tf_op jit(solution)/shard_map/ppermute | solution.py:278
  37.1 8.3 %collective-permute-start.11 = (bf16[512,128]{1,0:T(8,128)(2,1)S(1)}, bf16[512,128]{1,0:T(8,128)(2,1)S(1)}, u32[]{:S(2)}, u32[]{:S(2)}) collective-permute-start(bf16[512,128]{1,0:T(8,128)(2,1)S(1)} %shard_map.117.refs_0_), channel_id=1, source_target_pairs={{0,3},{1,2},{2,1},{3,0},{4,7},{5,6},{6,5},{7,4},{8,11},{9,10},{10,... | collective-permute-start | bytes 393224 | tf_op jit(solution)/shard_map/ppermute | solution.py:278
  40.7 10.5 %collective-permute-start.10 = (bf16[512,128]{1,0:T(8,128)(2,1)S(1)}, bf16[512,128]{1,0:T(8,128)(2,1)S(1)}, u32[]{:S(2)}, u32[]{:S(2)}) collective-permute-start(bf16[512,128]{1,0:T(8,128)(2,1)S(1)} %shard_map.117.refs_0_), channel_id=1, source_target_pairs={{0,2},{1,3},{2,0},{3,1},{4,6},{5,7},{6,4},{7,5},{8,10},{9,11},{10,... | collective-permute-start | bytes 393224 | tf_op jit(solution)/shard_map/ppermute | solution.py:278
  40.7 10.5 %collective-permute-start.9 = (bf16[512,128]{1,0:T(8,128)(2,1)S(1)}, bf16[512,128]{1,0:T(8,128)(2,1)S(1)}, u32[]{:S(2)}, u32[]{:S(2)}) collective-permute-start(bf16[512,128]{1,0:T(8,128)(2,1)S(1)} %shard_map.117.refs_0_), channel_id=1, source_target_pairs={{0,1},{1,0},{2,3},{3,2},{4,5},{5,4},{6,7},{7,6},{8,9},{9,8},{10,11... | collective-permute-start | bytes 393224 | tf_op jit(solution)/shard_map/ppermute | solution.py:278
  51.3 6.5 %collective-permute-start.17 = (bf16[512,128]{1,0:T(8,128)(2,1)S(1)}, bf16[512,128]{1,0:T(8,128)(2,1)S(1)}, u32[]{:S(2)}, u32[]{:S(2)}) collective-permute-start(bf16[512,128]{1,0:T(8,128)(2,1)S(1)} %shard_map.119.refs_0_), channel_id=1, source_target_pairs={{0,24},{4,28},{8,16},{12,20},{16,8},{20,12},{24,0},{28,4},{1,25},{... | collective-permute-start | bytes 393224 | tf_op jit(solution)/shard_map/ppermute | solution.py:278
  52.8 7.0 %collective-permute-start.15 = (bf16[512,128]{1,0:T(8,128)(2,1)S(1)}, bf16[512,128]{1,0:T(8,128)(2,1)S(1)}, u32[]{:S(2)}, u32[]{:S(2)}) collective-permute-start(bf16[512,128]{1,0:T(8,128)(2,1)S(1)} %shard_map.119.refs_0_), channel_id=1, source_target_pairs={{0,16},{4,20},{8,24},{12,28},{16,0},{20,4},{24,8},{28,12},{1,17},{... | collective-permute-start | bytes 393224 | tf_op jit(solution)/shard_map/ppermute | solution.py:278
  55.1 5.0 %collective-permute-start.13 = (bf16[512,128]{1,0:T(8,128)(2,1)S(1)}, bf16[512,128]{1,0:T(8,128)(2,1)S(1)}, u32[]{:S(2)}, u32[]{:S(2)}) collective-permute-start(bf16[512,128]{1,0:T(8,128)(2,1)S(1)} %shard_map.119.refs_0_), channel_id=1, source_target_pairs={{0,8},{4,12},{8,0},{12,4},{16,24},{20,28},{24,16},{28,20},{1,9},{5... | collective-permute-start | bytes 393224 | tf_op jit(solution)/shard_map/ppermute | solution.py:278
  55.1 5.2 %collective-permute-start.12 = (bf16[512,128]{1,0:T(8,128)(2,1)S(1)}, bf16[512,128]{1,0:T(8,128)(2,1)S(1)}, u32[]{:S(2)}, u32[]{:S(2)}) collective-permute-start(bf16[512,128]{1,0:T(8,128)(2,1)S(1)} %shard_map.119.refs_0_), channel_id=1, source_target_pairs={{0,4},{4,0},{8,12},{12,8},{16,20},{20,16},{24,28},{28,24},{1,5},{5... | collective-permute-start | bytes 393224 | tf_op jit(solution)/shard_map/ppermute | solution.py:278
  57.8 2.5 %collective-permute-start.18 = (bf16[512,128]{1,0:T(8,128)(2,1)S(1)}, bf16[512,128]{1,0:T(8,128)(2,1)S(1)}, u32[]{:S(2)}, u32[]{:S(2)}) collective-permute-start(bf16[512,128]{1,0:T(8,128)(2,1)S(1)} %collective-permute-done.17.refs_6_), channel_id=1, source_target_pairs={{0,4},{4,0},{8,12},{12,8},{16,20},{20,16},{24,28},{28,24},{1,5},{5... | collective-permute-start | bytes 393224 | tf_op jit(solution)/shard_map/ppermute | solution.py:278
  59.8 1.3 %collective-permute-start.16 = (bf16[512,128]{1,0:T(8,128)(2,1)S(1)}, bf16[512,128]{1,0:T(8,128)(2,1)S(1)}, u32[]{:S(2)}, u32[]{:S(2)}) collective-permute-start(bf16[512,128]{1,0:T(8,128)(2,1)S(1)} %collective-permute-done.15.refs_4_), channel_id=1, source_target_pairs={{0,4},{4,0},{8,12},{12,8},{16,20},{20,16},{24,28},{28,24},{1,5},{5... | collective-permute-start | bytes 393224 | tf_op jit(solution)/shard_map/ppermute | solution.py:278
  60.1 1.3 %collective-permute-start.14 = (bf16[512,128]{1,0:T(8,128)(2,1)S(1)}, bf16[512,128]{1,0:T(8,128)(2,1)S(1)}, u32[]{:S(2)}, u32[]{:S(2)}) collective-permute-start(bf16[512,128]{1,0:T(8,128)(2,1)S(1)} %collective-permute-done.13.refs_2_), channel_id=1, source_target_pairs={{0,4},{4,0},{8,12},{12,8},{16,20},{20,16},{24,28},{28,24},{1,5},{5... | collective-permute-start | bytes 393224 | tf_op jit(solution)/shard_map/ppermute | solution.py:278

commit v3 on v2

v3 whole, which is shorter than its diff:
```python
import functools

import jax
import jax.numpy as jnp
from jax import lax
from jax.experimental import pallas as pl
from jax.experimental.pallas import tpu as pltpu
from jax.sharding import PartitionSpec as P

F32, BF16, I32 = jnp.float32, jnp.bfloat16, jnp.int32
VMEM = pl.BlockSpec(memory_space=pltpu.VMEM)
HBM = pl.BlockSpec(memory_space=pltpu.HBM)
LANES = 128
BLOCK = 256
CHUNK = 9
WHOLE = 62 << 20
UNROLL = 9
NT = (((1,), (1,)), ((), ()))


def call(body, outs, args, scratch=(), flops=0, moved=0, args_in=VMEM, outs_in=VMEM, room=40 << 20):
    single = not isinstance(outs, (list, tuple))
    return pl.pallas_call(
        body,
        out_shape=outs if single else tuple(outs),
        in_specs=[args_in] * len(args),
        out_specs=outs_in if single or isinstance(outs_in, tuple) else (outs_in,) * len(outs),
        scratch_shapes=scratch,
        compiler_params=pltpu.CompilerParams(vmem_limit_bytes=room),
        cost_estimate=pl.CostEstimate(flops=flops, bytes_accessed=moved, transcendentals=0),
    )(*args)


def shape(dims, dtype):
    return jax.ShapeDtypeStruct(dims, dtype)


def loop(steps, body):
    unroll = next(u for u in range(UNROLL, 0, -1) if steps % u == 0)

    def step(i, carry):
        body(i)
        return carry

    lax.fori_loop(0, steps, step, 0, unroll=unroll)


def one_hot(rows, index):
    count = lax.broadcasted_iota(I32, (min(rows, BLOCK), index.shape[1]), 0).astype(F32).astype(BF16)
    blocks = []
    for start in range(0, rows, BLOCK):
        wanted = (index - start).astype(F32).astype(BF16)
        hit = count[: min(BLOCK, rows - start)] == wanted
        blocks.append(jnp.where(hit, jnp.ones((), BF16), jnp.zeros((), BF16)))
    return jnp.concatenate(blocks, 0)


def dot(a, b):
    return jnp.dot(a, b, preferred_element_type=F32)


def dot_nt(a, b):
    return lax.dot_general(a, b, NT, preferred_element_type=F32)


def offset_rows(k, chans):
    return pl.ds(pl.multiple_of(k * chans, chans), chans)


def rim_index(hi_ref, lo_ref):
    return jnp.concatenate([hi_ref[...], lo_ref[...]], 1)


def halves(x, y):
    x, y = x.astype(F32), y.astype(F32)
    width = x.shape[1]
    left = lax.broadcasted_iota(I32, x.shape, 1) < width // 2
    return jnp.where(left, x, pltpu.roll(y, width // 2, 1)), jnp.where(left, pltpu.roll(x, width // 2, 1), y)


def by_parity(x, y):
    even = lax.rem(lax.axis_index("space"), 2) == 0
    return jnp.where(even, x, y), jnp.where(even, y, x)


def put_edges(near_ref, far_ref, at, up, down):
    rows = slice(at, at + up.shape[0])
    for ref, value in zip((near_ref, far_ref), by_parity(up, down), strict=True):
        ref[rows] = value.astype(BF16)


def rim_gradients(near_ref, far_ref, total):
    high = total.astype(BF16).astype(F32)
    down, up = halves(high, total - high)
    put_edges(near_ref, far_ref, 0, up, down)


def add_back(weight_ref, t_ref, total_ref):
    count, chans = weight_ref.shape[0], weight_ref.shape[1]
    total_ref[...] = jnp.zeros_like(total_ref)

    def body(g):
        part = None
        for j in range(3):
            k = g * 3 + j
            term = dot(weight_ref[k], t_ref[offset_rows(k, chans), :])
            part = term if part is None else part + term
        total_ref[...] += part

    assert count % 3 == 0
    loop(count // 3, body)


def two_body(*refs):
    operands, (t_out, own_ref, near_ref, far_ref), scratch = refs[:8], refs[8:12], refs[12:]
    locals_, (t_ref, c_ref, total_ref, sems) = scratch[:8], scratch[8:]
    copies = [
        pltpu.make_async_copy(operand, local, sems.at[i]) for i, (operand, local) in enumerate(zip(operands, locals_, strict=True))
    ]
    for copy in copies:
        copy.start()
    outs_ref, cot_ref, ins_ref, weight_ref, hi_ref, lo_ref, zero_ref, pre_ref = locals_
    count, pairs = ins_ref.shape[0], ins_ref.shape[2]
    chans, rows = cot_ref.shape
    ext = t_ref.shape[1]
    tall = chans + 16
    row = lax.broadcasted_iota(I32, (16, pairs), 0)
    t_ref[count * chans :, :] = jnp.zeros((t_ref.shape[0] - count * chans, ext), BF16)

    def pick_outs(k):
        index = outs_ref[k]
        base = pl.multiple_of(k * tall, 16)
        c_ref[pl.ds(base, chans), :] = dot(cot_ref[...], one_hot(rows, index)).astype(BF16)
        left = rows - index
        code = jnp.where(row == 0, left // 16, jnp.where(row == 1, left % 16, 0))
        c_ref[pl.ds(base + chans, 16), :] = code.astype(F32).astype(BF16)

    copies[0].wait()
    copies[1].wait()
    loop(count, pick_outs)

    def put_ins(k):
        picked = c_ref[pl.ds(pl.multiple_of(k * tall, 16), tall), :]
        placed = dot_nt(picked, one_hot(ext, ins_ref[k]))
        t_ref[offset_rows(k, chans), :] = placed[:chans].astype(BF16)
        code = placed[chans : chans + 1] * 16.0 + placed[chans + 1 : chans + 2]
        own_ref[pl.ds(chans + k, 1), :] = rows - code

    copies[2].wait()
    loop(count, put_ins)
    stored = pltpu.make_async_copy(t_ref, t_out, sems.at[len(operands)])
    stored.start()
    copies[3].wait()
    add_back(weight_ref, t_ref, total_ref)
    own_ref[:chans] = total_ref[...]
    rim_gradients(near_ref, far_ref, total_ref[:, rows:])
    for copy in copies[4:]:
        copy.wait()
    pick = one_hot(rows, rim_index(hi_ref, lo_ref))
    one = jnp.maximum(pre_ref[...], jnp.zeros_like(pre_ref))
    up, down = halves(dot(zero_ref[...], pick), dot(one, pick))
    put_edges(near_ref, far_ref, chans, up, down)
    stored.wait()


def packed_products(feats, t_ref, columns, sum_ref, base_ref=None):
    chans = feats.shape[0]
    tiles = t_ref.shape[0] // LANES
    for start in range(0, tiles, 2):
        width = min(2, tiles - start)
        grad = dot_nt(feats, t_ref[start * LANES : (start + width) * LANES, columns])
        for j in range(width):
            rows = slice((start + j) * chans, (start + j + 1) * chans)
            block = grad[:, j * LANES : (j + 1) * LANES]
            sum_ref[rows, :] = block if base_ref is None else block + base_ref[rows, :]
    sum_ref[tiles * chans :, :] = jnp.zeros((sum_ref.shape[0] - tiles * chans, LANES), F32)


def cut(sum_ref, layer, keep_ref, send_ref):
    me = lax.axis_index("space")
    slots = lax.axis_size("space") // 2
    rows = sum_ref.shape[0] // (2 * slots)
    for slot in range(slots):
        there = pl.ds((layer * slots + slot) * rows, rows)
        for out_ref, bit in ((keep_ref, 0), (send_ref, 1)):
            piece = jnp.bitwise_xor(me, 2 * slot + bit)
            block = sum_ref[pl.ds(pl.multiple_of(piece * rows, rows), rows), :]
            out_ref[there, :] = block.astype(out_ref.dtype)


def two_weights_body(pre_ref, t_ref, sum_ref):
    one = jnp.maximum(pre_ref[...], jnp.zeros_like(pre_ref))
    packed_products(one, t_ref, slice(0, one.shape[1]), sum_ref)


def settled(own, near, far, hi_ref, lo_ref):
    above, below = by_parity(near, far)
    place = one_hot(own.shape[1], rim_index(hi_ref, lo_ref))
    for part in halves(above, below):
        own = own + dot_nt(part.astype(BF16), place)
    return own


def one_body(
    count, own_ref, near_ref, far_ref, hi_ref, lo_ref, pre_ref, zero_ref, t_two_ref, sum_two_ref, t_ref, keep_ref, send_ref, cot_ref, sum_ref
):
    chans, rows = pre_ref.shape
    ext = own_ref.shape[1]
    back = settled(own_ref[:chans, :rows], near_ref[:chans], far_ref[:chans], hi_ref, lo_ref)
    cot_ref[...] = jnp.where(pre_ref[...].astype(F32) > 0, back, 0.0).astype(BF16)

    def place(k):
        t_ref[offset_rows(k, chans), :] = dot(cot_ref[...], one_hot(rows, own_ref[pl.ds(chans + k, 1), :])).astype(BF16)

    loop(count, place)
    t_ref[count * chans :, :] = jnp.zeros((t_ref.shape[0] - count * chans, ext), BF16)
    above, below = by_parity(near_ref[chans:], far_ref[chans:])
    zero_rim, one_rim = halves(below, above)
    feats = jnp.concatenate([zero_ref[...], zero_rim.astype(BF16)], 1)
    packed_products(feats, t_ref, slice(0, ext), sum_ref)
    cut(sum_ref, 0, keep_ref, send_ref)
    packed_products(one_rim.astype(BF16), t_two_ref, slice(rows, ext), sum_ref, sum_two_ref)
    cut(sum_ref, 1, keep_ref, send_ref)


def back_body(weight_ref, t_ref, own_ref, near_ref, far_ref, total_ref):
    rows = own_ref.shape[1]
    add_back(weight_ref, t_ref, total_ref)
    own_ref[...] = total_ref[:, :rows]
    rim_gradients(near_ref, far_ref, total_ref[:, rows:])


def settle_body(own_ref, near_ref, far_ref, hi_ref, lo_ref, out_ref):
    out_ref[...] = settled(own_ref[...], near_ref[...], far_ref[...], hi_ref, lo_ref).astype(BF16)


def core_sum_body(layers, keep_ref, got_ref, own_ref, *send_refs):
    rows = own_ref.shape[0] // layers
    slots = len(send_refs) + 1
    for layer in range(layers):
        there = slice(layer * rows, (layer + 1) * rows)
        for slot, out_ref in enumerate((own_ref, *send_refs)):
            part = slice((layer * slots + slot) * rows, (layer * slots + slot + 1) * rows)
            out_ref[there] = (keep_ref[part] + got_ref[part].astype(F32)).astype(out_ref.dtype)


def chip_sum_body(own_ref, *refs):
    total = own_ref[...]
    for got_ref in refs[:-1]:
        total = total + got_ref[...].astype(F32)
    refs[-1][...] = total.astype(BF16)


def scan_sum_body(own_ref, got_ref, total_ref):
    total_ref[...] = (own_ref[...].astype(F32) + got_ref[...].astype(F32)).astype(BF16)


def unpack_body(scale, layers, *refs):
    *refs, all_ref, sems = refs
    piece_refs, outs, locals_ = refs[: -2 * layers], refs[-2 * layers : -layers], refs[-layers:]
    me = lax.axis_index("space")
    rows = piece_refs[0].shape[0] // layers
    count, chans = locals_[0].shape[0], locals_[0].shape[1]
    lane = lax.broadcasted_iota(I32, (chans, LANES), 1)
    copies = []
    for layer in range(layers):
        for slot, piece_ref in enumerate(piece_refs):
            piece = jnp.bitwise_xor(me, slot)
            block = piece_ref[layer * rows : (layer + 1) * rows].astype(F32)
            all_ref[pl.ds(pl.multiple_of(piece * rows, rows), rows), :] = block
        for first in range(0, count, CHUNK):
            chunk = pl.ds(first, min(CHUNK, count - first))
            for k in range(first, first + chunk.size):
                tile, shift = divmod(k * chans, LANES)
                block = all_ref[tile * chans : (tile + 1) * chans, :]
                if shift:
                    block = pltpu.roll(block, LANES - shift, 1)
                if shift + chans > LANES:
                    after = pltpu.roll(all_ref[(tile + 1) * chans : (tile + 2) * chans, :], LANES - shift, 1)
                    block = jnp.where(lane < LANES - shift, block, after)
                locals_[layer][k] = block[:, :chans] * scale
            copies.append(pltpu.make_async_copy(locals_[layer].at[chunk], outs[layer].at[chunk], sems.at[len(copies)]))
            copies[-1].start()
    for copy in copies:
        copy.wait()


def swap(block, axis, bit):
    return lax.ppermute(block, axis, [(i, i ^ bit) for i in range(lax.axis_size(axis))])


def swap_neighbours(near, far):
    inner = range(1, lax.axis_size("space") - 1)
    far = lax.ppermute(far, "space", [(i, i + 1 if i % 2 else i - 1) for i in inner])
    return swap(near, "space", 1), far


def swap_scans(block, step, steps):
    scans = lax.axis_size("scan")
    bits = (1 << step, 1 << (steps - 1 - step))
    bricks = range(lax.axis_size("space"))
    pairs = [(b * scans + z, b * scans + (z ^ bits[b % 2])) for b in bricks for z in range(scans)]
    return lax.ppermute(block, ("space", "scan"), pairs)


def summed(keep, got, layers, weight_shape, scale, beside):
    slots = lax.axis_size("space") // 2
    scans = lax.axis_size("scan")
    packed = 2 * keep.shape[0] // layers
    rows = keep.shape[0] // slots
    outs = [shape((rows, LANES), F32)] + [shape((rows, LANES), BF16)] * (slots - 1)
    own, *sends = call(functools.partial(core_sum_body, layers), outs, [keep, got])
    gots = [swap(block, "space", 2 * slot) for slot, block in enumerate(sends, 1)]
    total = call(chip_sum_body, shape((rows, LANES), BF16), [own, *gots])
    waiting = list(beside)
    state = None
    if scans & (scans - 1):
        total = lax.psum(total, "scan")
    else:
        steps = scans.bit_length() - 1
        for step in range(steps):
            more = swap_scans(total, step, steps)
            if waiting:
                total, state = waiting.pop(0)(total, state)
            total = call(scan_sum_body, shape((rows, LANES), BF16), [total, more])
    for work in waiting:
        total, state = work(total, state)
    pieces = []
    for slot in range(slots):
        piece = swap(total, "space", 2 * slot) if slot else total
        pieces += [piece, swap(piece, "space", 1)]
    return state, call(
        functools.partial(unpack_body, scale, layers),
        [shape(weight_shape, F32)] * layers,
        pieces,
        scratch=[pltpu.VMEM(weight_shape, F32)] * layers + [pltpu.VMEM((packed, LANES), F32), pltpu.SemaphoreType.DMA((layers * -(-weight_shape[0] // CHUNK),))],
        outs_in=HBM,
    )


def shards(act_zero, pre_act, cot_out, weight_one, weight_two, in_map, out_map, send_lo, send_hi):
    zero, pre, cot = (x[0, 0].T for x in (act_zero, pre_act, cot_out))
    ins, outs = (x[0, 0][:, None, :] for x in (in_map, out_map))
    lo, hi = send_lo[0], send_hi[0]
    chans, rows = zero.shape
    count, _, pairs = ins.shape
    rim = 2 * lo.shape[1]
    ext = rows + rim
    scenes = lax.axis_size("scan")
    bricks = lax.axis_size("space")
    tiles = -(-count * chans // LANES)
    tall = tiles * LANES
    unit = 16 * bricks
    packed = -(-tiles * chans // unit) * unit
    gather_flops = 2 * count * chans * ext * rows
    back_flops = 2 * count * chans * chans * ext

    operands = [outs, cot, ins, weight_two, hi, lo, zero, pre]
    t_two, own, near, far = call(
        two_body,
        [shape((tall, ext), BF16), shape((chans + -(-count // 8) * 8, ext), F32), shape((2 * chans, rim), BF16), shape((2 * chans, rim), BF16)],
        operands,
        scratch=[pltpu.VMEM(x.shape, x.dtype) for x in operands]
        + [
            pltpu.VMEM((tall, ext), BF16),
            pltpu.VMEM((count * (chans + 16), pairs), BF16),
            pltpu.VMEM((chans, ext), F32),
            pltpu.SemaphoreType.DMA((len(operands) + 1,)),
        ],
        flops=gather_flops + back_flops,
        moved=8 << 20,
        args_in=HBM,
        outs_in=(HBM, VMEM, VMEM, VMEM),
        room=WHOLE,
    )
    near, far = swap_neighbours(near, far)
    sum_two = call(two_weights_body, shape((packed, LANES), F32), [pre, t_two], flops=back_flops, moved=6 << 20)
    t_one, keep, send = call(
        functools.partial(one_body, count),
        [shape((tall, ext), BF16), shape((packed, LANES), F32), shape((packed, LANES), BF16)],
        [own, near, far, hi, lo, pre, zero, t_two, sum_two],
        scratch=[pltpu.VMEM((chans, rows), BF16), pltpu.VMEM((packed, LANES), F32)],
        flops=gather_flops + back_flops,
        moved=8 << 20,
    )
    got = swap(send, "space", 1)
    own, near, far = call(
        back_body,
        [shape((chans, rows), F32), shape((chans, rim), BF16), shape((chans, rim), BF16)],
        [weight_one, t_one],
        scratch=[pltpu.VMEM((chans, ext), F32)],
        flops=back_flops,
        moved=6 << 20,
    )
    keep, near, far = lax.optimization_barrier((keep, near, far))

    def swap_edges(held, _):
        held, *edges = lax.optimization_barrier((held, near, far))
        held, *edges = lax.optimization_barrier((held, *swap_neighbours(*edges)))
        return held, edges

    def settle(held, edges):
        held, own_rows, *edges = lax.optimization_barrier((held, own, *edges))
        grad_act = call(settle_body, shape((chans, rows), BF16), [own_rows, *edges, hi, lo])
        return lax.optimization_barrier((held, grad_act))

    grad_act, (grad_one, grad_two) = summed(keep, got, 2, weight_one.shape, 1.0 / scenes, (swap_edges, settle))
    return grad_act.T[None, None], grad_one, grad_two


def solution(mesh):
    return jax.shard_map(
        shards,
        mesh=mesh,
        in_specs=(
            P("scan", "space", None, None),
            P("scan", "space", None, None),
            P("scan", "space", None, None),
            P(),
            P(),
            P("scan", "space", None, None),
            P("scan", "space", None, None),
            P("scan", "space", None),
            P("scan", "space", None),
        ),
        out_specs=(P("scan", "space", None, None), P(), P()),
        check_vma=False,
    )
```

time: 64.1 us -> 60.1 us (0.938)
  starting transfers between devices: 23.9 us -> 19.5 us
  local copies, waits for them, and re-layouts: 0.99 us -> 2.99 us
  waiting for transfers between devices: 19.2 us -> 18 us
    ppermute x17 -> x13, starting transfers between devices: 22.6 us -> 13.8 us  [swap(): lax.ppermute(block, axis, [(i, i ^ bit) for i in range(lax.axis_size(axis...]
    ppermute x17 -> x13, waiting for transfers between devices: 19.2 us -> 13.3 us  [swap(): lax.ppermute(block, axis, [(i, i ^ bit) for i in range(lax.axis_size(axis...]
    ppermute x2 -> x4, waiting for transfers between devices: 0.01 us -> 4.67 us  [the longest x2 4.67 us: swap_scans(): return lax.ppermute(block, ('space', 'scan'), pairs)]
    ppermute x2 -> x4, starting transfers between devices: 1.32 us -> 5.76 us  [the longest x2 4.46 us: swap_scans(): return lax.ppermute(block, ('space', 'scan'), pairs)]
    unnamed x14 -> x16, local copies, waits for them, and re-layouts: 0.99 us -> 2.99 us
    pallas_call x9 -> x10, Pallas kernels: 19.1 us -> 18.6 us  [call(): pl.pallas_call(body, out_shape=outs if single else tuple(outs), in_specs=...]
  transfers between devices with their start and end apart: 19 -> 17, of which waited for: 12 -> 11; matrix products, arithmetic and copies ran while one was open for 0% -> 0% of each run, Pallas kernels for 3% -> 5%
where the time goes in v3:
time: 60.1 us; the launch traced here: 59.9 us
  starting transfers between devices  19.5 us (32%)
  Pallas kernels  18.6 us (31%)
  waiting for transfers between devices  18 us (30%)
  local copies, waits for them, and re-layouts  2.99 us (5%)
  between operations  0.79 us (1%)
    pallas_call x10, Pallas kernels, call(): pl.pallas_call(body, out_shape=outs if single else tuple(outs), in_specs=...  18.6 us
    ppermute x13, starting transfers between devices, swap(): lax.ppermute(block, axis, [(i, i ^ bit) for i in range(lax.axis_size(axis...  13.8 us
    ppermute x13, waiting for transfers between devices, swap(): lax.ppermute(block, axis, [(i, i ^ bit) for i in range(lax.axis_size(axis...  13.3 us
    ppermute x2, waiting for transfers between devices, swap_scans(): return lax.ppermute(block, ('space', 'scan'), pairs)  4.67 us
    ppermute x2, starting transfers between devices, swap_scans(): return lax.ppermute(block, ('space', 'scan'), pairs)  4.46 us
    unnamed x16, local copies, waits for them, and re-layouts  2.99 us
    ppermute x2, starting transfers between devices, swap_neighbours(): lax.ppermute(far, 'space', [(i, i + 1 if i % 2 else i - 1) for i in inner])  1.3 us
  transfers between devices with their start and end apart: 17, of which 11 were waited for; matrix products, arithmetic and copies ran while one was open for 0% of the time, Pallas kernels for 5%

profile of v3, /device:TPU:0, one launch (start us, length us, event | category | flops | bytes accessed | tf_op | source)
XLA Modules:
  0.0 59.9 jit_solution(15983217119978310290)
XLA Ops:
  0.7 8.2 %shard_map.112 = (bf16[2688,640]{1,0:T(8,128)(2,1)}, f32[128,640]{1,0:T(8,128)}, bf16[192,128]{1,0:T(8,128)(2,1)}, bf16[192,128]{1,0:T(8,128)(2,1)}) custom-call(s32[27,1,256]{2,1,0:T(1,128)} %bitcast.29, bf16[96,512]{1,0:T(8,128)(2,1)} %bitcast.28, s32[27,1,256]{2,1,0:T(1,128)} %bitcast.30, bf16[27,96,96]{2,1,0:T(8,128)(2,1)} %refs_3_.1, s32[1,64]{1,0:T(1,128)} %bitcast.19, ...), custom_call_target="tpu_custom_call" | custom-call | flops 2017198080 | bytes 8388608 | tf_op jit(solution)/shard_map/pallas_call | solution.py:23
  8.8 0.5 collective-permute-start
  9.4 0.7 %collective-permute-start.1 = (bf16[192,128]{1,0:T(8,128)(2,1)}, bf16[192,128]{1,0:T(8,128)(2,1)S(1)}, u32[]{:S(2)}, u32[]{:S(2)}) collective-permute-start(bf16[192,128]{1,0:T(8,128)(2,1)} %get-tuple-element.36), channel_id=1, source_target_pairs={{4,8},{8,4},{12,16},{16,12},{20,24},{24,20},{5,9},{9,5},{13,17},{1... | collective-permute-start | bytes 147464 | tf_op jit(solution)/shard_map/ppermute | solution.py:294
  10.0 2.0 %copy-done = bf16[2688,640]{1,0:T(8,128)(2,1)S(1)} copy-done((bf16[2688,640]{1,0:T(8,128)(2,1)S(1)}, bf16[2688,640]{1,0:T(8,128)(2,1)}, u32[]{:S(2)}) %copy-start) | copy-done | bytes 3440664
  12.0 1.0 %shard_map.113.sum_two_ref = f32[2048,128]{1,0:T(8,128)S(1)} custom-call(bf16[96,512]{1,0:T(8,128)(2,1)S(1)} %bitcast.17, bf16[2688,640]{1,0:T(8,128)(2,1)S(1)} %copy-done), custom_call_target="tpu_custom_call" | custom-call | flops 318504960 | bytes 6291456 | tf_op jit(solution)/shard_map/pallas_call | solution.py:23
  13.0 1.0 %copy-done.1 = bf16[2688,640]{1,0:T(8,128)(2,1)S(1)} copy-done((bf16[2688,640]{1,0:T(8,128)(2,1)S(1)}, bf16[2688,640]{1,0:T(8,128)(2,1)}, u32[]{:S(2)}) %copy-start.1) | copy-done | bytes 3440664
  14.0 5.4 %shard_map.114 = (bf16[2688,640]{1,0:T(8,128)(2,1)S(1)}, f32[2048,128]{1,0:T(8,128)S(1)}, bf16[2048,128]{1,0:T(8,128)(2,1)S(1)}) custom-call(f32[128,640]{1,0:T(8,128)S(1)} %copy-done.7, bf16[192,128]{1,0:T(8,128)(2,1)S(1)} %collective-permute-done.near_ref, bf16[192,128]{1,0:T(8,128)(2,1)S(1)} %collective-permute-done.1.far_ref, s32[1,64]{1,0:T(1,128)S(1)} %bitcast.20, ...), custom_call_target="tpu_custom_call" | custom-call | flops 2017198080 | bytes 8388608 | tf_op jit(solution)/shard_map/pallas_call | solution.py:23
  19.4 3.9 %collective-permute-start.2 = (bf16[2048,128]{1,0:T(8,128)(2,1)S(1)}, bf16[2048,128]{1,0:T(8,128)(2,1)S(1)}, u32[]{:S(2)}, u32[]{:S(2)}) collective-permute-start(bf16[2048,128]{1,0:T(8,128)(2,1)S(1)} %get-tuple-element.43), channel_id=1, source_target_pairs={{0,4},{4,0},{8,12},{12,8},{16,20},{20,16},{24,28},{28,24},{1,5},{5... | collective-permute-start | bytes 1572872 | tf_op jit(solution)/shard_map/ppermute | solution.py:289
  23.3 1.1 %shard_map.115 = (f32[96,512]{1,0:T(8,128)S(1)}, bf16[96,128]{1,0:T(8,128)(2,1)S(1)}, bf16[96,128]{1,0:T(8,128)(2,1)S(1)}) custom-call(bf16[27,96,96]{2,1,0:T(8,128)(2,1)S(1)} %copy-done.2, bf16[2688,640]{1,0:T(8,128)(2,1)S(1)} %get-tuple-element.39.t_ref), custom_call_target="tpu_custom_call" | custom-call | flops 318504960 | bytes 6291456 | tf_op jit(solution)/shard_map/pallas_call | solution.py:23
  24.4 0.4 collective-permute-done.2.got_ref
  24.9 0.1 shard_map.116
  25.0 1.6 %collective-permute-start.3 = (bf16[512,128]{1,0:T(8,128)(2,1)S(1)}, bf16[512,128]{1,0:T(8,128)(2,1)S(1)}, u32[]{:S(2)}, u32[]{:S(2)}) collective-permute-start(bf16[512,128]{1,0:T(8,128)(2,1)S(1)} %get-tuple-element.45), channel_id=1, source_target_pairs={{0,8},{4,12},{8,0},{12,4},{16,24},{20,28},{24,16},{28,20},{1,9},{5... | collective-permute-start | bytes 393224 | tf_op jit(solution)/shard_map/ppermute | solution.py:289
  26.5 0.9 %collective-permute-start.4 = (bf16[512,128]{1,0:T(8,128)(2,1)S(1)}, bf16[512,128]{1,0:T(8,128)(2,1)S(1)}, u32[]{:S(2)}, u32[]{:S(2)}) collective-permute-start(bf16[512,128]{1,0:T(8,128)(2,1)S(1)} %get-tuple-element.46), channel_id=1, source_target_pairs={{0,16},{4,20},{8,24},{12,28},{16,0},{20,4},{24,8},{28,12},{1,17},{... | collective-permute-start | bytes 393224 | tf_op jit(solution)/shard_map/ppermute | solution.py:289
  27.4 1.1 %collective-permute-start.5 = (bf16[512,128]{1,0:T(8,128)(2,1)S(1)}, bf16[512,128]{1,0:T(8,128)(2,1)S(1)}, u32[]{:S(2)}, u32[]{:S(2)}) collective-permute-start(bf16[512,128]{1,0:T(8,128)(2,1)S(1)} %get-tuple-element.47), channel_id=1, source_target_pairs={{0,24},{4,28},{8,16},{12,20},{16,8},{20,12},{24,0},{28,4},{1,25},{... | collective-permute-start | bytes 393224 | tf_op jit(solution)/shard_map/ppermute | solution.py:289
  28.5 2.6 %collective-permute-done.3.refs_0_ = bf16[512,128]{1,0:T(8,128)(2,1)S(1)} collective-permute-done((bf16[512,128]{1,0:T(8,128)(2,1)S(1)}, bf16[512,128]{1,0:T(8,128)(2,1)S(1)}, u32[]{:S(2)}, u32[]{:S(2)}) %collective-permute-start.3) | collective-permute-done | bytes 131104 | tf_op jit(solution)/shard_map/ppermute | solution.py:289
  31.1 3.7 %collective-permute-done.4.refs_1_ = bf16[512,128]{1,0:T(8,128)(2,1)S(1)} collective-permute-done((bf16[512,128]{1,0:T(8,128)(2,1)S(1)}, bf16[512,128]{1,0:T(8,128)(2,1)S(1)}, u32[]{:S(2)}, u32[]{:S(2)}) %collective-permute-start.4) | collective-permute-done | bytes 131104 | tf_op jit(solution)/shard_map/ppermute | solution.py:289
  34.9 1.6 %collective-permute-start.8 = (bf16[512,128]{1,0:T(8,128)(2,1)S(1)}, bf16[512,128]{1,0:T(8,128)(2,1)S(1)}, u32[]{:S(2)}, u32[]{:S(2)}) collective-permute-start(bf16[512,128]{1,0:T(8,128)(2,1)S(1)} %shard_map.117.own_ref), channel_id=1, source_target_pairs={{0,1},{1,0},{2,3},{3,2},{4,6},{5,7},{6,4},{7,5},{8,9},{9,8},{10,11... | collective-permute-start | bytes 393224 | tf_op jit(solution)/shard_map/ppermute | solution.py:303
  36.5 0.7 %collective-permute-start.7 = (bf16[96,128]{1,0:T(8,128)(2,1)S(1)}, bf16[96,128]{1,0:T(8,128)(2,1)S(1)}, u32[]{:S(2)}, u32[]{:S(2)}) collective-permute-start(bf16[96,128]{1,0:T(8,128)(2,1)S(1)} %get-tuple-element.52), channel_id=1, source_target_pairs={{4,8},{8,4},{12,16},{16,12},{20,24},{24,20},{5,9},{9,5},{13,17},{1... | collective-permute-start | bytes 73736 | tf_op jit(solution)/shard_map/ppermute | solution.py:294
  37.2 0.5 collective-permute-done.6.near_ref
  37.7 2.4 %collective-permute-done.8.got_ref = bf16[512,128]{1,0:T(8,128)(2,1)S(1)} collective-permute-done((bf16[512,128]{1,0:T(8,128)(2,1)S(1)}, bf16[512,128]{1,0:T(8,128)(2,1)S(1)}, u32[]{:S(2)}, u32[]{:S(2)}) %collective-permute-start.8) | collective-permute-done | bytes 131104 | tf_op jit(solution)/shard_map/ppermute | solution.py:303
  40.1 2.8 %collective-permute-start.9 = (bf16[512,128]{1,0:T(8,128)(2,1)S(1)}, bf16[512,128]{1,0:T(8,128)(2,1)S(1)}, u32[]{:S(2)}, u32[]{:S(2)}) collective-permute-start(bf16[512,128]{1,0:T(8,128)(2,1)S(1)} %shard_map.118.own_ref), channel_id=1, source_target_pairs={{0,2},{1,3},{2,0},{3,1},{4,5},{5,4},{6,7},{7,6},{8,10},{9,11},{10,... | collective-permute-start | bytes 393224 | tf_op jit(solution)/shard_map/ppermute | solution.py:303
  43.0 0.9 %shard_map.119 = bf16[96,512]{1,0:T(8,128)(2,1)} custom-call(f32[96,512]{1,0:T(8,128)S(1)} %get-tuple-element.58.own_ref, bf16[96,128]{1,0:T(8,128)(2,1)S(1)} %collective-permute-done.6.near_ref, bf16[96,128]{1,0:T(8,128)(2,1)S(1)} %collective-permute-done.7.far_ref, s32[1,64]{1,0:T(1,128)S(1)} %bitcast.21, s32[1,64]{1,0:T(1,128)S(1)} %bitcast.24), custom_call_target="tpu_custom_call" | custom-call | tf_op jit(solution)/shard_map/pallas_call | solution.py:23
  43.9 2.3 %collective-permute-done.9.got_ref = bf16[512,128]{1,0:T(8,128)(2,1)S(1)} collective-permute-done((bf16[512,128]{1,0:T(8,128)(2,1)S(1)}, bf16[512,128]{1,0:T(8,128)(2,1)S(1)}, u32[]{:S(2)}, u32[]{:S(2)}) %collective-permute-start.9) | collective-permute-done | bytes 131104 | tf_op jit(solution)/shard_map/ppermute | solution.py:303
  46.2 4.5 %collective-permute-start.15 = (bf16[512,128]{1,0:T(8,128)(2,1)S(1)}, bf16[512,128]{1,0:T(8,128)(2,1)S(1)}, u32[]{:S(2)}, u32[]{:S(2)}) collective-permute-start(bf16[512,128]{1,0:T(8,128)(2,1)S(1)} %shard_map.120.refs_0_), channel_id=1, source_target_pairs={{0,24},{4,28},{8,16},{12,20},{16,8},{20,12},{24,0},{28,4},{1,25},{... | collective-permute-start | bytes 393224 | tf_op jit(solution)/shard_map/ppermute | solution.py:289
  50.7 0.4 collective-permute-start.13
  51.1 0.4 collective-permute-start.11
  51.5 3.5 %collective-permute-done.15.refs_6_ = bf16[512,128]{1,0:T(8,128)(2,1)S(1)} collective-permute-done((bf16[512,128]{1,0:T(8,128)(2,1)S(1)}, bf16[512,128]{1,0:T(8,128)(2,1)S(1)}, u32[]{:S(2)}, u32[]{:S(2)}) %collective-permute-start.15) | collective-permute-done | bytes 131104 | tf_op jit(solution)/shard_map/ppermute | solution.py:289
  55.1 1.4 %collective-permute-done.13.refs_4_ = bf16[512,128]{1,0:T(8,128)(2,1)S(1)} collective-permute-done((bf16[512,128]{1,0:T(8,128)(2,1)S(1)}, bf16[512,128]{1,0:T(8,128)(2,1)S(1)}, u32[]{:S(2)}, u32[]{:S(2)}) %collective-permute-start.13) | collective-permute-done | bytes 131104 | tf_op jit(solution)/shard_map/ppermute | solution.py:289
  56.6 0.4 collective-permute-start.12
  57.0 0.8 %collective-permute-done.14.refs_5_ = bf16[512,128]{1,0:T(8,128)(2,1)S(1)} collective-permute-done((bf16[512,128]{1,0:T(8,128)(2,1)S(1)}, bf16[512,128]{1,0:T(8,128)(2,1)S(1)}, u32[]{:S(2)}, u32[]{:S(2)}) %collective-permute-start.14) | collective-permute-done | bytes 131104 | tf_op jit(solution)/shard_map/ppermute | solution.py:289
  57.9 0.2 collective-permute-done.12.refs_3_
  58.1 1.9 %shard_map.121 = (f32[27,96,96]{2,1,0:T(8,128)}, f32[27,96,96]{2,1,0:T(8,128)}) custom-call(bf16[512,128]{1,0:T(8,128)(2,1)S(1)} %shard_map.120.refs_0_, bf16[512,128]{1,0:T(8,128)(2,1)S(1)} %collective-permute-done.10.refs_1_, bf16[512,128]{1,0:T(8,128)(2,1)S(1)} %collective-permute-done.11.refs_2_, bf16[512,128]{1,0:T(8,128)(2,1)S(1)} %collective-permute-done.12.refs_3_, ...), custom_call_target="tpu_custom_call" | custom-call | tf_op jit(solution)/shard_map/pallas_call | solution.py:23
  (28 shorter events, 0.3 us)
Async XLA Ops:
  0.6 9.4 %copy-start.3 = (bf16[1,1,512,96]{2,3,1,0:T(8,128)(2,1)S(1)}, bf16[1,1,512,96]{2,3,1,0:T(8,128)(2,1)}, u32[]{:S(2)}) copy-start(bf16[1,1,512,96]{2,3,1,0:T(8,128)(2,1)} %param.10) | copy-start | bytes 294916
  0.6 12.3 %copy-start.6 = (bf16[1,1,512,96]{2,3,1,0:T(8,128)(2,1)S(1)}, bf16[1,1,512,96]{2,3,1,0:T(8,128)(2,1)}, u32[]{:S(2)}) copy-start(bf16[1,1,512,96]{2,3,1,0:T(8,128)(2,1)} %param.9) | copy-start | bytes 294916
  8.8 4.2 %copy-start.4 = (s32[1,1,64]{2,1,0:T(1,128)S(1)}, s32[1,1,64]{2,1,0:T(1,128)}, u32[]{:S(2)}) copy-start(s32[1,1,64]{2,1,0:T(1,128)} %param.17) | copy-start | bytes 772
  8.8 4.2 %copy-start.5 = (s32[1,1,64]{2,1,0:T(1,128)S(1)}, s32[1,1,64]{2,1,0:T(1,128)}, u32[]{:S(2)}) copy-start(s32[1,1,64]{2,1,0:T(1,128)} %param.16) | copy-start | bytes 772
  8.8 4.1 %collective-permute-start = (bf16[192,128]{1,0:T(8,128)(2,1)}, bf16[192,128]{1,0:T(8,128)(2,1)S(1)}, u32[]{:S(2)}, u32[]{:S(2)}) collective-permute-start(bf16[192,128]{1,0:T(8,128)(2,1)} %get-tuple-element.35), channel_id=1, source_target_pairs={{0,4},{4,0},{8,12},{12,8},{16,20},{20,16},{24,28},{28,24},{1,5},{5... | collective-permute-start | bytes 147464 | tf_op jit(solution)/shard_map/ppermute | solution.py:289
  9.4 3.6 %collective-permute-start.1 = (bf16[192,128]{1,0:T(8,128)(2,1)}, bf16[192,128]{1,0:T(8,128)(2,1)S(1)}, u32[]{:S(2)}, u32[]{:S(2)}) collective-permute-start(bf16[192,128]{1,0:T(8,128)(2,1)} %get-tuple-element.36), channel_id=1, source_target_pairs={{4,8},{8,4},{12,16},{16,12},{20,24},{24,20},{5,9},{9,5},{13,17},{1... | collective-permute-start | bytes 147464 | tf_op jit(solution)/shard_map/ppermute | solution.py:294
  10.0 2.0 %copy-start = (bf16[2688,640]{1,0:T(8,128)(2,1)S(1)}, bf16[2688,640]{1,0:T(8,128)(2,1)}, u32[]{:S(2)}) copy-start(bf16[2688,640]{1,0:T(8,128)(2,1)} %get-tuple-element.37.t_ref.t_two_ref) | copy-start | bytes 10321924
  12.0 2.0 %copy-start.1 = (bf16[2688,640]{1,0:T(8,128)(2,1)S(1)}, bf16[2688,640]{1,0:T(8,128)(2,1)}, u32[]{:S(2)}) copy-start(bf16[2688,640]{1,0:T(8,128)(2,1)} %get-tuple-element.37.t_ref.t_two_ref) | copy-start | bytes 10321924
  12.0 2.0 %copy-start.7 = (f32[128,640]{1,0:T(8,128)S(1)}, f32[128,640]{1,0:T(8,128)}, u32[]{:S(2)}) copy-start(f32[128,640]{1,0:T(8,128)} %get-tuple-element.34.own_ref) | copy-start | bytes 983044
  14.0 9.3 %copy-start.2 = (bf16[27,96,96]{2,1,0:T(8,128)(2,1)S(1)}, bf16[27,96,96]{2,1,0:T(8,128)(2,1)}, u32[]{:S(2)}) copy-start(bf16[27,96,96]{2,1,0:T(8,128)(2,1)} %weight_ref.1) | copy-start | bytes 1492996
  19.4 5.5 %collective-permute-start.2 = (bf16[2048,128]{1,0:T(8,128)(2,1)S(1)}, bf16[2048,128]{1,0:T(8,128)(2,1)S(1)}, u32[]{:S(2)}, u32[]{:S(2)}) collective-permute-start(bf16[2048,128]{1,0:T(8,128)(2,1)S(1)} %get-tuple-element.43), channel_id=1, source_target_pairs={{0,4},{4,0},{8,12},{12,8},{16,20},{20,16},{24,28},{28,24},{1,5},{5... | collective-permute-start | bytes 1572872 | tf_op jit(solution)/shard_map/ppermute | solution.py:289
  25.0 6.2 %collective-permute-start.3 = (bf16[512,128]{1,0:T(8,128)(2,1)S(1)}, bf16[512,128]{1,0:T(8,128)(2,1)S(1)}, u32[]{:S(2)}, u32[]{:S(2)}) collective-permute-start(bf16[512,128]{1,0:T(8,128)(2,1)S(1)} %get-tuple-element.45), channel_id=1, source_target_pairs={{0,8},{4,12},{8,0},{12,4},{16,24},{20,28},{24,16},{28,20},{1,9},{5... | collective-permute-start | bytes 393224 | tf_op jit(solution)/shard_map/ppermute | solution.py:289
  26.5 8.3 %collective-permute-start.4 = (bf16[512,128]{1,0:T(8,128)(2,1)S(1)}, bf16[512,128]{1,0:T(8,128)(2,1)S(1)}, u32[]{:S(2)}, u32[]{:S(2)}) collective-permute-start(bf16[512,128]{1,0:T(8,128)(2,1)S(1)} %get-tuple-element.46), channel_id=1, source_target_pairs={{0,16},{4,20},{8,24},{12,28},{16,0},{20,4},{24,8},{28,12},{1,17},{... | collective-permute-start | bytes 393224 | tf_op jit(solution)/shard_map/ppermute | solution.py:289
  27.4 7.4 %collective-permute-start.5 = (bf16[512,128]{1,0:T(8,128)(2,1)S(1)}, bf16[512,128]{1,0:T(8,128)(2,1)S(1)}, u32[]{:S(2)}, u32[]{:S(2)}) collective-permute-start(bf16[512,128]{1,0:T(8,128)(2,1)S(1)} %get-tuple-element.47), channel_id=1, source_target_pairs={{0,24},{4,28},{8,16},{12,20},{16,8},{20,12},{24,0},{28,4},{1,25},{... | collective-permute-start | bytes 393224 | tf_op jit(solution)/shard_map/ppermute | solution.py:289
  34.9 5.2 %collective-permute-start.8 = (bf16[512,128]{1,0:T(8,128)(2,1)S(1)}, bf16[512,128]{1,0:T(8,128)(2,1)S(1)}, u32[]{:S(2)}, u32[]{:S(2)}) collective-permute-start(bf16[512,128]{1,0:T(8,128)(2,1)S(1)} %shard_map.117.own_ref), channel_id=1, source_target_pairs={{0,1},{1,0},{2,3},{3,2},{4,6},{5,7},{6,4},{7,5},{8,9},{9,8},{10,11... | collective-permute-start | bytes 393224 | tf_op jit(solution)/shard_map/ppermute | solution.py:303
  36.5 1.2 %collective-permute-start.6 = (bf16[96,128]{1,0:T(8,128)(2,1)S(1)}, bf16[96,128]{1,0:T(8,128)(2,1)S(1)}, u32[]{:S(2)}, u32[]{:S(2)}) collective-permute-start(bf16[96,128]{1,0:T(8,128)(2,1)S(1)} %get-tuple-element.51), channel_id=1, source_target_pairs={{0,4},{4,0},{8,12},{12,8},{16,20},{20,16},{24,28},{28,24},{1,5},{5... | collective-permute-start | bytes 73736 | tf_op jit(solution)/shard_map/ppermute | solution.py:289
  36.5 1.2 %collective-permute-start.7 = (bf16[96,128]{1,0:T(8,128)(2,1)S(1)}, bf16[96,128]{1,0:T(8,128)(2,1)S(1)}, u32[]{:S(2)}, u32[]{:S(2)}) collective-permute-start(bf16[96,128]{1,0:T(8,128)(2,1)S(1)} %get-tuple-element.52), channel_id=1, source_target_pairs={{4,8},{8,4},{12,16},{16,12},{20,24},{24,20},{5,9},{9,5},{13,17},{1... | collective-permute-start | bytes 73736 | tf_op jit(solution)/shard_map/ppermute | solution.py:294
  40.1 6.0 %collective-permute-start.9 = (bf16[512,128]{1,0:T(8,128)(2,1)S(1)}, bf16[512,128]{1,0:T(8,128)(2,1)S(1)}, u32[]{:S(2)}, u32[]{:S(2)}) collective-permute-start(bf16[512,128]{1,0:T(8,128)(2,1)S(1)} %shard_map.118.own_ref), channel_id=1, source_target_pairs={{0,2},{1,3},{2,0},{3,1},{4,5},{5,4},{6,7},{7,6},{8,10},{9,11},{10,... | collective-permute-start | bytes 393224 | tf_op jit(solution)/shard_map/ppermute | solution.py:303
  46.2 8.9 %collective-permute-start.15 = (bf16[512,128]{1,0:T(8,128)(2,1)S(1)}, bf16[512,128]{1,0:T(8,128)(2,1)S(1)}, u32[]{:S(2)}, u32[]{:S(2)}) collective-permute-start(bf16[512,128]{1,0:T(8,128)(2,1)S(1)} %shard_map.120.refs_0_), channel_id=1, source_target_pairs={{0,24},{4,28},{8,16},{12,20},{16,8},{20,12},{24,0},{28,4},{1,25},{... | collective-permute-start | bytes 393224 | tf_op jit(solution)/shard_map/ppermute | solution.py:289
  50.7 5.8 %collective-permute-start.13 = (bf16[512,128]{1,0:T(8,128)(2,1)S(1)}, bf16[512,128]{1,0:T(8,128)(2,1)S(1)}, u32[]{:S(2)}, u32[]{:S(2)}) collective-permute-start(bf16[512,128]{1,0:T(8,128)(2,1)S(1)} %shard_map.120.refs_0_), channel_id=1, source_target_pairs={{0,16},{4,20},{8,24},{12,28},{16,0},{20,4},{24,8},{28,12},{1,17},{... | collective-permute-start | bytes 393224 | tf_op jit(solution)/shard_map/ppermute | solution.py:289
  51.1 5.5 %collective-permute-start.11 = (bf16[512,128]{1,0:T(8,128)(2,1)S(1)}, bf16[512,128]{1,0:T(8,128)(2,1)S(1)}, u32[]{:S(2)}, u32[]{:S(2)}) collective-permute-start(bf16[512,128]{1,0:T(8,128)(2,1)S(1)} %shard_map.120.refs_0_), channel_id=1, source_target_pairs={{0,8},{4,12},{8,0},{12,4},{16,24},{20,28},{24,16},{28,20},{1,9},{5... | collective-permute-start | bytes 393224 | tf_op jit(solution)/shard_map/ppermute | solution.py:289
  51.5 5.5 %collective-permute-start.10 = (bf16[512,128]{1,0:T(8,128)(2,1)S(1)}, bf16[512,128]{1,0:T(8,128)(2,1)S(1)}, u32[]{:S(2)}, u32[]{:S(2)}) collective-permute-start(bf16[512,128]{1,0:T(8,128)(2,1)S(1)} %shard_map.120.refs_0_), channel_id=1, source_target_pairs={{0,4},{4,0},{8,12},{12,8},{16,20},{20,16},{24,28},{28,24},{1,5},{5... | collective-permute-start | bytes 393224 | tf_op jit(solution)/shard_map/ppermute | solution.py:289
  55.1 2.0 %collective-permute-start.16 = (bf16[512,128]{1,0:T(8,128)(2,1)S(1)}, bf16[512,128]{1,0:T(8,128)(2,1)S(1)}, u32[]{:S(2)}, u32[]{:S(2)}) collective-permute-start(bf16[512,128]{1,0:T(8,128)(2,1)S(1)} %collective-permute-done.15.refs_6_), channel_id=1, source_target_pairs={{0,4},{4,0},{8,12},{12,8},{16,20},{20,16},{24,28},{28,24},{1,5},{5... | collective-permute-start | bytes 393224 | tf_op jit(solution)/shard_map/ppermute | solution.py:289
  56.5 1.3 %collective-permute-start.14 = (bf16[512,128]{1,0:T(8,128)(2,1)S(1)}, bf16[512,128]{1,0:T(8,128)(2,1)S(1)}, u32[]{:S(2)}, u32[]{:S(2)}) collective-permute-start(bf16[512,128]{1,0:T(8,128)(2,1)S(1)} %collective-permute-done.13.refs_4_), channel_id=1, source_target_pairs={{0,4},{4,0},{8,12},{12,8},{16,20},{20,16},{24,28},{28,24},{1,5},{5... | collective-permute-start | bytes 393224 | tf_op jit(solution)/shard_map/ppermute | solution.py:289
  56.6 1.5 %collective-permute-start.12 = (bf16[512,128]{1,0:T(8,128)(2,1)S(1)}, bf16[512,128]{1,0:T(8,128)(2,1)S(1)}, u32[]{:S(2)}, u32[]{:S(2)}) collective-permute-start(bf16[512,128]{1,0:T(8,128)(2,1)S(1)} %collective-permute-done.11.refs_2_), channel_id=1, source_target_pairs={{0,4},{4,0},{8,12},{12,8},{16,20},{20,16},{24,28},{28,24},{1,5},{5... | collective-permute-start | bytes 393224 | tf_op jit(solution)/shard_map/ppermute | solution.py:289

commit v4 on v3

--- a/solution.py
+++ b/solution.py
@@ -111,23 +111,13 @@
     loop(count // 3, body)
 
 
-def two_body(*refs):
-    operands, (t_out, own_ref, near_ref, far_ref), scratch = refs[:8], refs[8:12], refs[12:]
-    locals_, (t_ref, c_ref, total_ref, sems) = scratch[:8], scratch[8:]
-    copies = [
-        pltpu.make_async_copy(operand, local, sems.at[i]) for i, (operand, local) in enumerate(zip(operands, locals_, strict=True))
-    ]
-    for copy in copies:
-        copy.start()
-    outs_ref, cot_ref, ins_ref, weight_ref, hi_ref, lo_ref, zero_ref, pre_ref = locals_
-    count, pairs = ins_ref.shape[0], ins_ref.shape[2]
+def pick_body(outs_ref, cot_ref, c_ref):
     chans, rows = cot_ref.shape
-    ext = t_ref.shape[1]
+    pairs = outs_ref.shape[2]
     tall = chans + 16
     row = lax.broadcasted_iota(I32, (16, pairs), 0)
-    t_ref[count * chans :, :] = jnp.zeros((t_ref.shape[0] - count * chans, ext), BF16)
-
-    def pick_outs(k):
+
+    def pick(k):
         index = outs_ref[k]
         base = pl.multiple_of(k * tall, 16)
         c_ref[pl.ds(base, chans), :] = dot(cot_ref[...], one_hot(rows, index)).astype(BF16)
@@ -135,32 +125,31 @@
         code = jnp.where(row == 0, left // 16, jnp.where(row == 1, left % 16, 0))
         c_ref[pl.ds(base + chans, 16), :] = code.astype(F32).astype(BF16)
 
-    copies[0].wait()
-    copies[1].wait()
-    loop(count, pick_outs)
-
-    def put_ins(k):
+    loop(outs_ref.shape[0], pick)
+
+
+def two_body(ins_ref, c_ref, weight_ref, hi_ref, lo_ref, zero_ref, pre_ref, t_ref, own_ref, near_ref, far_ref, total_ref):
+    count = ins_ref.shape[0]
+    chans, rows = zero_ref.shape
+    ext = t_ref.shape[1]
+    tall = chans + 16
+    t_ref[count * chans :, :] = jnp.zeros((t_ref.shape[0] - count * chans, ext), BF16)
+
+    def place(k):
         picked = c_ref[pl.ds(pl.multiple_of(k * tall, 16), tall), :]
         placed = dot_nt(picked, one_hot(ext, ins_ref[k]))
         t_ref[offset_rows(k, chans), :] = placed[:chans].astype(BF16)
         code = placed[chans : chans + 1] * 16.0 + placed[chans + 1 : chans + 2]
         own_ref[pl.ds(chans + k, 1), :] = rows - code
 
-    copies[2].wait()
-    loop(count, put_ins)
-    stored = pltpu.make_async_copy(t_ref, t_out, sems.at[len(operands)])
-    stored.start()
-    copies[3].wait()
+    loop(count, place)
     add_back(weight_ref, t_ref, total_ref)
     own_ref[:chans] = total_ref[...]
     rim_gradients(near_ref, far_ref, total_ref[:, rows:])
-    for copy in copies[4:]:
-        copy.wait()
     pick = one_hot(rows, rim_index(hi_ref, lo_ref))
     one = jnp.maximum(pre_ref[...], jnp.zeros_like(pre_ref))
     up, down = halves(dot(zero_ref[...], pick), dot(one, pick))
     put_edges(near_ref, far_ref, chans, up, down)
-    stored.wait()
 
 
 def packed_products(feats, t_ref, columns, sum_ref, base_ref=None):
@@ -311,9 +300,9 @@
     outs = [shape((rows, LANES), F32)] + [shape((rows, LANES), BF16)] * (slots - 1)
     own, *sends = call(functools.partial(core_sum_body, layers), outs, [keep, got])
     gots = [swap(block, "space", 2 * slot) for slot, block in enumerate(sends, 1)]
+    waiting = list(beside)
+    own, state = waiting.pop(0)(own, None)
     total = call(chip_sum_body, shape((rows, LANES), BF16), [own, *gots])
-    waiting = list(beside)
-    state = None
     if scans & (scans - 1):
         total = lax.psum(total, "scan")
     else:
@@ -355,23 +344,25 @@
     gather_flops = 2 * count * chans * ext * rows
     back_flops = 2 * count * chans * chans * ext
 
-    operands = [outs, cot, ins, weight_two, hi, lo, zero, pre]
+    picked = call(
+        pick_body,
+        shape((count * (chans + 16), pairs), BF16),
+        [outs, cot],
+        flops=2 * count * chans * rows * pairs,
+        moved=2 << 20,
+    )
     t_two, own, near, far = call(
         two_body,
-        [shape((tall, ext), BF16), shape((chans + -(-count // 8) * 8, ext), F32), shape((2 * chans, rim), BF16), shape((2 * chans, rim), BF16)],
-        operands,
-        scratch=[pltpu.VMEM(x.shape, x.dtype) for x in operands]
-        + [
-            pltpu.VMEM((tall, ext), BF16),
-            pltpu.VMEM((count * (chans + 16), pairs), BF16),
-            pltpu.VMEM((chans, ext), F32),
-            pltpu.SemaphoreType.DMA((len(operands) + 1,)),
+        [
+            shape((tall, ext), BF16),
+            shape((chans + -(-count // 8) * 8, ext), F32),
+            shape((2 * chans, rim), BF16),
+            shape((2 * chans, rim), BF16),
         ],
+        [ins, picked, weight_two, hi, lo, zero, pre],
+        scratch=[pltpu.VMEM((chans, ext), F32)],
         flops=gather_flops + back_flops,
         moved=8 << 20,
-        args_in=HBM,
-        outs_in=(HBM, VMEM, VMEM, VMEM),
-        room=WHOLE,
     )
     near, far = swap_neighbours(near, far)
     sum_two = call(two_weights_body, shape((packed, LANES), F32), [pre, t_two], flops=back_flops, moved=6 << 20)

time: 60.1 us -> 57.7 us (0.960)
  Pallas kernels: 18.6 us -> 16.2 us
  local copies, waits for them, and re-layouts: 2.99 us -> 1.73 us
  waiting for transfers between devices: 18 us -> 18.8 us
    pallas_call x10 -> x11, Pallas kernels: 18.6 us -> 16.2 us  [call(): pl.pallas_call(body, out_shape=outs if single else tuple(outs), in_specs=...]
    ppermute x2, waiting for transfers between devices: 4.67 us -> 6.01 us  [swap_scans(): return lax.ppermute(block, ('space', 'scan'), pairs)]
    unnamed x16 -> x18, local copies, waits for them, and re-layouts: 2.99 us -> 1.73 us
  transfers between devices with their start and end apart: 17 -> 17, of which waited for: 11 -> 10; matrix products, arithmetic and copies ran while one was open for 0% -> 0% of each run, Pallas kernels for 5% -> 5%
where the time goes in v4:
time: 57.7 us; the launch traced here: 57.5 us
  starting transfers between devices  19.9 us (34%)
  waiting for transfers between devices  18.8 us (33%)
  Pallas kernels  16.2 us (28%)
  local copies, waits for them, and re-layouts  1.73 us (3%)
  between operations  0.84 us (1%)
    pallas_call x11, Pallas kernels, call(): pl.pallas_call(body, out_shape=outs if single else tuple(outs), in_specs=...  16.2 us
    ppermute x13, starting transfers between devices, swap(): lax.ppermute(block, axis, [(i, i ^ bit) for i in range(lax.axis_size(axis...  14.3 us
    ppermute x13, waiting for transfers between devices, swap(): lax.ppermute(block, axis, [(i, i ^ bit) for i in range(lax.axis_size(axis...  12.8 us
    ppermute x2, waiting for transfers between devices, swap_scans(): return lax.ppermute(block, ('space', 'scan'), pairs)  6.01 us
    ppermute x2, starting transfers between devices, swap_scans(): return lax.ppermute(block, ('space', 'scan'), pairs)  4.33 us
    unnamed x18, local copies, waits for them, and re-layouts  1.73 us
    ppermute x2, starting transfers between devices, swap_neighbours(): lax.ppermute(far, 'space', [(i, i + 1 if i % 2 else i - 1) for i in inner])  1.3 us
  transfers between devices with their start and end apart: 17, of which 10 were waited for; matrix products, arithmetic and copies ran while one was open for 0% of the time, Pallas kernels for 5%

profile of v4, /device:TPU:0, one launch (start us, length us, event | category | flops | bytes accessed | tf_op | source)
XLA Modules:
  0.0 57.5 jit_solution(4192966276924047177)
XLA Ops:
  0.7 1.0 %copy-done.5 = bf16[1,1,512,96]{2,3,1,0:T(8,128)(2,1)S(1)} copy-done((bf16[1,1,512,96]{2,3,1,0:T(8,128)(2,1)S(1)}, bf16[1,1,512,96]{2,3,1,0:T(8,128)(2,1)}, u32[]{:S(2)}) %copy-start.5) | copy-done | bytes 98328
  1.6 0.7 %copy-done.7 = s32[1,1,27,256]{3,1,2,0:T(1,128)S(1)} copy-done((s32[1,1,27,256]{3,1,2,0:T(1,128)S(1)}, s32[1,1,27,256]{3,1,2,0:T(1,128)}, u32[]{:S(2)}) %copy-start.7) | copy-done | bytes 27672
  2.4 1.6 %shard_map.112.c_ref = bf16[3024,256]{1,0:T(8,128)(2,1)S(1)} custom-call(s32[27,1,256]{2,1,0:T(1,128)S(1)} %bitcast.28, bf16[96,512]{1,0:T(8,128)(2,1)S(1)} %bitcast.25), custom_call_target="tpu_custom_call" | custom-call | flops 679477248 | bytes 2097152 | tf_op jit(solution)/shard_map/pallas_call | solution.py:23
  4.0 4.2 %shard_map.113 = (bf16[2688,640]{1,0:T(8,128)(2,1)S(1)}, f32[128,640]{1,0:T(8,128)S(1)}, bf16[192,128]{1,0:T(8,128)(2,1)S(1)}, bf16[192,128]{1,0:T(8,128)(2,1)S(1)}) custom-call(s32[27,1,256]{2,1,0:T(1,128)S(1)} %bitcast.29, bf16[3024,256]{1,0:T(8,128)(2,1)S(1)} %shard_map.112.c_ref, bf16[27,96,96]{2,1,0:T(8,128)(2,1)S(1)} %copy-done.4, ...), custom_call_target="tpu_custom_call" | custom-call | flops 2017198080 | bytes 8388608 | tf_op jit(solution)/shard_map/pallas_call | solution.py:23
  8.3 0.5 collective-permute-start
  8.8 0.7 %collective-permute-start.1 = (bf16[192,128]{1,0:T(8,128)(2,1)S(1)}, bf16[192,128]{1,0:T(8,128)(2,1)S(1)}, u32[]{:S(2)}, u32[]{:S(2)}) collective-permute-start(bf16[192,128]{1,0:T(8,128)(2,1)S(1)} %get-tuple-element.36), channel_id=1, source_target_pairs={{4,8},{8,4},{12,16},{16,12},{20,24},{24,20},{5,9},{9,5},{13,17},{1... | collective-permute-start | bytes 147464 | tf_op jit(solution)/shard_map/ppermute | solution.py:283
  9.5 1.0 %shard_map.114.sum_two_ref = f32[2048,128]{1,0:T(8,128)S(1)} custom-call(bf16[96,512]{1,0:T(8,128)(2,1)S(1)} %bitcast.17, bf16[2688,640]{1,0:T(8,128)(2,1)S(1)} %get-tuple-element.37.t_ref.t_two_ref), custom_call_target="tpu_custom_call" | custom-call | flops 318504960 | bytes 6291456 | tf_op jit(solution)/shard_map/pallas_call | solution.py:23
  10.5 5.4 %shard_map.115 = (bf16[2688,640]{1,0:T(8,128)(2,1)S(1)}, f32[2048,128]{1,0:T(8,128)S(1)}, bf16[2048,128]{1,0:T(8,128)(2,1)S(1)}) custom-call(f32[128,640]{1,0:T(8,128)S(1)} %get-tuple-element.34.own_ref, bf16[192,128]{1,0:T(8,128)(2,1)S(1)} %collective-permute-done.near_ref, bf16[192,128]{1,0:T(8,128)(2,1)S(1)} %collective-permute-done.1.far_ref, ...), custom_call_target="tpu_custom_call" | custom-call | flops 2017198080 | bytes 8388608 | tf_op jit(solution)/shard_map/pallas_call | solution.py:23
  15.8 4.7 %collective-permute-start.2 = (bf16[2048,128]{1,0:T(8,128)(2,1)S(1)}, bf16[2048,128]{1,0:T(8,128)(2,1)S(1)}, u32[]{:S(2)}, u32[]{:S(2)}) collective-permute-start(bf16[2048,128]{1,0:T(8,128)(2,1)S(1)} %get-tuple-element.43), channel_id=1, source_target_pairs={{0,4},{4,0},{8,12},{12,8},{16,20},{20,16},{24,28},{28,24},{1,5},{5... | collective-permute-start | bytes 1572872 | tf_op jit(solution)/shard_map/ppermute | solution.py:278
  20.5 1.1 %shard_map.116 = (f32[96,512]{1,0:T(8,128)S(1)}, bf16[96,128]{1,0:T(8,128)(2,1)S(1)}, bf16[96,128]{1,0:T(8,128)(2,1)S(1)}) custom-call(bf16[27,96,96]{2,1,0:T(8,128)(2,1)S(1)} %copy-done, bf16[2688,640]{1,0:T(8,128)(2,1)S(1)} %get-tuple-element.39.t_ref), custom_call_target="tpu_custom_call" | custom-call | flops 318504960 | bytes 6291456 | tf_op jit(solution)/shard_map/pallas_call | solution.py:23
  21.6 0.4 collective-permute-done.2.got_ref
  22.1 0.1 shard_map.117
  22.2 3.1 %collective-permute-start.5 = (bf16[512,128]{1,0:T(8,128)(2,1)S(1)}, bf16[512,128]{1,0:T(8,128)(2,1)S(1)}, u32[]{:S(2)}, u32[]{:S(2)}) collective-permute-start(bf16[512,128]{1,0:T(8,128)(2,1)S(1)} %get-tuple-element.51), channel_id=1, source_target_pairs={{0,8},{4,12},{8,0},{12,4},{16,24},{20,28},{24,16},{28,20},{1,9},{5... | collective-permute-start | bytes 393224 | tf_op jit(solution)/shard_map/ppermute | solution.py:278
  25.3 0.5 collective-permute-start.6
  25.8 1.1 %collective-permute-start.7 = (bf16[512,128]{1,0:T(8,128)(2,1)S(1)}, bf16[512,128]{1,0:T(8,128)(2,1)S(1)}, u32[]{:S(2)}, u32[]{:S(2)}) collective-permute-start(bf16[512,128]{1,0:T(8,128)(2,1)S(1)} %get-tuple-element.53), channel_id=1, source_target_pairs={{0,24},{4,28},{8,16},{12,20},{16,8},{20,12},{24,0},{28,4},{1,25},{... | collective-permute-start | bytes 393224 | tf_op jit(solution)/shard_map/ppermute | solution.py:278
  26.8 0.7 %collective-permute-start.4 = (bf16[96,128]{1,0:T(8,128)(2,1)S(1)}, bf16[96,128]{1,0:T(8,128)(2,1)S(1)}, u32[]{:S(2)}, u32[]{:S(2)}) collective-permute-start(bf16[96,128]{1,0:T(8,128)(2,1)S(1)} %get-tuple-element.49), channel_id=1, source_target_pairs={{4,8},{8,4},{12,16},{16,12},{20,24},{24,20},{5,9},{9,5},{13,17},{1... | collective-permute-start | bytes 73736 | tf_op jit(solution)/shard_map/ppermute | solution.py:283
  27.5 0.5 collective-permute-done.3.near_ref
  28.0 1.4 %collective-permute-done.5.refs_0_ = bf16[512,128]{1,0:T(8,128)(2,1)S(1)} collective-permute-done((bf16[512,128]{1,0:T(8,128)(2,1)S(1)}, bf16[512,128]{1,0:T(8,128)(2,1)S(1)}, u32[]{:S(2)}, u32[]{:S(2)}) %collective-permute-start.5) | collective-permute-done | bytes 131104 | tf_op jit(solution)/shard_map/ppermute | solution.py:278
  29.4 4.2 %collective-permute-done.6.refs_1_ = bf16[512,128]{1,0:T(8,128)(2,1)S(1)} collective-permute-done((bf16[512,128]{1,0:T(8,128)(2,1)S(1)}, bf16[512,128]{1,0:T(8,128)(2,1)S(1)}, u32[]{:S(2)}, u32[]{:S(2)}) %collective-permute-start.6) | collective-permute-done | bytes 131104 | tf_op jit(solution)/shard_map/ppermute | solution.py:278
  33.6 0.1 shard_map.118.own_ref
  33.6 1.6 %collective-permute-start.8 = (bf16[512,128]{1,0:T(8,128)(2,1)S(1)}, bf16[512,128]{1,0:T(8,128)(2,1)S(1)}, u32[]{:S(2)}, u32[]{:S(2)}) collective-permute-start(bf16[512,128]{1,0:T(8,128)(2,1)S(1)} %shard_map.118.own_ref), channel_id=1, source_target_pairs={{0,1},{1,0},{2,3},{3,2},{4,6},{5,7},{6,4},{7,5},{8,9},{9,8},{10,11... | collective-permute-start | bytes 393224 | tf_op jit(solution)/shard_map/ppermute | solution.py:292
  35.3 0.9 %shard_map.119 = bf16[96,512]{1,0:T(8,128)(2,1)} custom-call(f32[96,512]{1,0:T(8,128)S(1)} %get-tuple-element.58.own_ref, bf16[96,128]{1,0:T(8,128)(2,1)S(1)} %collective-permute-done.3.near_ref, bf16[96,128]{1,0:T(8,128)(2,1)S(1)} %collective-permute-done.4.far_ref, s32[1,64]{1,0:T(1,128)S(1)} %bitcast.21, s32[1,64]{1,0:T(1,128)S(1)} %bitcast.24), custom_call_target="tpu_custom_call" | custom-call | tf_op jit(solution)/shard_map/pallas_call | solution.py:23
  36.2 2.8 %collective-permute-done.8.got_ref = bf16[512,128]{1,0:T(8,128)(2,1)S(1)} collective-permute-done((bf16[512,128]{1,0:T(8,128)(2,1)S(1)}, bf16[512,128]{1,0:T(8,128)(2,1)S(1)}, u32[]{:S(2)}, u32[]{:S(2)}) %collective-permute-start.8) | collective-permute-done | bytes 131104 | tf_op jit(solution)/shard_map/ppermute | solution.py:292
  39.0 2.7 %collective-permute-start.9 = (bf16[512,128]{1,0:T(8,128)(2,1)S(1)}, bf16[512,128]{1,0:T(8,128)(2,1)S(1)}, u32[]{:S(2)}, u32[]{:S(2)}) collective-permute-start(bf16[512,128]{1,0:T(8,128)(2,1)S(1)} %shard_map.120.own_ref), channel_id=1, source_target_pairs={{0,2},{1,3},{2,0},{3,1},{4,5},{5,4},{6,7},{7,6},{8,10},{9,11},{10,... | collective-permute-start | bytes 393224 | tf_op jit(solution)/shard_map/ppermute | solution.py:292
  41.7 3.2 %collective-permute-done.9.got_ref = bf16[512,128]{1,0:T(8,128)(2,1)S(1)} collective-permute-done((bf16[512,128]{1,0:T(8,128)(2,1)S(1)}, bf16[512,128]{1,0:T(8,128)(2,1)S(1)}, u32[]{:S(2)}, u32[]{:S(2)}) %collective-permute-start.9) | collective-permute-done | bytes 131104 | tf_op jit(solution)/shard_map/ppermute | solution.py:292
  45.0 1.6 %collective-permute-start.15 = (bf16[512,128]{1,0:T(8,128)(2,1)S(1)}, bf16[512,128]{1,0:T(8,128)(2,1)S(1)}, u32[]{:S(2)}, u32[]{:S(2)}) collective-permute-start(bf16[512,128]{1,0:T(8,128)(2,1)S(1)} %shard_map.121.refs_0_), channel_id=1, source_target_pairs={{0,24},{4,28},{8,16},{12,20},{16,8},{20,12},{24,0},{28,4},{1,25},{... | collective-permute-start | bytes 393224 | tf_op jit(solution)/shard_map/ppermute | solution.py:278
  46.5 2.8 %collective-permute-start.13 = (bf16[512,128]{1,0:T(8,128)(2,1)S(1)}, bf16[512,128]{1,0:T(8,128)(2,1)S(1)}, u32[]{:S(2)}, u32[]{:S(2)}) collective-permute-start(bf16[512,128]{1,0:T(8,128)(2,1)S(1)} %shard_map.121.refs_0_), channel_id=1, source_target_pairs={{0,16},{4,20},{8,24},{12,28},{16,0},{20,4},{24,8},{28,12},{1,17},{... | collective-permute-start | bytes 393224 | tf_op jit(solution)/shard_map/ppermute | solution.py:278
  49.4 2.5 %collective-permute-done.15.refs_6_ = bf16[512,128]{1,0:T(8,128)(2,1)S(1)} collective-permute-done((bf16[512,128]{1,0:T(8,128)(2,1)S(1)}, bf16[512,128]{1,0:T(8,128)(2,1)S(1)}, u32[]{:S(2)}, u32[]{:S(2)}) %collective-permute-start.15) | collective-permute-done | bytes 131104 | tf_op jit(solution)/shard_map/ppermute | solution.py:278
  51.9 1.1 %collective-permute-done.13.refs_4_ = bf16[512,128]{1,0:T(8,128)(2,1)S(1)} collective-permute-done((bf16[512,128]{1,0:T(8,128)(2,1)S(1)}, bf16[512,128]{1,0:T(8,128)(2,1)S(1)}, u32[]{:S(2)}, u32[]{:S(2)}) %collective-permute-start.13) | collective-permute-done | bytes 131104 | tf_op jit(solution)/shard_map/ppermute | solution.py:278
  53.0 1.3 %collective-permute-done.11.refs_2_ = bf16[512,128]{1,0:T(8,128)(2,1)S(1)} collective-permute-done((bf16[512,128]{1,0:T(8,128)(2,1)S(1)}, bf16[512,128]{1,0:T(8,128)(2,1)S(1)}, u32[]{:S(2)}, u32[]{:S(2)}) %collective-permute-start.11) | collective-permute-done | bytes 131104 | tf_op jit(solution)/shard_map/ppermute | solution.py:278
  54.3 1.3 %collective-permute-done.12.refs_3_ = bf16[512,128]{1,0:T(8,128)(2,1)S(1)} collective-permute-done((bf16[512,128]{1,0:T(8,128)(2,1)S(1)}, bf16[512,128]{1,0:T(8,128)(2,1)S(1)}, u32[]{:S(2)}, u32[]{:S(2)}) %collective-permute-start.12) | collective-permute-done | bytes 131104 | tf_op jit(solution)/shard_map/ppermute | solution.py:278
  55.7 1.9 %shard_map.122 = (f32[27,96,96]{2,1,0:T(8,128)}, f32[27,96,96]{2,1,0:T(8,128)}) custom-call(bf16[512,128]{1,0:T(8,128)(2,1)S(1)} %shard_map.121.refs_0_, bf16[512,128]{1,0:T(8,128)(2,1)S(1)} %collective-permute-done.10.refs_1_, bf16[512,128]{1,0:T(8,128)(2,1)S(1)} %collective-permute-done.11.refs_2_, bf16[512,128]{1,0:T(8,128)(2,1)S(1)} %collective-permute-done.12.refs_3_, ...), custom_call_target="tpu_custom_call" | custom-call | tf_op jit(solution)/shard_map/pallas_call | solution.py:23
  (31 shorter events, 0.1 us)
Async XLA Ops:
  0.6 3.3 %copy-start.2 = (s32[1,1,64]{2,1,0:T(1,128)S(1)}, s32[1,1,64]{2,1,0:T(1,128)}, u32[]{:S(2)}) copy-start(s32[1,1,64]{2,1,0:T(1,128)} %param.17) | copy-start | bytes 772
  0.6 3.3 %copy-start.3 = (s32[1,1,64]{2,1,0:T(1,128)S(1)}, s32[1,1,64]{2,1,0:T(1,128)}, u32[]{:S(2)}) copy-start(s32[1,1,64]{2,1,0:T(1,128)} %param.16) | copy-start | bytes 772
  0.7 3.3 %copy-start.4 = (bf16[27,96,96]{2,1,0:T(8,128)(2,1)S(1)}, bf16[27,96,96]{2,1,0:T(8,128)(2,1)}, u32[]{:S(2)}) copy-start(bf16[27,96,96]{2,1,0:T(8,128)(2,1)} %weight_ref.2) | copy-start | bytes 1492996
  0.7 3.3 %copy-start.1 = (bf16[1,1,512,96]{2,3,1,0:T(8,128)(2,1)S(1)}, bf16[1,1,512,96]{2,3,1,0:T(8,128)(2,1)}, u32[]{:S(2)}) copy-start(bf16[1,1,512,96]{2,3,1,0:T(8,128)(2,1)} %param.10) | copy-start | bytes 294916
  0.7 1.0 %copy-start.5 = (bf16[1,1,512,96]{2,3,1,0:T(8,128)(2,1)S(1)}, bf16[1,1,512,96]{2,3,1,0:T(8,128)(2,1)}, u32[]{:S(2)}) copy-start(bf16[1,1,512,96]{2,3,1,0:T(8,128)(2,1)} %param.11) | copy-start | bytes 294916
  1.6 0.7 %copy-start.7 = (s32[1,1,27,256]{3,1,2,0:T(1,128)S(1)}, s32[1,1,27,256]{3,1,2,0:T(1,128)}, u32[]{:S(2)}) copy-start(s32[1,1,27,256]{3,1,2,0:T(1,128)} %param.15) | copy-start | bytes 82948
  2.4 1.6 %copy-start.6 = (bf16[1,1,512,96]{2,3,1,0:T(8,128)(2,1)S(1)}, bf16[1,1,512,96]{2,3,1,0:T(8,128)(2,1)}, u32[]{:S(2)}) copy-start(bf16[1,1,512,96]{2,3,1,0:T(8,128)(2,1)} %param.9) | copy-start | bytes 294916
  2.4 1.6 %copy-start.8 = (s32[1,1,27,256]{3,1,2,0:T(1,128)S(1)}, s32[1,1,27,256]{3,1,2,0:T(1,128)}, u32[]{:S(2)}) copy-start(s32[1,1,27,256]{3,1,2,0:T(1,128)} %param.14) | copy-start | bytes 82948
  8.3 2.2 %collective-permute-start = (bf16[192,128]{1,0:T(8,128)(2,1)S(1)}, bf16[192,128]{1,0:T(8,128)(2,1)S(1)}, u32[]{:S(2)}, u32[]{:S(2)}) collective-permute-start(bf16[192,128]{1,0:T(8,128)(2,1)S(1)} %get-tuple-element.35), channel_id=1, source_target_pairs={{0,4},{4,0},{8,12},{12,8},{16,20},{20,16},{24,28},{28,24},{1,5},{5... | collective-permute-start | bytes 147464 | tf_op jit(solution)/shard_map/ppermute | solution.py:278
  8.8 1.6 %collective-permute-start.1 = (bf16[192,128]{1,0:T(8,128)(2,1)S(1)}, bf16[192,128]{1,0:T(8,128)(2,1)S(1)}, u32[]{:S(2)}, u32[]{:S(2)}) collective-permute-start(bf16[192,128]{1,0:T(8,128)(2,1)S(1)} %get-tuple-element.36), channel_id=1, source_target_pairs={{4,8},{8,4},{12,16},{16,12},{20,24},{24,20},{5,9},{9,5},{13,17},{1... | collective-permute-start | bytes 147464 | tf_op jit(solution)/shard_map/ppermute | solution.py:283
  10.4 10.1 %copy-start = (bf16[27,96,96]{2,1,0:T(8,128)(2,1)S(1)}, bf16[27,96,96]{2,1,0:T(8,128)(2,1)}, u32[]{:S(2)}) copy-start(bf16[27,96,96]{2,1,0:T(8,128)(2,1)} %weight_ref.3) | copy-start | bytes 1492996
  15.8 6.2 %collective-permute-start.2 = (bf16[2048,128]{1,0:T(8,128)(2,1)S(1)}, bf16[2048,128]{1,0:T(8,128)(2,1)S(1)}, u32[]{:S(2)}, u32[]{:S(2)}) collective-permute-start(bf16[2048,128]{1,0:T(8,128)(2,1)S(1)} %get-tuple-element.43), channel_id=1, source_target_pairs={{0,4},{4,0},{8,12},{12,8},{16,20},{20,16},{24,28},{28,24},{1,5},{5... | collective-permute-start | bytes 1572872 | tf_op jit(solution)/shard_map/ppermute | solution.py:278
  22.2 7.2 %collective-permute-start.5 = (bf16[512,128]{1,0:T(8,128)(2,1)S(1)}, bf16[512,128]{1,0:T(8,128)(2,1)S(1)}, u32[]{:S(2)}, u32[]{:S(2)}) collective-permute-start(bf16[512,128]{1,0:T(8,128)(2,1)S(1)} %get-tuple-element.51), channel_id=1, source_target_pairs={{0,8},{4,12},{8,0},{12,4},{16,24},{20,28},{24,16},{28,20},{1,9},{5... | collective-permute-start | bytes 393224 | tf_op jit(solution)/shard_map/ppermute | solution.py:278
  25.3 8.3 %collective-permute-start.6 = (bf16[512,128]{1,0:T(8,128)(2,1)S(1)}, bf16[512,128]{1,0:T(8,128)(2,1)S(1)}, u32[]{:S(2)}, u32[]{:S(2)}) collective-permute-start(bf16[512,128]{1,0:T(8,128)(2,1)S(1)} %get-tuple-element.52), channel_id=1, source_target_pairs={{0,16},{4,20},{8,24},{12,28},{16,0},{20,4},{24,8},{28,12},{1,17},{... | collective-permute-start | bytes 393224 | tf_op jit(solution)/shard_map/ppermute | solution.py:278
  25.8 7.8 %collective-permute-start.7 = (bf16[512,128]{1,0:T(8,128)(2,1)S(1)}, bf16[512,128]{1,0:T(8,128)(2,1)S(1)}, u32[]{:S(2)}, u32[]{:S(2)}) collective-permute-start(bf16[512,128]{1,0:T(8,128)(2,1)S(1)} %get-tuple-element.53), channel_id=1, source_target_pairs={{0,24},{4,28},{8,16},{12,20},{16,8},{20,12},{24,0},{28,4},{1,25},{... | collective-permute-start | bytes 393224 | tf_op jit(solution)/shard_map/ppermute | solution.py:278
  26.8 1.2 %collective-permute-start.3 = (bf16[96,128]{1,0:T(8,128)(2,1)S(1)}, bf16[96,128]{1,0:T(8,128)(2,1)S(1)}, u32[]{:S(2)}, u32[]{:S(2)}) collective-permute-start(bf16[96,128]{1,0:T(8,128)(2,1)S(1)} %get-tuple-element.48), channel_id=1, source_target_pairs={{0,4},{4,0},{8,12},{12,8},{16,20},{20,16},{24,28},{28,24},{1,5},{5... | collective-permute-start | bytes 73736 | tf_op jit(solution)/shard_map/ppermute | solution.py:278
  26.8 1.2 %collective-permute-start.4 = (bf16[96,128]{1,0:T(8,128)(2,1)S(1)}, bf16[96,128]{1,0:T(8,128)(2,1)S(1)}, u32[]{:S(2)}, u32[]{:S(2)}) collective-permute-start(bf16[96,128]{1,0:T(8,128)(2,1)S(1)} %get-tuple-element.49), channel_id=1, source_target_pairs={{4,8},{8,4},{12,16},{16,12},{20,24},{24,20},{5,9},{9,5},{13,17},{1... | collective-permute-start | bytes 73736 | tf_op jit(solution)/shard_map/ppermute | solution.py:283
  33.6 5.3 %collective-permute-start.8 = (bf16[512,128]{1,0:T(8,128)(2,1)S(1)}, bf16[512,128]{1,0:T(8,128)(2,1)S(1)}, u32[]{:S(2)}, u32[]{:S(2)}) collective-permute-start(bf16[512,128]{1,0:T(8,128)(2,1)S(1)} %shard_map.118.own_ref), channel_id=1, source_target_pairs={{0,1},{1,0},{2,3},{3,2},{4,6},{5,7},{6,4},{7,5},{8,9},{9,8},{10,11... | collective-permute-start | bytes 393224 | tf_op jit(solution)/shard_map/ppermute | solution.py:292
  39.0 5.9 %collective-permute-start.9 = (bf16[512,128]{1,0:T(8,128)(2,1)S(1)}, bf16[512,128]{1,0:T(8,128)(2,1)S(1)}, u32[]{:S(2)}, u32[]{:S(2)}) collective-permute-start(bf16[512,128]{1,0:T(8,128)(2,1)S(1)} %shard_map.120.own_ref), channel_id=1, source_target_pairs={{0,2},{1,3},{2,0},{3,1},{4,5},{5,4},{6,7},{7,6},{8,10},{9,11},{10,... | collective-permute-start | bytes 393224 | tf_op jit(solution)/shard_map/ppermute | solution.py:292
  45.0 6.9 %collective-permute-start.15 = (bf16[512,128]{1,0:T(8,128)(2,1)S(1)}, bf16[512,128]{1,0:T(8,128)(2,1)S(1)}, u32[]{:S(2)}, u32[]{:S(2)}) collective-permute-start(bf16[512,128]{1,0:T(8,128)(2,1)S(1)} %shard_map.121.refs_0_), channel_id=1, source_target_pairs={{0,24},{4,28},{8,16},{12,20},{16,8},{20,12},{24,0},{28,4},{1,25},{... | collective-permute-start | bytes 393224 | tf_op jit(solution)/shard_map/ppermute | solution.py:278
  46.5 6.4 %collective-permute-start.13 = (bf16[512,128]{1,0:T(8,128)(2,1)S(1)}, bf16[512,128]{1,0:T(8,128)(2,1)S(1)}, u32[]{:S(2)}, u32[]{:S(2)}) collective-permute-start(bf16[512,128]{1,0:T(8,128)(2,1)S(1)} %shard_map.121.refs_0_), channel_id=1, source_target_pairs={{0,16},{4,20},{8,24},{12,28},{16,0},{20,4},{24,8},{28,12},{1,17},{... | collective-permute-start | bytes 393224 | tf_op jit(solution)/shard_map/ppermute | solution.py:278
  49.3 5.0 %collective-permute-start.11 = (bf16[512,128]{1,0:T(8,128)(2,1)S(1)}, bf16[512,128]{1,0:T(8,128)(2,1)S(1)}, u32[]{:S(2)}, u32[]{:S(2)}) collective-permute-start(bf16[512,128]{1,0:T(8,128)(2,1)S(1)} %shard_map.121.refs_0_), channel_id=1, source_target_pairs={{0,8},{4,12},{8,0},{12,4},{16,24},{20,28},{24,16},{28,20},{1,9},{5... | collective-permute-start | bytes 393224 | tf_op jit(solution)/shard_map/ppermute | solution.py:278
  49.4 5.0 %collective-permute-start.10 = (bf16[512,128]{1,0:T(8,128)(2,1)S(1)}, bf16[512,128]{1,0:T(8,128)(2,1)S(1)}, u32[]{:S(2)}, u32[]{:S(2)}) collective-permute-start(bf16[512,128]{1,0:T(8,128)(2,1)S(1)} %shard_map.121.refs_0_), channel_id=1, source_target_pairs={{0,4},{4,0},{8,12},{12,8},{16,20},{20,16},{24,28},{28,24},{1,5},{5... | collective-permute-start | bytes 393224 | tf_op jit(solution)/shard_map/ppermute | solution.py:278
  51.9 2.4 %collective-permute-start.16 = (bf16[512,128]{1,0:T(8,128)(2,1)S(1)}, bf16[512,128]{1,0:T(8,128)(2,1)S(1)}, u32[]{:S(2)}, u32[]{:S(2)}) collective-permute-start(bf16[512,128]{1,0:T(8,128)(2,1)S(1)} %collective-permute-done.15.refs_6_), channel_id=1, source_target_pairs={{0,4},{4,0},{8,12},{12,8},{16,20},{20,16},{24,28},{28,24},{1,5},{5... | collective-permute-start | bytes 393224 | tf_op jit(solution)/shard_map/ppermute | solution.py:278
  53.0 1.4 %collective-permute-start.14 = (bf16[512,128]{1,0:T(8,128)(2,1)S(1)}, bf16[512,128]{1,0:T(8,128)(2,1)S(1)}, u32[]{:S(2)}, u32[]{:S(2)}) collective-permute-start(bf16[512,128]{1,0:T(8,128)(2,1)S(1)} %collective-permute-done.13.refs_4_), channel_id=1, source_target_pairs={{0,4},{4,0},{8,12},{12,8},{16,20},{20,16},{24,28},{28,24},{1,5},{5... | collective-permute-start | bytes 393224 | tf_op jit(solution)/shard_map/ppermute | solution.py:278
  54.3 1.3 %collective-permute-start.12 = (bf16[512,128]{1,0:T(8,128)(2,1)S(1)}, bf16[512,128]{1,0:T(8,128)(2,1)S(1)}, u32[]{:S(2)}, u32[]{:S(2)}) collective-permute-start(bf16[512,128]{1,0:T(8,128)(2,1)S(1)} %collective-permute-done.11.refs_2_), channel_id=1, source_target_pairs={{0,4},{4,0},{8,12},{12,8},{16,20},{20,16},{24,28},{28,24},{1,5},{5... | collective-permute-start | bytes 393224 | tf_op jit(solution)/shard_map/ppermute | solution.py:278

commit v5 on v3

--- a/solution.py
+++ b/solution.py
@@ -111,9 +111,26 @@
     loop(count // 3, body)
 
 
-def two_body(*refs):
-    operands, (t_out, own_ref, near_ref, far_ref), scratch = refs[:8], refs[8:12], refs[12:]
-    locals_, (t_ref, c_ref, total_ref, sems) = scratch[:8], scratch[8:]
+def place_rows(ins_ref, c_ref, first, t_ref, inv_ref, inv_at):
+    count = ins_ref.shape[0]
+    ext = t_ref.shape[1]
+    tall = c_ref.shape[0] // count
+    chans = tall - 16
+    t_ref[count * chans :, :] = jnp.zeros((t_ref.shape[0] - count * chans, ext), BF16)
+
+    def place(k):
+        picked = c_ref[pl.ds(pl.multiple_of(k * tall, 16), tall), :]
+        placed = dot_nt(picked, one_hot(ext, ins_ref[k] - first))
+        t_ref[offset_rows(k, chans), :] = placed[:chans].astype(BF16)
+        code = placed[chans : chans + 1] * 16.0 + placed[chans + 1 : chans + 2]
+        inv_ref[pl.ds(inv_at + k, 1), :] = code
+
+    loop(count, place)
+
+
+def rim_body(*refs):
+    operands, (c_ref, t_ref, inv_ref, near_ref, far_ref), scratch = refs[:8], refs[8:13], refs[13:]
+    locals_, (total_ref, sems) = scratch[:8], scratch[8:]
     copies = [
         pltpu.make_async_copy(operand, local, sems.at[i]) for i, (operand, local) in enumerate(zip(operands, locals_, strict=True))
     ]
@@ -122,12 +139,10 @@
     outs_ref, cot_ref, ins_ref, weight_ref, hi_ref, lo_ref, zero_ref, pre_ref = locals_
     count, pairs = ins_ref.shape[0], ins_ref.shape[2]
     chans, rows = cot_ref.shape
-    ext = t_ref.shape[1]
     tall = chans + 16
     row = lax.broadcasted_iota(I32, (16, pairs), 0)
-    t_ref[count * chans :, :] = jnp.zeros((t_ref.shape[0] - count * chans, ext), BF16)
-
-    def pick_outs(k):
+
+    def pick(k):
         index = outs_ref[k]
         base = pl.multiple_of(k * tall, 16)
         c_ref[pl.ds(base, chans), :] = dot(cot_ref[...], one_hot(rows, index)).astype(BF16)
@@ -137,38 +152,33 @@
 
     copies[0].wait()
     copies[1].wait()
-    loop(count, pick_outs)
-
-    def put_ins(k):
-        picked = c_ref[pl.ds(pl.multiple_of(k * tall, 16), tall), :]
-        placed = dot_nt(picked, one_hot(ext, ins_ref[k]))
-        t_ref[offset_rows(k, chans), :] = placed[:chans].astype(BF16)
-        code = placed[chans : chans + 1] * 16.0 + placed[chans + 1 : chans + 2]
-        own_ref[pl.ds(chans + k, 1), :] = rows - code
-
+    loop(count, pick)
     copies[2].wait()
-    loop(count, put_ins)
-    stored = pltpu.make_async_copy(t_ref, t_out, sems.at[len(operands)])
-    stored.start()
+    place_rows(ins_ref, c_ref, rows, t_ref, inv_ref, 0)
     copies[3].wait()
     add_back(weight_ref, t_ref, total_ref)
-    own_ref[:chans] = total_ref[...]
-    rim_gradients(near_ref, far_ref, total_ref[:, rows:])
+    rim_gradients(near_ref, far_ref, total_ref[...])
     for copy in copies[4:]:
         copy.wait()
-    pick = one_hot(rows, rim_index(hi_ref, lo_ref))
+    wanted = one_hot(rows, rim_index(hi_ref, lo_ref))
     one = jnp.maximum(pre_ref[...], jnp.zeros_like(pre_ref))
-    up, down = halves(dot(zero_ref[...], pick), dot(one, pick))
+    up, down = halves(dot(zero_ref[...], wanted), dot(one, wanted))
     put_edges(near_ref, far_ref, chans, up, down)
-    stored.wait()
-
-
-def packed_products(feats, t_ref, columns, sum_ref, base_ref=None):
+
+
+def own_body(ins_ref, c_ref, weight_ref, t_ref, own_ref, total_ref):
+    chans = total_ref.shape[0]
+    place_rows(ins_ref, c_ref, 0, t_ref, own_ref, chans)
+    add_back(weight_ref, t_ref, total_ref)
+    own_ref[:chans] = total_ref[...]
+
+
+def packed_products(feats, t_ref, sum_ref, base_ref=None):
     chans = feats.shape[0]
     tiles = t_ref.shape[0] // LANES
     for start in range(0, tiles, 2):
         width = min(2, tiles - start)
-        grad = dot_nt(feats, t_ref[start * LANES : (start + width) * LANES, columns])
+        grad = dot_nt(feats, t_ref[start * LANES : (start + width) * LANES, :])
         for j in range(width):
             rows = slice((start + j) * chans, (start + j + 1) * chans)
             block = grad[:, j * LANES : (j + 1) * LANES]
@@ -190,7 +200,7 @@
 
 def two_weights_body(pre_ref, t_ref, sum_ref):
     one = jnp.maximum(pre_ref[...], jnp.zeros_like(pre_ref))
-    packed_products(one, t_ref, slice(0, one.shape[1]), sum_ref)
+    packed_products(one, t_ref, sum_ref)
 
 
 def settled(own, near, far, hi_ref, lo_ref):
@@ -202,24 +212,25 @@
 
 
 def one_body(
-    count, own_ref, near_ref, far_ref, hi_ref, lo_ref, pre_ref, zero_ref, t_two_ref, sum_two_ref, t_ref, keep_ref, send_ref, cot_ref, sum_ref
+    count, own_ref, inv_ref, near_ref, far_ref, hi_ref, lo_ref, pre_ref, zero_ref, t_two_ref, sum_two_ref, t_ref, keep_ref, send_ref, cot_ref, sum_ref
 ):
     chans, rows = pre_ref.shape
-    ext = own_ref.shape[1]
-    back = settled(own_ref[:chans, :rows], near_ref[:chans], far_ref[:chans], hi_ref, lo_ref)
+    back = settled(own_ref[:chans], near_ref[:chans], far_ref[:chans], hi_ref, lo_ref)
     cot_ref[...] = jnp.where(pre_ref[...].astype(F32) > 0, back, 0.0).astype(BF16)
 
     def place(k):
-        t_ref[offset_rows(k, chans), :] = dot(cot_ref[...], one_hot(rows, own_ref[pl.ds(chans + k, 1), :])).astype(BF16)
+        there = offset_rows(k, chans)
+        for index, columns in ((own_ref[pl.ds(chans + k, 1), :], slice(0, rows)), (inv_ref[pl.ds(k, 1), :], slice(rows, None))):
+            t_ref[there, columns] = dot(cot_ref[...], one_hot(rows, rows - index)).astype(BF16)
 
     loop(count, place)
-    t_ref[count * chans :, :] = jnp.zeros((t_ref.shape[0] - count * chans, ext), BF16)
+    t_ref[count * chans :, :] = jnp.zeros((t_ref.shape[0] - count * chans, t_ref.shape[1]), BF16)
     above, below = by_parity(near_ref[chans:], far_ref[chans:])
     zero_rim, one_rim = halves(below, above)
     feats = jnp.concatenate([zero_ref[...], zero_rim.astype(BF16)], 1)
-    packed_products(feats, t_ref, slice(0, ext), sum_ref)
+    packed_products(feats, t_ref, sum_ref)
     cut(sum_ref, 0, keep_ref, send_ref)
-    packed_products(one_rim.astype(BF16), t_two_ref, slice(rows, ext), sum_ref, sum_two_ref)
+    packed_products(one_rim.astype(BF16), t_two_ref, sum_ref, sum_two_ref)
     cut(sum_ref, 1, keep_ref, send_ref)
 
 
@@ -245,14 +256,20 @@
 
 
 def chip_sum_body(own_ref, *refs):
+    layers = 2
     total = own_ref[...]
-    for got_ref in refs[:-1]:
+    for got_ref in refs[:-layers]:
         total = total + got_ref[...].astype(F32)
-    refs[-1][...] = total.astype(BF16)
-
-
-def scan_sum_body(own_ref, got_ref, total_ref):
-    total_ref[...] = (own_ref[...].astype(F32) + got_ref[...].astype(F32)).astype(BF16)
+    rows = total.shape[0] // layers
+    for layer, out_ref in enumerate(refs[-layers:]):
+        out_ref[...] = total[layer * rows : (layer + 1) * rows].astype(BF16)
+
+
+def scan_sum_body(*refs):
+    *terms, total_ref = refs
+    rows = terms[0].shape[0]
+    for i in range(0, len(terms), 2):
+        total_ref[i // 2 * rows : (i // 2 + 1) * rows] = (terms[i][...].astype(F32) + terms[i + 1][...].astype(F32)).astype(BF16)
 
 
 def unpack_body(scale, layers, *refs):
@@ -311,18 +328,22 @@
     outs = [shape((rows, LANES), F32)] + [shape((rows, LANES), BF16)] * (slots - 1)
     own, *sends = call(functools.partial(core_sum_body, layers), outs, [keep, got])
     gots = [swap(block, "space", 2 * slot) for slot, block in enumerate(sends, 1)]
-    total = call(chip_sum_body, shape((rows, LANES), BF16), [own, *gots])
     waiting = list(beside)
-    state = None
+    own, state = waiting.pop(0)(own, None)
+    part = rows // layers
+    totals = call(chip_sum_body, [shape((part, LANES), BF16)] * layers, [own, *gots])
     if scans & (scans - 1):
-        total = lax.psum(total, "scan")
+        total = lax.psum(jnp.concatenate(totals), "scan")
     else:
         steps = scans.bit_length() - 1
         for step in range(steps):
-            more = swap_scans(total, step, steps)
+            more = [swap_scans(total, step, steps) for total in totals]
             if waiting:
-                total, state = waiting.pop(0)(total, state)
-            total = call(scan_sum_body, shape((rows, LANES), BF16), [total, more])
+                totals, state = waiting.pop(0)(totals, state)
+            if step + 1 < steps:
+                totals = [call(scan_sum_body, shape((part, LANES), BF16), [x, y]) for x, y in zip(totals, more, strict=True)]
+            else:
+                total = call(scan_sum_body, shape((rows, LANES), BF16), [x for pair in zip(totals, more, strict=True) for x in pair])
     for work in waiting:
         total, state = work(total, state)
     pieces = []
@@ -355,30 +376,38 @@
     gather_flops = 2 * count * chans * ext * rows
     back_flops = 2 * count * chans * chans * ext
 
-    operands = [outs, cot, ins, weight_two, hi, lo, zero, pre]
-    t_two, own, near, far = call(
-        two_body,
-        [shape((tall, ext), BF16), shape((chans + -(-count // 8) * 8, ext), F32), shape((2 * chans, rim), BF16), shape((2 * chans, rim), BF16)],
+    operands = [pltpu.with_memory_space_constraint(x, pltpu.HBM) for x in (outs, cot, ins, weight_two, hi, lo, zero, pre)]
+    rounded = -(-count // 8) * 8
+    c_two, t_rim, inv_rim, near, far = call(
+        rim_body,
+        [
+            shape((count * (chans + 16), pairs), BF16),
+            shape((tall, rim), BF16),
+            shape((rounded, rim), F32),
+            shape((2 * chans, rim), BF16),
+            shape((2 * chans, rim), BF16),
+        ],
         operands,
         scratch=[pltpu.VMEM(x.shape, x.dtype) for x in operands]
-        + [
-            pltpu.VMEM((tall, ext), BF16),
-            pltpu.VMEM((count * (chans + 16), pairs), BF16),
-            pltpu.VMEM((chans, ext), F32),
-            pltpu.SemaphoreType.DMA((len(operands) + 1,)),
-        ],
-        flops=gather_flops + back_flops,
+        + [pltpu.VMEM((chans, rim), F32), pltpu.SemaphoreType.DMA((len(operands),))],
+        flops=2 * count * chans * rows * pairs,
+        moved=4 << 20,
+        args_in=HBM,
+    )
+    near, far = swap_neighbours(near, far)
+    t_own, own = call(
+        own_body,
+        [shape((tall, rows), BF16), shape((chans + rounded, rows), F32)],
+        [ins, c_two, weight_two],
+        scratch=[pltpu.VMEM((chans, rows), F32)],
+        flops=gather_flops // 2,
         moved=8 << 20,
-        args_in=HBM,
-        outs_in=(HBM, VMEM, VMEM, VMEM),
-        room=WHOLE,
-    )
-    near, far = swap_neighbours(near, far)
-    sum_two = call(two_weights_body, shape((packed, LANES), F32), [pre, t_two], flops=back_flops, moved=6 << 20)
+    )
+    sum_two = call(two_weights_body, shape((packed, LANES), F32), [pre, t_own], flops=back_flops, moved=6 << 20)
     t_one, keep, send = call(
         functools.partial(one_body, count),
         [shape((tall, ext), BF16), shape((packed, LANES), F32), shape((packed, LANES), BF16)],
-        [own, near, far, hi, lo, pre, zero, t_two, sum_two],
+        [own, inv_rim, near, far, hi, lo, pre, zero, t_rim, sum_two],
         scratch=[pltpu.VMEM((chans, rows), BF16), pltpu.VMEM((packed, LANES), F32)],
         flops=gather_flops + back_flops,
         moved=8 << 20,

time: 60.1 us -> 55.7 us (0.927)
  local copies, waits for them, and re-layouts: 2.99 us -> 0.04 us
  waiting for transfers between devices: 18 us -> 17.3 us
    unnamed x16 -> x14, local copies, waits for them, and re-layouts: 2.99 us -> 0.04 us
    ppermute x13, starting transfers between devices: 13.8 us -> 11.6 us  [swap(): lax.ppermute(block, axis, [(i, i ^ bit) for i in range(lax.axis_size(axis...]
    ppermute x2 -> x4, starting transfers between devices: 4.46 us -> 6.01 us  [swap_scans(): return lax.ppermute(block, ('space', 'scan'), pairs)]
    ppermute x13, waiting for transfers between devices: 13.3 us -> 11.8 us  [swap(): lax.ppermute(block, axis, [(i, i ^ bit) for i in range(lax.axis_size(axis...]
    ppermute x2 -> x4, waiting for transfers between devices: 4.67 us -> 5.42 us  [swap_scans(): return lax.ppermute(block, ('space', 'scan'), pairs)]
    pallas_call x10 -> x12, Pallas kernels: 18.6 us -> 18.5 us  [call(): pl.pallas_call(body, out_shape=outs if single else tuple(outs), in_specs=...]
  transfers between devices with their start and end apart: 17 -> 19, of which waited for: 11 -> 12; matrix products, arithmetic and copies ran while one was open for 0% -> 0% of each run, Pallas kernels for 5% -> 12%
where the time goes in v5:
time: 55.7 us; the launch traced here: 55.5 us
  starting transfers between devices  18.9 us (34%)
  Pallas kernels  18.5 us (33%)
  waiting for transfers between devices  17.3 us (31%)
  between operations  0.84 us (2%)
    pallas_call x12, Pallas kernels, call(): pl.pallas_call(body, out_shape=outs if single else tuple(outs), in_specs=...  18.5 us
    ppermute x13, waiting for transfers between devices, swap(): lax.ppermute(block, axis, [(i, i ^ bit) for i in range(lax.axis_size(axis...  11.8 us
    ppermute x13, starting transfers between devices, swap(): lax.ppermute(block, axis, [(i, i ^ bit) for i in range(lax.axis_size(axis...  11.6 us
    ppermute x4, starting transfers between devices, swap_scans(): return lax.ppermute(block, ('space', 'scan'), pairs)  6.01 us
    ppermute x4, waiting for transfers between devices, swap_scans(): return lax.ppermute(block, ('space', 'scan'), pairs)  5.42 us
    ppermute x2, starting transfers between devices, swap_neighbours(): lax.ppermute(far, 'space', [(i, i + 1 if i % 2 else i - 1) for i in inner])  1.3 us
  transfers between devices with their start and end apart: 19, of which 12 were waited for; matrix products, arithmetic and copies ran while one was open for 0% of the time, Pallas kernels for 12%

profile of v5, /device:TPU:0, one launch (start us, length us, event | category | flops | bytes accessed | tf_op | source)
XLA Modules:
  0.0 55.5 jit_solution(16064414869118367164)
XLA Ops:
  0.7 4.5 %shard_map.112 = (bf16[3024,256]{1,0:T(8,128)(2,1)S(1)}, bf16[2688,128]{1,0:T(8,128)(2,1)S(1)}, f32[32,128]{1,0:T(8,128)S(1)}, bf16[192,128]{1,0:T(8,128)(2,1)S(1)}, bf16[192,128]{1,0:T(8,128)(2,1)S(1)}) custom-call(s32[27,1,256]{2,1,0:T(1,128)} %bitcast.31, bf16[96,512]{1,0:T(8,128)(2,1)} %bitcast.30, s32[27,1,256]{2,1,0:T(1,128)} %bitcast.27, ...), custom_call_target="tpu_custom_call" | custom-call | flops 679477248 | bytes 4194304 | tf_op jit(solution)/shard_map/pallas_call | solution.py:23
  5.1 0.5 collective-permute-start
  5.6 0.7 %collective-permute-start.1 = (bf16[192,128]{1,0:T(8,128)(2,1)S(1)}, bf16[192,128]{1,0:T(8,128)(2,1)S(1)}, u32[]{:S(2)}, u32[]{:S(2)}) collective-permute-start(bf16[192,128]{1,0:T(8,128)(2,1)S(1)} %get-tuple-element.45), channel_id=1, source_target_pairs={{4,8},{8,4},{12,16},{16,12},{20,24},{24,20},{5,9},{9,5},{13,17},{1... | collective-permute-start | bytes 147464 | tf_op jit(solution)/shard_map/ppermute | solution.py:311
  6.3 3.5 %shard_map.113 = (bf16[2688,512]{1,0:T(8,128)(2,1)S(1)}, f32[128,512]{1,0:T(8,128)S(1)}) custom-call(s32[27,1,256]{2,1,0:T(1,128)S(1)} %bitcast.28, bf16[3024,256]{1,0:T(8,128)(2,1)S(1)} %get-tuple-element.41.c_ref, bf16[27,96,96]{2,1,0:T(8,128)(2,1)S(1)} %copy-done.4), custom_call_target="tpu_custom_call" | custom-call | flops 849346560 | bytes 8388608 | tf_op jit(solution)/shard_map/pallas_call | solution.py:23
  9.9 1.0 %shard_map.114.sum_two_ref = f32[2048,128]{1,0:T(8,128)S(1)} custom-call(bf16[96,512]{1,0:T(8,128)(2,1)S(1)} %bitcast.17, bf16[2688,512]{1,0:T(8,128)(2,1)S(1)} %get-tuple-element.47.t_ref), custom_call_target="tpu_custom_call" | custom-call | flops 318504960 | bytes 6291456 | tf_op jit(solution)/shard_map/pallas_call | solution.py:23
  11.0 5.4 %shard_map.115 = (bf16[2688,640]{1,0:T(8,128)(2,1)S(1)}, f32[2048,128]{1,0:T(8,128)S(1)}, bf16[2048,128]{1,0:T(8,128)(2,1)S(1)}) custom-call(f32[128,512]{1,0:T(8,128)S(1)} %get-tuple-element.42.own_ref, f32[32,128]{1,0:T(8,128)S(1)} %get-tuple-element.43.inv_ref, bf16[192,128]{1,0:T(8,128)(2,1)S(1)} %collective-permute-done.near_ref, ...), custom_call_target="tpu_custom_call" | custom-call | flops 2017198080 | bytes 8388608 | tf_op jit(solution)/shard_map/pallas_call | solution.py:23
  16.3 3.9 %collective-permute-start.2 = (bf16[2048,128]{1,0:T(8,128)(2,1)S(1)}, bf16[2048,128]{1,0:T(8,128)(2,1)S(1)}, u32[]{:S(2)}, u32[]{:S(2)}) collective-permute-start(bf16[2048,128]{1,0:T(8,128)(2,1)S(1)} %get-tuple-element.53), channel_id=1, source_target_pairs={{0,4},{4,0},{8,12},{12,8},{16,20},{20,16},{24,28},{28,24},{1,5},{5... | collective-permute-start | bytes 1572872 | tf_op jit(solution)/shard_map/ppermute | solution.py:306
  20.3 1.1 %shard_map.116 = (f32[96,512]{1,0:T(8,128)S(1)}, bf16[96,128]{1,0:T(8,128)(2,1)S(1)}, bf16[96,128]{1,0:T(8,128)(2,1)S(1)}) custom-call(bf16[27,96,96]{2,1,0:T(8,128)(2,1)S(1)} %copy-done, bf16[2688,640]{1,0:T(8,128)(2,1)S(1)} %get-tuple-element.49.t_ref), custom_call_target="tpu_custom_call" | custom-call | flops 318504960 | bytes 6291456 | tf_op jit(solution)/shard_map/pallas_call | solution.py:23
  21.9 1.6 %collective-permute-start.5 = (bf16[512,128]{1,0:T(8,128)(2,1)S(1)}, bf16[512,128]{1,0:T(8,128)(2,1)S(1)}, u32[]{:S(2)}, u32[]{:S(2)}) collective-permute-start(bf16[512,128]{1,0:T(8,128)(2,1)S(1)} %get-tuple-element.61), channel_id=1, source_target_pairs={{0,8},{4,12},{8,0},{12,4},{16,24},{20,28},{24,16},{28,20},{1,9},{5... | collective-permute-start | bytes 393224 | tf_op jit(solution)/shard_map/ppermute | solution.py:306
  23.5 0.9 %collective-permute-start.6 = (bf16[512,128]{1,0:T(8,128)(2,1)S(1)}, bf16[512,128]{1,0:T(8,128)(2,1)S(1)}, u32[]{:S(2)}, u32[]{:S(2)}) collective-permute-start(bf16[512,128]{1,0:T(8,128)(2,1)S(1)} %get-tuple-element.62), channel_id=1, source_target_pairs={{0,16},{4,20},{8,24},{12,28},{16,0},{20,4},{24,8},{28,12},{1,17},{... | collective-permute-start | bytes 393224 | tf_op jit(solution)/shard_map/ppermute | solution.py:306
  24.4 1.1 %collective-permute-start.7 = (bf16[512,128]{1,0:T(8,128)(2,1)S(1)}, bf16[512,128]{1,0:T(8,128)(2,1)S(1)}, u32[]{:S(2)}, u32[]{:S(2)}) collective-permute-start(bf16[512,128]{1,0:T(8,128)(2,1)S(1)} %get-tuple-element.63), channel_id=1, source_target_pairs={{0,24},{4,28},{8,16},{12,20},{16,8},{20,12},{24,0},{28,4},{1,25},{... | collective-permute-start | bytes 393224 | tf_op jit(solution)/shard_map/ppermute | solution.py:306
  25.5 0.7 %collective-permute-start.4 = (bf16[96,128]{1,0:T(8,128)(2,1)S(1)}, bf16[96,128]{1,0:T(8,128)(2,1)S(1)}, u32[]{:S(2)}, u32[]{:S(2)}) collective-permute-start(bf16[96,128]{1,0:T(8,128)(2,1)S(1)} %get-tuple-element.59), channel_id=1, source_target_pairs={{4,8},{8,4},{12,16},{16,12},{20,24},{24,20},{5,9},{9,5},{13,17},{1... | collective-permute-start | bytes 73736 | tf_op jit(solution)/shard_map/ppermute | solution.py:311
  26.2 0.5 collective-permute-done.3.near_ref
  26.7 1.4 %collective-permute-done.5.refs_0_ = bf16[512,128]{1,0:T(8,128)(2,1)S(1)} collective-permute-done((bf16[512,128]{1,0:T(8,128)(2,1)S(1)}, bf16[512,128]{1,0:T(8,128)(2,1)S(1)}, u32[]{:S(2)}, u32[]{:S(2)}) %collective-permute-start.5) | collective-permute-done | bytes 131104 | tf_op jit(solution)/shard_map/ppermute | solution.py:306
  28.1 3.7 %collective-permute-done.6.refs_1_ = bf16[512,128]{1,0:T(8,128)(2,1)S(1)} collective-permute-done((bf16[512,128]{1,0:T(8,128)(2,1)S(1)}, bf16[512,128]{1,0:T(8,128)(2,1)S(1)}, u32[]{:S(2)}, u32[]{:S(2)}) %collective-permute-start.6) | collective-permute-done | bytes 131104 | tf_op jit(solution)/shard_map/ppermute | solution.py:306
  31.9 1.6 %collective-permute-start.8 = (bf16[256,128]{1,0:T(8,128)(2,1)S(1)}, bf16[256,128]{1,0:T(8,128)(2,1)S(1)}, u32[]{:S(2)}, u32[]{:S(2)}) collective-permute-start(bf16[256,128]{1,0:T(8,128)(2,1)S(1)} %get-tuple-element.75.refs_0_), channel_id=1, source_target_pairs={{0,1},{1,0},{2,3},{3,2},{4,6},{5,7},{6,4},{7,5},{8,9},{9,8},{10,11... | collective-permute-start | bytes 196616 | tf_op jit(solution)/shard_map/ppermute | solution.py:320
  33.5 0.5 collective-permute-start.10
  34.0 0.9 %shard_map.119 = bf16[96,512]{1,0:T(8,128)(2,1)} custom-call(f32[96,512]{1,0:T(8,128)S(1)} %get-tuple-element.71.own_ref, bf16[96,128]{1,0:T(8,128)(2,1)S(1)} %collective-permute-done.3.near_ref, bf16[96,128]{1,0:T(8,128)(2,1)S(1)} %collective-permute-done.4.far_ref, s32[1,64]{1,0:T(1,128)S(1)} %bitcast.21, s32[1,64]{1,0:T(1,128)S(1)} %bitcast.24), custom_call_target="tpu_custom_call" | custom-call | tf_op jit(solution)/shard_map/pallas_call | solution.py:23
  34.9 1.6 %collective-permute-done.8.refs_1_ = bf16[256,128]{1,0:T(8,128)(2,1)S(1)} collective-permute-done((bf16[256,128]{1,0:T(8,128)(2,1)S(1)}, bf16[256,128]{1,0:T(8,128)(2,1)S(1)}, u32[]{:S(2)}, u32[]{:S(2)}) %collective-permute-start.8) | collective-permute-done | bytes 65568 | tf_op jit(solution)/shard_map/ppermute | solution.py:320
  36.5 2.4 %collective-permute-start.9 = (bf16[256,128]{1,0:T(8,128)(2,1)S(1)}, bf16[256,128]{1,0:T(8,128)(2,1)S(1)}, u32[]{:S(2)}, u32[]{:S(2)}) collective-permute-start(bf16[256,128]{1,0:T(8,128)(2,1)S(1)} %shard_map.120.refs_0_), channel_id=1, source_target_pairs={{0,2},{1,3},{2,0},{3,1},{4,5},{5,4},{6,7},{7,6},{8,10},{9,11},{10,... | collective-permute-start | bytes 196616 | tf_op jit(solution)/shard_map/ppermute | solution.py:320
  38.9 1.6 %collective-permute-start.11 = (bf16[256,128]{1,0:T(8,128)(2,1)S(1)}, bf16[256,128]{1,0:T(8,128)(2,1)S(1)}, u32[]{:S(2)}, u32[]{:S(2)}) collective-permute-start(bf16[256,128]{1,0:T(8,128)(2,1)S(1)} %shard_map.121.refs_2_), channel_id=1, source_target_pairs={{0,2},{1,3},{2,0},{3,1},{4,5},{5,4},{6,7},{7,6},{8,10},{9,11},{10,... | collective-permute-start | bytes 196616 | tf_op jit(solution)/shard_map/ppermute | solution.py:320
  40.5 1.4 %collective-permute-done.9.refs_1_ = bf16[256,128]{1,0:T(8,128)(2,1)S(1)} collective-permute-done((bf16[256,128]{1,0:T(8,128)(2,1)S(1)}, bf16[256,128]{1,0:T(8,128)(2,1)S(1)}, u32[]{:S(2)}, u32[]{:S(2)}) %collective-permute-start.9) | collective-permute-done | bytes 65568 | tf_op jit(solution)/shard_map/ppermute | solution.py:320
  41.8 2.4 %collective-permute-done.11.refs_3_ = bf16[256,128]{1,0:T(8,128)(2,1)S(1)} collective-permute-done((bf16[256,128]{1,0:T(8,128)(2,1)S(1)}, bf16[256,128]{1,0:T(8,128)(2,1)S(1)}, u32[]{:S(2)}, u32[]{:S(2)}) %collective-permute-start.11) | collective-permute-done | bytes 65568 | tf_op jit(solution)/shard_map/ppermute | solution.py:320
  44.3 2.0 %collective-permute-start.17 = (bf16[512,128]{1,0:T(8,128)(2,1)S(1)}, bf16[512,128]{1,0:T(8,128)(2,1)S(1)}, u32[]{:S(2)}, u32[]{:S(2)}) collective-permute-start(bf16[512,128]{1,0:T(8,128)(2,1)S(1)} %shard_map.122.refs_0_), channel_id=1, source_target_pairs={{0,24},{4,28},{8,16},{12,20},{16,8},{20,12},{24,0},{28,4},{1,25},{... | collective-permute-start | bytes 393224 | tf_op jit(solution)/shard_map/ppermute | solution.py:306
  46.3 1.1 %collective-permute-start.15 = (bf16[512,128]{1,0:T(8,128)(2,1)S(1)}, bf16[512,128]{1,0:T(8,128)(2,1)S(1)}, u32[]{:S(2)}, u32[]{:S(2)}) collective-permute-start(bf16[512,128]{1,0:T(8,128)(2,1)S(1)} %shard_map.122.refs_0_), channel_id=1, source_target_pairs={{0,16},{4,20},{8,24},{12,28},{16,0},{20,4},{24,8},{28,12},{1,17},{... | collective-permute-start | bytes 393224 | tf_op jit(solution)/shard_map/ppermute | solution.py:306
  47.3 0.5 collective-permute-start.13
  47.9 2.4 %collective-permute-done.17.refs_6_ = bf16[512,128]{1,0:T(8,128)(2,1)S(1)} collective-permute-done((bf16[512,128]{1,0:T(8,128)(2,1)S(1)}, bf16[512,128]{1,0:T(8,128)(2,1)S(1)}, u32[]{:S(2)}, u32[]{:S(2)}) %collective-permute-start.17) | collective-permute-done | bytes 131104 | tf_op jit(solution)/shard_map/ppermute | solution.py:306
  50.3 1.4 %collective-permute-done.15.refs_4_ = bf16[512,128]{1,0:T(8,128)(2,1)S(1)} collective-permute-done((bf16[512,128]{1,0:T(8,128)(2,1)S(1)}, bf16[512,128]{1,0:T(8,128)(2,1)S(1)}, u32[]{:S(2)}, u32[]{:S(2)}) %collective-permute-start.15) | collective-permute-done | bytes 131104 | tf_op jit(solution)/shard_map/ppermute | solution.py:306
  51.6 0.7 %collective-permute-done.13.refs_2_ = bf16[512,128]{1,0:T(8,128)(2,1)S(1)} collective-permute-done((bf16[512,128]{1,0:T(8,128)(2,1)S(1)}, bf16[512,128]{1,0:T(8,128)(2,1)S(1)}, u32[]{:S(2)}, u32[]{:S(2)}) %collective-permute-start.13) | collective-permute-done | bytes 131104 | tf_op jit(solution)/shard_map/ppermute | solution.py:306
  52.3 0.7 %collective-permute-done.16.refs_5_ = bf16[512,128]{1,0:T(8,128)(2,1)S(1)} collective-permute-done((bf16[512,128]{1,0:T(8,128)(2,1)S(1)}, bf16[512,128]{1,0:T(8,128)(2,1)S(1)}, u32[]{:S(2)}, u32[]{:S(2)}) %collective-permute-start.16) | collective-permute-done | bytes 131104 | tf_op jit(solution)/shard_map/ppermute | solution.py:306
  53.0 0.7 %collective-permute-done.14.refs_3_ = bf16[512,128]{1,0:T(8,128)(2,1)S(1)} collective-permute-done((bf16[512,128]{1,0:T(8,128)(2,1)S(1)}, bf16[512,128]{1,0:T(8,128)(2,1)S(1)}, u32[]{:S(2)}, u32[]{:S(2)}) %collective-permute-start.14) | collective-permute-done | bytes 131104 | tf_op jit(solution)/shard_map/ppermute | solution.py:306
  53.7 1.9 %shard_map.123 = (f32[27,96,96]{2,1,0:T(8,128)}, f32[27,96,96]{2,1,0:T(8,128)}) custom-call(bf16[512,128]{1,0:T(8,128)(2,1)S(1)} %shard_map.122.refs_0_, bf16[512,128]{1,0:T(8,128)(2,1)S(1)} %collective-permute-done.12.refs_1_, bf16[512,128]{1,0:T(8,128)(2,1)S(1)} %collective-permute-done.13.refs_2_, bf16[512,128]{1,0:T(8,128)(2,1)S(1)} %collective-permute-done.14.refs_3_, ...), custom_call_target="tpu_custom_call" | custom-call | tf_op jit(solution)/shard_map/pallas_call | solution.py:23
  (32 shorter events, 0.8 us)
Async XLA Ops:
  0.6 5.7 %copy-start.4 = (bf16[27,96,96]{2,1,0:T(8,128)(2,1)S(1)}, bf16[27,96,96]{2,1,0:T(8,128)(2,1)}, u32[]{:S(2)}) copy-start(bf16[27,96,96]{2,1,0:T(8,128)(2,1)} %weight_ref.2) | copy-start | bytes 1492996
  0.6 5.7 %copy-start.6 = (s32[1,1,27,256]{3,1,2,0:T(1,128)S(1)}, s32[1,1,27,256]{3,1,2,0:T(1,128)}, u32[]{:S(2)}) copy-start(s32[1,1,27,256]{3,1,2,0:T(1,128)} %param.14) | copy-start | bytes 82948
  5.1 5.8 %collective-permute-start = (bf16[192,128]{1,0:T(8,128)(2,1)S(1)}, bf16[192,128]{1,0:T(8,128)(2,1)S(1)}, u32[]{:S(2)}, u32[]{:S(2)}) collective-permute-start(bf16[192,128]{1,0:T(8,128)(2,1)S(1)} %get-tuple-element.44), channel_id=1, source_target_pairs={{0,4},{4,0},{8,12},{12,8},{16,20},{20,16},{24,28},{28,24},{1,5},{5... | collective-permute-start | bytes 147464 | tf_op jit(solution)/shard_map/ppermute | solution.py:306
  5.6 5.3 %collective-permute-start.1 = (bf16[192,128]{1,0:T(8,128)(2,1)S(1)}, bf16[192,128]{1,0:T(8,128)(2,1)S(1)}, u32[]{:S(2)}, u32[]{:S(2)}) collective-permute-start(bf16[192,128]{1,0:T(8,128)(2,1)S(1)} %get-tuple-element.45), channel_id=1, source_target_pairs={{4,8},{8,4},{12,16},{16,12},{20,24},{24,20},{5,9},{9,5},{13,17},{1... | collective-permute-start | bytes 147464 | tf_op jit(solution)/shard_map/ppermute | solution.py:311
  6.3 3.6 %copy-start.1 = (bf16[1,1,512,96]{2,3,1,0:T(8,128)(2,1)S(1)}, bf16[1,1,512,96]{2,3,1,0:T(8,128)(2,1)}, u32[]{:S(2)}) copy-start(bf16[1,1,512,96]{2,3,1,0:T(8,128)(2,1)} %param.10) | copy-start | bytes 294916
  9.9 1.0 %copy-start.2 = (s32[1,1,64]{2,1,0:T(1,128)S(1)}, s32[1,1,64]{2,1,0:T(1,128)}, u32[]{:S(2)}) copy-start(s32[1,1,64]{2,1,0:T(1,128)} %param.17) | copy-start | bytes 772
  9.9 1.0 %copy-start.3 = (s32[1,1,64]{2,1,0:T(1,128)S(1)}, s32[1,1,64]{2,1,0:T(1,128)}, u32[]{:S(2)}) copy-start(s32[1,1,64]{2,1,0:T(1,128)} %param.16) | copy-start | bytes 772
  9.9 1.0 %copy-start.5 = (bf16[1,1,512,96]{2,3,1,0:T(8,128)(2,1)S(1)}, bf16[1,1,512,96]{2,3,1,0:T(8,128)(2,1)}, u32[]{:S(2)}) copy-start(bf16[1,1,512,96]{2,3,1,0:T(8,128)(2,1)} %param.9) | copy-start | bytes 294916
  10.9 9.3 %copy-start = (bf16[27,96,96]{2,1,0:T(8,128)(2,1)S(1)}, bf16[27,96,96]{2,1,0:T(8,128)(2,1)}, u32[]{:S(2)}) copy-start(bf16[27,96,96]{2,1,0:T(8,128)(2,1)} %weight_ref.3) | copy-start | bytes 1492996
  16.3 5.5 %collective-permute-start.2 = (bf16[2048,128]{1,0:T(8,128)(2,1)S(1)}, bf16[2048,128]{1,0:T(8,128)(2,1)S(1)}, u32[]{:S(2)}, u32[]{:S(2)}) collective-permute-start(bf16[2048,128]{1,0:T(8,128)(2,1)S(1)} %get-tuple-element.53), channel_id=1, source_target_pairs={{0,4},{4,0},{8,12},{12,8},{16,20},{20,16},{24,28},{28,24},{1,5},{5... | collective-permute-start | bytes 1572872 | tf_op jit(solution)/shard_map/ppermute | solution.py:306
  21.9 6.2 %collective-permute-start.5 = (bf16[512,128]{1,0:T(8,128)(2,1)S(1)}, bf16[512,128]{1,0:T(8,128)(2,1)S(1)}, u32[]{:S(2)}, u32[]{:S(2)}) collective-permute-start(bf16[512,128]{1,0:T(8,128)(2,1)S(1)} %get-tuple-element.61), channel_id=1, source_target_pairs={{0,8},{4,12},{8,0},{12,4},{16,24},{20,28},{24,16},{28,20},{1,9},{5... | collective-permute-start | bytes 393224 | tf_op jit(solution)/shard_map/ppermute | solution.py:306
  23.5 8.3 %collective-permute-start.6 = (bf16[512,128]{1,0:T(8,128)(2,1)S(1)}, bf16[512,128]{1,0:T(8,128)(2,1)S(1)}, u32[]{:S(2)}, u32[]{:S(2)}) collective-permute-start(bf16[512,128]{1,0:T(8,128)(2,1)S(1)} %get-tuple-element.62), channel_id=1, source_target_pairs={{0,16},{4,20},{8,24},{12,28},{16,0},{20,4},{24,8},{28,12},{1,17},{... | collective-permute-start | bytes 393224 | tf_op jit(solution)/shard_map/ppermute | solution.py:306
  24.4 7.4 %collective-permute-start.7 = (bf16[512,128]{1,0:T(8,128)(2,1)S(1)}, bf16[512,128]{1,0:T(8,128)(2,1)S(1)}, u32[]{:S(2)}, u32[]{:S(2)}) collective-permute-start(bf16[512,128]{1,0:T(8,128)(2,1)S(1)} %get-tuple-element.63), channel_id=1, source_target_pairs={{0,24},{4,28},{8,16},{12,20},{16,8},{20,12},{24,0},{28,4},{1,25},{... | collective-permute-start | bytes 393224 | tf_op jit(solution)/shard_map/ppermute | solution.py:306
  25.5 1.2 %collective-permute-start.3 = (bf16[96,128]{1,0:T(8,128)(2,1)S(1)}, bf16[96,128]{1,0:T(8,128)(2,1)S(1)}, u32[]{:S(2)}, u32[]{:S(2)}) collective-permute-start(bf16[96,128]{1,0:T(8,128)(2,1)S(1)} %get-tuple-element.58), channel_id=1, source_target_pairs={{0,4},{4,0},{8,12},{12,8},{16,20},{20,16},{24,28},{28,24},{1,5},{5... | collective-permute-start | bytes 73736 | tf_op jit(solution)/shard_map/ppermute | solution.py:306
  25.5 1.2 %collective-permute-start.4 = (bf16[96,128]{1,0:T(8,128)(2,1)S(1)}, bf16[96,128]{1,0:T(8,128)(2,1)S(1)}, u32[]{:S(2)}, u32[]{:S(2)}) collective-permute-start(bf16[96,128]{1,0:T(8,128)(2,1)S(1)} %get-tuple-element.59), channel_id=1, source_target_pairs={{4,8},{8,4},{12,16},{16,12},{20,24},{24,20},{5,9},{9,5},{13,17},{1... | collective-permute-start | bytes 73736 | tf_op jit(solution)/shard_map/ppermute | solution.py:311
  31.9 4.6 %collective-permute-start.8 = (bf16[256,128]{1,0:T(8,128)(2,1)S(1)}, bf16[256,128]{1,0:T(8,128)(2,1)S(1)}, u32[]{:S(2)}, u32[]{:S(2)}) collective-permute-start(bf16[256,128]{1,0:T(8,128)(2,1)S(1)} %get-tuple-element.75.refs_0_), channel_id=1, source_target_pairs={{0,1},{1,0},{2,3},{3,2},{4,6},{5,7},{6,4},{7,5},{8,9},{9,8},{10,11... | collective-permute-start | bytes 196616 | tf_op jit(solution)/shard_map/ppermute | solution.py:320
  33.5 5.4 %collective-permute-start.10 = (bf16[256,128]{1,0:T(8,128)(2,1)S(1)}, bf16[256,128]{1,0:T(8,128)(2,1)S(1)}, u32[]{:S(2)}, u32[]{:S(2)}) collective-permute-start(bf16[256,128]{1,0:T(8,128)(2,1)S(1)} %get-tuple-element.76.refs_0_), channel_id=1, source_target_pairs={{0,1},{1,0},{2,3},{3,2},{4,6},{5,7},{6,4},{7,5},{8,9},{9,8},{10,11... | collective-permute-start | bytes 196616 | tf_op jit(solution)/shard_map/ppermute | solution.py:320
  36.5 5.3 %collective-permute-start.9 = (bf16[256,128]{1,0:T(8,128)(2,1)S(1)}, bf16[256,128]{1,0:T(8,128)(2,1)S(1)}, u32[]{:S(2)}, u32[]{:S(2)}) collective-permute-start(bf16[256,128]{1,0:T(8,128)(2,1)S(1)} %shard_map.120.refs_0_), channel_id=1, source_target_pairs={{0,2},{1,3},{2,0},{3,1},{4,5},{5,4},{6,7},{7,6},{8,10},{9,11},{10,... | collective-permute-start | bytes 196616 | tf_op jit(solution)/shard_map/ppermute | solution.py:320
  38.9 5.4 %collective-permute-start.11 = (bf16[256,128]{1,0:T(8,128)(2,1)S(1)}, bf16[256,128]{1,0:T(8,128)(2,1)S(1)}, u32[]{:S(2)}, u32[]{:S(2)}) collective-permute-start(bf16[256,128]{1,0:T(8,128)(2,1)S(1)} %shard_map.121.refs_2_), channel_id=1, source_target_pairs={{0,2},{1,3},{2,0},{3,1},{4,5},{5,4},{6,7},{7,6},{8,10},{9,11},{10,... | collective-permute-start | bytes 196616 | tf_op jit(solution)/shard_map/ppermute | solution.py:320
  44.3 6.0 %collective-permute-start.17 = (bf16[512,128]{1,0:T(8,128)(2,1)S(1)}, bf16[512,128]{1,0:T(8,128)(2,1)S(1)}, u32[]{:S(2)}, u32[]{:S(2)}) collective-permute-start(bf16[512,128]{1,0:T(8,128)(2,1)S(1)} %shard_map.122.refs_0_), channel_id=1, source_target_pairs={{0,24},{4,28},{8,16},{12,20},{16,8},{20,12},{24,0},{28,4},{1,25},{... | collective-permute-start | bytes 393224 | tf_op jit(solution)/shard_map/ppermute | solution.py:306
  46.3 5.4 %collective-permute-start.15 = (bf16[512,128]{1,0:T(8,128)(2,1)S(1)}, bf16[512,128]{1,0:T(8,128)(2,1)S(1)}, u32[]{:S(2)}, u32[]{:S(2)}) collective-permute-start(bf16[512,128]{1,0:T(8,128)(2,1)S(1)} %shard_map.122.refs_0_), channel_id=1, source_target_pairs={{0,16},{4,20},{8,24},{12,28},{16,0},{20,4},{24,8},{28,12},{1,17},{... | collective-permute-start | bytes 393224 | tf_op jit(solution)/shard_map/ppermute | solution.py:306
  47.3 5.0 %collective-permute-start.13 = (bf16[512,128]{1,0:T(8,128)(2,1)S(1)}, bf16[512,128]{1,0:T(8,128)(2,1)S(1)}, u32[]{:S(2)}, u32[]{:S(2)}) collective-permute-start(bf16[512,128]{1,0:T(8,128)(2,1)S(1)} %shard_map.122.refs_0_), channel_id=1, source_target_pairs={{0,8},{4,12},{8,0},{12,4},{16,24},{20,28},{24,16},{28,20},{1,9},{5... | collective-permute-start | bytes 393224 | tf_op jit(solution)/shard_map/ppermute | solution.py:306
  47.9 4.5 %collective-permute-start.12 = (bf16[512,128]{1,0:T(8,128)(2,1)S(1)}, bf16[512,128]{1,0:T(8,128)(2,1)S(1)}, u32[]{:S(2)}, u32[]{:S(2)}) collective-permute-start(bf16[512,128]{1,0:T(8,128)(2,1)S(1)} %shard_map.122.refs_0_), channel_id=1, source_target_pairs={{0,4},{4,0},{8,12},{12,8},{16,20},{20,16},{24,28},{28,24},{1,5},{5... | collective-permute-start | bytes 393224 | tf_op jit(solution)/shard_map/ppermute | solution.py:306
  50.3 2.0 %collective-permute-start.18 = (bf16[512,128]{1,0:T(8,128)(2,1)S(1)}, bf16[512,128]{1,0:T(8,128)(2,1)S(1)}, u32[]{:S(2)}, u32[]{:S(2)}) collective-permute-start(bf16[512,128]{1,0:T(8,128)(2,1)S(1)} %collective-permute-done.17.refs_6_), channel_id=1, source_target_pairs={{0,4},{4,0},{8,12},{12,8},{16,20},{20,16},{24,28},{28,24},{1,5},{5... | collective-permute-start | bytes 393224 | tf_op jit(solution)/shard_map/ppermute | solution.py:306
  51.6 1.3 %collective-permute-start.16 = (bf16[512,128]{1,0:T(8,128)(2,1)S(1)}, bf16[512,128]{1,0:T(8,128)(2,1)S(1)}, u32[]{:S(2)}, u32[]{:S(2)}) collective-permute-start(bf16[512,128]{1,0:T(8,128)(2,1)S(1)} %collective-permute-done.15.refs_4_), channel_id=1, source_target_pairs={{0,4},{4,0},{8,12},{12,8},{16,20},{20,16},{24,28},{28,24},{1,5},{5... | collective-permute-start | bytes 393224 | tf_op jit(solution)/shard_map/ppermute | solution.py:306
  52.3 1.3 %collective-permute-start.14 = (bf16[512,128]{1,0:T(8,128)(2,1)S(1)}, bf16[512,128]{1,0:T(8,128)(2,1)S(1)}, u32[]{:S(2)}, u32[]{:S(2)}) collective-permute-start(bf16[512,128]{1,0:T(8,128)(2,1)S(1)} %collective-permute-done.13.refs_2_), channel_id=1, source_target_pairs={{0,4},{4,0},{8,12},{12,8},{16,20},{20,16},{24,28},{28,24},{1,5},{5... | collective-permute-start | bytes 393224 | tf_op jit(solution)/shard_map/ppermute | solution.py:306

commit v6 on v5

--- a/solution.py
+++ b/solution.py
@@ -14,7 +14,7 @@
 BLOCK = 256
 CHUNK = 9
 WHOLE = 62 << 20
-UNROLL = 9
+UNROLL = 27
 NT = (((1,), (1,)), ((), ()))
 
 
@@ -55,6 +55,26 @@
     return jnp.concatenate(blocks, 0)
 
 
+def one_hot_columns(index, width):
+    count = lax.broadcasted_iota(I32, (index.shape[0], min(width, BLOCK)), 1).astype(F32).astype(BF16)
+    blocks = []
+    for start in range(0, width, BLOCK):
+        size = min(BLOCK, width - start)
+        hit = count[:, :size] == jnp.broadcast_to((index - start).astype(BF16), (index.shape[0], size))
+        blocks.append(jnp.where(hit, jnp.ones((), BF16), jnp.zeros((), BF16)))
+    return jnp.concatenate(blocks, 1)
+
+
+def take_columns(source_ref, index):
+    dims = (source_ref.shape[0], LANES)
+    lane, tile = jnp.broadcast_to(index % LANES, dims), jnp.broadcast_to(index // LANES, dims)
+    taken = jnp.zeros(dims, F32)
+    for t in range(source_ref.shape[1] // LANES):
+        block = source_ref[:, t * LANES : (t + 1) * LANES]
+        taken = jnp.where(tile == t, jnp.take_along_axis(block, lane, axis=1, mode="promise_in_bounds"), taken)
+    return taken
+
+
 def dot(a, b):
     return jnp.dot(a, b, preferred_element_type=F32)
 
@@ -130,7 +150,7 @@
 
 def rim_body(*refs):
     operands, (c_ref, t_ref, inv_ref, near_ref, far_ref), scratch = refs[:8], refs[8:13], refs[13:]
-    locals_, (total_ref, sems) = scratch[:8], scratch[8:]
+    locals_, (source_ref, total_ref, sems) = scratch[:8], scratch[8:]
     copies = [
         pltpu.make_async_copy(operand, local, sems.at[i]) for i, (operand, local) in enumerate(zip(operands, locals_, strict=True))
     ]
@@ -145,13 +165,16 @@
     def pick(k):
         index = outs_ref[k]
         base = pl.multiple_of(k * tall, 16)
-        c_ref[pl.ds(base, chans), :] = dot(cot_ref[...], one_hot(rows, index)).astype(BF16)
+        half = pairs - LANES
+        c_ref[pl.ds(base, chans), :half] = dot(cot_ref[...], one_hot(rows, index[:, :half])).astype(BF16)
+        c_ref[pl.ds(base, chans), half:] = take_columns(source_ref, index[:, half:]).astype(BF16)
         left = rows - index
         code = jnp.where(row == 0, left // 16, jnp.where(row == 1, left % 16, 0))
         c_ref[pl.ds(base + chans, 16), :] = code.astype(F32).astype(BF16)
 
     copies[0].wait()
     copies[1].wait()
+    source_ref[...] = cot_ref[...].astype(F32)
     loop(count, pick)
     copies[2].wait()
     place_rows(ins_ref, c_ref, rows, t_ref, inv_ref, 0)
@@ -166,9 +189,28 @@
     put_edges(near_ref, far_ref, chans, up, down)
 
 
-def own_body(ins_ref, c_ref, weight_ref, t_ref, own_ref, total_ref):
-    chans = total_ref.shape[0]
-    place_rows(ins_ref, c_ref, 0, t_ref, own_ref, chans)
+def own_body(ins_ref, c_ref, weight_ref, t_ref, own_ref, total_ref, columns_ref):
+    count, pairs = ins_ref.shape[0], ins_ref.shape[2]
+    chans, rows = total_ref.shape
+    tall = chans + 16
+    step = columns_ref.shape[0]
+    lot = count // step
+    t_ref[count * chans :, :] = jnp.zeros((t_ref.shape[0] - count * chans, rows), BF16)
+    for g in range(step):
+        lines = [ins_ref[g * lot + j] for j in range(lot)] + [jnp.zeros((-lot % 8, pairs), I32)]
+        columns_ref[g, :, : lot + -lot % 8] = jnp.concatenate(lines, 0).astype(F32).T
+
+    def place(g, carry):
+        index = columns_ref[g]
+        for j in range(lot):
+            k = g * lot + j
+            picked = c_ref[pl.ds(pl.multiple_of(k * tall, 16), tall), :]
+            placed = dot(picked, one_hot_columns(index[:, j : j + 1], rows))
+            t_ref[offset_rows(k, chans), :] = placed[:chans].astype(BF16)
+            own_ref[pl.ds(chans + k, 1), :] = placed[chans : chans + 1] * 16.0 + placed[chans + 1 : chans + 2]
+        return carry
+
+    lax.fori_loop(0, step, place, 0)
     add_back(weight_ref, t_ref, total_ref)
     own_ref[:chans] = total_ref[...]
 
@@ -212,16 +254,22 @@
 
 
 def one_body(
-    count, own_ref, inv_ref, near_ref, far_ref, hi_ref, lo_ref, pre_ref, zero_ref, t_two_ref, sum_two_ref, t_ref, keep_ref, send_ref, cot_ref, sum_ref
+    count, own_ref, inv_ref, near_ref, far_ref, hi_ref, lo_ref, pre_ref, zero_ref, t_two_ref, sum_two_ref, t_ref, keep_ref, send_ref, cot_ref, source_ref, sum_ref
 ):
     chans, rows = pre_ref.shape
     back = settled(own_ref[:chans], near_ref[:chans], far_ref[:chans], hi_ref, lo_ref)
     cot_ref[...] = jnp.where(pre_ref[...].astype(F32) > 0, back, 0.0).astype(BF16)
 
+    source_ref[...] = cot_ref[...].astype(F32)
+    part = rows - LANES
+
     def place(k):
         there = offset_rows(k, chans)
-        for index, columns in ((own_ref[pl.ds(chans + k, 1), :], slice(0, rows)), (inv_ref[pl.ds(k, 1), :], slice(rows, None))):
-            t_ref[there, columns] = dot(cot_ref[...], one_hot(rows, rows - index)).astype(BF16)
+        index = rows - own_ref[pl.ds(chans + k, 1), :]
+        t_ref[there, :part] = dot(cot_ref[...], one_hot(rows, index[:, :part])).astype(BF16)
+        t_ref[there, part:rows] = take_columns(source_ref, index[:, part:].astype(I32)).astype(BF16)
+        index = rows - inv_ref[pl.ds(k, 1), :]
+        t_ref[there, rows:] = take_columns(source_ref, index.astype(I32)).astype(BF16)
 
     loop(count, place)
     t_ref[count * chans :, :] = jnp.zeros((t_ref.shape[0] - count * chans, t_ref.shape[1]), BF16)
@@ -389,7 +437,7 @@
         ],
         operands,
         scratch=[pltpu.VMEM(x.shape, x.dtype) for x in operands]
-        + [pltpu.VMEM((chans, rim), F32), pltpu.SemaphoreType.DMA((len(operands),))],
+        + [pltpu.VMEM((chans, rows), F32), pltpu.VMEM((chans, rim), F32), pltpu.SemaphoreType.DMA((len(operands),))],
         flops=2 * count * chans * rows * pairs,
         moved=4 << 20,
         args_in=HBM,
@@ -399,7 +447,7 @@
         own_body,
         [shape((tall, rows), BF16), shape((chans + rounded, rows), F32)],
         [ins, c_two, weight_two],
-        scratch=[pltpu.VMEM((chans, rows), F32)],
+        scratch=[pltpu.VMEM((chans, rows), F32), pltpu.VMEM((-(-count // UNROLL), pairs, LANES), F32)],
         flops=gather_flops // 2,
         moved=8 << 20,
     )
@@ -408,7 +456,7 @@
         functools.partial(one_body, count),
         [shape((tall, ext), BF16), shape((packed, LANES), F32), shape((packed, LANES), BF16)],
         [own, inv_rim, near, far, hi, lo, pre, zero, t_rim, sum_two],
-        scratch=[pltpu.VMEM((chans, rows), BF16), pltpu.VMEM((packed, LANES), F32)],
+        scratch=[pltpu.VMEM((chans, rows), BF16), pltpu.VMEM((chans, rows), F32), pltpu.VMEM((packed, LANES), F32)],
         flops=gather_flops + back_flops,
         moved=8 << 20,
     )

time: 55.7 us -> 52.8 us (0.948)
  Pallas kernels: 18.5 us -> 15.4 us
    pallas_call x12, Pallas kernels: 18.5 us -> 15.4 us  [call(): pl.pallas_call(body, out_shape=outs if single else tuple(outs), in_specs=...]
  transfers between devices with their start and end apart: 19 -> 19, of which waited for: 12 -> 12; matrix products, arithmetic and copies ran while one was open for 0% -> 0% of each run, Pallas kernels for 12% -> 10%
where the time goes in v6:
time: 52.8 us; the launch traced here: 52.6 us
  starting transfers between devices  19 us (36%)
  waiting for transfers between devices  17.3 us (33%)
  Pallas kernels  15.4 us (29%)
  between operations  0.84 us (2%)
    pallas_call x12, Pallas kernels, call(): pl.pallas_call(body, out_shape=outs if single else tuple(outs), in_specs=...  15.4 us
    ppermute x13, waiting for transfers between devices, swap(): lax.ppermute(block, axis, [(i, i ^ bit) for i in range(lax.axis_size(axis...  12 us
    ppermute x13, starting transfers between devices, swap(): lax.ppermute(block, axis, [(i, i ^ bit) for i in range(lax.axis_size(axis...  11.6 us
    ppermute x4, starting transfers between devices, swap_scans(): return lax.ppermute(block, ('space', 'scan'), pairs)  6.14 us
    ppermute x4, waiting for transfers between devices, swap_scans(): return lax.ppermute(block, ('space', 'scan'), pairs)  5.25 us
    ppermute x2, starting transfers between devices, swap_neighbours(): lax.ppermute(far, 'space', [(i, i + 1 if i % 2 else i - 1) for i in inner])  1.3 us
  transfers between devices with their start and end apart: 19, of which 12 were waited for; matrix products, arithmetic and copies ran while one was open for 0% of the time, Pallas kernels for 10%

profile of v6, /device:TPU:0, one launch (start us, length us, event | category | flops | bytes accessed | tf_op | source)
XLA Modules:
  0.0 52.6 jit_solution(14057469459455886223)
XLA Ops:
  0.7 4.1 %shard_map.112 = (bf16[3024,256]{1,0:T(8,128)(2,1)S(1)}, bf16[2688,128]{1,0:T(8,128)(2,1)S(1)}, f32[32,128]{1,0:T(8,128)S(1)}, bf16[192,128]{1,0:T(8,128)(2,1)S(1)}, bf16[192,128]{1,0:T(8,128)(2,1)S(1)}) custom-call(s32[27,1,256]{2,1,0:T(1,128)} %bitcast.31, bf16[96,512]{1,0:T(8,128)(2,1)} %bitcast.30, s32[27,1,256]{2,1,0:T(1,128)} %bitcast.27, ...), custom_call_target="tpu_custom_call" | custom-call | flops 679477248 | bytes 4194304 | tf_op jit(solution)/shard_map/pallas_call | solution.py:23
  4.8 0.5 collective-permute-start
  5.3 0.7 %collective-permute-start.1 = (bf16[192,128]{1,0:T(8,128)(2,1)S(1)}, bf16[192,128]{1,0:T(8,128)(2,1)S(1)}, u32[]{:S(2)}, u32[]{:S(2)}) collective-permute-start(bf16[192,128]{1,0:T(8,128)(2,1)S(1)} %get-tuple-element.45), channel_id=1, source_target_pairs={{4,8},{8,4},{12,16},{16,12},{20,24},{24,20},{5,9},{9,5},{13,17},{1... | collective-permute-start | bytes 147464 | tf_op jit(solution)/shard_map/ppermute | solution.py:359
  6.0 2.0 %shard_map.113 = (bf16[2688,512]{1,0:T(8,128)(2,1)S(1)}, f32[128,512]{1,0:T(8,128)S(1)}) custom-call(s32[27,1,256]{2,1,0:T(1,128)S(1)} %bitcast.28, bf16[3024,256]{1,0:T(8,128)(2,1)S(1)} %get-tuple-element.41.c_ref, bf16[27,96,96]{2,1,0:T(8,128)(2,1)S(1)} %copy-done.4), custom_call_target="tpu_custom_call" | custom-call | flops 849346560 | bytes 8388608 | tf_op jit(solution)/shard_map/pallas_call | solution.py:23
  8.1 1.0 %shard_map.114.sum_two_ref = f32[2048,128]{1,0:T(8,128)S(1)} custom-call(bf16[96,512]{1,0:T(8,128)(2,1)S(1)} %bitcast.17, bf16[2688,512]{1,0:T(8,128)(2,1)S(1)} %get-tuple-element.47.t_ref), custom_call_target="tpu_custom_call" | custom-call | flops 318504960 | bytes 6291456 | tf_op jit(solution)/shard_map/pallas_call | solution.py:23
  9.1 4.2 %shard_map.115 = (bf16[2688,640]{1,0:T(8,128)(2,1)S(1)}, f32[2048,128]{1,0:T(8,128)S(1)}, bf16[2048,128]{1,0:T(8,128)(2,1)S(1)}) custom-call(f32[128,512]{1,0:T(8,128)S(1)} %get-tuple-element.42.own_ref, f32[32,128]{1,0:T(8,128)S(1)} %get-tuple-element.43.inv_ref, bf16[192,128]{1,0:T(8,128)(2,1)S(1)} %collective-permute-done.near_ref, ...), custom_call_target="tpu_custom_call" | custom-call | flops 2017198080 | bytes 8388608 | tf_op jit(solution)/shard_map/pallas_call | solution.py:23
  13.3 3.9 %collective-permute-start.2 = (bf16[2048,128]{1,0:T(8,128)(2,1)S(1)}, bf16[2048,128]{1,0:T(8,128)(2,1)S(1)}, u32[]{:S(2)}, u32[]{:S(2)}) collective-permute-start(bf16[2048,128]{1,0:T(8,128)(2,1)S(1)} %get-tuple-element.53), channel_id=1, source_target_pairs={{0,4},{4,0},{8,12},{12,8},{16,20},{20,16},{24,28},{28,24},{1,5},{5... | collective-permute-start | bytes 1572872 | tf_op jit(solution)/shard_map/ppermute | solution.py:354
  17.2 1.1 %shard_map.116 = (f32[96,512]{1,0:T(8,128)S(1)}, bf16[96,128]{1,0:T(8,128)(2,1)S(1)}, bf16[96,128]{1,0:T(8,128)(2,1)S(1)}) custom-call(bf16[27,96,96]{2,1,0:T(8,128)(2,1)S(1)} %copy-done, bf16[2688,640]{1,0:T(8,128)(2,1)S(1)} %get-tuple-element.49.t_ref), custom_call_target="tpu_custom_call" | custom-call | flops 318504960 | bytes 6291456 | tf_op jit(solution)/shard_map/pallas_call | solution.py:23
  18.9 1.7 %collective-permute-start.5 = (bf16[512,128]{1,0:T(8,128)(2,1)S(1)}, bf16[512,128]{1,0:T(8,128)(2,1)S(1)}, u32[]{:S(2)}, u32[]{:S(2)}) collective-permute-start(bf16[512,128]{1,0:T(8,128)(2,1)S(1)} %get-tuple-element.61), channel_id=1, source_target_pairs={{0,8},{4,12},{8,0},{12,4},{16,24},{20,28},{24,16},{28,20},{1,9},{5... | collective-permute-start | bytes 393224 | tf_op jit(solution)/shard_map/ppermute | solution.py:354
  20.6 0.8 %collective-permute-start.6 = (bf16[512,128]{1,0:T(8,128)(2,1)S(1)}, bf16[512,128]{1,0:T(8,128)(2,1)S(1)}, u32[]{:S(2)}, u32[]{:S(2)}) collective-permute-start(bf16[512,128]{1,0:T(8,128)(2,1)S(1)} %get-tuple-element.62), channel_id=1, source_target_pairs={{0,16},{4,20},{8,24},{12,28},{16,0},{20,4},{24,8},{28,12},{1,17},{... | collective-permute-start | bytes 393224 | tf_op jit(solution)/shard_map/ppermute | solution.py:354
  21.4 1.1 %collective-permute-start.7 = (bf16[512,128]{1,0:T(8,128)(2,1)S(1)}, bf16[512,128]{1,0:T(8,128)(2,1)S(1)}, u32[]{:S(2)}, u32[]{:S(2)}) collective-permute-start(bf16[512,128]{1,0:T(8,128)(2,1)S(1)} %get-tuple-element.63), channel_id=1, source_target_pairs={{0,24},{4,28},{8,16},{12,20},{16,8},{20,12},{24,0},{28,4},{1,25},{... | collective-permute-start | bytes 393224 | tf_op jit(solution)/shard_map/ppermute | solution.py:354
  22.5 0.7 %collective-permute-start.4 = (bf16[96,128]{1,0:T(8,128)(2,1)S(1)}, bf16[96,128]{1,0:T(8,128)(2,1)S(1)}, u32[]{:S(2)}, u32[]{:S(2)}) collective-permute-start(bf16[96,128]{1,0:T(8,128)(2,1)S(1)} %get-tuple-element.59), channel_id=1, source_target_pairs={{4,8},{8,4},{12,16},{16,12},{20,24},{24,20},{5,9},{9,5},{13,17},{1... | collective-permute-start | bytes 73736 | tf_op jit(solution)/shard_map/ppermute | solution.py:359
  23.1 0.5 %collective-permute-done.3.near_ref = bf16[96,128]{1,0:T(8,128)(2,1)S(1)} collective-permute-done((bf16[96,128]{1,0:T(8,128)(2,1)S(1)}, bf16[96,128]{1,0:T(8,128)(2,1)S(1)}, u32[]{:S(2)}, u32[]{:S(2)}) %collective-permute-start.3) | collective-permute-done | bytes 24608 | tf_op jit(solution)/shard_map/ppermute | solution.py:354
  23.7 1.3 %collective-permute-done.5.refs_0_ = bf16[512,128]{1,0:T(8,128)(2,1)S(1)} collective-permute-done((bf16[512,128]{1,0:T(8,128)(2,1)S(1)}, bf16[512,128]{1,0:T(8,128)(2,1)S(1)}, u32[]{:S(2)}, u32[]{:S(2)}) %collective-permute-start.5) | collective-permute-done | bytes 131104 | tf_op jit(solution)/shard_map/ppermute | solution.py:354
  24.9 4.0 %collective-permute-done.6.refs_1_ = bf16[512,128]{1,0:T(8,128)(2,1)S(1)} collective-permute-done((bf16[512,128]{1,0:T(8,128)(2,1)S(1)}, bf16[512,128]{1,0:T(8,128)(2,1)S(1)}, u32[]{:S(2)}, u32[]{:S(2)}) %collective-permute-start.6) | collective-permute-done | bytes 131104 | tf_op jit(solution)/shard_map/ppermute | solution.py:354
  29.0 1.6 %collective-permute-start.8 = (bf16[256,128]{1,0:T(8,128)(2,1)S(1)}, bf16[256,128]{1,0:T(8,128)(2,1)S(1)}, u32[]{:S(2)}, u32[]{:S(2)}) collective-permute-start(bf16[256,128]{1,0:T(8,128)(2,1)S(1)} %get-tuple-element.75.refs_0_), channel_id=1, source_target_pairs={{0,1},{1,0},{2,3},{3,2},{4,6},{5,7},{6,4},{7,5},{8,9},{9,8},{10,11... | collective-permute-start | bytes 196616 | tf_op jit(solution)/shard_map/ppermute | solution.py:368
  30.6 0.4 collective-permute-start.10
  31.1 0.9 %shard_map.119 = bf16[96,512]{1,0:T(8,128)(2,1)} custom-call(f32[96,512]{1,0:T(8,128)S(1)} %get-tuple-element.71.own_ref, bf16[96,128]{1,0:T(8,128)(2,1)S(1)} %collective-permute-done.3.near_ref, bf16[96,128]{1,0:T(8,128)(2,1)S(1)} %collective-permute-done.4.far_ref, s32[1,64]{1,0:T(1,128)S(1)} %bitcast.21, s32[1,64]{1,0:T(1,128)S(1)} %bitcast.24), custom_call_target="tpu_custom_call" | custom-call | tf_op jit(solution)/shard_map/pallas_call | solution.py:23
  32.0 1.4 %collective-permute-done.8.refs_1_ = bf16[256,128]{1,0:T(8,128)(2,1)S(1)} collective-permute-done((bf16[256,128]{1,0:T(8,128)(2,1)S(1)}, bf16[256,128]{1,0:T(8,128)(2,1)S(1)}, u32[]{:S(2)}, u32[]{:S(2)}) %collective-permute-start.8) | collective-permute-done | bytes 65568 | tf_op jit(solution)/shard_map/ppermute | solution.py:368
  33.5 2.5 %collective-permute-start.9 = (bf16[256,128]{1,0:T(8,128)(2,1)S(1)}, bf16[256,128]{1,0:T(8,128)(2,1)S(1)}, u32[]{:S(2)}, u32[]{:S(2)}) collective-permute-start(bf16[256,128]{1,0:T(8,128)(2,1)S(1)} %shard_map.120.refs_0_), channel_id=1, source_target_pairs={{0,2},{1,3},{2,0},{3,1},{4,5},{5,4},{6,7},{7,6},{8,10},{9,11},{10,... | collective-permute-start | bytes 196616 | tf_op jit(solution)/shard_map/ppermute | solution.py:368
  36.0 1.5 %collective-permute-start.11 = (bf16[256,128]{1,0:T(8,128)(2,1)S(1)}, bf16[256,128]{1,0:T(8,128)(2,1)S(1)}, u32[]{:S(2)}, u32[]{:S(2)}) collective-permute-start(bf16[256,128]{1,0:T(8,128)(2,1)S(1)} %shard_map.121.refs_2_), channel_id=1, source_target_pairs={{0,2},{1,3},{2,0},{3,1},{4,5},{5,4},{6,7},{7,6},{8,10},{9,11},{10,... | collective-permute-start | bytes 196616 | tf_op jit(solution)/shard_map/ppermute | solution.py:368
  37.5 1.3 %collective-permute-done.9.refs_1_ = bf16[256,128]{1,0:T(8,128)(2,1)S(1)} collective-permute-done((bf16[256,128]{1,0:T(8,128)(2,1)S(1)}, bf16[256,128]{1,0:T(8,128)(2,1)S(1)}, u32[]{:S(2)}, u32[]{:S(2)}) %collective-permute-start.9) | collective-permute-done | bytes 65568 | tf_op jit(solution)/shard_map/ppermute | solution.py:368
  38.8 2.5 %collective-permute-done.11.refs_3_ = bf16[256,128]{1,0:T(8,128)(2,1)S(1)} collective-permute-done((bf16[256,128]{1,0:T(8,128)(2,1)S(1)}, bf16[256,128]{1,0:T(8,128)(2,1)S(1)}, u32[]{:S(2)}, u32[]{:S(2)}) %collective-permute-start.11) | collective-permute-done | bytes 65568 | tf_op jit(solution)/shard_map/ppermute | solution.py:368
  41.4 1.6 %collective-permute-start.17 = (bf16[512,128]{1,0:T(8,128)(2,1)S(1)}, bf16[512,128]{1,0:T(8,128)(2,1)S(1)}, u32[]{:S(2)}, u32[]{:S(2)}) collective-permute-start(bf16[512,128]{1,0:T(8,128)(2,1)S(1)} %shard_map.122.refs_0_), channel_id=1, source_target_pairs={{0,24},{4,28},{8,16},{12,20},{16,8},{20,12},{24,0},{28,4},{1,25},{... | collective-permute-start | bytes 393224 | tf_op jit(solution)/shard_map/ppermute | solution.py:354
  42.9 1.5 %collective-permute-start.15 = (bf16[512,128]{1,0:T(8,128)(2,1)S(1)}, bf16[512,128]{1,0:T(8,128)(2,1)S(1)}, u32[]{:S(2)}, u32[]{:S(2)}) collective-permute-start(bf16[512,128]{1,0:T(8,128)(2,1)S(1)} %shard_map.122.refs_0_), channel_id=1, source_target_pairs={{0,16},{4,20},{8,24},{12,28},{16,0},{20,4},{24,8},{28,12},{1,17},{... | collective-permute-start | bytes 393224 | tf_op jit(solution)/shard_map/ppermute | solution.py:354
  44.5 0.5 collective-permute-start.13
  44.9 2.5 %collective-permute-done.17.refs_6_ = bf16[512,128]{1,0:T(8,128)(2,1)S(1)} collective-permute-done((bf16[512,128]{1,0:T(8,128)(2,1)S(1)}, bf16[512,128]{1,0:T(8,128)(2,1)S(1)}, u32[]{:S(2)}, u32[]{:S(2)}) %collective-permute-start.17) | collective-permute-done | bytes 131104 | tf_op jit(solution)/shard_map/ppermute | solution.py:354
  47.4 1.3 %collective-permute-done.15.refs_4_ = bf16[512,128]{1,0:T(8,128)(2,1)S(1)} collective-permute-done((bf16[512,128]{1,0:T(8,128)(2,1)S(1)}, bf16[512,128]{1,0:T(8,128)(2,1)S(1)}, u32[]{:S(2)}, u32[]{:S(2)}) %collective-permute-start.15) | collective-permute-done | bytes 131104 | tf_op jit(solution)/shard_map/ppermute | solution.py:354
  48.7 0.7 %collective-permute-done.13.refs_2_ = bf16[512,128]{1,0:T(8,128)(2,1)S(1)} collective-permute-done((bf16[512,128]{1,0:T(8,128)(2,1)S(1)}, bf16[512,128]{1,0:T(8,128)(2,1)S(1)}, u32[]{:S(2)}, u32[]{:S(2)}) %collective-permute-start.13) | collective-permute-done | bytes 131104 | tf_op jit(solution)/shard_map/ppermute | solution.py:354
  49.4 0.6 %collective-permute-done.16.refs_5_ = bf16[512,128]{1,0:T(8,128)(2,1)S(1)} collective-permute-done((bf16[512,128]{1,0:T(8,128)(2,1)S(1)}, bf16[512,128]{1,0:T(8,128)(2,1)S(1)}, u32[]{:S(2)}, u32[]{:S(2)}) %collective-permute-start.16) | collective-permute-done | bytes 131104 | tf_op jit(solution)/shard_map/ppermute | solution.py:354
  50.1 0.7 %collective-permute-done.14.refs_3_ = bf16[512,128]{1,0:T(8,128)(2,1)S(1)} collective-permute-done((bf16[512,128]{1,0:T(8,128)(2,1)S(1)}, bf16[512,128]{1,0:T(8,128)(2,1)S(1)}, u32[]{:S(2)}, u32[]{:S(2)}) %collective-permute-start.14) | collective-permute-done | bytes 131104 | tf_op jit(solution)/shard_map/ppermute | solution.py:354
  50.8 1.9 %shard_map.123 = (f32[27,96,96]{2,1,0:T(8,128)}, f32[27,96,96]{2,1,0:T(8,128)}) custom-call(bf16[512,128]{1,0:T(8,128)(2,1)S(1)} %shard_map.122.refs_0_, bf16[512,128]{1,0:T(8,128)(2,1)S(1)} %collective-permute-done.12.refs_1_, bf16[512,128]{1,0:T(8,128)(2,1)S(1)} %collective-permute-done.13.refs_2_, bf16[512,128]{1,0:T(8,128)(2,1)S(1)} %collective-permute-done.14.refs_3_, ...), custom_call_target="tpu_custom_call" | custom-call | tf_op jit(solution)/shard_map/pallas_call | solution.py:23
  (32 shorter events, 0.8 us)
Async XLA Ops:
  0.6 5.3 %copy-start.4 = (bf16[27,96,96]{2,1,0:T(8,128)(2,1)S(1)}, bf16[27,96,96]{2,1,0:T(8,128)(2,1)}, u32[]{:S(2)}) copy-start(bf16[27,96,96]{2,1,0:T(8,128)(2,1)} %weight_ref.2) | copy-start | bytes 1492996
  0.6 5.3 %copy-start.6 = (s32[1,1,27,256]{3,1,2,0:T(1,128)S(1)}, s32[1,1,27,256]{3,1,2,0:T(1,128)}, u32[]{:S(2)}) copy-start(s32[1,1,27,256]{3,1,2,0:T(1,128)} %param.14) | copy-start | bytes 82948
  4.8 4.3 %collective-permute-start = (bf16[192,128]{1,0:T(8,128)(2,1)S(1)}, bf16[192,128]{1,0:T(8,128)(2,1)S(1)}, u32[]{:S(2)}, u32[]{:S(2)}) collective-permute-start(bf16[192,128]{1,0:T(8,128)(2,1)S(1)} %get-tuple-element.44), channel_id=1, source_target_pairs={{0,4},{4,0},{8,12},{12,8},{16,20},{20,16},{24,28},{28,24},{1,5},{5... | collective-permute-start | bytes 147464 | tf_op jit(solution)/shard_map/ppermute | solution.py:354
  5.3 3.8 %collective-permute-start.1 = (bf16[192,128]{1,0:T(8,128)(2,1)S(1)}, bf16[192,128]{1,0:T(8,128)(2,1)S(1)}, u32[]{:S(2)}, u32[]{:S(2)}) collective-permute-start(bf16[192,128]{1,0:T(8,128)(2,1)S(1)} %get-tuple-element.45), channel_id=1, source_target_pairs={{4,8},{8,4},{12,16},{16,12},{20,24},{24,20},{5,9},{9,5},{13,17},{1... | collective-permute-start | bytes 147464 | tf_op jit(solution)/shard_map/ppermute | solution.py:359
  6.0 2.1 %copy-start.1 = (bf16[1,1,512,96]{2,3,1,0:T(8,128)(2,1)S(1)}, bf16[1,1,512,96]{2,3,1,0:T(8,128)(2,1)}, u32[]{:S(2)}) copy-start(bf16[1,1,512,96]{2,3,1,0:T(8,128)(2,1)} %param.10) | copy-start | bytes 294916
  8.0 1.0 %copy-start.2 = (s32[1,1,64]{2,1,0:T(1,128)S(1)}, s32[1,1,64]{2,1,0:T(1,128)}, u32[]{:S(2)}) copy-start(s32[1,1,64]{2,1,0:T(1,128)} %param.17) | copy-start | bytes 772
  8.0 1.0 %copy-start.3 = (s32[1,1,64]{2,1,0:T(1,128)S(1)}, s32[1,1,64]{2,1,0:T(1,128)}, u32[]{:S(2)}) copy-start(s32[1,1,64]{2,1,0:T(1,128)} %param.16) | copy-start | bytes 772
  8.1 1.0 %copy-start.5 = (bf16[1,1,512,96]{2,3,1,0:T(8,128)(2,1)S(1)}, bf16[1,1,512,96]{2,3,1,0:T(8,128)(2,1)}, u32[]{:S(2)}) copy-start(bf16[1,1,512,96]{2,3,1,0:T(8,128)(2,1)} %param.9) | copy-start | bytes 294916
  9.1 8.2 %copy-start = (bf16[27,96,96]{2,1,0:T(8,128)(2,1)S(1)}, bf16[27,96,96]{2,1,0:T(8,128)(2,1)}, u32[]{:S(2)}) copy-start(bf16[27,96,96]{2,1,0:T(8,128)(2,1)} %weight_ref.3) | copy-start | bytes 1492996
  13.3 5.5 %collective-permute-start.2 = (bf16[2048,128]{1,0:T(8,128)(2,1)S(1)}, bf16[2048,128]{1,0:T(8,128)(2,1)S(1)}, u32[]{:S(2)}, u32[]{:S(2)}) collective-permute-start(bf16[2048,128]{1,0:T(8,128)(2,1)S(1)} %get-tuple-element.53), channel_id=1, source_target_pairs={{0,4},{4,0},{8,12},{12,8},{16,20},{20,16},{24,28},{28,24},{1,5},{5... | collective-permute-start | bytes 1572872 | tf_op jit(solution)/shard_map/ppermute | solution.py:354
  18.9 6.0 %collective-permute-start.5 = (bf16[512,128]{1,0:T(8,128)(2,1)S(1)}, bf16[512,128]{1,0:T(8,128)(2,1)S(1)}, u32[]{:S(2)}, u32[]{:S(2)}) collective-permute-start(bf16[512,128]{1,0:T(8,128)(2,1)S(1)} %get-tuple-element.61), channel_id=1, source_target_pairs={{0,8},{4,12},{8,0},{12,4},{16,24},{20,28},{24,16},{28,20},{1,9},{5... | collective-permute-start | bytes 393224 | tf_op jit(solution)/shard_map/ppermute | solution.py:354
  20.6 8.3 %collective-permute-start.6 = (bf16[512,128]{1,0:T(8,128)(2,1)S(1)}, bf16[512,128]{1,0:T(8,128)(2,1)S(1)}, u32[]{:S(2)}, u32[]{:S(2)}) collective-permute-start(bf16[512,128]{1,0:T(8,128)(2,1)S(1)} %get-tuple-element.62), channel_id=1, source_target_pairs={{0,16},{4,20},{8,24},{12,28},{16,0},{20,4},{24,8},{28,12},{1,17},{... | collective-permute-start | bytes 393224 | tf_op jit(solution)/shard_map/ppermute | solution.py:354
  21.4 7.5 %collective-permute-start.7 = (bf16[512,128]{1,0:T(8,128)(2,1)S(1)}, bf16[512,128]{1,0:T(8,128)(2,1)S(1)}, u32[]{:S(2)}, u32[]{:S(2)}) collective-permute-start(bf16[512,128]{1,0:T(8,128)(2,1)S(1)} %get-tuple-element.63), channel_id=1, source_target_pairs={{0,24},{4,28},{8,16},{12,20},{16,8},{20,12},{24,0},{28,4},{1,25},{... | collective-permute-start | bytes 393224 | tf_op jit(solution)/shard_map/ppermute | solution.py:354
  22.5 1.2 %collective-permute-start.3 = (bf16[96,128]{1,0:T(8,128)(2,1)S(1)}, bf16[96,128]{1,0:T(8,128)(2,1)S(1)}, u32[]{:S(2)}, u32[]{:S(2)}) collective-permute-start(bf16[96,128]{1,0:T(8,128)(2,1)S(1)} %get-tuple-element.58), channel_id=1, source_target_pairs={{0,4},{4,0},{8,12},{12,8},{16,20},{20,16},{24,28},{28,24},{1,5},{5... | collective-permute-start | bytes 73736 | tf_op jit(solution)/shard_map/ppermute | solution.py:354
  22.5 1.2 %collective-permute-start.4 = (bf16[96,128]{1,0:T(8,128)(2,1)S(1)}, bf16[96,128]{1,0:T(8,128)(2,1)S(1)}, u32[]{:S(2)}, u32[]{:S(2)}) collective-permute-start(bf16[96,128]{1,0:T(8,128)(2,1)S(1)} %get-tuple-element.59), channel_id=1, source_target_pairs={{4,8},{8,4},{12,16},{16,12},{20,24},{24,20},{5,9},{9,5},{13,17},{1... | collective-permute-start | bytes 73736 | tf_op jit(solution)/shard_map/ppermute | solution.py:359
  29.0 4.5 %collective-permute-start.8 = (bf16[256,128]{1,0:T(8,128)(2,1)S(1)}, bf16[256,128]{1,0:T(8,128)(2,1)S(1)}, u32[]{:S(2)}, u32[]{:S(2)}) collective-permute-start(bf16[256,128]{1,0:T(8,128)(2,1)S(1)} %get-tuple-element.75.refs_0_), channel_id=1, source_target_pairs={{0,1},{1,0},{2,3},{3,2},{4,6},{5,7},{6,4},{7,5},{8,9},{9,8},{10,11... | collective-permute-start | bytes 196616 | tf_op jit(solution)/shard_map/ppermute | solution.py:368
  30.6 5.4 %collective-permute-start.10 = (bf16[256,128]{1,0:T(8,128)(2,1)S(1)}, bf16[256,128]{1,0:T(8,128)(2,1)S(1)}, u32[]{:S(2)}, u32[]{:S(2)}) collective-permute-start(bf16[256,128]{1,0:T(8,128)(2,1)S(1)} %get-tuple-element.76.refs_0_), channel_id=1, source_target_pairs={{0,1},{1,0},{2,3},{3,2},{4,6},{5,7},{6,4},{7,5},{8,9},{9,8},{10,11... | collective-permute-start | bytes 196616 | tf_op jit(solution)/shard_map/ppermute | solution.py:368
  33.5 5.3 %collective-permute-start.9 = (bf16[256,128]{1,0:T(8,128)(2,1)S(1)}, bf16[256,128]{1,0:T(8,128)(2,1)S(1)}, u32[]{:S(2)}, u32[]{:S(2)}) collective-permute-start(bf16[256,128]{1,0:T(8,128)(2,1)S(1)} %shard_map.120.refs_0_), channel_id=1, source_target_pairs={{0,2},{1,3},{2,0},{3,1},{4,5},{5,4},{6,7},{7,6},{8,10},{9,11},{10,... | collective-permute-start | bytes 196616 | tf_op jit(solution)/shard_map/ppermute | solution.py:368
  36.0 5.3 %collective-permute-start.11 = (bf16[256,128]{1,0:T(8,128)(2,1)S(1)}, bf16[256,128]{1,0:T(8,128)(2,1)S(1)}, u32[]{:S(2)}, u32[]{:S(2)}) collective-permute-start(bf16[256,128]{1,0:T(8,128)(2,1)S(1)} %shard_map.121.refs_2_), channel_id=1, source_target_pairs={{0,2},{1,3},{2,0},{3,1},{4,5},{5,4},{6,7},{7,6},{8,10},{9,11},{10,... | collective-permute-start | bytes 196616 | tf_op jit(solution)/shard_map/ppermute | solution.py:368
  41.4 6.0 %collective-permute-start.17 = (bf16[512,128]{1,0:T(8,128)(2,1)S(1)}, bf16[512,128]{1,0:T(8,128)(2,1)S(1)}, u32[]{:S(2)}, u32[]{:S(2)}) collective-permute-start(bf16[512,128]{1,0:T(8,128)(2,1)S(1)} %shard_map.122.refs_0_), channel_id=1, source_target_pairs={{0,24},{4,28},{8,16},{12,20},{16,8},{20,12},{24,0},{28,4},{1,25},{... | collective-permute-start | bytes 393224 | tf_op jit(solution)/shard_map/ppermute | solution.py:354
  42.9 5.8 %collective-permute-start.15 = (bf16[512,128]{1,0:T(8,128)(2,1)S(1)}, bf16[512,128]{1,0:T(8,128)(2,1)S(1)}, u32[]{:S(2)}, u32[]{:S(2)}) collective-permute-start(bf16[512,128]{1,0:T(8,128)(2,1)S(1)} %shard_map.122.refs_0_), channel_id=1, source_target_pairs={{0,16},{4,20},{8,24},{12,28},{16,0},{20,4},{24,8},{28,12},{1,17},{... | collective-permute-start | bytes 393224 | tf_op jit(solution)/shard_map/ppermute | solution.py:354
  44.5 5.0 %collective-permute-start.13 = (bf16[512,128]{1,0:T(8,128)(2,1)S(1)}, bf16[512,128]{1,0:T(8,128)(2,1)S(1)}, u32[]{:S(2)}, u32[]{:S(2)}) collective-permute-start(bf16[512,128]{1,0:T(8,128)(2,1)S(1)} %shard_map.122.refs_0_), channel_id=1, source_target_pairs={{0,8},{4,12},{8,0},{12,4},{16,24},{20,28},{24,16},{28,20},{1,9},{5... | collective-permute-start | bytes 393224 | tf_op jit(solution)/shard_map/ppermute | solution.py:354
  44.9 4.5 %collective-permute-start.12 = (bf16[512,128]{1,0:T(8,128)(2,1)S(1)}, bf16[512,128]{1,0:T(8,128)(2,1)S(1)}, u32[]{:S(2)}, u32[]{:S(2)}) collective-permute-start(bf16[512,128]{1,0:T(8,128)(2,1)S(1)} %shard_map.122.refs_0_), channel_id=1, source_target_pairs={{0,4},{4,0},{8,12},{12,8},{16,20},{20,16},{24,28},{28,24},{1,5},{5... | collective-permute-start | bytes 393224 | tf_op jit(solution)/shard_map/ppermute | solution.py:354
  47.4 2.0 %collective-permute-start.18 = (bf16[512,128]{1,0:T(8,128)(2,1)S(1)}, bf16[512,128]{1,0:T(8,128)(2,1)S(1)}, u32[]{:S(2)}, u32[]{:S(2)}) collective-permute-start(bf16[512,128]{1,0:T(8,128)(2,1)S(1)} %collective-permute-done.17.refs_6_), channel_id=1, source_target_pairs={{0,4},{4,0},{8,12},{12,8},{16,20},{20,16},{24,28},{28,24},{1,5},{5... | collective-permute-start | bytes 393224 | tf_op jit(solution)/shard_map/ppermute | solution.py:354
  48.7 1.3 %collective-permute-start.16 = (bf16[512,128]{1,0:T(8,128)(2,1)S(1)}, bf16[512,128]{1,0:T(8,128)(2,1)S(1)}, u32[]{:S(2)}, u32[]{:S(2)}) collective-permute-start(bf16[512,128]{1,0:T(8,128)(2,1)S(1)} %collective-permute-done.15.refs_4_), channel_id=1, source_target_pairs={{0,4},{4,0},{8,12},{12,8},{16,20},{20,16},{24,28},{28,24},{1,5},{5... | collective-permute-start | bytes 393224 | tf_op jit(solution)/shard_map/ppermute | solution.py:354
  49.4 1.3 %collective-permute-start.14 = (bf16[512,128]{1,0:T(8,128)(2,1)S(1)}, bf16[512,128]{1,0:T(8,128)(2,1)S(1)}, u32[]{:S(2)}, u32[]{:S(2)}) collective-permute-start(bf16[512,128]{1,0:T(8,128)(2,1)S(1)} %collective-permute-done.13.refs_2_), channel_id=1, source_target_pairs={{0,4},{4,0},{8,12},{12,8},{16,20},{20,16},{24,28},{28,24},{1,5},{5... | collective-permute-start | bytes 393224 | tf_op jit(solution)/shard_map/ppermute | solution.py:354

commit v7 on v6

--- a/solution.py
+++ b/solution.py
@@ -14,7 +14,6 @@
 BLOCK = 256
 CHUNK = 9
 WHOLE = 62 << 20
-UNROLL = 27
 NT = (((1,), (1,)), ((), ()))
 
 
@@ -35,16 +34,6 @@
     return jax.ShapeDtypeStruct(dims, dtype)
 
 
-def loop(steps, body):
-    unroll = next(u for u in range(UNROLL, 0, -1) if steps % u == 0)
-
-    def step(i, carry):
-        body(i)
-        return carry
-
-    lax.fori_loop(0, steps, step, 0, unroll=unroll)
-
-
 def one_hot(rows, index):
     count = lax.broadcasted_iota(I32, (min(rows, BLOCK), index.shape[1]), 0).astype(F32).astype(BF16)
     blocks = []
@@ -84,7 +73,7 @@
 
 
 def offset_rows(k, chans):
-    return pl.ds(pl.multiple_of(k * chans, chans), chans)
+    return slice(k * chans, (k + 1) * chans)
 
 
 def rim_index(hi_ref, lo_ref):
@@ -128,7 +117,8 @@
         total_ref[...] += part
 
     assert count % 3 == 0
-    loop(count // 3, body)
+    for g in range(count // 3):
+        body(g)
 
 
 def place_rows(ins_ref, c_ref, first, t_ref, inv_ref, inv_at):
@@ -139,13 +129,14 @@
     t_ref[count * chans :, :] = jnp.zeros((t_ref.shape[0] - count * chans, ext), BF16)
 
     def place(k):
-        picked = c_ref[pl.ds(pl.multiple_of(k * tall, 16), tall), :]
+        picked = c_ref[k * tall : (k + 1) * tall, :]
         placed = dot_nt(picked, one_hot(ext, ins_ref[k] - first))
         t_ref[offset_rows(k, chans), :] = placed[:chans].astype(BF16)
         code = placed[chans : chans + 1] * 16.0 + placed[chans + 1 : chans + 2]
         inv_ref[pl.ds(inv_at + k, 1), :] = code
 
-    loop(count, place)
+    for k in range(count):
+        place(k)
 
 
 def rim_body(*refs):
@@ -164,10 +155,13 @@
 
     def pick(k):
         index = outs_ref[k]
-        base = pl.multiple_of(k * tall, 16)
-        half = pairs - LANES
-        c_ref[pl.ds(base, chans), :half] = dot(cot_ref[...], one_hot(rows, index[:, :half])).astype(BF16)
-        c_ref[pl.ds(base, chans), half:] = take_columns(source_ref, index[:, half:]).astype(BF16)
+        base = k * tall
+        if k % 4:
+            there = dot(cot_ref[...], one_hot(rows, index)).astype(BF16)
+        else:
+            there = [take_columns(source_ref, index[:, at : at + LANES]).astype(BF16) for at in range(0, pairs, LANES)]
+            there = jnp.concatenate(there, 1)
+        c_ref[pl.ds(base, chans), :] = there
         left = rows - index
         code = jnp.where(row == 0, left // 16, jnp.where(row == 1, left % 16, 0))
         c_ref[pl.ds(base + chans, 16), :] = code.astype(F32).astype(BF16)
@@ -175,7 +169,8 @@
     copies[0].wait()
     copies[1].wait()
     source_ref[...] = cot_ref[...].astype(F32)
-    loop(count, pick)
+    for k in range(count):
+        pick(k)
     copies[2].wait()
     place_rows(ins_ref, c_ref, rows, t_ref, inv_ref, 0)
     copies[3].wait()
@@ -193,24 +188,15 @@
     count, pairs = ins_ref.shape[0], ins_ref.shape[2]
     chans, rows = total_ref.shape
     tall = chans + 16
-    step = columns_ref.shape[0]
-    lot = count // step
     t_ref[count * chans :, :] = jnp.zeros((t_ref.shape[0] - count * chans, rows), BF16)
-    for g in range(step):
-        lines = [ins_ref[g * lot + j] for j in range(lot)] + [jnp.zeros((-lot % 8, pairs), I32)]
-        columns_ref[g, :, : lot + -lot % 8] = jnp.concatenate(lines, 0).astype(F32).T
-
-    def place(g, carry):
-        index = columns_ref[g]
-        for j in range(lot):
-            k = g * lot + j
-            picked = c_ref[pl.ds(pl.multiple_of(k * tall, 16), tall), :]
-            placed = dot(picked, one_hot_columns(index[:, j : j + 1], rows))
-            t_ref[offset_rows(k, chans), :] = placed[:chans].astype(BF16)
-            own_ref[pl.ds(chans + k, 1), :] = placed[chans : chans + 1] * 16.0 + placed[chans + 1 : chans + 2]
-        return carry
-
-    lax.fori_loop(0, step, place, 0)
+    lines = [ins_ref[k] for k in range(count)] + [jnp.zeros((-count % 8, pairs), I32)]
+    columns_ref[:, : count + -count % 8] = jnp.concatenate(lines, 0).astype(F32).T
+    index = columns_ref[...]
+    for k in range(count):
+        picked = c_ref[k * tall : (k + 1) * tall, :]
+        placed = dot(picked, one_hot_columns(index[:, k : k + 1], rows))
+        t_ref[offset_rows(k, chans), :] = placed[:chans].astype(BF16)
+        own_ref[chans + k : chans + k + 1, :] = placed[chans : chans + 1] * 16.0 + placed[chans + 1 : chans + 2]
     add_back(weight_ref, t_ref, total_ref)
     own_ref[:chans] = total_ref[...]
 
@@ -261,17 +247,18 @@
     cot_ref[...] = jnp.where(pre_ref[...].astype(F32) > 0, back, 0.0).astype(BF16)
 
     source_ref[...] = cot_ref[...].astype(F32)
-    part = rows - LANES
 
     def place(k):
         there = offset_rows(k, chans)
-        index = rows - own_ref[pl.ds(chans + k, 1), :]
+        part = rows - (LANES if k % 3 else 2 * LANES)
+        index = rows - own_ref[chans + k : chans + k + 1, :]
         t_ref[there, :part] = dot(cot_ref[...], one_hot(rows, index[:, :part])).astype(BF16)
-        t_ref[there, part:rows] = take_columns(source_ref, index[:, part:].astype(I32)).astype(BF16)
-        index = rows - inv_ref[pl.ds(k, 1), :]
-        t_ref[there, rows:] = take_columns(source_ref, index.astype(I32)).astype(BF16)
-
-    loop(count, place)
+        index = jnp.concatenate([index[:, part:], rows - inv_ref[k : k + 1, :]], 1).astype(I32)
+        for at in range(0, index.shape[1], LANES):
+            t_ref[there, part + at : part + at + LANES] = take_columns(source_ref, index[:, at : at + LANES]).astype(BF16)
+
+    for k in range(count):
+        place(k)
     t_ref[count * chans :, :] = jnp.zeros((t_ref.shape[0] - count * chans, t_ref.shape[1]), BF16)
     above, below = by_parity(near_ref[chans:], far_ref[chans:])
     zero_rim, one_rim = halves(below, above)
@@ -447,7 +434,7 @@
         own_body,
         [shape((tall, rows), BF16), shape((chans + rounded, rows), F32)],
         [ins, c_two, weight_two],
-        scratch=[pltpu.VMEM((chans, rows), F32), pltpu.VMEM((-(-count // UNROLL), pairs, LANES), F32)],
+        scratch=[pltpu.VMEM((chans, rows), F32), pltpu.VMEM((pairs, LANES), F32)],
         flops=gather_flops // 2,
         moved=8 << 20,
     )

time: 52.8 us -> 52.4 us (level)
  no operation moved by 1% of the time
where the time goes in v7:
time: 52.4 us; the launch traced here: 52.2 us
  starting transfers between devices  19.1 us (36%)
  waiting for transfers between devices  17.3 us (33%)
  Pallas kernels  15 us (29%)
  between operations  0.84 us (2%)
    pallas_call x12, Pallas kernels, call(): pl.pallas_call(body, out_shape=outs if single else tuple(outs), in_specs=...  15 us
    ppermute x13, waiting for transfers between devices, swap(): lax.ppermute(block, axis, [(i, i ^ bit) for i in range(lax.axis_size(axis...  12.1 us
    ppermute x13, starting transfers between devices, swap(): lax.ppermute(block, axis, [(i, i ^ bit) for i in range(lax.axis_size(axis...  11.6 us
    ppermute x4, starting transfers between devices, swap_scans(): return lax.ppermute(block, ('space', 'scan'), pairs)  6.15 us
    ppermute x4, waiting for transfers between devices, swap_scans(): return lax.ppermute(block, ('space', 'scan'), pairs)  5.23 us
    ppermute x2, starting transfers between devices, swap_neighbours(): lax.ppermute(far, 'space', [(i, i + 1 if i % 2 else i - 1) for i in inner])  1.3 us
  transfers between devices with their start and end apart: 19, of which 12 were waited for; matrix products, arithmetic and copies ran while one was open for 0% of the time, Pallas kernels for 10%

profile of v7, /device:TPU:0, one launch (start us, length us, event | category | flops | bytes accessed | tf_op | source)
XLA Modules:
  0.0 52.2 jit_solution(18278269432730930866)
XLA Ops:
  0.7 3.8 %shard_map.112 = (bf16[3024,256]{1,0:T(8,128)(2,1)S(1)}, bf16[2688,128]{1,0:T(8,128)(2,1)S(1)}, f32[32,128]{1,0:T(8,128)S(1)}, bf16[192,128]{1,0:T(8,128)(2,1)S(1)}, bf16[192,128]{1,0:T(8,128)(2,1)S(1)}) custom-call(s32[27,1,256]{2,1,0:T(1,128)} %bitcast.31, bf16[96,512]{1,0:T(8,128)(2,1)} %bitcast.30, s32[27,1,256]{2,1,0:T(1,128)} %bitcast.27, ...), custom_call_target="tpu_custom_call" | custom-call | flops 679477248 | bytes 4194304 | tf_op jit(solution)/shard_map/pallas_call | solution.py:22
  4.4 0.5 %collective-permute-start = (bf16[192,128]{1,0:T(8,128)(2,1)S(1)}, bf16[192,128]{1,0:T(8,128)(2,1)S(1)}, u32[]{:S(2)}, u32[]{:S(2)}) collective-permute-start(bf16[192,128]{1,0:T(8,128)(2,1)S(1)} %get-tuple-element.44), channel_id=1, source_target_pairs={{0,4},{4,0},{8,12},{12,8},{16,20},{20,16},{24,28},{28,24},{1,5},{5... | collective-permute-start | bytes 147464 | tf_op jit(solution)/shard_map/ppermute | solution.py:341
  5.0 0.7 %collective-permute-start.1 = (bf16[192,128]{1,0:T(8,128)(2,1)S(1)}, bf16[192,128]{1,0:T(8,128)(2,1)S(1)}, u32[]{:S(2)}, u32[]{:S(2)}) collective-permute-start(bf16[192,128]{1,0:T(8,128)(2,1)S(1)} %get-tuple-element.45), channel_id=1, source_target_pairs={{4,8},{8,4},{12,16},{16,12},{20,24},{24,20},{5,9},{9,5},{13,17},{1... | collective-permute-start | bytes 147464 | tf_op jit(solution)/shard_map/ppermute | solution.py:346
  5.7 2.0 %shard_map.113 = (bf16[2688,512]{1,0:T(8,128)(2,1)S(1)}, f32[128,512]{1,0:T(8,128)S(1)}) custom-call(s32[27,1,256]{2,1,0:T(1,128)S(1)} %bitcast.28, bf16[3024,256]{1,0:T(8,128)(2,1)S(1)} %get-tuple-element.41.c_ref, bf16[27,96,96]{2,1,0:T(8,128)(2,1)S(1)} %copy-done.4), custom_call_target="tpu_custom_call" | custom-call | flops 849346560 | bytes 8388608 | tf_op jit(solution)/shard_map/pallas_call | solution.py:22
  7.8 1.0 %shard_map.114.sum_two_ref = f32[2048,128]{1,0:T(8,128)S(1)} custom-call(bf16[96,512]{1,0:T(8,128)(2,1)S(1)} %bitcast.17, bf16[2688,512]{1,0:T(8,128)(2,1)S(1)} %get-tuple-element.47.t_ref), custom_call_target="tpu_custom_call" | custom-call | flops 318504960 | bytes 6291456 | tf_op jit(solution)/shard_map/pallas_call | solution.py:22
  8.8 4.1 %shard_map.115 = (bf16[2688,640]{1,0:T(8,128)(2,1)S(1)}, f32[2048,128]{1,0:T(8,128)S(1)}, bf16[2048,128]{1,0:T(8,128)(2,1)S(1)}) custom-call(f32[128,512]{1,0:T(8,128)S(1)} %get-tuple-element.42.own_ref, f32[32,128]{1,0:T(8,128)S(1)} %get-tuple-element.43.inv_ref, bf16[192,128]{1,0:T(8,128)(2,1)S(1)} %collective-permute-done.near_ref, ...), custom_call_target="tpu_custom_call" | custom-call | flops 2017198080 | bytes 8388608 | tf_op jit(solution)/shard_map/pallas_call | solution.py:22
  12.8 3.9 %collective-permute-start.2 = (bf16[2048,128]{1,0:T(8,128)(2,1)S(1)}, bf16[2048,128]{1,0:T(8,128)(2,1)S(1)}, u32[]{:S(2)}, u32[]{:S(2)}) collective-permute-start(bf16[2048,128]{1,0:T(8,128)(2,1)S(1)} %get-tuple-element.53), channel_id=1, source_target_pairs={{0,4},{4,0},{8,12},{12,8},{16,20},{20,16},{24,28},{28,24},{1,5},{5... | collective-permute-start | bytes 1572872 | tf_op jit(solution)/shard_map/ppermute | solution.py:341
  16.8 1.1 %shard_map.116 = (f32[96,512]{1,0:T(8,128)S(1)}, bf16[96,128]{1,0:T(8,128)(2,1)S(1)}, bf16[96,128]{1,0:T(8,128)(2,1)S(1)}) custom-call(bf16[27,96,96]{2,1,0:T(8,128)(2,1)S(1)} %copy-done, bf16[2688,640]{1,0:T(8,128)(2,1)S(1)} %get-tuple-element.49.t_ref), custom_call_target="tpu_custom_call" | custom-call | flops 318504960 | bytes 6291456 | tf_op jit(solution)/shard_map/pallas_call | solution.py:22
  18.4 1.7 %collective-permute-start.5 = (bf16[512,128]{1,0:T(8,128)(2,1)S(1)}, bf16[512,128]{1,0:T(8,128)(2,1)S(1)}, u32[]{:S(2)}, u32[]{:S(2)}) collective-permute-start(bf16[512,128]{1,0:T(8,128)(2,1)S(1)} %get-tuple-element.61), channel_id=1, source_target_pairs={{0,8},{4,12},{8,0},{12,4},{16,24},{20,28},{24,16},{28,20},{1,9},{5... | collective-permute-start | bytes 393224 | tf_op jit(solution)/shard_map/ppermute | solution.py:341
  20.2 0.7 %collective-permute-start.6 = (bf16[512,128]{1,0:T(8,128)(2,1)S(1)}, bf16[512,128]{1,0:T(8,128)(2,1)S(1)}, u32[]{:S(2)}, u32[]{:S(2)}) collective-permute-start(bf16[512,128]{1,0:T(8,128)(2,1)S(1)} %get-tuple-element.62), channel_id=1, source_target_pairs={{0,16},{4,20},{8,24},{12,28},{16,0},{20,4},{24,8},{28,12},{1,17},{... | collective-permute-start | bytes 393224 | tf_op jit(solution)/shard_map/ppermute | solution.py:341
  20.9 1.1 %collective-permute-start.7 = (bf16[512,128]{1,0:T(8,128)(2,1)S(1)}, bf16[512,128]{1,0:T(8,128)(2,1)S(1)}, u32[]{:S(2)}, u32[]{:S(2)}) collective-permute-start(bf16[512,128]{1,0:T(8,128)(2,1)S(1)} %get-tuple-element.63), channel_id=1, source_target_pairs={{0,24},{4,28},{8,16},{12,20},{16,8},{20,12},{24,0},{28,4},{1,25},{... | collective-permute-start | bytes 393224 | tf_op jit(solution)/shard_map/ppermute | solution.py:341
  22.0 0.7 %collective-permute-start.4 = (bf16[96,128]{1,0:T(8,128)(2,1)S(1)}, bf16[96,128]{1,0:T(8,128)(2,1)S(1)}, u32[]{:S(2)}, u32[]{:S(2)}) collective-permute-start(bf16[96,128]{1,0:T(8,128)(2,1)S(1)} %get-tuple-element.59), channel_id=1, source_target_pairs={{4,8},{8,4},{12,16},{16,12},{20,24},{24,20},{5,9},{9,5},{13,17},{1... | collective-permute-start | bytes 73736 | tf_op jit(solution)/shard_map/ppermute | solution.py:346
  22.7 0.5 %collective-permute-done.3.near_ref = bf16[96,128]{1,0:T(8,128)(2,1)S(1)} collective-permute-done((bf16[96,128]{1,0:T(8,128)(2,1)S(1)}, bf16[96,128]{1,0:T(8,128)(2,1)S(1)}, u32[]{:S(2)}, u32[]{:S(2)}) %collective-permute-start.3) | collective-permute-done | bytes 24608 | tf_op jit(solution)/shard_map/ppermute | solution.py:341
  23.2 1.3 %collective-permute-done.5.refs_0_ = bf16[512,128]{1,0:T(8,128)(2,1)S(1)} collective-permute-done((bf16[512,128]{1,0:T(8,128)(2,1)S(1)}, bf16[512,128]{1,0:T(8,128)(2,1)S(1)}, u32[]{:S(2)}, u32[]{:S(2)}) %collective-permute-start.5) | collective-permute-done | bytes 131104 | tf_op jit(solution)/shard_map/ppermute | solution.py:341
  24.5 4.0 %collective-permute-done.6.refs_1_ = bf16[512,128]{1,0:T(8,128)(2,1)S(1)} collective-permute-done((bf16[512,128]{1,0:T(8,128)(2,1)S(1)}, bf16[512,128]{1,0:T(8,128)(2,1)S(1)}, u32[]{:S(2)}, u32[]{:S(2)}) %collective-permute-start.6) | collective-permute-done | bytes 131104 | tf_op jit(solution)/shard_map/ppermute | solution.py:341
  28.5 1.6 %collective-permute-start.8 = (bf16[256,128]{1,0:T(8,128)(2,1)S(1)}, bf16[256,128]{1,0:T(8,128)(2,1)S(1)}, u32[]{:S(2)}, u32[]{:S(2)}) collective-permute-start(bf16[256,128]{1,0:T(8,128)(2,1)S(1)} %get-tuple-element.75.refs_0_), channel_id=1, source_target_pairs={{0,1},{1,0},{2,3},{3,2},{4,6},{5,7},{6,4},{7,5},{8,9},{9,8},{10,11... | collective-permute-start | bytes 196616 | tf_op jit(solution)/shard_map/ppermute | solution.py:355
  30.1 0.5 collective-permute-start.10
  30.6 0.9 %shard_map.119 = bf16[96,512]{1,0:T(8,128)(2,1)} custom-call(f32[96,512]{1,0:T(8,128)S(1)} %get-tuple-element.71.own_ref, bf16[96,128]{1,0:T(8,128)(2,1)S(1)} %collective-permute-done.3.near_ref, bf16[96,128]{1,0:T(8,128)(2,1)S(1)} %collective-permute-done.4.far_ref, s32[1,64]{1,0:T(1,128)S(1)} %bitcast.21, s32[1,64]{1,0:T(1,128)S(1)} %bitcast.24), custom_call_target="tpu_custom_call" | custom-call | tf_op jit(solution)/shard_map/pallas_call | solution.py:22
  31.6 1.4 %collective-permute-done.8.refs_1_ = bf16[256,128]{1,0:T(8,128)(2,1)S(1)} collective-permute-done((bf16[256,128]{1,0:T(8,128)(2,1)S(1)}, bf16[256,128]{1,0:T(8,128)(2,1)S(1)}, u32[]{:S(2)}, u32[]{:S(2)}) %collective-permute-start.8) | collective-permute-done | bytes 65568 | tf_op jit(solution)/shard_map/ppermute | solution.py:355
  33.0 2.5 %collective-permute-start.9 = (bf16[256,128]{1,0:T(8,128)(2,1)S(1)}, bf16[256,128]{1,0:T(8,128)(2,1)S(1)}, u32[]{:S(2)}, u32[]{:S(2)}) collective-permute-start(bf16[256,128]{1,0:T(8,128)(2,1)S(1)} %shard_map.120.refs_0_), channel_id=1, source_target_pairs={{0,2},{1,3},{2,0},{3,1},{4,5},{5,4},{6,7},{7,6},{8,10},{9,11},{10,... | collective-permute-start | bytes 196616 | tf_op jit(solution)/shard_map/ppermute | solution.py:355
  35.5 1.6 %collective-permute-start.11 = (bf16[256,128]{1,0:T(8,128)(2,1)S(1)}, bf16[256,128]{1,0:T(8,128)(2,1)S(1)}, u32[]{:S(2)}, u32[]{:S(2)}) collective-permute-start(bf16[256,128]{1,0:T(8,128)(2,1)S(1)} %shard_map.121.refs_2_), channel_id=1, source_target_pairs={{0,2},{1,3},{2,0},{3,1},{4,5},{5,4},{6,7},{7,6},{8,10},{9,11},{10,... | collective-permute-start | bytes 196616 | tf_op jit(solution)/shard_map/ppermute | solution.py:355
  37.1 1.3 %collective-permute-done.9.refs_1_ = bf16[256,128]{1,0:T(8,128)(2,1)S(1)} collective-permute-done((bf16[256,128]{1,0:T(8,128)(2,1)S(1)}, bf16[256,128]{1,0:T(8,128)(2,1)S(1)}, u32[]{:S(2)}, u32[]{:S(2)}) %collective-permute-start.9) | collective-permute-done | bytes 65568 | tf_op jit(solution)/shard_map/ppermute | solution.py:355
  38.4 2.5 %collective-permute-done.11.refs_3_ = bf16[256,128]{1,0:T(8,128)(2,1)S(1)} collective-permute-done((bf16[256,128]{1,0:T(8,128)(2,1)S(1)}, bf16[256,128]{1,0:T(8,128)(2,1)S(1)}, u32[]{:S(2)}, u32[]{:S(2)}) %collective-permute-start.11) | collective-permute-done | bytes 65568 | tf_op jit(solution)/shard_map/ppermute | solution.py:355
  40.9 1.6 %collective-permute-start.17 = (bf16[512,128]{1,0:T(8,128)(2,1)S(1)}, bf16[512,128]{1,0:T(8,128)(2,1)S(1)}, u32[]{:S(2)}, u32[]{:S(2)}) collective-permute-start(bf16[512,128]{1,0:T(8,128)(2,1)S(1)} %shard_map.122.refs_0_), channel_id=1, source_target_pairs={{0,24},{4,28},{8,16},{12,20},{16,8},{20,12},{24,0},{28,4},{1,25},{... | collective-permute-start | bytes 393224 | tf_op jit(solution)/shard_map/ppermute | solution.py:341
  42.5 1.5 %collective-permute-start.15 = (bf16[512,128]{1,0:T(8,128)(2,1)S(1)}, bf16[512,128]{1,0:T(8,128)(2,1)S(1)}, u32[]{:S(2)}, u32[]{:S(2)}) collective-permute-start(bf16[512,128]{1,0:T(8,128)(2,1)S(1)} %shard_map.122.refs_0_), channel_id=1, source_target_pairs={{0,16},{4,20},{8,24},{12,28},{16,0},{20,4},{24,8},{28,12},{1,17},{... | collective-permute-start | bytes 393224 | tf_op jit(solution)/shard_map/ppermute | solution.py:341
  44.0 0.5 collective-permute-start.13
  44.5 2.5 %collective-permute-done.17.refs_6_ = bf16[512,128]{1,0:T(8,128)(2,1)S(1)} collective-permute-done((bf16[512,128]{1,0:T(8,128)(2,1)S(1)}, bf16[512,128]{1,0:T(8,128)(2,1)S(1)}, u32[]{:S(2)}, u32[]{:S(2)}) %collective-permute-start.17) | collective-permute-done | bytes 131104 | tf_op jit(solution)/shard_map/ppermute | solution.py:341
  46.9 1.3 %collective-permute-done.15.refs_4_ = bf16[512,128]{1,0:T(8,128)(2,1)S(1)} collective-permute-done((bf16[512,128]{1,0:T(8,128)(2,1)S(1)}, bf16[512,128]{1,0:T(8,128)(2,1)S(1)}, u32[]{:S(2)}, u32[]{:S(2)}) %collective-permute-start.15) | collective-permute-done | bytes 131104 | tf_op jit(solution)/shard_map/ppermute | solution.py:341
  48.3 0.7 %collective-permute-done.13.refs_2_ = bf16[512,128]{1,0:T(8,128)(2,1)S(1)} collective-permute-done((bf16[512,128]{1,0:T(8,128)(2,1)S(1)}, bf16[512,128]{1,0:T(8,128)(2,1)S(1)}, u32[]{:S(2)}, u32[]{:S(2)}) %collective-permute-start.13) | collective-permute-done | bytes 131104 | tf_op jit(solution)/shard_map/ppermute | solution.py:341
  49.0 0.6 %collective-permute-done.16.refs_5_ = bf16[512,128]{1,0:T(8,128)(2,1)S(1)} collective-permute-done((bf16[512,128]{1,0:T(8,128)(2,1)S(1)}, bf16[512,128]{1,0:T(8,128)(2,1)S(1)}, u32[]{:S(2)}, u32[]{:S(2)}) %collective-permute-start.16) | collective-permute-done | bytes 131104 | tf_op jit(solution)/shard_map/ppermute | solution.py:341
  49.6 0.7 %collective-permute-done.14.refs_3_ = bf16[512,128]{1,0:T(8,128)(2,1)S(1)} collective-permute-done((bf16[512,128]{1,0:T(8,128)(2,1)S(1)}, bf16[512,128]{1,0:T(8,128)(2,1)S(1)}, u32[]{:S(2)}, u32[]{:S(2)}) %collective-permute-start.14) | collective-permute-done | bytes 131104 | tf_op jit(solution)/shard_map/ppermute | solution.py:341
  50.3 1.9 %shard_map.123 = (f32[27,96,96]{2,1,0:T(8,128)}, f32[27,96,96]{2,1,0:T(8,128)}) custom-call(bf16[512,128]{1,0:T(8,128)(2,1)S(1)} %shard_map.122.refs_0_, bf16[512,128]{1,0:T(8,128)(2,1)S(1)} %collective-permute-done.12.refs_1_, bf16[512,128]{1,0:T(8,128)(2,1)S(1)} %collective-permute-done.13.refs_2_, bf16[512,128]{1,0:T(8,128)(2,1)S(1)} %collective-permute-done.14.refs_3_, ...), custom_call_target="tpu_custom_call" | custom-call | tf_op jit(solution)/shard_map/pallas_call | solution.py:22
  (32 shorter events, 0.8 us)
Async XLA Ops:
  0.6 5.0 %copy-start.4 = (bf16[27,96,96]{2,1,0:T(8,128)(2,1)S(1)}, bf16[27,96,96]{2,1,0:T(8,128)(2,1)}, u32[]{:S(2)}) copy-start(bf16[27,96,96]{2,1,0:T(8,128)(2,1)} %weight_ref.2) | copy-start | bytes 1492996
  0.6 5.0 %copy-start.6 = (s32[1,1,27,256]{3,1,2,0:T(1,128)S(1)}, s32[1,1,27,256]{3,1,2,0:T(1,128)}, u32[]{:S(2)}) copy-start(s32[1,1,27,256]{3,1,2,0:T(1,128)} %param.14) | copy-start | bytes 82948
  4.4 4.3 %collective-permute-start = (bf16[192,128]{1,0:T(8,128)(2,1)S(1)}, bf16[192,128]{1,0:T(8,128)(2,1)S(1)}, u32[]{:S(2)}, u32[]{:S(2)}) collective-permute-start(bf16[192,128]{1,0:T(8,128)(2,1)S(1)} %get-tuple-element.44), channel_id=1, source_target_pairs={{0,4},{4,0},{8,12},{12,8},{16,20},{20,16},{24,28},{28,24},{1,5},{5... | collective-permute-start | bytes 147464 | tf_op jit(solution)/shard_map/ppermute | solution.py:341
  5.0 3.8 %collective-permute-start.1 = (bf16[192,128]{1,0:T(8,128)(2,1)S(1)}, bf16[192,128]{1,0:T(8,128)(2,1)S(1)}, u32[]{:S(2)}, u32[]{:S(2)}) collective-permute-start(bf16[192,128]{1,0:T(8,128)(2,1)S(1)} %get-tuple-element.45), channel_id=1, source_target_pairs={{4,8},{8,4},{12,16},{16,12},{20,24},{24,20},{5,9},{9,5},{13,17},{1... | collective-permute-start | bytes 147464 | tf_op jit(solution)/shard_map/ppermute | solution.py:346
  5.7 2.1 %copy-start.1 = (bf16[1,1,512,96]{2,3,1,0:T(8,128)(2,1)S(1)}, bf16[1,1,512,96]{2,3,1,0:T(8,128)(2,1)}, u32[]{:S(2)}) copy-start(bf16[1,1,512,96]{2,3,1,0:T(8,128)(2,1)} %param.10) | copy-start | bytes 294916
  7.7 1.0 %copy-start.2 = (s32[1,1,64]{2,1,0:T(1,128)S(1)}, s32[1,1,64]{2,1,0:T(1,128)}, u32[]{:S(2)}) copy-start(s32[1,1,64]{2,1,0:T(1,128)} %param.17) | copy-start | bytes 772
  7.7 1.0 %copy-start.3 = (s32[1,1,64]{2,1,0:T(1,128)S(1)}, s32[1,1,64]{2,1,0:T(1,128)}, u32[]{:S(2)}) copy-start(s32[1,1,64]{2,1,0:T(1,128)} %param.16) | copy-start | bytes 772
  7.7 1.0 %copy-start.5 = (bf16[1,1,512,96]{2,3,1,0:T(8,128)(2,1)S(1)}, bf16[1,1,512,96]{2,3,1,0:T(8,128)(2,1)}, u32[]{:S(2)}) copy-start(bf16[1,1,512,96]{2,3,1,0:T(8,128)(2,1)} %param.9) | copy-start | bytes 294916
  8.8 8.0 %copy-start = (bf16[27,96,96]{2,1,0:T(8,128)(2,1)S(1)}, bf16[27,96,96]{2,1,0:T(8,128)(2,1)}, u32[]{:S(2)}) copy-start(bf16[27,96,96]{2,1,0:T(8,128)(2,1)} %weight_ref.3) | copy-start | bytes 1492996
  12.8 5.5 %collective-permute-start.2 = (bf16[2048,128]{1,0:T(8,128)(2,1)S(1)}, bf16[2048,128]{1,0:T(8,128)(2,1)S(1)}, u32[]{:S(2)}, u32[]{:S(2)}) collective-permute-start(bf16[2048,128]{1,0:T(8,128)(2,1)S(1)} %get-tuple-element.53), channel_id=1, source_target_pairs={{0,4},{4,0},{8,12},{12,8},{16,20},{20,16},{24,28},{28,24},{1,5},{5... | collective-permute-start | bytes 1572872 | tf_op jit(solution)/shard_map/ppermute | solution.py:341
  18.4 6.0 %collective-permute-start.5 = (bf16[512,128]{1,0:T(8,128)(2,1)S(1)}, bf16[512,128]{1,0:T(8,128)(2,1)S(1)}, u32[]{:S(2)}, u32[]{:S(2)}) collective-permute-start(bf16[512,128]{1,0:T(8,128)(2,1)S(1)} %get-tuple-element.61), channel_id=1, source_target_pairs={{0,8},{4,12},{8,0},{12,4},{16,24},{20,28},{24,16},{28,20},{1,9},{5... | collective-permute-start | bytes 393224 | tf_op jit(solution)/shard_map/ppermute | solution.py:341
  20.2 8.3 %collective-permute-start.6 = (bf16[512,128]{1,0:T(8,128)(2,1)S(1)}, bf16[512,128]{1,0:T(8,128)(2,1)S(1)}, u32[]{:S(2)}, u32[]{:S(2)}) collective-permute-start(bf16[512,128]{1,0:T(8,128)(2,1)S(1)} %get-tuple-element.62), channel_id=1, source_target_pairs={{0,16},{4,20},{8,24},{12,28},{16,0},{20,4},{24,8},{28,12},{1,17},{... | collective-permute-start | bytes 393224 | tf_op jit(solution)/shard_map/ppermute | solution.py:341
  20.9 7.6 %collective-permute-start.7 = (bf16[512,128]{1,0:T(8,128)(2,1)S(1)}, bf16[512,128]{1,0:T(8,128)(2,1)S(1)}, u32[]{:S(2)}, u32[]{:S(2)}) collective-permute-start(bf16[512,128]{1,0:T(8,128)(2,1)S(1)} %get-tuple-element.63), channel_id=1, source_target_pairs={{0,24},{4,28},{8,16},{12,20},{16,8},{20,12},{24,0},{28,4},{1,25},{... | collective-permute-start | bytes 393224 | tf_op jit(solution)/shard_map/ppermute | solution.py:341
  22.0 1.2 %collective-permute-start.3 = (bf16[96,128]{1,0:T(8,128)(2,1)S(1)}, bf16[96,128]{1,0:T(8,128)(2,1)S(1)}, u32[]{:S(2)}, u32[]{:S(2)}) collective-permute-start(bf16[96,128]{1,0:T(8,128)(2,1)S(1)} %get-tuple-element.58), channel_id=1, source_target_pairs={{0,4},{4,0},{8,12},{12,8},{16,20},{20,16},{24,28},{28,24},{1,5},{5... | collective-permute-start | bytes 73736 | tf_op jit(solution)/shard_map/ppermute | solution.py:341
  22.0 1.2 %collective-permute-start.4 = (bf16[96,128]{1,0:T(8,128)(2,1)S(1)}, bf16[96,128]{1,0:T(8,128)(2,1)S(1)}, u32[]{:S(2)}, u32[]{:S(2)}) collective-permute-start(bf16[96,128]{1,0:T(8,128)(2,1)S(1)} %get-tuple-element.59), channel_id=1, source_target_pairs={{4,8},{8,4},{12,16},{16,12},{20,24},{24,20},{5,9},{9,5},{13,17},{1... | collective-permute-start | bytes 73736 | tf_op jit(solution)/shard_map/ppermute | solution.py:346
  28.5 4.5 %collective-permute-start.8 = (bf16[256,128]{1,0:T(8,128)(2,1)S(1)}, bf16[256,128]{1,0:T(8,128)(2,1)S(1)}, u32[]{:S(2)}, u32[]{:S(2)}) collective-permute-start(bf16[256,128]{1,0:T(8,128)(2,1)S(1)} %get-tuple-element.75.refs_0_), channel_id=1, source_target_pairs={{0,1},{1,0},{2,3},{3,2},{4,6},{5,7},{6,4},{7,5},{8,9},{9,8},{10,11... | collective-permute-start | bytes 196616 | tf_op jit(solution)/shard_map/ppermute | solution.py:355
  30.1 5.4 %collective-permute-start.10 = (bf16[256,128]{1,0:T(8,128)(2,1)S(1)}, bf16[256,128]{1,0:T(8,128)(2,1)S(1)}, u32[]{:S(2)}, u32[]{:S(2)}) collective-permute-start(bf16[256,128]{1,0:T(8,128)(2,1)S(1)} %get-tuple-element.76.refs_0_), channel_id=1, source_target_pairs={{0,1},{1,0},{2,3},{3,2},{4,6},{5,7},{6,4},{7,5},{8,9},{9,8},{10,11... | collective-permute-start | bytes 196616 | tf_op jit(solution)/shard_map/ppermute | solution.py:355
  33.0 5.3 %collective-permute-start.9 = (bf16[256,128]{1,0:T(8,128)(2,1)S(1)}, bf16[256,128]{1,0:T(8,128)(2,1)S(1)}, u32[]{:S(2)}, u32[]{:S(2)}) collective-permute-start(bf16[256,128]{1,0:T(8,128)(2,1)S(1)} %shard_map.120.refs_0_), channel_id=1, source_target_pairs={{0,2},{1,3},{2,0},{3,1},{4,5},{5,4},{6,7},{7,6},{8,10},{9,11},{10,... | collective-permute-start | bytes 196616 | tf_op jit(solution)/shard_map/ppermute | solution.py:355
  35.5 5.3 %collective-permute-start.11 = (bf16[256,128]{1,0:T(8,128)(2,1)S(1)}, bf16[256,128]{1,0:T(8,128)(2,1)S(1)}, u32[]{:S(2)}, u32[]{:S(2)}) collective-permute-start(bf16[256,128]{1,0:T(8,128)(2,1)S(1)} %shard_map.121.refs_2_), channel_id=1, source_target_pairs={{0,2},{1,3},{2,0},{3,1},{4,5},{5,4},{6,7},{7,6},{8,10},{9,11},{10,... | collective-permute-start | bytes 196616 | tf_op jit(solution)/shard_map/ppermute | solution.py:355
  40.9 6.0 %collective-permute-start.17 = (bf16[512,128]{1,0:T(8,128)(2,1)S(1)}, bf16[512,128]{1,0:T(8,128)(2,1)S(1)}, u32[]{:S(2)}, u32[]{:S(2)}) collective-permute-start(bf16[512,128]{1,0:T(8,128)(2,1)S(1)} %shard_map.122.refs_0_), channel_id=1, source_target_pairs={{0,24},{4,28},{8,16},{12,20},{16,8},{20,12},{24,0},{28,4},{1,25},{... | collective-permute-start | bytes 393224 | tf_op jit(solution)/shard_map/ppermute | solution.py:341
  42.5 5.8 %collective-permute-start.15 = (bf16[512,128]{1,0:T(8,128)(2,1)S(1)}, bf16[512,128]{1,0:T(8,128)(2,1)S(1)}, u32[]{:S(2)}, u32[]{:S(2)}) collective-permute-start(bf16[512,128]{1,0:T(8,128)(2,1)S(1)} %shard_map.122.refs_0_), channel_id=1, source_target_pairs={{0,16},{4,20},{8,24},{12,28},{16,0},{20,4},{24,8},{28,12},{1,17},{... | collective-permute-start | bytes 393224 | tf_op jit(solution)/shard_map/ppermute | solution.py:341
  44.0 5.0 %collective-permute-start.13 = (bf16[512,128]{1,0:T(8,128)(2,1)S(1)}, bf16[512,128]{1,0:T(8,128)(2,1)S(1)}, u32[]{:S(2)}, u32[]{:S(2)}) collective-permute-start(bf16[512,128]{1,0:T(8,128)(2,1)S(1)} %shard_map.122.refs_0_), channel_id=1, source_target_pairs={{0,8},{4,12},{8,0},{12,4},{16,24},{20,28},{24,16},{28,20},{1,9},{5... | collective-permute-start | bytes 393224 | tf_op jit(solution)/shard_map/ppermute | solution.py:341
  44.5 4.5 %collective-permute-start.12 = (bf16[512,128]{1,0:T(8,128)(2,1)S(1)}, bf16[512,128]{1,0:T(8,128)(2,1)S(1)}, u32[]{:S(2)}, u32[]{:S(2)}) collective-permute-start(bf16[512,128]{1,0:T(8,128)(2,1)S(1)} %shard_map.122.refs_0_), channel_id=1, source_target_pairs={{0,4},{4,0},{8,12},{12,8},{16,20},{20,16},{24,28},{28,24},{1,5},{5... | collective-permute-start | bytes 393224 | tf_op jit(solution)/shard_map/ppermute | solution.py:341
  46.9 2.1 %collective-permute-start.18 = (bf16[512,128]{1,0:T(8,128)(2,1)S(1)}, bf16[512,128]{1,0:T(8,128)(2,1)S(1)}, u32[]{:S(2)}, u32[]{:S(2)}) collective-permute-start(bf16[512,128]{1,0:T(8,128)(2,1)S(1)} %collective-permute-done.17.refs_6_), channel_id=1, source_target_pairs={{0,4},{4,0},{8,12},{12,8},{16,20},{20,16},{24,28},{28,24},{1,5},{5... | collective-permute-start | bytes 393224 | tf_op jit(solution)/shard_map/ppermute | solution.py:341
  48.3 1.3 %collective-permute-start.16 = (bf16[512,128]{1,0:T(8,128)(2,1)S(1)}, bf16[512,128]{1,0:T(8,128)(2,1)S(1)}, u32[]{:S(2)}, u32[]{:S(2)}) collective-permute-start(bf16[512,128]{1,0:T(8,128)(2,1)S(1)} %collective-permute-done.15.refs_4_), channel_id=1, source_target_pairs={{0,4},{4,0},{8,12},{12,8},{16,20},{20,16},{24,28},{28,24},{1,5},{5... | collective-permute-start | bytes 393224 | tf_op jit(solution)/shard_map/ppermute | solution.py:341
  49.0 1.3 %collective-permute-start.14 = (bf16[512,128]{1,0:T(8,128)(2,1)S(1)}, bf16[512,128]{1,0:T(8,128)(2,1)S(1)}, u32[]{:S(2)}, u32[]{:S(2)}) collective-permute-start(bf16[512,128]{1,0:T(8,128)(2,1)S(1)} %collective-permute-done.13.refs_2_), channel_id=1, source_target_pairs={{0,4},{4,0},{8,12},{12,8},{16,20},{20,16},{24,28},{28,24},{1,5},{5... | collective-permute-start | bytes 393224 | tf_op jit(solution)/shard_map/ppermute | solution.py:341

commit v8 on v7

--- a/solution.py
+++ b/solution.py
@@ -12,17 +12,17 @@
 HBM = pl.BlockSpec(memory_space=pltpu.HBM)
 LANES = 128
 BLOCK = 256
-CHUNK = 9
 WHOLE = 62 << 20
 NT = (((1,), (1,)), ((), ()))
 
 
-def call(body, outs, args, scratch=(), flops=0, moved=0, args_in=VMEM, outs_in=VMEM, room=40 << 20):
+def call(body, outs, args, scratch=(), flops=0, moved=0, args_in=VMEM, outs_in=VMEM, room=40 << 20, aliases=()):
     single = not isinstance(outs, (list, tuple))
     return pl.pallas_call(
         body,
         out_shape=outs if single else tuple(outs),
-        in_specs=[args_in] * len(args),
+        in_specs=list(args_in) if isinstance(args_in, (list, tuple)) else [args_in] * len(args),
+        input_output_aliases=dict(aliases),
         out_specs=outs_in if single or isinstance(outs_in, tuple) else (outs_in,) * len(outs),
         scratch_shapes=scratch,
         compiler_params=pltpu.CompilerParams(vmem_limit_bytes=room),
@@ -214,6 +214,10 @@
     sum_ref[tiles * chans :, :] = jnp.zeros((sum_ref.shape[0] - tiles * chans, LANES), F32)
 
 
+def place_of(device, slots):
+    return jnp.bitwise_and(device, 1) * slots + lax.shift_right_logical(device, 1)
+
+
 def cut(sum_ref, layer, keep_ref, send_ref):
     me = lax.axis_index("space")
     slots = lax.axis_size("space") // 2
@@ -221,7 +225,7 @@
     for slot in range(slots):
         there = pl.ds((layer * slots + slot) * rows, rows)
         for out_ref, bit in ((keep_ref, 0), (send_ref, 1)):
-            piece = jnp.bitwise_xor(me, 2 * slot + bit)
+            piece = place_of(jnp.bitwise_xor(me, 2 * slot + bit), slots)
             block = sum_ref[pl.ds(pl.multiple_of(piece * rows, rows), rows), :]
             out_ref[there, :] = block.astype(out_ref.dtype)
 
@@ -307,34 +311,53 @@
         total_ref[i // 2 * rows : (i // 2 + 1) * rows] = (terms[i][...].astype(F32) + terms[i + 1][...].astype(F32)).astype(BF16)
 
 
-def unpack_body(scale, layers, *refs):
+def tiles_of(k, chans):
+    return k * chans // LANES, -(-(k + 1) * chans // LANES)
+
+
+def unpack_body(scale, layers, early, *refs):
     *refs, all_ref, sems = refs
     piece_refs, outs, locals_ = refs[: -2 * layers], refs[-2 * layers : -layers], refs[-layers:]
+    if not early:
+        piece_refs = piece_refs[:-layers]
     me = lax.axis_index("space")
+    slots = lax.axis_size("space") // 2
+    step = 2 * slots // len(piece_refs)
     rows = piece_refs[0].shape[0] // layers
+    half = rows * slots
     count, chans = locals_[0].shape[0], locals_[0].shape[1]
     lane = lax.broadcasted_iota(I32, (chans, LANES), 1)
-    copies = []
-    for layer in range(layers):
-        for slot, piece_ref in enumerate(piece_refs):
-            piece = jnp.bitwise_xor(me, slot)
-            block = piece_ref[layer * rows : (layer + 1) * rows].astype(F32)
-            all_ref[pl.ds(pl.multiple_of(piece * rows, rows), rows), :] = block
-        for first in range(0, count, CHUNK):
-            chunk = pl.ds(first, min(CHUNK, count - first))
-            for k in range(first, first + chunk.size):
-                tile, shift = divmod(k * chans, LANES)
-                block = all_ref[tile * chans : (tile + 1) * chans, :]
-                if shift:
-                    block = pltpu.roll(block, LANES - shift, 1)
-                if shift + chans > LANES:
-                    after = pltpu.roll(all_ref[(tile + 1) * chans : (tile + 2) * chans, :], LANES - shift, 1)
-                    block = jnp.where(lane < LANES - shift, block, after)
-                locals_[layer][k] = block[:, :chans] * scale
-            copies.append(pltpu.make_async_copy(locals_[layer].at[chunk], outs[layer].at[chunk], sems.at[len(copies)]))
-            copies[-1].start()
-    for copy in copies:
-        copy.wait()
+
+    def unpack(core):
+        spans = [tiles_of(k, chans) for k in range(count)]
+        inside = [last * chans <= half if core == 0 else first * chans >= half for first, last in spans]
+        wanted = [k for k in range(count) if inside[k] == early]
+        assert wanted == list(range(wanted[0], wanted[-1] + 1))
+        middle = (wanted[0] + wanted[-1] + 1) // 2
+        copies = []
+        for layer in range(layers):
+            for i, piece_ref in enumerate(piece_refs):
+                piece = place_of(jnp.bitwise_xor(me, step * i), slots)
+                block = piece_ref[layer * rows : (layer + 1) * rows].astype(F32)
+                all_ref[pl.ds(pl.multiple_of(piece * rows, rows), rows), :] = block
+            for first, last in ((wanted[0], middle), (middle, wanted[-1] + 1)):
+                for k in range(first, last):
+                    tile, shift = divmod(k * chans, LANES)
+                    block = all_ref[tile * chans : (tile + 1) * chans, :]
+                    if shift:
+                        block = pltpu.roll(block, LANES - shift, 1)
+                    if shift + chans > LANES:
+                        after = pltpu.roll(all_ref[(tile + 1) * chans : (tile + 2) * chans, :], LANES - shift, 1)
+                        block = jnp.where(lane < LANES - shift, block, after)
+                    locals_[layer][k] = block[:, :chans] * scale
+                chunk = pl.ds(first, last - first)
+                copies.append(pltpu.make_async_copy(locals_[layer].at[chunk], outs[layer].at[chunk], sems.at[len(copies)]))
+                copies[-1].start()
+        for copy in copies:
+            copy.wait()
+
+    for core in range(2):
+        pl.when(jnp.bitwise_and(me, 1) == core)(functools.partial(unpack, core))
 
 
 def swap(block, axis, bit):
@@ -385,13 +408,20 @@
     for slot in range(slots):
         piece = swap(total, "space", 2 * slot) if slot else total
         pieces += [piece, swap(piece, "space", 1)]
-    return state, call(
-        functools.partial(unpack_body, scale, layers),
-        [shape(weight_shape, F32)] * layers,
-        pieces,
-        scratch=[pltpu.VMEM(weight_shape, F32)] * layers + [pltpu.VMEM((packed, LANES), F32), pltpu.SemaphoreType.DMA((layers * -(-weight_shape[0] // CHUNK),))],
-        outs_in=HBM,
-    )
+    outs = ()
+    for early, given in ((True, pieces[::2]), (False, pieces)):
+        outs = call(
+            functools.partial(unpack_body, scale, layers, early),
+            [shape(weight_shape, F32)] * layers,
+            [*given, *outs],
+            scratch=[pltpu.VMEM(weight_shape, F32)] * layers
+            + [pltpu.VMEM((packed, LANES), F32), pltpu.SemaphoreType.DMA((2 * layers,))],
+            args_in=[VMEM] * len(given) + [HBM] * len(outs),
+            outs_in=HBM,
+            aliases=[(len(given) + i, i) for i in range(len(outs))],
+            moved=4 << 20,
+        )
+    return state, outs
 
 
 def shards(act_zero, pre_act, cot_out, weight_one, weight_two, in_map, out_map, send_lo, send_hi):

time: 52.4 us -> 52 us (level)
  waiting for transfers between devices: 17.3 us -> 16 us
  Pallas kernels: 15 us -> 15.8 us
    ppermute x13, waiting for transfers between devices: 12.1 us -> 10.8 us  [swap(): lax.ppermute(block, axis, [(i, i ^ bit) for i in range(lax.axis_size(axis...]
    pallas_call x12 -> x13, Pallas kernels: 15 us -> 15.8 us  [call(): pl.pallas_call(body, out_shape=outs if single else tuple(outs), in_specs=...]
  transfers between devices with their start and end apart: 19 -> 19, of which waited for: 12 -> 10; matrix products, arithmetic and copies ran while one was open for 0% -> 0% of each run, Pallas kernels for 10% -> 12%
where the time goes in v8:
time: 52 us; the launch traced here: 51.8 us
  starting transfers between devices  19.1 us (37%)
  waiting for transfers between devices  16 us (31%)
  Pallas kernels  15.8 us (30%)
  between operations  0.86 us (2%)
    pallas_call x13, Pallas kernels, call(): pl.pallas_call(body, out_shape=outs if single else tuple(outs), in_specs=...  15.8 us
    ppermute x13, starting transfers between devices, swap(): lax.ppermute(block, axis, [(i, i ^ bit) for i in range(lax.axis_size(axis...  11.6 us
    ppermute x13, waiting for transfers between devices, swap(): lax.ppermute(block, axis, [(i, i ^ bit) for i in range(lax.axis_size(axis...  10.8 us
    ppermute x4, starting transfers between devices, swap_scans(): return lax.ppermute(block, ('space', 'scan'), pairs)  6.15 us
    ppermute x4, waiting for transfers between devices, swap_scans(): return lax.ppermute(block, ('space', 'scan'), pairs)  5.23 us
    ppermute x2, starting transfers between devices, swap_neighbours(): lax.ppermute(far, 'space', [(i, i + 1 if i % 2 else i - 1) for i in inner])  1.3 us
  transfers between devices with their start and end apart: 19, of which 10 were waited for; matrix products, arithmetic and copies ran while one was open for 0% of the time, Pallas kernels for 12%

profile of v8, /device:TPU:0, one launch (start us, length us, event | category | flops | bytes accessed | tf_op | source)
XLA Modules:
  0.0 51.8 jit_solution(15005765012072921284)
XLA Ops:
  0.7 3.8 %shard_map.112 = (bf16[3024,256]{1,0:T(8,128)(2,1)S(1)}, bf16[2688,128]{1,0:T(8,128)(2,1)S(1)}, f32[32,128]{1,0:T(8,128)S(1)}, bf16[192,128]{1,0:T(8,128)(2,1)S(1)}, bf16[192,128]{1,0:T(8,128)(2,1)S(1)}) custom-call(s32[27,1,256]{2,1,0:T(1,128)} %bitcast.31, bf16[96,512]{1,0:T(8,128)(2,1)} %bitcast.30, s32[27,1,256]{2,1,0:T(1,128)} %bitcast.27, ...), custom_call_target="tpu_custom_call" | custom-call | flops 679477248 | bytes 4194304 | tf_op jit(solution)/shard_map/pallas_call | solution.py:21
  4.4 0.5 %collective-permute-start = (bf16[192,128]{1,0:T(8,128)(2,1)S(1)}, bf16[192,128]{1,0:T(8,128)(2,1)S(1)}, u32[]{:S(2)}, u32[]{:S(2)}) collective-permute-start(bf16[192,128]{1,0:T(8,128)(2,1)S(1)} %get-tuple-element.46), channel_id=1, source_target_pairs={{0,4},{4,0},{8,12},{12,8},{16,20},{20,16},{24,28},{28,24},{1,5},{5... | collective-permute-start | bytes 147464 | tf_op jit(solution)/shard_map/ppermute | solution.py:364
  5.0 0.7 %collective-permute-start.1 = (bf16[192,128]{1,0:T(8,128)(2,1)S(1)}, bf16[192,128]{1,0:T(8,128)(2,1)S(1)}, u32[]{:S(2)}, u32[]{:S(2)}) collective-permute-start(bf16[192,128]{1,0:T(8,128)(2,1)S(1)} %get-tuple-element.47), channel_id=1, source_target_pairs={{4,8},{8,4},{12,16},{16,12},{20,24},{24,20},{5,9},{9,5},{13,17},{1... | collective-permute-start | bytes 147464 | tf_op jit(solution)/shard_map/ppermute | solution.py:369
  5.7 2.0 %shard_map.113 = (bf16[2688,512]{1,0:T(8,128)(2,1)S(1)}, f32[128,512]{1,0:T(8,128)S(1)}) custom-call(s32[27,1,256]{2,1,0:T(1,128)S(1)} %bitcast.28, bf16[3024,256]{1,0:T(8,128)(2,1)S(1)} %get-tuple-element.43.c_ref, bf16[27,96,96]{2,1,0:T(8,128)(2,1)S(1)} %copy-done.4), custom_call_target="tpu_custom_call" | custom-call | flops 849346560 | bytes 8388608 | tf_op jit(solution)/shard_map/pallas_call | solution.py:21
  7.8 1.0 %shard_map.114.sum_two_ref = f32[2048,128]{1,0:T(8,128)S(1)} custom-call(bf16[96,512]{1,0:T(8,128)(2,1)S(1)} %bitcast.17, bf16[2688,512]{1,0:T(8,128)(2,1)S(1)} %get-tuple-element.49.t_ref), custom_call_target="tpu_custom_call" | custom-call | flops 318504960 | bytes 6291456 | tf_op jit(solution)/shard_map/pallas_call | solution.py:21
  8.8 4.1 %shard_map.115 = (bf16[2688,640]{1,0:T(8,128)(2,1)S(1)}, f32[2048,128]{1,0:T(8,128)S(1)}, bf16[2048,128]{1,0:T(8,128)(2,1)S(1)}) custom-call(f32[128,512]{1,0:T(8,128)S(1)} %get-tuple-element.44.own_ref, f32[32,128]{1,0:T(8,128)S(1)} %get-tuple-element.45.inv_ref, bf16[192,128]{1,0:T(8,128)(2,1)S(1)} %collective-permute-done.near_ref, ...), custom_call_target="tpu_custom_call" | custom-call | flops 2017198080 | bytes 8388608 | tf_op jit(solution)/shard_map/pallas_call | solution.py:21
  12.8 3.9 %collective-permute-start.2 = (bf16[2048,128]{1,0:T(8,128)(2,1)S(1)}, bf16[2048,128]{1,0:T(8,128)(2,1)S(1)}, u32[]{:S(2)}, u32[]{:S(2)}) collective-permute-start(bf16[2048,128]{1,0:T(8,128)(2,1)S(1)} %get-tuple-element.55), channel_id=1, source_target_pairs={{0,4},{4,0},{8,12},{12,8},{16,20},{20,16},{24,28},{28,24},{1,5},{5... | collective-permute-start | bytes 1572872 | tf_op jit(solution)/shard_map/ppermute | solution.py:364
  16.8 1.1 %shard_map.116 = (f32[96,512]{1,0:T(8,128)S(1)}, bf16[96,128]{1,0:T(8,128)(2,1)S(1)}, bf16[96,128]{1,0:T(8,128)(2,1)S(1)}) custom-call(bf16[27,96,96]{2,1,0:T(8,128)(2,1)S(1)} %copy-done, bf16[2688,640]{1,0:T(8,128)(2,1)S(1)} %get-tuple-element.51.t_ref), custom_call_target="tpu_custom_call" | custom-call | flops 318504960 | bytes 6291456 | tf_op jit(solution)/shard_map/pallas_call | solution.py:21
  17.9 0.4 collective-permute-done.2.got_ref
  18.4 1.7 %collective-permute-start.5 = (bf16[512,128]{1,0:T(8,128)(2,1)S(1)}, bf16[512,128]{1,0:T(8,128)(2,1)S(1)}, u32[]{:S(2)}, u32[]{:S(2)}) collective-permute-start(bf16[512,128]{1,0:T(8,128)(2,1)S(1)} %get-tuple-element.63), channel_id=1, source_target_pairs={{0,8},{4,12},{8,0},{12,4},{16,24},{20,28},{24,16},{28,20},{1,9},{5... | collective-permute-start | bytes 393224 | tf_op jit(solution)/shard_map/ppermute | solution.py:364
  20.2 0.7 %collective-permute-start.6 = (bf16[512,128]{1,0:T(8,128)(2,1)S(1)}, bf16[512,128]{1,0:T(8,128)(2,1)S(1)}, u32[]{:S(2)}, u32[]{:S(2)}) collective-permute-start(bf16[512,128]{1,0:T(8,128)(2,1)S(1)} %get-tuple-element.64), channel_id=1, source_target_pairs={{0,16},{4,20},{8,24},{12,28},{16,0},{20,4},{24,8},{28,12},{1,17},{... | collective-permute-start | bytes 393224 | tf_op jit(solution)/shard_map/ppermute | solution.py:364
  20.9 1.1 %collective-permute-start.7 = (bf16[512,128]{1,0:T(8,128)(2,1)S(1)}, bf16[512,128]{1,0:T(8,128)(2,1)S(1)}, u32[]{:S(2)}, u32[]{:S(2)}) collective-permute-start(bf16[512,128]{1,0:T(8,128)(2,1)S(1)} %get-tuple-element.65), channel_id=1, source_target_pairs={{0,24},{4,28},{8,16},{12,20},{16,8},{20,12},{24,0},{28,4},{1,25},{... | collective-permute-start | bytes 393224 | tf_op jit(solution)/shard_map/ppermute | solution.py:364
  22.0 0.7 %collective-permute-start.4 = (bf16[96,128]{1,0:T(8,128)(2,1)S(1)}, bf16[96,128]{1,0:T(8,128)(2,1)S(1)}, u32[]{:S(2)}, u32[]{:S(2)}) collective-permute-start(bf16[96,128]{1,0:T(8,128)(2,1)S(1)} %get-tuple-element.61), channel_id=1, source_target_pairs={{4,8},{8,4},{12,16},{16,12},{20,24},{24,20},{5,9},{9,5},{13,17},{1... | collective-permute-start | bytes 73736 | tf_op jit(solution)/shard_map/ppermute | solution.py:369
  22.7 0.5 %collective-permute-done.3.near_ref = bf16[96,128]{1,0:T(8,128)(2,1)S(1)} collective-permute-done((bf16[96,128]{1,0:T(8,128)(2,1)S(1)}, bf16[96,128]{1,0:T(8,128)(2,1)S(1)}, u32[]{:S(2)}, u32[]{:S(2)}) %collective-permute-start.3) | collective-permute-done | bytes 24608 | tf_op jit(solution)/shard_map/ppermute | solution.py:364
  23.2 1.3 %collective-permute-done.5.refs_0_ = bf16[512,128]{1,0:T(8,128)(2,1)S(1)} collective-permute-done((bf16[512,128]{1,0:T(8,128)(2,1)S(1)}, bf16[512,128]{1,0:T(8,128)(2,1)S(1)}, u32[]{:S(2)}, u32[]{:S(2)}) %collective-permute-start.5) | collective-permute-done | bytes 131104 | tf_op jit(solution)/shard_map/ppermute | solution.py:364
  24.5 4.0 %collective-permute-done.6.refs_1_ = bf16[512,128]{1,0:T(8,128)(2,1)S(1)} collective-permute-done((bf16[512,128]{1,0:T(8,128)(2,1)S(1)}, bf16[512,128]{1,0:T(8,128)(2,1)S(1)}, u32[]{:S(2)}, u32[]{:S(2)}) %collective-permute-start.6) | collective-permute-done | bytes 131104 | tf_op jit(solution)/shard_map/ppermute | solution.py:364
  28.5 1.6 %collective-permute-start.8 = (bf16[256,128]{1,0:T(8,128)(2,1)S(1)}, bf16[256,128]{1,0:T(8,128)(2,1)S(1)}, u32[]{:S(2)}, u32[]{:S(2)}) collective-permute-start(bf16[256,128]{1,0:T(8,128)(2,1)S(1)} %get-tuple-element.77.refs_0_), channel_id=1, source_target_pairs={{0,1},{1,0},{2,3},{3,2},{4,6},{5,7},{6,4},{7,5},{8,9},{9,8},{10,11... | collective-permute-start | bytes 196616 | tf_op jit(solution)/shard_map/ppermute | solution.py:378
  30.1 0.5 collective-permute-start.10
  30.6 0.9 %shard_map.119 = bf16[96,512]{1,0:T(8,128)(2,1)} custom-call(f32[96,512]{1,0:T(8,128)S(1)} %get-tuple-element.73.own_ref, bf16[96,128]{1,0:T(8,128)(2,1)S(1)} %collective-permute-done.3.near_ref, bf16[96,128]{1,0:T(8,128)(2,1)S(1)} %collective-permute-done.4.far_ref, s32[1,64]{1,0:T(1,128)S(1)} %bitcast.21, s32[1,64]{1,0:T(1,128)S(1)} %bitcast.24), custom_call_target="tpu_custom_call" | custom-call | tf_op jit(solution)/shard_map/pallas_call | solution.py:21
  31.6 1.4 %collective-permute-done.8.refs_1_ = bf16[256,128]{1,0:T(8,128)(2,1)S(1)} collective-permute-done((bf16[256,128]{1,0:T(8,128)(2,1)S(1)}, bf16[256,128]{1,0:T(8,128)(2,1)S(1)}, u32[]{:S(2)}, u32[]{:S(2)}) %collective-permute-start.8) | collective-permute-done | bytes 65568 | tf_op jit(solution)/shard_map/ppermute | solution.py:378
  33.0 2.5 %collective-permute-start.9 = (bf16[256,128]{1,0:T(8,128)(2,1)S(1)}, bf16[256,128]{1,0:T(8,128)(2,1)S(1)}, u32[]{:S(2)}, u32[]{:S(2)}) collective-permute-start(bf16[256,128]{1,0:T(8,128)(2,1)S(1)} %shard_map.120.refs_0_), channel_id=1, source_target_pairs={{0,2},{1,3},{2,0},{3,1},{4,5},{5,4},{6,7},{7,6},{8,10},{9,11},{10,... | collective-permute-start | bytes 196616 | tf_op jit(solution)/shard_map/ppermute | solution.py:378
  35.5 1.6 %collective-permute-start.11 = (bf16[256,128]{1,0:T(8,128)(2,1)S(1)}, bf16[256,128]{1,0:T(8,128)(2,1)S(1)}, u32[]{:S(2)}, u32[]{:S(2)}) collective-permute-start(bf16[256,128]{1,0:T(8,128)(2,1)S(1)} %shard_map.121.refs_2_), channel_id=1, source_target_pairs={{0,2},{1,3},{2,0},{3,1},{4,5},{5,4},{6,7},{7,6},{8,10},{9,11},{10,... | collective-permute-start | bytes 196616 | tf_op jit(solution)/shard_map/ppermute | solution.py:378
  37.1 1.3 %collective-permute-done.9.refs_1_ = bf16[256,128]{1,0:T(8,128)(2,1)S(1)} collective-permute-done((bf16[256,128]{1,0:T(8,128)(2,1)S(1)}, bf16[256,128]{1,0:T(8,128)(2,1)S(1)}, u32[]{:S(2)}, u32[]{:S(2)}) %collective-permute-start.9) | collective-permute-done | bytes 65568 | tf_op jit(solution)/shard_map/ppermute | solution.py:378
  38.4 2.5 %collective-permute-done.11.refs_3_ = bf16[256,128]{1,0:T(8,128)(2,1)S(1)} collective-permute-done((bf16[256,128]{1,0:T(8,128)(2,1)S(1)}, bf16[256,128]{1,0:T(8,128)(2,1)S(1)}, u32[]{:S(2)}, u32[]{:S(2)}) %collective-permute-start.11) | collective-permute-done | bytes 65568 | tf_op jit(solution)/shard_map/ppermute | solution.py:378
  40.9 1.6 %collective-permute-start.17 = (bf16[512,128]{1,0:T(8,128)(2,1)S(1)}, bf16[512,128]{1,0:T(8,128)(2,1)S(1)}, u32[]{:S(2)}, u32[]{:S(2)}) collective-permute-start(bf16[512,128]{1,0:T(8,128)(2,1)S(1)} %shard_map.122.refs_0_), channel_id=1, source_target_pairs={{0,24},{4,28},{8,16},{12,20},{16,8},{20,12},{24,0},{28,4},{1,25},{... | collective-permute-start | bytes 393224 | tf_op jit(solution)/shard_map/ppermute | solution.py:364
  42.5 1.5 %collective-permute-start.15 = (bf16[512,128]{1,0:T(8,128)(2,1)S(1)}, bf16[512,128]{1,0:T(8,128)(2,1)S(1)}, u32[]{:S(2)}, u32[]{:S(2)}) collective-permute-start(bf16[512,128]{1,0:T(8,128)(2,1)S(1)} %shard_map.122.refs_0_), channel_id=1, source_target_pairs={{0,16},{4,20},{8,24},{12,28},{16,0},{20,4},{24,8},{28,12},{1,17},{... | collective-permute-start | bytes 393224 | tf_op jit(solution)/shard_map/ppermute | solution.py:364
  44.0 0.5 collective-permute-start.13
  44.5 2.5 %collective-permute-done.17.refs_3_.refs_6_ = bf16[512,128]{1,0:T(8,128)(2,1)S(1)} collective-permute-done((bf16[512,128]{1,0:T(8,128)(2,1)S(1)}, bf16[512,128]{1,0:T(8,128)(2,1)S(1)}, u32[]{:S(2)}, u32[]{:S(2)}) %collective-permute-start.17) | collective-permute-done | bytes 131104 | tf_op jit(solution)/shard_map/ppermute | solution.py:364
  46.9 1.3 %collective-permute-done.15.refs_2_.refs_4_ = bf16[512,128]{1,0:T(8,128)(2,1)S(1)} collective-permute-done((bf16[512,128]{1,0:T(8,128)(2,1)S(1)}, bf16[512,128]{1,0:T(8,128)(2,1)S(1)}, u32[]{:S(2)}, u32[]{:S(2)}) %collective-permute-start.15) | collective-permute-done | bytes 131104 | tf_op jit(solution)/shard_map/ppermute | solution.py:364
  48.3 0.7 %collective-permute-done.13.refs_1_.refs_2_ = bf16[512,128]{1,0:T(8,128)(2,1)S(1)} collective-permute-done((bf16[512,128]{1,0:T(8,128)(2,1)S(1)}, bf16[512,128]{1,0:T(8,128)(2,1)S(1)}, u32[]{:S(2)}, u32[]{:S(2)}) %collective-permute-start.13) | collective-permute-done | bytes 131104 | tf_op jit(solution)/shard_map/ppermute | solution.py:364
  49.0 1.3 %shard_map.123 = (f32[27,96,96]{2,1,0:T(8,128)}, f32[27,96,96]{2,1,0:T(8,128)}) custom-call(bf16[512,128]{1,0:T(8,128)(2,1)S(1)} %shard_map.122.refs_0_, bf16[512,128]{1,0:T(8,128)(2,1)S(1)} %collective-permute-done.13.refs_1_.refs_2_, bf16[512,128]{1,0:T(8,128)(2,1)S(1)} %collective-permute-done.15.refs_2_.refs_4_, ...), custom_call_target="tpu_custom_call" | custom-call | bytes 4194304 | tf_op jit(solution)/shard_map/pallas_call | solution.py:21
  50.3 1.4 %shard_map.124 = (f32[27,96,96]{2,1,0:T(8,128)}, f32[27,96,96]{2,1,0:T(8,128)}) custom-call(bf16[512,128]{1,0:T(8,128)(2,1)S(1)} %shard_map.122.refs_0_, bf16[512,128]{1,0:T(8,128)(2,1)S(1)} %collective-permute-done.12.refs_1_, bf16[512,128]{1,0:T(8,128)(2,1)S(1)} %collective-permute-done.13.refs_1_.refs_2_, ...), custom_call_target="tpu_custom_call", output_to_operand_aliasing={{0}: (8, {}), {1}: (9, {})} | custom-call | bytes 4194304 | tf_op jit(solution)/shard_map/pallas_call | solution.py:21
  (33 shorter events, 0.3 us)
Async XLA Ops:
  0.6 5.0 %copy-start.4 = (bf16[27,96,96]{2,1,0:T(8,128)(2,1)S(1)}, bf16[27,96,96]{2,1,0:T(8,128)(2,1)}, u32[]{:S(2)}) copy-start(bf16[27,96,96]{2,1,0:T(8,128)(2,1)} %weight_ref.2) | copy-start | bytes 1492996
  0.6 5.0 %copy-start.6 = (s32[1,1,27,256]{3,1,2,0:T(1,128)S(1)}, s32[1,1,27,256]{3,1,2,0:T(1,128)}, u32[]{:S(2)}) copy-start(s32[1,1,27,256]{3,1,2,0:T(1,128)} %param.14) | copy-start | bytes 82948
  4.4 4.3 %collective-permute-start = (bf16[192,128]{1,0:T(8,128)(2,1)S(1)}, bf16[192,128]{1,0:T(8,128)(2,1)S(1)}, u32[]{:S(2)}, u32[]{:S(2)}) collective-permute-start(bf16[192,128]{1,0:T(8,128)(2,1)S(1)} %get-tuple-element.46), channel_id=1, source_target_pairs={{0,4},{4,0},{8,12},{12,8},{16,20},{20,16},{24,28},{28,24},{1,5},{5... | collective-permute-start | bytes 147464 | tf_op jit(solution)/shard_map/ppermute | solution.py:364
  5.0 3.8 %collective-permute-start.1 = (bf16[192,128]{1,0:T(8,128)(2,1)S(1)}, bf16[192,128]{1,0:T(8,128)(2,1)S(1)}, u32[]{:S(2)}, u32[]{:S(2)}) collective-permute-start(bf16[192,128]{1,0:T(8,128)(2,1)S(1)} %get-tuple-element.47), channel_id=1, source_target_pairs={{4,8},{8,4},{12,16},{16,12},{20,24},{24,20},{5,9},{9,5},{13,17},{1... | collective-permute-start | bytes 147464 | tf_op jit(solution)/shard_map/ppermute | solution.py:369
  5.7 2.1 %copy-start.1 = (bf16[1,1,512,96]{2,3,1,0:T(8,128)(2,1)S(1)}, bf16[1,1,512,96]{2,3,1,0:T(8,128)(2,1)}, u32[]{:S(2)}) copy-start(bf16[1,1,512,96]{2,3,1,0:T(8,128)(2,1)} %param.10) | copy-start | bytes 294916
  7.7 1.0 %copy-start.2 = (s32[1,1,64]{2,1,0:T(1,128)S(1)}, s32[1,1,64]{2,1,0:T(1,128)}, u32[]{:S(2)}) copy-start(s32[1,1,64]{2,1,0:T(1,128)} %param.17) | copy-start | bytes 772
  7.7 1.0 %copy-start.3 = (s32[1,1,64]{2,1,0:T(1,128)S(1)}, s32[1,1,64]{2,1,0:T(1,128)}, u32[]{:S(2)}) copy-start(s32[1,1,64]{2,1,0:T(1,128)} %param.16) | copy-start | bytes 772
  7.7 1.0 %copy-start.5 = (bf16[1,1,512,96]{2,3,1,0:T(8,128)(2,1)S(1)}, bf16[1,1,512,96]{2,3,1,0:T(8,128)(2,1)}, u32[]{:S(2)}) copy-start(bf16[1,1,512,96]{2,3,1,0:T(8,128)(2,1)} %param.9) | copy-start | bytes 294916
  8.8 8.0 %copy-start = (bf16[27,96,96]{2,1,0:T(8,128)(2,1)S(1)}, bf16[27,96,96]{2,1,0:T(8,128)(2,1)}, u32[]{:S(2)}) copy-start(bf16[27,96,96]{2,1,0:T(8,128)(2,1)} %weight_ref.3) | copy-start | bytes 1492996
  12.8 5.5 %collective-permute-start.2 = (bf16[2048,128]{1,0:T(8,128)(2,1)S(1)}, bf16[2048,128]{1,0:T(8,128)(2,1)S(1)}, u32[]{:S(2)}, u32[]{:S(2)}) collective-permute-start(bf16[2048,128]{1,0:T(8,128)(2,1)S(1)} %get-tuple-element.55), channel_id=1, source_target_pairs={{0,4},{4,0},{8,12},{12,8},{16,20},{20,16},{24,28},{28,24},{1,5},{5... | collective-permute-start | bytes 1572872 | tf_op jit(solution)/shard_map/ppermute | solution.py:364
  18.4 6.0 %collective-permute-start.5 = (bf16[512,128]{1,0:T(8,128)(2,1)S(1)}, bf16[512,128]{1,0:T(8,128)(2,1)S(1)}, u32[]{:S(2)}, u32[]{:S(2)}) collective-permute-start(bf16[512,128]{1,0:T(8,128)(2,1)S(1)} %get-tuple-element.63), channel_id=1, source_target_pairs={{0,8},{4,12},{8,0},{12,4},{16,24},{20,28},{24,16},{28,20},{1,9},{5... | collective-permute-start | bytes 393224 | tf_op jit(solution)/shard_map/ppermute | solution.py:364
  20.2 8.3 %collective-permute-start.6 = (bf16[512,128]{1,0:T(8,128)(2,1)S(1)}, bf16[512,128]{1,0:T(8,128)(2,1)S(1)}, u32[]{:S(2)}, u32[]{:S(2)}) collective-permute-start(bf16[512,128]{1,0:T(8,128)(2,1)S(1)} %get-tuple-element.64), channel_id=1, source_target_pairs={{0,16},{4,20},{8,24},{12,28},{16,0},{20,4},{24,8},{28,12},{1,17},{... | collective-permute-start | bytes 393224 | tf_op jit(solution)/shard_map/ppermute | solution.py:364
  20.9 7.6 %collective-permute-start.7 = (bf16[512,128]{1,0:T(8,128)(2,1)S(1)}, bf16[512,128]{1,0:T(8,128)(2,1)S(1)}, u32[]{:S(2)}, u32[]{:S(2)}) collective-permute-start(bf16[512,128]{1,0:T(8,128)(2,1)S(1)} %get-tuple-element.65), channel_id=1, source_target_pairs={{0,24},{4,28},{8,16},{12,20},{16,8},{20,12},{24,0},{28,4},{1,25},{... | collective-permute-start | bytes 393224 | tf_op jit(solution)/shard_map/ppermute | solution.py:364
  22.0 1.2 %collective-permute-start.3 = (bf16[96,128]{1,0:T(8,128)(2,1)S(1)}, bf16[96,128]{1,0:T(8,128)(2,1)S(1)}, u32[]{:S(2)}, u32[]{:S(2)}) collective-permute-start(bf16[96,128]{1,0:T(8,128)(2,1)S(1)} %get-tuple-element.60), channel_id=1, source_target_pairs={{0,4},{4,0},{8,12},{12,8},{16,20},{20,16},{24,28},{28,24},{1,5},{5... | collective-permute-start | bytes 73736 | tf_op jit(solution)/shard_map/ppermute | solution.py:364
  22.0 1.2 %collective-permute-start.4 = (bf16[96,128]{1,0:T(8,128)(2,1)S(1)}, bf16[96,128]{1,0:T(8,128)(2,1)S(1)}, u32[]{:S(2)}, u32[]{:S(2)}) collective-permute-start(bf16[96,128]{1,0:T(8,128)(2,1)S(1)} %get-tuple-element.61), channel_id=1, source_target_pairs={{4,8},{8,4},{12,16},{16,12},{20,24},{24,20},{5,9},{9,5},{13,17},{1... | collective-permute-start | bytes 73736 | tf_op jit(solution)/shard_map/ppermute | solution.py:369
  28.5 4.5 %collective-permute-start.8 = (bf16[256,128]{1,0:T(8,128)(2,1)S(1)}, bf16[256,128]{1,0:T(8,128)(2,1)S(1)}, u32[]{:S(2)}, u32[]{:S(2)}) collective-permute-start(bf16[256,128]{1,0:T(8,128)(2,1)S(1)} %get-tuple-element.77.refs_0_), channel_id=1, source_target_pairs={{0,1},{1,0},{2,3},{3,2},{4,6},{5,7},{6,4},{7,5},{8,9},{9,8},{10,11... | collective-permute-start | bytes 196616 | tf_op jit(solution)/shard_map/ppermute | solution.py:378
  30.1 5.4 %collective-permute-start.10 = (bf16[256,128]{1,0:T(8,128)(2,1)S(1)}, bf16[256,128]{1,0:T(8,128)(2,1)S(1)}, u32[]{:S(2)}, u32[]{:S(2)}) collective-permute-start(bf16[256,128]{1,0:T(8,128)(2,1)S(1)} %get-tuple-element.78.refs_0_), channel_id=1, source_target_pairs={{0,1},{1,0},{2,3},{3,2},{4,6},{5,7},{6,4},{7,5},{8,9},{9,8},{10,11... | collective-permute-start | bytes 196616 | tf_op jit(solution)/shard_map/ppermute | solution.py:378
  33.0 5.3 %collective-permute-start.9 = (bf16[256,128]{1,0:T(8,128)(2,1)S(1)}, bf16[256,128]{1,0:T(8,128)(2,1)S(1)}, u32[]{:S(2)}, u32[]{:S(2)}) collective-permute-start(bf16[256,128]{1,0:T(8,128)(2,1)S(1)} %shard_map.120.refs_0_), channel_id=1, source_target_pairs={{0,2},{1,3},{2,0},{3,1},{4,5},{5,4},{6,7},{7,6},{8,10},{9,11},{10,... | collective-permute-start | bytes 196616 | tf_op jit(solution)/shard_map/ppermute | solution.py:378
  35.5 5.3 %collective-permute-start.11 = (bf16[256,128]{1,0:T(8,128)(2,1)S(1)}, bf16[256,128]{1,0:T(8,128)(2,1)S(1)}, u32[]{:S(2)}, u32[]{:S(2)}) collective-permute-start(bf16[256,128]{1,0:T(8,128)(2,1)S(1)} %shard_map.121.refs_2_), channel_id=1, source_target_pairs={{0,2},{1,3},{2,0},{3,1},{4,5},{5,4},{6,7},{7,6},{8,10},{9,11},{10,... | collective-permute-start | bytes 196616 | tf_op jit(solution)/shard_map/ppermute | solution.py:378
  40.9 6.0 %collective-permute-start.17 = (bf16[512,128]{1,0:T(8,128)(2,1)S(1)}, bf16[512,128]{1,0:T(8,128)(2,1)S(1)}, u32[]{:S(2)}, u32[]{:S(2)}) collective-permute-start(bf16[512,128]{1,0:T(8,128)(2,1)S(1)} %shard_map.122.refs_0_), channel_id=1, source_target_pairs={{0,24},{4,28},{8,16},{12,20},{16,8},{20,12},{24,0},{28,4},{1,25},{... | collective-permute-start | bytes 393224 | tf_op jit(solution)/shard_map/ppermute | solution.py:364
  42.5 5.8 %collective-permute-start.15 = (bf16[512,128]{1,0:T(8,128)(2,1)S(1)}, bf16[512,128]{1,0:T(8,128)(2,1)S(1)}, u32[]{:S(2)}, u32[]{:S(2)}) collective-permute-start(bf16[512,128]{1,0:T(8,128)(2,1)S(1)} %shard_map.122.refs_0_), channel_id=1, source_target_pairs={{0,16},{4,20},{8,24},{12,28},{16,0},{20,4},{24,8},{28,12},{1,17},{... | collective-permute-start | bytes 393224 | tf_op jit(solution)/shard_map/ppermute | solution.py:364
  44.0 5.0 %collective-permute-start.13 = (bf16[512,128]{1,0:T(8,128)(2,1)S(1)}, bf16[512,128]{1,0:T(8,128)(2,1)S(1)}, u32[]{:S(2)}, u32[]{:S(2)}) collective-permute-start(bf16[512,128]{1,0:T(8,128)(2,1)S(1)} %shard_map.122.refs_0_), channel_id=1, source_target_pairs={{0,8},{4,12},{8,0},{12,4},{16,24},{20,28},{24,16},{28,20},{1,9},{5... | collective-permute-start | bytes 393224 | tf_op jit(solution)/shard_map/ppermute | solution.py:364
  44.5 5.8 %collective-permute-start.12 = (bf16[512,128]{1,0:T(8,128)(2,1)S(1)}, bf16[512,128]{1,0:T(8,128)(2,1)S(1)}, u32[]{:S(2)}, u32[]{:S(2)}) collective-permute-start(bf16[512,128]{1,0:T(8,128)(2,1)S(1)} %shard_map.122.refs_0_), channel_id=1, source_target_pairs={{0,4},{4,0},{8,12},{12,8},{16,20},{20,16},{24,28},{28,24},{1,5},{5... | collective-permute-start | bytes 393224 | tf_op jit(solution)/shard_map/ppermute | solution.py:364
  46.9 3.4 %collective-permute-start.18 = (bf16[512,128]{1,0:T(8,128)(2,1)S(1)}, bf16[512,128]{1,0:T(8,128)(2,1)S(1)}, u32[]{:S(2)}, u32[]{:S(2)}) collective-permute-start(bf16[512,128]{1,0:T(8,128)(2,1)S(1)} %collective-permute-done.17.refs_3_.refs_6_), channel_id=1, source_target_pairs={{0,4},{4,0},{8,12},{12,8},{16,20},{20,16},{24,28},{28,24},{1,5},{5... | collective-permute-start | bytes 393224 | tf_op jit(solution)/shard_map/ppermute | solution.py:364
  48.3 2.1 %collective-permute-start.16 = (bf16[512,128]{1,0:T(8,128)(2,1)S(1)}, bf16[512,128]{1,0:T(8,128)(2,1)S(1)}, u32[]{:S(2)}, u32[]{:S(2)}) collective-permute-start(bf16[512,128]{1,0:T(8,128)(2,1)S(1)} %collective-permute-done.15.refs_2_.refs_4_), channel_id=1, source_target_pairs={{0,4},{4,0},{8,12},{12,8},{16,20},{20,16},{24,28},{28,24},{1,5},{5... | collective-permute-start | bytes 393224 | tf_op jit(solution)/shard_map/ppermute | solution.py:364
  49.0 1.3 %collective-permute-start.14 = (bf16[512,128]{1,0:T(8,128)(2,1)S(1)}, bf16[512,128]{1,0:T(8,128)(2,1)S(1)}, u32[]{:S(2)}, u32[]{:S(2)}) collective-permute-start(bf16[512,128]{1,0:T(8,128)(2,1)S(1)} %collective-permute-done.13.refs_1_.refs_2_), channel_id=1, source_target_pairs={{0,4},{4,0},{8,12},{12,8},{16,20},{20,16},{24,28},{28,24},{1,5},{5... | collective-permute-start | bytes 393224 | tf_op jit(solution)/shard_map/ppermute | solution.py:364

commit v9 on v8

--- a/solution.py
+++ b/solution.py
@@ -385,7 +385,7 @@
     rows = keep.shape[0] // slots
     outs = [shape((rows, LANES), F32)] + [shape((rows, LANES), BF16)] * (slots - 1)
     own, *sends = call(functools.partial(core_sum_body, layers), outs, [keep, got])
-    gots = [swap(block, "space", 2 * slot) for slot, block in enumerate(sends, 1)]
+    gots = [swap(block, "space", 2 * slot) for slot, block in reversed(list(enumerate(sends, 1)))]
     waiting = list(beside)
     own, state = waiting.pop(0)(own, None)
     part = rows // layers

time: 52 us -> 51.6 us (level)
  transfers between devices with their start and end apart: 19 -> 19, of which waited for: 10 -> 11; matrix products, arithmetic and copies ran while one was open for 0% -> 0% of each run, Pallas kernels for 12% -> 12%
where the time goes in v9:
time: 51.6 us; the launch traced here: 51.5 us
  starting transfers between devices  19.3 us (37%)
  Pallas kernels  15.8 us (31%)
  waiting for transfers between devices  15.5 us (30%)
  between operations  0.87 us (2%)
    pallas_call x13, Pallas kernels, call(): pl.pallas_call(body, out_shape=outs if single else tuple(outs), in_specs=...  15.8 us
    ppermute x13, starting transfers between devices, swap(): lax.ppermute(block, axis, [(i, i ^ bit) for i in range(lax.axis_size(axis...  11.7 us
    ppermute x13, waiting for transfers between devices, swap(): lax.ppermute(block, axis, [(i, i ^ bit) for i in range(lax.axis_size(axis...  10.4 us
    ppermute x4, starting transfers between devices, swap_scans(): return lax.ppermute(block, ('space', 'scan'), pairs)  6.24 us
    ppermute x4, waiting for transfers between devices, swap_scans(): return lax.ppermute(block, ('space', 'scan'), pairs)  5.03 us
    ppermute x2, starting transfers between devices, swap_neighbours(): lax.ppermute(far, 'space', [(i, i + 1 if i % 2 else i - 1) for i in inner])  1.3 us
  transfers between devices with their start and end apart: 19, of which 11 were waited for; matrix products, arithmetic and copies ran while one was open for 0% of the time, Pallas kernels for 12%

profile of v9, /device:TPU:0, one launch (start us, length us, event | category | flops | bytes accessed | tf_op | source)
XLA Modules:
  0.0 51.5 jit_solution(16973873321561810668)
XLA Ops:
  0.7 3.8 %shard_map.112 = (bf16[3024,256]{1,0:T(8,128)(2,1)S(1)}, bf16[2688,128]{1,0:T(8,128)(2,1)S(1)}, f32[32,128]{1,0:T(8,128)S(1)}, bf16[192,128]{1,0:T(8,128)(2,1)S(1)}, bf16[192,128]{1,0:T(8,128)(2,1)S(1)}) custom-call(s32[27,1,256]{2,1,0:T(1,128)} %bitcast.31, bf16[96,512]{1,0:T(8,128)(2,1)} %bitcast.30, s32[27,1,256]{2,1,0:T(1,128)} %bitcast.27, ...), custom_call_target="tpu_custom_call" | custom-call | flops 679477248 | bytes 4194304 | tf_op jit(solution)/shard_map/pallas_call | solution.py:21
  4.4 0.5 %collective-permute-start = (bf16[192,128]{1,0:T(8,128)(2,1)S(1)}, bf16[192,128]{1,0:T(8,128)(2,1)S(1)}, u32[]{:S(2)}, u32[]{:S(2)}) collective-permute-start(bf16[192,128]{1,0:T(8,128)(2,1)S(1)} %get-tuple-element.46), channel_id=1, source_target_pairs={{0,4},{4,0},{8,12},{12,8},{16,20},{20,16},{24,28},{28,24},{1,5},{5... | collective-permute-start | bytes 147464 | tf_op jit(solution)/shard_map/ppermute | solution.py:364
  5.0 0.7 %collective-permute-start.1 = (bf16[192,128]{1,0:T(8,128)(2,1)S(1)}, bf16[192,128]{1,0:T(8,128)(2,1)S(1)}, u32[]{:S(2)}, u32[]{:S(2)}) collective-permute-start(bf16[192,128]{1,0:T(8,128)(2,1)S(1)} %get-tuple-element.47), channel_id=1, source_target_pairs={{4,8},{8,4},{12,16},{16,12},{20,24},{24,20},{5,9},{9,5},{13,17},{1... | collective-permute-start | bytes 147464 | tf_op jit(solution)/shard_map/ppermute | solution.py:369
  5.7 2.0 %shard_map.113 = (bf16[2688,512]{1,0:T(8,128)(2,1)S(1)}, f32[128,512]{1,0:T(8,128)S(1)}) custom-call(s32[27,1,256]{2,1,0:T(1,128)S(1)} %bitcast.28, bf16[3024,256]{1,0:T(8,128)(2,1)S(1)} %get-tuple-element.43.c_ref, bf16[27,96,96]{2,1,0:T(8,128)(2,1)S(1)} %copy-done.4), custom_call_target="tpu_custom_call" | custom-call | flops 849346560 | bytes 8388608 | tf_op jit(solution)/shard_map/pallas_call | solution.py:21
  7.8 1.0 %shard_map.114.sum_two_ref = f32[2048,128]{1,0:T(8,128)S(1)} custom-call(bf16[96,512]{1,0:T(8,128)(2,1)S(1)} %bitcast.17, bf16[2688,512]{1,0:T(8,128)(2,1)S(1)} %get-tuple-element.49.t_ref), custom_call_target="tpu_custom_call" | custom-call | flops 318504960 | bytes 6291456 | tf_op jit(solution)/shard_map/pallas_call | solution.py:21
  8.8 4.1 %shard_map.115 = (bf16[2688,640]{1,0:T(8,128)(2,1)S(1)}, f32[2048,128]{1,0:T(8,128)S(1)}, bf16[2048,128]{1,0:T(8,128)(2,1)S(1)}) custom-call(f32[128,512]{1,0:T(8,128)S(1)} %get-tuple-element.44.own_ref, f32[32,128]{1,0:T(8,128)S(1)} %get-tuple-element.45.inv_ref, bf16[192,128]{1,0:T(8,128)(2,1)S(1)} %collective-permute-done.near_ref, ...), custom_call_target="tpu_custom_call" | custom-call | flops 2017198080 | bytes 8388608 | tf_op jit(solution)/shard_map/pallas_call | solution.py:21
  12.8 3.9 %collective-permute-start.2 = (bf16[2048,128]{1,0:T(8,128)(2,1)S(1)}, bf16[2048,128]{1,0:T(8,128)(2,1)S(1)}, u32[]{:S(2)}, u32[]{:S(2)}) collective-permute-start(bf16[2048,128]{1,0:T(8,128)(2,1)S(1)} %get-tuple-element.55), channel_id=1, source_target_pairs={{0,4},{4,0},{8,12},{12,8},{16,20},{20,16},{24,28},{28,24},{1,5},{5... | collective-permute-start | bytes 1572872 | tf_op jit(solution)/shard_map/ppermute | solution.py:364
  16.8 1.1 %shard_map.116 = (f32[96,512]{1,0:T(8,128)S(1)}, bf16[96,128]{1,0:T(8,128)(2,1)S(1)}, bf16[96,128]{1,0:T(8,128)(2,1)S(1)}) custom-call(bf16[27,96,96]{2,1,0:T(8,128)(2,1)S(1)} %copy-done, bf16[2688,640]{1,0:T(8,128)(2,1)S(1)} %get-tuple-element.51.t_ref), custom_call_target="tpu_custom_call" | custom-call | flops 318504960 | bytes 6291456 | tf_op jit(solution)/shard_map/pallas_call | solution.py:21
  17.9 0.4 collective-permute-done.2.got_ref
  18.4 1.9 %collective-permute-start.5 = (bf16[512,128]{1,0:T(8,128)(2,1)S(1)}, bf16[512,128]{1,0:T(8,128)(2,1)S(1)}, u32[]{:S(2)}, u32[]{:S(2)}) collective-permute-start(bf16[512,128]{1,0:T(8,128)(2,1)S(1)} %get-tuple-element.63), channel_id=1, source_target_pairs={{0,24},{4,28},{8,16},{12,20},{16,8},{20,12},{24,0},{28,4},{1,25},{... | collective-permute-start | bytes 393224 | tf_op jit(solution)/shard_map/ppermute | solution.py:364
  20.3 1.3 %collective-permute-start.6 = (bf16[512,128]{1,0:T(8,128)(2,1)S(1)}, bf16[512,128]{1,0:T(8,128)(2,1)S(1)}, u32[]{:S(2)}, u32[]{:S(2)}) collective-permute-start(bf16[512,128]{1,0:T(8,128)(2,1)S(1)} %get-tuple-element.64), channel_id=1, source_target_pairs={{0,16},{4,20},{8,24},{12,28},{16,0},{20,4},{24,8},{28,12},{1,17},{... | collective-permute-start | bytes 393224 | tf_op jit(solution)/shard_map/ppermute | solution.py:364
  21.6 0.4 collective-permute-start.7
  22.0 0.7 %collective-permute-start.4 = (bf16[96,128]{1,0:T(8,128)(2,1)S(1)}, bf16[96,128]{1,0:T(8,128)(2,1)S(1)}, u32[]{:S(2)}, u32[]{:S(2)}) collective-permute-start(bf16[96,128]{1,0:T(8,128)(2,1)S(1)} %get-tuple-element.61), channel_id=1, source_target_pairs={{4,8},{8,4},{12,16},{16,12},{20,24},{24,20},{5,9},{9,5},{13,17},{1... | collective-permute-start | bytes 73736 | tf_op jit(solution)/shard_map/ppermute | solution.py:369
  22.7 0.5 %collective-permute-done.3.near_ref = bf16[96,128]{1,0:T(8,128)(2,1)S(1)} collective-permute-done((bf16[96,128]{1,0:T(8,128)(2,1)S(1)}, bf16[96,128]{1,0:T(8,128)(2,1)S(1)}, u32[]{:S(2)}, u32[]{:S(2)}) %collective-permute-start.3) | collective-permute-done | bytes 24608 | tf_op jit(solution)/shard_map/ppermute | solution.py:364
  23.2 2.6 %collective-permute-done.5.refs_0_ = bf16[512,128]{1,0:T(8,128)(2,1)S(1)} collective-permute-done((bf16[512,128]{1,0:T(8,128)(2,1)S(1)}, bf16[512,128]{1,0:T(8,128)(2,1)S(1)}, u32[]{:S(2)}, u32[]{:S(2)}) %collective-permute-start.5) | collective-permute-done | bytes 131104 | tf_op jit(solution)/shard_map/ppermute | solution.py:364
  25.8 2.2 %collective-permute-done.6.refs_1_ = bf16[512,128]{1,0:T(8,128)(2,1)S(1)} collective-permute-done((bf16[512,128]{1,0:T(8,128)(2,1)S(1)}, bf16[512,128]{1,0:T(8,128)(2,1)S(1)}, u32[]{:S(2)}, u32[]{:S(2)}) %collective-permute-start.6) | collective-permute-done | bytes 131104 | tf_op jit(solution)/shard_map/ppermute | solution.py:364
  28.2 1.6 %collective-permute-start.8 = (bf16[256,128]{1,0:T(8,128)(2,1)S(1)}, bf16[256,128]{1,0:T(8,128)(2,1)S(1)}, u32[]{:S(2)}, u32[]{:S(2)}) collective-permute-start(bf16[256,128]{1,0:T(8,128)(2,1)S(1)} %get-tuple-element.77.refs_0_), channel_id=1, source_target_pairs={{0,1},{1,0},{2,3},{3,2},{4,6},{5,7},{6,4},{7,5},{8,9},{9,8},{10,11... | collective-permute-start | bytes 196616 | tf_op jit(solution)/shard_map/ppermute | solution.py:378
  29.8 0.5 collective-permute-start.10
  30.3 0.9 %shard_map.119 = bf16[96,512]{1,0:T(8,128)(2,1)} custom-call(f32[96,512]{1,0:T(8,128)S(1)} %get-tuple-element.73.own_ref, bf16[96,128]{1,0:T(8,128)(2,1)S(1)} %collective-permute-done.3.near_ref, bf16[96,128]{1,0:T(8,128)(2,1)S(1)} %collective-permute-done.4.far_ref, s32[1,64]{1,0:T(1,128)S(1)} %bitcast.21, s32[1,64]{1,0:T(1,128)S(1)} %bitcast.24), custom_call_target="tpu_custom_call" | custom-call | tf_op jit(solution)/shard_map/pallas_call | solution.py:21
  31.2 2.0 %collective-permute-done.8.refs_1_ = bf16[256,128]{1,0:T(8,128)(2,1)S(1)} collective-permute-done((bf16[256,128]{1,0:T(8,128)(2,1)S(1)}, bf16[256,128]{1,0:T(8,128)(2,1)S(1)}, u32[]{:S(2)}, u32[]{:S(2)}) %collective-permute-start.8) | collective-permute-done | bytes 65568 | tf_op jit(solution)/shard_map/ppermute | solution.py:378
  33.2 1.9 %collective-permute-start.9 = (bf16[256,128]{1,0:T(8,128)(2,1)S(1)}, bf16[256,128]{1,0:T(8,128)(2,1)S(1)}, u32[]{:S(2)}, u32[]{:S(2)}) collective-permute-start(bf16[256,128]{1,0:T(8,128)(2,1)S(1)} %shard_map.120.refs_0_), channel_id=1, source_target_pairs={{0,2},{1,3},{2,0},{3,1},{4,5},{5,4},{6,7},{7,6},{8,10},{9,11},{10,... | collective-permute-start | bytes 196616 | tf_op jit(solution)/shard_map/ppermute | solution.py:378
  35.2 2.2 %collective-permute-start.11 = (bf16[256,128]{1,0:T(8,128)(2,1)S(1)}, bf16[256,128]{1,0:T(8,128)(2,1)S(1)}, u32[]{:S(2)}, u32[]{:S(2)}) collective-permute-start(bf16[256,128]{1,0:T(8,128)(2,1)S(1)} %shard_map.121.refs_2_), channel_id=1, source_target_pairs={{0,2},{1,3},{2,0},{3,1},{4,5},{5,4},{6,7},{7,6},{8,10},{9,11},{10,... | collective-permute-start | bytes 196616 | tf_op jit(solution)/shard_map/ppermute | solution.py:378
  37.4 1.1 %collective-permute-done.9.refs_1_ = bf16[256,128]{1,0:T(8,128)(2,1)S(1)} collective-permute-done((bf16[256,128]{1,0:T(8,128)(2,1)S(1)}, bf16[256,128]{1,0:T(8,128)(2,1)S(1)}, u32[]{:S(2)}, u32[]{:S(2)}) %collective-permute-start.9) | collective-permute-done | bytes 65568 | tf_op jit(solution)/shard_map/ppermute | solution.py:378
  38.5 1.9 %collective-permute-done.11.refs_3_ = bf16[256,128]{1,0:T(8,128)(2,1)S(1)} collective-permute-done((bf16[256,128]{1,0:T(8,128)(2,1)S(1)}, bf16[256,128]{1,0:T(8,128)(2,1)S(1)}, u32[]{:S(2)}, u32[]{:S(2)}) %collective-permute-start.11) | collective-permute-done | bytes 65568 | tf_op jit(solution)/shard_map/ppermute | solution.py:378
  40.5 2.0 %collective-permute-start.17 = (bf16[512,128]{1,0:T(8,128)(2,1)S(1)}, bf16[512,128]{1,0:T(8,128)(2,1)S(1)}, u32[]{:S(2)}, u32[]{:S(2)}) collective-permute-start(bf16[512,128]{1,0:T(8,128)(2,1)S(1)} %shard_map.122.refs_0_), channel_id=1, source_target_pairs={{0,24},{4,28},{8,16},{12,20},{16,8},{20,12},{24,0},{28,4},{1,25},{... | collective-permute-start | bytes 393224 | tf_op jit(solution)/shard_map/ppermute | solution.py:364
  42.5 1.2 %collective-permute-start.15 = (bf16[512,128]{1,0:T(8,128)(2,1)S(1)}, bf16[512,128]{1,0:T(8,128)(2,1)S(1)}, u32[]{:S(2)}, u32[]{:S(2)}) collective-permute-start(bf16[512,128]{1,0:T(8,128)(2,1)S(1)} %shard_map.122.refs_0_), channel_id=1, source_target_pairs={{0,16},{4,20},{8,24},{12,28},{16,0},{20,4},{24,8},{28,12},{1,17},{... | collective-permute-start | bytes 393224 | tf_op jit(solution)/shard_map/ppermute | solution.py:364
  43.7 0.4 collective-permute-start.13
  44.1 2.7 %collective-permute-done.17.refs_3_.refs_6_ = bf16[512,128]{1,0:T(8,128)(2,1)S(1)} collective-permute-done((bf16[512,128]{1,0:T(8,128)(2,1)S(1)}, bf16[512,128]{1,0:T(8,128)(2,1)S(1)}, u32[]{:S(2)}, u32[]{:S(2)}) %collective-permute-start.17) | collective-permute-done | bytes 131104 | tf_op jit(solution)/shard_map/ppermute | solution.py:364
  46.9 1.3 %collective-permute-done.15.refs_2_.refs_4_ = bf16[512,128]{1,0:T(8,128)(2,1)S(1)} collective-permute-done((bf16[512,128]{1,0:T(8,128)(2,1)S(1)}, bf16[512,128]{1,0:T(8,128)(2,1)S(1)}, u32[]{:S(2)}, u32[]{:S(2)}) %collective-permute-start.15) | collective-permute-done | bytes 131104 | tf_op jit(solution)/shard_map/ppermute | solution.py:364
  48.2 0.5 collective-permute-done.13.refs_1_.refs_2_
  48.7 1.3 %shard_map.123 = (f32[27,96,96]{2,1,0:T(8,128)}, f32[27,96,96]{2,1,0:T(8,128)}) custom-call(bf16[512,128]{1,0:T(8,128)(2,1)S(1)} %shard_map.122.refs_0_, bf16[512,128]{1,0:T(8,128)(2,1)S(1)} %collective-permute-done.13.refs_1_.refs_2_, bf16[512,128]{1,0:T(8,128)(2,1)S(1)} %collective-permute-done.15.refs_2_.refs_4_, ...), custom_call_target="tpu_custom_call" | custom-call | bytes 4194304 | tf_op jit(solution)/shard_map/pallas_call | solution.py:21
  50.1 1.4 %shard_map.124 = (f32[27,96,96]{2,1,0:T(8,128)}, f32[27,96,96]{2,1,0:T(8,128)}) custom-call(bf16[512,128]{1,0:T(8,128)(2,1)S(1)} %shard_map.122.refs_0_, bf16[512,128]{1,0:T(8,128)(2,1)S(1)} %collective-permute-done.12.refs_1_, bf16[512,128]{1,0:T(8,128)(2,1)S(1)} %collective-permute-done.13.refs_1_.refs_2_, ...), custom_call_target="tpu_custom_call", output_to_operand_aliasing={{0}: (8, {}), {1}: (9, {})} | custom-call | bytes 4194304 | tf_op jit(solution)/shard_map/pallas_call | solution.py:21
  (33 shorter events, 0.5 us)
Async XLA Ops:
  0.6 5.0 %copy-start.4 = (bf16[27,96,96]{2,1,0:T(8,128)(2,1)S(1)}, bf16[27,96,96]{2,1,0:T(8,128)(2,1)}, u32[]{:S(2)}) copy-start(bf16[27,96,96]{2,1,0:T(8,128)(2,1)} %weight_ref.2) | copy-start | bytes 1492996
  0.6 5.0 %copy-start.6 = (s32[1,1,27,256]{3,1,2,0:T(1,128)S(1)}, s32[1,1,27,256]{3,1,2,0:T(1,128)}, u32[]{:S(2)}) copy-start(s32[1,1,27,256]{3,1,2,0:T(1,128)} %param.14) | copy-start | bytes 82948
  4.4 4.3 %collective-permute-start = (bf16[192,128]{1,0:T(8,128)(2,1)S(1)}, bf16[192,128]{1,0:T(8,128)(2,1)S(1)}, u32[]{:S(2)}, u32[]{:S(2)}) collective-permute-start(bf16[192,128]{1,0:T(8,128)(2,1)S(1)} %get-tuple-element.46), channel_id=1, source_target_pairs={{0,4},{4,0},{8,12},{12,8},{16,20},{20,16},{24,28},{28,24},{1,5},{5... | collective-permute-start | bytes 147464 | tf_op jit(solution)/shard_map/ppermute | solution.py:364
  5.0 3.8 %collective-permute-start.1 = (bf16[192,128]{1,0:T(8,128)(2,1)S(1)}, bf16[192,128]{1,0:T(8,128)(2,1)S(1)}, u32[]{:S(2)}, u32[]{:S(2)}) collective-permute-start(bf16[192,128]{1,0:T(8,128)(2,1)S(1)} %get-tuple-element.47), channel_id=1, source_target_pairs={{4,8},{8,4},{12,16},{16,12},{20,24},{24,20},{5,9},{9,5},{13,17},{1... | collective-permute-start | bytes 147464 | tf_op jit(solution)/shard_map/ppermute | solution.py:369
  5.7 2.1 %copy-start.1 = (bf16[1,1,512,96]{2,3,1,0:T(8,128)(2,1)S(1)}, bf16[1,1,512,96]{2,3,1,0:T(8,128)(2,1)}, u32[]{:S(2)}) copy-start(bf16[1,1,512,96]{2,3,1,0:T(8,128)(2,1)} %param.10) | copy-start | bytes 294916
  7.7 1.0 %copy-start.2 = (s32[1,1,64]{2,1,0:T(1,128)S(1)}, s32[1,1,64]{2,1,0:T(1,128)}, u32[]{:S(2)}) copy-start(s32[1,1,64]{2,1,0:T(1,128)} %param.17) | copy-start | bytes 772
  7.7 1.0 %copy-start.3 = (s32[1,1,64]{2,1,0:T(1,128)S(1)}, s32[1,1,64]{2,1,0:T(1,128)}, u32[]{:S(2)}) copy-start(s32[1,1,64]{2,1,0:T(1,128)} %param.16) | copy-start | bytes 772
  7.7 1.0 %copy-start.5 = (bf16[1,1,512,96]{2,3,1,0:T(8,128)(2,1)S(1)}, bf16[1,1,512,96]{2,3,1,0:T(8,128)(2,1)}, u32[]{:S(2)}) copy-start(bf16[1,1,512,96]{2,3,1,0:T(8,128)(2,1)} %param.9) | copy-start | bytes 294916
  8.8 8.0 %copy-start = (bf16[27,96,96]{2,1,0:T(8,128)(2,1)S(1)}, bf16[27,96,96]{2,1,0:T(8,128)(2,1)}, u32[]{:S(2)}) copy-start(bf16[27,96,96]{2,1,0:T(8,128)(2,1)} %weight_ref.3) | copy-start | bytes 1492996
  12.8 5.5 %collective-permute-start.2 = (bf16[2048,128]{1,0:T(8,128)(2,1)S(1)}, bf16[2048,128]{1,0:T(8,128)(2,1)S(1)}, u32[]{:S(2)}, u32[]{:S(2)}) collective-permute-start(bf16[2048,128]{1,0:T(8,128)(2,1)S(1)} %get-tuple-element.55), channel_id=1, source_target_pairs={{0,4},{4,0},{8,12},{12,8},{16,20},{20,16},{24,28},{28,24},{1,5},{5... | collective-permute-start | bytes 1572872 | tf_op jit(solution)/shard_map/ppermute | solution.py:364
  18.4 7.3 %collective-permute-start.5 = (bf16[512,128]{1,0:T(8,128)(2,1)S(1)}, bf16[512,128]{1,0:T(8,128)(2,1)S(1)}, u32[]{:S(2)}, u32[]{:S(2)}) collective-permute-start(bf16[512,128]{1,0:T(8,128)(2,1)S(1)} %get-tuple-element.63), channel_id=1, source_target_pairs={{0,24},{4,28},{8,16},{12,20},{16,8},{20,12},{24,0},{28,4},{1,25},{... | collective-permute-start | bytes 393224 | tf_op jit(solution)/shard_map/ppermute | solution.py:364
  20.3 7.7 %collective-permute-start.6 = (bf16[512,128]{1,0:T(8,128)(2,1)S(1)}, bf16[512,128]{1,0:T(8,128)(2,1)S(1)}, u32[]{:S(2)}, u32[]{:S(2)}) collective-permute-start(bf16[512,128]{1,0:T(8,128)(2,1)S(1)} %get-tuple-element.64), channel_id=1, source_target_pairs={{0,16},{4,20},{8,24},{12,28},{16,0},{20,4},{24,8},{28,12},{1,17},{... | collective-permute-start | bytes 393224 | tf_op jit(solution)/shard_map/ppermute | solution.py:364
  21.6 6.5 %collective-permute-start.7 = (bf16[512,128]{1,0:T(8,128)(2,1)S(1)}, bf16[512,128]{1,0:T(8,128)(2,1)S(1)}, u32[]{:S(2)}, u32[]{:S(2)}) collective-permute-start(bf16[512,128]{1,0:T(8,128)(2,1)S(1)} %get-tuple-element.65), channel_id=1, source_target_pairs={{0,8},{4,12},{8,0},{12,4},{16,24},{20,28},{24,16},{28,20},{1,9},{5... | collective-permute-start | bytes 393224 | tf_op jit(solution)/shard_map/ppermute | solution.py:364
  22.0 1.2 %collective-permute-start.3 = (bf16[96,128]{1,0:T(8,128)(2,1)S(1)}, bf16[96,128]{1,0:T(8,128)(2,1)S(1)}, u32[]{:S(2)}, u32[]{:S(2)}) collective-permute-start(bf16[96,128]{1,0:T(8,128)(2,1)S(1)} %get-tuple-element.60), channel_id=1, source_target_pairs={{0,4},{4,0},{8,12},{12,8},{16,20},{20,16},{24,28},{28,24},{1,5},{5... | collective-permute-start | bytes 73736 | tf_op jit(solution)/shard_map/ppermute | solution.py:364
  22.0 1.2 %collective-permute-start.4 = (bf16[96,128]{1,0:T(8,128)(2,1)S(1)}, bf16[96,128]{1,0:T(8,128)(2,1)S(1)}, u32[]{:S(2)}, u32[]{:S(2)}) collective-permute-start(bf16[96,128]{1,0:T(8,128)(2,1)S(1)} %get-tuple-element.61), channel_id=1, source_target_pairs={{4,8},{8,4},{12,16},{16,12},{20,24},{24,20},{5,9},{9,5},{13,17},{1... | collective-permute-start | bytes 73736 | tf_op jit(solution)/shard_map/ppermute | solution.py:369
  28.2 5.0 %collective-permute-start.8 = (bf16[256,128]{1,0:T(8,128)(2,1)S(1)}, bf16[256,128]{1,0:T(8,128)(2,1)S(1)}, u32[]{:S(2)}, u32[]{:S(2)}) collective-permute-start(bf16[256,128]{1,0:T(8,128)(2,1)S(1)} %get-tuple-element.77.refs_0_), channel_id=1, source_target_pairs={{0,1},{1,0},{2,3},{3,2},{4,6},{5,7},{6,4},{7,5},{8,9},{9,8},{10,11... | collective-permute-start | bytes 196616 | tf_op jit(solution)/shard_map/ppermute | solution.py:378
  29.8 5.4 %collective-permute-start.10 = (bf16[256,128]{1,0:T(8,128)(2,1)S(1)}, bf16[256,128]{1,0:T(8,128)(2,1)S(1)}, u32[]{:S(2)}, u32[]{:S(2)}) collective-permute-start(bf16[256,128]{1,0:T(8,128)(2,1)S(1)} %get-tuple-element.78.refs_0_), channel_id=1, source_target_pairs={{0,1},{1,0},{2,3},{3,2},{4,6},{5,7},{6,4},{7,5},{8,9},{9,8},{10,11... | collective-permute-start | bytes 196616 | tf_op jit(solution)/shard_map/ppermute | solution.py:378
  33.2 5.3 %collective-permute-start.9 = (bf16[256,128]{1,0:T(8,128)(2,1)S(1)}, bf16[256,128]{1,0:T(8,128)(2,1)S(1)}, u32[]{:S(2)}, u32[]{:S(2)}) collective-permute-start(bf16[256,128]{1,0:T(8,128)(2,1)S(1)} %shard_map.120.refs_0_), channel_id=1, source_target_pairs={{0,2},{1,3},{2,0},{3,1},{4,5},{5,4},{6,7},{7,6},{8,10},{9,11},{10,... | collective-permute-start | bytes 196616 | tf_op jit(solution)/shard_map/ppermute | solution.py:378
  35.2 5.2 %collective-permute-start.11 = (bf16[256,128]{1,0:T(8,128)(2,1)S(1)}, bf16[256,128]{1,0:T(8,128)(2,1)S(1)}, u32[]{:S(2)}, u32[]{:S(2)}) collective-permute-start(bf16[256,128]{1,0:T(8,128)(2,1)S(1)} %shard_map.121.refs_2_), channel_id=1, source_target_pairs={{0,2},{1,3},{2,0},{3,1},{4,5},{5,4},{6,7},{7,6},{8,10},{9,11},{10,... | collective-permute-start | bytes 196616 | tf_op jit(solution)/shard_map/ppermute | solution.py:378
  40.5 6.4 %collective-permute-start.17 = (bf16[512,128]{1,0:T(8,128)(2,1)S(1)}, bf16[512,128]{1,0:T(8,128)(2,1)S(1)}, u32[]{:S(2)}, u32[]{:S(2)}) collective-permute-start(bf16[512,128]{1,0:T(8,128)(2,1)S(1)} %shard_map.122.refs_0_), channel_id=1, source_target_pairs={{0,24},{4,28},{8,16},{12,20},{16,8},{20,12},{24,0},{28,4},{1,25},{... | collective-permute-start | bytes 393224 | tf_op jit(solution)/shard_map/ppermute | solution.py:364
  42.5 5.7 %collective-permute-start.15 = (bf16[512,128]{1,0:T(8,128)(2,1)S(1)}, bf16[512,128]{1,0:T(8,128)(2,1)S(1)}, u32[]{:S(2)}, u32[]{:S(2)}) collective-permute-start(bf16[512,128]{1,0:T(8,128)(2,1)S(1)} %shard_map.122.refs_0_), channel_id=1, source_target_pairs={{0,16},{4,20},{8,24},{12,28},{16,0},{20,4},{24,8},{28,12},{1,17},{... | collective-permute-start | bytes 393224 | tf_op jit(solution)/shard_map/ppermute | solution.py:364
  43.7 5.0 %collective-permute-start.13 = (bf16[512,128]{1,0:T(8,128)(2,1)S(1)}, bf16[512,128]{1,0:T(8,128)(2,1)S(1)}, u32[]{:S(2)}, u32[]{:S(2)}) collective-permute-start(bf16[512,128]{1,0:T(8,128)(2,1)S(1)} %shard_map.122.refs_0_), channel_id=1, source_target_pairs={{0,8},{4,12},{8,0},{12,4},{16,24},{20,28},{24,16},{28,20},{1,9},{5... | collective-permute-start | bytes 393224 | tf_op jit(solution)/shard_map/ppermute | solution.py:364
  44.1 5.9 %collective-permute-start.12 = (bf16[512,128]{1,0:T(8,128)(2,1)S(1)}, bf16[512,128]{1,0:T(8,128)(2,1)S(1)}, u32[]{:S(2)}, u32[]{:S(2)}) collective-permute-start(bf16[512,128]{1,0:T(8,128)(2,1)S(1)} %shard_map.122.refs_0_), channel_id=1, source_target_pairs={{0,4},{4,0},{8,12},{12,8},{16,20},{20,16},{24,28},{28,24},{1,5},{5... | collective-permute-start | bytes 393224 | tf_op jit(solution)/shard_map/ppermute | solution.py:364
  46.9 3.1 %collective-permute-start.18 = (bf16[512,128]{1,0:T(8,128)(2,1)S(1)}, bf16[512,128]{1,0:T(8,128)(2,1)S(1)}, u32[]{:S(2)}, u32[]{:S(2)}) collective-permute-start(bf16[512,128]{1,0:T(8,128)(2,1)S(1)} %collective-permute-done.17.refs_3_.refs_6_), channel_id=1, source_target_pairs={{0,4},{4,0},{8,12},{12,8},{16,20},{20,16},{24,28},{28,24},{1,5},{5... | collective-permute-start | bytes 393224 | tf_op jit(solution)/shard_map/ppermute | solution.py:364
  48.2 1.8 %collective-permute-start.16 = (bf16[512,128]{1,0:T(8,128)(2,1)S(1)}, bf16[512,128]{1,0:T(8,128)(2,1)S(1)}, u32[]{:S(2)}, u32[]{:S(2)}) collective-permute-start(bf16[512,128]{1,0:T(8,128)(2,1)S(1)} %collective-permute-done.15.refs_2_.refs_4_), channel_id=1, source_target_pairs={{0,4},{4,0},{8,12},{12,8},{16,20},{20,16},{24,28},{28,24},{1,5},{5... | collective-permute-start | bytes 393224 | tf_op jit(solution)/shard_map/ppermute | solution.py:364
  48.7 1.4 %collective-permute-start.14 = (bf16[512,128]{1,0:T(8,128)(2,1)S(1)}, bf16[512,128]{1,0:T(8,128)(2,1)S(1)}, u32[]{:S(2)}, u32[]{:S(2)}) collective-permute-start(bf16[512,128]{1,0:T(8,128)(2,1)S(1)} %collective-permute-done.13.refs_1_.refs_2_), channel_id=1, source_target_pairs={{0,4},{4,0},{8,12},{12,8},{16,20},{20,16},{24,28},{28,24},{1,5},{5... | collective-permute-start | bytes 393224 | tf_op jit(solution)/shard_map/ppermute | solution.py:364

commit v10 on v9

--- a/solution.py
+++ b/solution.py
@@ -110,14 +110,14 @@
 
     def body(g):
         part = None
-        for j in range(3):
-            k = g * 3 + j
+        for j in range(9):
+            k = g * 9 + j
             term = dot(weight_ref[k], t_ref[offset_rows(k, chans), :])
             part = term if part is None else part + term
         total_ref[...] += part
 
-    assert count % 3 == 0
-    for g in range(count // 3):
+    assert count % 9 == 0
+    for g in range(count // 9):
         body(g)
 
 
@@ -204,8 +204,8 @@
 def packed_products(feats, t_ref, sum_ref, base_ref=None):
     chans = feats.shape[0]
     tiles = t_ref.shape[0] // LANES
-    for start in range(0, tiles, 2):
-        width = min(2, tiles - start)
+    for start in range(0, tiles, 4):
+        width = min(4, tiles - start)
         grad = dot_nt(feats, t_ref[start * LANES : (start + width) * LANES, :])
         for j in range(width):
             rows = slice((start + j) * chans, (start + j + 1) * chans)
@@ -333,14 +333,14 @@
         inside = [last * chans <= half if core == 0 else first * chans >= half for first, last in spans]
         wanted = [k for k in range(count) if inside[k] == early]
         assert wanted == list(range(wanted[0], wanted[-1] + 1))
-        middle = (wanted[0] + wanted[-1] + 1) // 2
+        ends = [wanted[0] + len(wanted) * i // 3 for i in range(4)]
         copies = []
         for layer in range(layers):
             for i, piece_ref in enumerate(piece_refs):
                 piece = place_of(jnp.bitwise_xor(me, step * i), slots)
                 block = piece_ref[layer * rows : (layer + 1) * rows].astype(F32)
                 all_ref[pl.ds(pl.multiple_of(piece * rows, rows), rows), :] = block
-            for first, last in ((wanted[0], middle), (middle, wanted[-1] + 1)):
+            for first, last in zip(ends, ends[1:]):
                 for k in range(first, last):
                     tile, shift = divmod(k * chans, LANES)
                     block = all_ref[tile * chans : (tile + 1) * chans, :]
@@ -415,7 +415,7 @@
             [shape(weight_shape, F32)] * layers,
             [*given, *outs],
             scratch=[pltpu.VMEM(weight_shape, F32)] * layers
-            + [pltpu.VMEM((packed, LANES), F32), pltpu.SemaphoreType.DMA((2 * layers,))],
+            + [pltpu.VMEM((packed, LANES), F32), pltpu.SemaphoreType.DMA((3 * layers,))],
             args_in=[VMEM] * len(given) + [HBM] * len(outs),
             outs_in=HBM,
             aliases=[(len(given) + i, i) for i in range(len(outs))],

time: 51.6 us -> 51.6 us (level)
  no operation moved by 1% of the time
where the time goes in v10:
time: 51.6 us; the launch traced here: 51.4 us
  starting transfers between devices  19.3 us (37%)
  Pallas kernels  15.8 us (31%)
  waiting for transfers between devices  15.5 us (30%)
  between operations  0.87 us (2%)
    pallas_call x13, Pallas kernels, call(): pl.pallas_call(body, out_shape=outs if single else tuple(outs), in_specs=...  15.8 us
    ppermute x13, starting transfers between devices, swap(): lax.ppermute(block, axis, [(i, i ^ bit) for i in range(lax.axis_size(axis...  11.7 us
    ppermute x13, waiting for transfers between devices, swap(): lax.ppermute(block, axis, [(i, i ^ bit) for i in range(lax.axis_size(axis...  10.4 us
    ppermute x4, starting transfers between devices, swap_scans(): return lax.ppermute(block, ('space', 'scan'), pairs)  6.23 us
    ppermute x4, waiting for transfers between devices, swap_scans(): return lax.ppermute(block, ('space', 'scan'), pairs)  5.04 us
    ppermute x2, starting transfers between devices, swap_neighbours(): lax.ppermute(far, 'space', [(i, i + 1 if i % 2 else i - 1) for i in inner])  1.3 us
  transfers between devices with their start and end apart: 19, of which 11 were waited for; matrix products, arithmetic and copies ran while one was open for 0% of the time, Pallas kernels for 12%

profile of v10, /device:TPU:0, one launch (start us, length us, event | category | flops | bytes accessed | tf_op | source)
XLA Modules:
  0.0 51.4 jit_solution(8589806760179349855)
XLA Ops:
  0.7 3.8 %shard_map.112 = (bf16[3024,256]{1,0:T(8,128)(2,1)S(1)}, bf16[2688,128]{1,0:T(8,128)(2,1)S(1)}, f32[32,128]{1,0:T(8,128)S(1)}, bf16[192,128]{1,0:T(8,128)(2,1)S(1)}, bf16[192,128]{1,0:T(8,128)(2,1)S(1)}) custom-call(s32[27,1,256]{2,1,0:T(1,128)} %bitcast.31, bf16[96,512]{1,0:T(8,128)(2,1)} %bitcast.30, s32[27,1,256]{2,1,0:T(1,128)} %bitcast.27, ...), custom_call_target="tpu_custom_call" | custom-call | flops 679477248 | bytes 4194304 | tf_op jit(solution)/shard_map/pallas_call | solution.py:21
  4.4 0.5 %collective-permute-start = (bf16[192,128]{1,0:T(8,128)(2,1)S(1)}, bf16[192,128]{1,0:T(8,128)(2,1)S(1)}, u32[]{:S(2)}, u32[]{:S(2)}) collective-permute-start(bf16[192,128]{1,0:T(8,128)(2,1)S(1)} %get-tuple-element.46), channel_id=1, source_target_pairs={{0,4},{4,0},{8,12},{12,8},{16,20},{20,16},{24,28},{28,24},{1,5},{5... | collective-permute-start | bytes 147464 | tf_op jit(solution)/shard_map/ppermute | solution.py:364
  5.0 0.7 %collective-permute-start.1 = (bf16[192,128]{1,0:T(8,128)(2,1)S(1)}, bf16[192,128]{1,0:T(8,128)(2,1)S(1)}, u32[]{:S(2)}, u32[]{:S(2)}) collective-permute-start(bf16[192,128]{1,0:T(8,128)(2,1)S(1)} %get-tuple-element.47), channel_id=1, source_target_pairs={{4,8},{8,4},{12,16},{16,12},{20,24},{24,20},{5,9},{9,5},{13,17},{1... | collective-permute-start | bytes 147464 | tf_op jit(solution)/shard_map/ppermute | solution.py:369
  5.7 2.0 %shard_map.113 = (bf16[2688,512]{1,0:T(8,128)(2,1)S(1)}, f32[128,512]{1,0:T(8,128)S(1)}) custom-call(s32[27,1,256]{2,1,0:T(1,128)S(1)} %bitcast.28, bf16[3024,256]{1,0:T(8,128)(2,1)S(1)} %get-tuple-element.43.c_ref, bf16[27,96,96]{2,1,0:T(8,128)(2,1)S(1)} %copy-done.4), custom_call_target="tpu_custom_call" | custom-call | flops 849346560 | bytes 8388608 | tf_op jit(solution)/shard_map/pallas_call | solution.py:21
  7.8 1.0 %shard_map.114.sum_two_ref = f32[2048,128]{1,0:T(8,128)S(1)} custom-call(bf16[96,512]{1,0:T(8,128)(2,1)S(1)} %bitcast.17, bf16[2688,512]{1,0:T(8,128)(2,1)S(1)} %get-tuple-element.49.t_ref), custom_call_target="tpu_custom_call" | custom-call | flops 318504960 | bytes 6291456 | tf_op jit(solution)/shard_map/pallas_call | solution.py:21
  8.8 4.1 %shard_map.115 = (bf16[2688,640]{1,0:T(8,128)(2,1)S(1)}, f32[2048,128]{1,0:T(8,128)S(1)}, bf16[2048,128]{1,0:T(8,128)(2,1)S(1)}) custom-call(f32[128,512]{1,0:T(8,128)S(1)} %get-tuple-element.44.own_ref, f32[32,128]{1,0:T(8,128)S(1)} %get-tuple-element.45.inv_ref, bf16[192,128]{1,0:T(8,128)(2,1)S(1)} %collective-permute-done.near_ref, ...), custom_call_target="tpu_custom_call" | custom-call | flops 2017198080 | bytes 8388608 | tf_op jit(solution)/shard_map/pallas_call | solution.py:21
  12.8 3.9 %collective-permute-start.2 = (bf16[2048,128]{1,0:T(8,128)(2,1)S(1)}, bf16[2048,128]{1,0:T(8,128)(2,1)S(1)}, u32[]{:S(2)}, u32[]{:S(2)}) collective-permute-start(bf16[2048,128]{1,0:T(8,128)(2,1)S(1)} %get-tuple-element.55), channel_id=1, source_target_pairs={{0,4},{4,0},{8,12},{12,8},{16,20},{20,16},{24,28},{28,24},{1,5},{5... | collective-permute-start | bytes 1572872 | tf_op jit(solution)/shard_map/ppermute | solution.py:364
  16.8 1.1 %shard_map.116 = (f32[96,512]{1,0:T(8,128)S(1)}, bf16[96,128]{1,0:T(8,128)(2,1)S(1)}, bf16[96,128]{1,0:T(8,128)(2,1)S(1)}) custom-call(bf16[27,96,96]{2,1,0:T(8,128)(2,1)S(1)} %copy-done, bf16[2688,640]{1,0:T(8,128)(2,1)S(1)} %get-tuple-element.51.t_ref), custom_call_target="tpu_custom_call" | custom-call | flops 318504960 | bytes 6291456 | tf_op jit(solution)/shard_map/pallas_call | solution.py:21
  17.9 0.4 collective-permute-done.2.got_ref
  18.4 1.9 %collective-permute-start.5 = (bf16[512,128]{1,0:T(8,128)(2,1)S(1)}, bf16[512,128]{1,0:T(8,128)(2,1)S(1)}, u32[]{:S(2)}, u32[]{:S(2)}) collective-permute-start(bf16[512,128]{1,0:T(8,128)(2,1)S(1)} %get-tuple-element.63), channel_id=1, source_target_pairs={{0,24},{4,28},{8,16},{12,20},{16,8},{20,12},{24,0},{28,4},{1,25},{... | collective-permute-start | bytes 393224 | tf_op jit(solution)/shard_map/ppermute | solution.py:364
  20.3 1.3 %collective-permute-start.6 = (bf16[512,128]{1,0:T(8,128)(2,1)S(1)}, bf16[512,128]{1,0:T(8,128)(2,1)S(1)}, u32[]{:S(2)}, u32[]{:S(2)}) collective-permute-start(bf16[512,128]{1,0:T(8,128)(2,1)S(1)} %get-tuple-element.64), channel_id=1, source_target_pairs={{0,16},{4,20},{8,24},{12,28},{16,0},{20,4},{24,8},{28,12},{1,17},{... | collective-permute-start | bytes 393224 | tf_op jit(solution)/shard_map/ppermute | solution.py:364
  21.6 0.4 collective-permute-start.7
  22.0 0.7 %collective-permute-start.4 = (bf16[96,128]{1,0:T(8,128)(2,1)S(1)}, bf16[96,128]{1,0:T(8,128)(2,1)S(1)}, u32[]{:S(2)}, u32[]{:S(2)}) collective-permute-start(bf16[96,128]{1,0:T(8,128)(2,1)S(1)} %get-tuple-element.61), channel_id=1, source_target_pairs={{4,8},{8,4},{12,16},{16,12},{20,24},{24,20},{5,9},{9,5},{13,17},{1... | collective-permute-start | bytes 73736 | tf_op jit(solution)/shard_map/ppermute | solution.py:369
  22.7 0.5 %collective-permute-done.3.near_ref = bf16[96,128]{1,0:T(8,128)(2,1)S(1)} collective-permute-done((bf16[96,128]{1,0:T(8,128)(2,1)S(1)}, bf16[96,128]{1,0:T(8,128)(2,1)S(1)}, u32[]{:S(2)}, u32[]{:S(2)}) %collective-permute-start.3) | collective-permute-done | bytes 24608 | tf_op jit(solution)/shard_map/ppermute | solution.py:364
  23.2 2.6 %collective-permute-done.5.refs_0_ = bf16[512,128]{1,0:T(8,128)(2,1)S(1)} collective-permute-done((bf16[512,128]{1,0:T(8,128)(2,1)S(1)}, bf16[512,128]{1,0:T(8,128)(2,1)S(1)}, u32[]{:S(2)}, u32[]{:S(2)}) %collective-permute-start.5) | collective-permute-done | bytes 131104 | tf_op jit(solution)/shard_map/ppermute | solution.py:364
  25.8 2.2 %collective-permute-done.6.refs_1_ = bf16[512,128]{1,0:T(8,128)(2,1)S(1)} collective-permute-done((bf16[512,128]{1,0:T(8,128)(2,1)S(1)}, bf16[512,128]{1,0:T(8,128)(2,1)S(1)}, u32[]{:S(2)}, u32[]{:S(2)}) %collective-permute-start.6) | collective-permute-done | bytes 131104 | tf_op jit(solution)/shard_map/ppermute | solution.py:364
  28.2 1.6 %collective-permute-start.8 = (bf16[256,128]{1,0:T(8,128)(2,1)S(1)}, bf16[256,128]{1,0:T(8,128)(2,1)S(1)}, u32[]{:S(2)}, u32[]{:S(2)}) collective-permute-start(bf16[256,128]{1,0:T(8,128)(2,1)S(1)} %get-tuple-element.77.refs_0_), channel_id=1, source_target_pairs={{0,1},{1,0},{2,3},{3,2},{4,6},{5,7},{6,4},{7,5},{8,9},{9,8},{10,11... | collective-permute-start | bytes 196616 | tf_op jit(solution)/shard_map/ppermute | solution.py:378
  29.8 0.5 collective-permute-start.10
  30.3 0.9 %shard_map.119 = bf16[96,512]{1,0:T(8,128)(2,1)} custom-call(f32[96,512]{1,0:T(8,128)S(1)} %get-tuple-element.73.own_ref, bf16[96,128]{1,0:T(8,128)(2,1)S(1)} %collective-permute-done.3.near_ref, bf16[96,128]{1,0:T(8,128)(2,1)S(1)} %collective-permute-done.4.far_ref, s32[1,64]{1,0:T(1,128)S(1)} %bitcast.21, s32[1,64]{1,0:T(1,128)S(1)} %bitcast.24), custom_call_target="tpu_custom_call" | custom-call | tf_op jit(solution)/shard_map/pallas_call | solution.py:21
  31.2 2.0 %collective-permute-done.8.refs_1_ = bf16[256,128]{1,0:T(8,128)(2,1)S(1)} collective-permute-done((bf16[256,128]{1,0:T(8,128)(2,1)S(1)}, bf16[256,128]{1,0:T(8,128)(2,1)S(1)}, u32[]{:S(2)}, u32[]{:S(2)}) %collective-permute-start.8) | collective-permute-done | bytes 65568 | tf_op jit(solution)/shard_map/ppermute | solution.py:378
  33.2 1.9 %collective-permute-start.9 = (bf16[256,128]{1,0:T(8,128)(2,1)S(1)}, bf16[256,128]{1,0:T(8,128)(2,1)S(1)}, u32[]{:S(2)}, u32[]{:S(2)}) collective-permute-start(bf16[256,128]{1,0:T(8,128)(2,1)S(1)} %shard_map.120.refs_0_), channel_id=1, source_target_pairs={{0,2},{1,3},{2,0},{3,1},{4,5},{5,4},{6,7},{7,6},{8,10},{9,11},{10,... | collective-permute-start | bytes 196616 | tf_op jit(solution)/shard_map/ppermute | solution.py:378
  35.2 2.2 %collective-permute-start.11 = (bf16[256,128]{1,0:T(8,128)(2,1)S(1)}, bf16[256,128]{1,0:T(8,128)(2,1)S(1)}, u32[]{:S(2)}, u32[]{:S(2)}) collective-permute-start(bf16[256,128]{1,0:T(8,128)(2,1)S(1)} %shard_map.121.refs_2_), channel_id=1, source_target_pairs={{0,2},{1,3},{2,0},{3,1},{4,5},{5,4},{6,7},{7,6},{8,10},{9,11},{10,... | collective-permute-start | bytes 196616 | tf_op jit(solution)/shard_map/ppermute | solution.py:378
  37.4 1.1 %collective-permute-done.9.refs_1_ = bf16[256,128]{1,0:T(8,128)(2,1)S(1)} collective-permute-done((bf16[256,128]{1,0:T(8,128)(2,1)S(1)}, bf16[256,128]{1,0:T(8,128)(2,1)S(1)}, u32[]{:S(2)}, u32[]{:S(2)}) %collective-permute-start.9) | collective-permute-done | bytes 65568 | tf_op jit(solution)/shard_map/ppermute | solution.py:378
  38.5 1.9 %collective-permute-done.11.refs_3_ = bf16[256,128]{1,0:T(8,128)(2,1)S(1)} collective-permute-done((bf16[256,128]{1,0:T(8,128)(2,1)S(1)}, bf16[256,128]{1,0:T(8,128)(2,1)S(1)}, u32[]{:S(2)}, u32[]{:S(2)}) %collective-permute-start.11) | collective-permute-done | bytes 65568 | tf_op jit(solution)/shard_map/ppermute | solution.py:378
  40.5 2.0 %collective-permute-start.17 = (bf16[512,128]{1,0:T(8,128)(2,1)S(1)}, bf16[512,128]{1,0:T(8,128)(2,1)S(1)}, u32[]{:S(2)}, u32[]{:S(2)}) collective-permute-start(bf16[512,128]{1,0:T(8,128)(2,1)S(1)} %shard_map.122.refs_0_), channel_id=1, source_target_pairs={{0,24},{4,28},{8,16},{12,20},{16,8},{20,12},{24,0},{28,4},{1,25},{... | collective-permute-start | bytes 393224 | tf_op jit(solution)/shard_map/ppermute | solution.py:364
  42.5 1.2 %collective-permute-start.15 = (bf16[512,128]{1,0:T(8,128)(2,1)S(1)}, bf16[512,128]{1,0:T(8,128)(2,1)S(1)}, u32[]{:S(2)}, u32[]{:S(2)}) collective-permute-start(bf16[512,128]{1,0:T(8,128)(2,1)S(1)} %shard_map.122.refs_0_), channel_id=1, source_target_pairs={{0,16},{4,20},{8,24},{12,28},{16,0},{20,4},{24,8},{28,12},{1,17},{... | collective-permute-start | bytes 393224 | tf_op jit(solution)/shard_map/ppermute | solution.py:364
  43.7 0.4 collective-permute-start.13
  44.1 2.8 %collective-permute-done.17.refs_3_.refs_6_ = bf16[512,128]{1,0:T(8,128)(2,1)S(1)} collective-permute-done((bf16[512,128]{1,0:T(8,128)(2,1)S(1)}, bf16[512,128]{1,0:T(8,128)(2,1)S(1)}, u32[]{:S(2)}, u32[]{:S(2)}) %collective-permute-start.17) | collective-permute-done | bytes 131104 | tf_op jit(solution)/shard_map/ppermute | solution.py:364
  46.9 1.3 %collective-permute-done.15.refs_2_.refs_4_ = bf16[512,128]{1,0:T(8,128)(2,1)S(1)} collective-permute-done((bf16[512,128]{1,0:T(8,128)(2,1)S(1)}, bf16[512,128]{1,0:T(8,128)(2,1)S(1)}, u32[]{:S(2)}, u32[]{:S(2)}) %collective-permute-start.15) | collective-permute-done | bytes 131104 | tf_op jit(solution)/shard_map/ppermute | solution.py:364
  48.2 0.5 collective-permute-done.13.refs_1_.refs_2_
  48.7 1.3 %shard_map.123 = (f32[27,96,96]{2,1,0:T(8,128)}, f32[27,96,96]{2,1,0:T(8,128)}) custom-call(bf16[512,128]{1,0:T(8,128)(2,1)S(1)} %shard_map.122.refs_0_, bf16[512,128]{1,0:T(8,128)(2,1)S(1)} %collective-permute-done.13.refs_1_.refs_2_, bf16[512,128]{1,0:T(8,128)(2,1)S(1)} %collective-permute-done.15.refs_2_.refs_4_, ...), custom_call_target="tpu_custom_call" | custom-call | bytes 4194304 | tf_op jit(solution)/shard_map/pallas_call | solution.py:21
  50.0 1.4 %shard_map.124 = (f32[27,96,96]{2,1,0:T(8,128)}, f32[27,96,96]{2,1,0:T(8,128)}) custom-call(bf16[512,128]{1,0:T(8,128)(2,1)S(1)} %shard_map.122.refs_0_, bf16[512,128]{1,0:T(8,128)(2,1)S(1)} %collective-permute-done.12.refs_1_, bf16[512,128]{1,0:T(8,128)(2,1)S(1)} %collective-permute-done.13.refs_1_.refs_2_, ...), custom_call_target="tpu_custom_call", output_to_operand_aliasing={{0}: (8, {}), {1}: (9, {})} | custom-call | bytes 4194304 | tf_op jit(solution)/shard_map/pallas_call | solution.py:21
  (33 shorter events, 0.5 us)
Async XLA Ops:
  0.6 5.0 %copy-start.4 = (bf16[27,96,96]{2,1,0:T(8,128)(2,1)S(1)}, bf16[27,96,96]{2,1,0:T(8,128)(2,1)}, u32[]{:S(2)}) copy-start(bf16[27,96,96]{2,1,0:T(8,128)(2,1)} %weight_ref.2) | copy-start | bytes 1492996
  0.6 5.0 %copy-start.6 = (s32[1,1,27,256]{3,1,2,0:T(1,128)S(1)}, s32[1,1,27,256]{3,1,2,0:T(1,128)}, u32[]{:S(2)}) copy-start(s32[1,1,27,256]{3,1,2,0:T(1,128)} %param.14) | copy-start | bytes 82948
  4.4 4.3 %collective-permute-start = (bf16[192,128]{1,0:T(8,128)(2,1)S(1)}, bf16[192,128]{1,0:T(8,128)(2,1)S(1)}, u32[]{:S(2)}, u32[]{:S(2)}) collective-permute-start(bf16[192,128]{1,0:T(8,128)(2,1)S(1)} %get-tuple-element.46), channel_id=1, source_target_pairs={{0,4},{4,0},{8,12},{12,8},{16,20},{20,16},{24,28},{28,24},{1,5},{5... | collective-permute-start | bytes 147464 | tf_op jit(solution)/shard_map/ppermute | solution.py:364
  5.0 3.8 %collective-permute-start.1 = (bf16[192,128]{1,0:T(8,128)(2,1)S(1)}, bf16[192,128]{1,0:T(8,128)(2,1)S(1)}, u32[]{:S(2)}, u32[]{:S(2)}) collective-permute-start(bf16[192,128]{1,0:T(8,128)(2,1)S(1)} %get-tuple-element.47), channel_id=1, source_target_pairs={{4,8},{8,4},{12,16},{16,12},{20,24},{24,20},{5,9},{9,5},{13,17},{1... | collective-permute-start | bytes 147464 | tf_op jit(solution)/shard_map/ppermute | solution.py:369
  5.7 2.1 %copy-start.1 = (bf16[1,1,512,96]{2,3,1,0:T(8,128)(2,1)S(1)}, bf16[1,1,512,96]{2,3,1,0:T(8,128)(2,1)}, u32[]{:S(2)}) copy-start(bf16[1,1,512,96]{2,3,1,0:T(8,128)(2,1)} %param.10) | copy-start | bytes 294916
  7.7 1.0 %copy-start.2 = (s32[1,1,64]{2,1,0:T(1,128)S(1)}, s32[1,1,64]{2,1,0:T(1,128)}, u32[]{:S(2)}) copy-start(s32[1,1,64]{2,1,0:T(1,128)} %param.17) | copy-start | bytes 772
  7.7 1.0 %copy-start.3 = (s32[1,1,64]{2,1,0:T(1,128)S(1)}, s32[1,1,64]{2,1,0:T(1,128)}, u32[]{:S(2)}) copy-start(s32[1,1,64]{2,1,0:T(1,128)} %param.16) | copy-start | bytes 772
  7.7 1.0 %copy-start.5 = (bf16[1,1,512,96]{2,3,1,0:T(8,128)(2,1)S(1)}, bf16[1,1,512,96]{2,3,1,0:T(8,128)(2,1)}, u32[]{:S(2)}) copy-start(bf16[1,1,512,96]{2,3,1,0:T(8,128)(2,1)} %param.9) | copy-start | bytes 294916
  8.8 8.0 %copy-start = (bf16[27,96,96]{2,1,0:T(8,128)(2,1)S(1)}, bf16[27,96,96]{2,1,0:T(8,128)(2,1)}, u32[]{:S(2)}) copy-start(bf16[27,96,96]{2,1,0:T(8,128)(2,1)} %weight_ref.3) | copy-start | bytes 1492996
  12.8 5.5 %collective-permute-start.2 = (bf16[2048,128]{1,0:T(8,128)(2,1)S(1)}, bf16[2048,128]{1,0:T(8,128)(2,1)S(1)}, u32[]{:S(2)}, u32[]{:S(2)}) collective-permute-start(bf16[2048,128]{1,0:T(8,128)(2,1)S(1)} %get-tuple-element.55), channel_id=1, source_target_pairs={{0,4},{4,0},{8,12},{12,8},{16,20},{20,16},{24,28},{28,24},{1,5},{5... | collective-permute-start | bytes 1572872 | tf_op jit(solution)/shard_map/ppermute | solution.py:364
  18.4 7.3 %collective-permute-start.5 = (bf16[512,128]{1,0:T(8,128)(2,1)S(1)}, bf16[512,128]{1,0:T(8,128)(2,1)S(1)}, u32[]{:S(2)}, u32[]{:S(2)}) collective-permute-start(bf16[512,128]{1,0:T(8,128)(2,1)S(1)} %get-tuple-element.63), channel_id=1, source_target_pairs={{0,24},{4,28},{8,16},{12,20},{16,8},{20,12},{24,0},{28,4},{1,25},{... | collective-permute-start | bytes 393224 | tf_op jit(solution)/shard_map/ppermute | solution.py:364
  20.3 7.6 %collective-permute-start.6 = (bf16[512,128]{1,0:T(8,128)(2,1)S(1)}, bf16[512,128]{1,0:T(8,128)(2,1)S(1)}, u32[]{:S(2)}, u32[]{:S(2)}) collective-permute-start(bf16[512,128]{1,0:T(8,128)(2,1)S(1)} %get-tuple-element.64), channel_id=1, source_target_pairs={{0,16},{4,20},{8,24},{12,28},{16,0},{20,4},{24,8},{28,12},{1,17},{... | collective-permute-start | bytes 393224 | tf_op jit(solution)/shard_map/ppermute | solution.py:364
  21.6 6.5 %collective-permute-start.7 = (bf16[512,128]{1,0:T(8,128)(2,1)S(1)}, bf16[512,128]{1,0:T(8,128)(2,1)S(1)}, u32[]{:S(2)}, u32[]{:S(2)}) collective-permute-start(bf16[512,128]{1,0:T(8,128)(2,1)S(1)} %get-tuple-element.65), channel_id=1, source_target_pairs={{0,8},{4,12},{8,0},{12,4},{16,24},{20,28},{24,16},{28,20},{1,9},{5... | collective-permute-start | bytes 393224 | tf_op jit(solution)/shard_map/ppermute | solution.py:364
  22.0 1.2 %collective-permute-start.3 = (bf16[96,128]{1,0:T(8,128)(2,1)S(1)}, bf16[96,128]{1,0:T(8,128)(2,1)S(1)}, u32[]{:S(2)}, u32[]{:S(2)}) collective-permute-start(bf16[96,128]{1,0:T(8,128)(2,1)S(1)} %get-tuple-element.60), channel_id=1, source_target_pairs={{0,4},{4,0},{8,12},{12,8},{16,20},{20,16},{24,28},{28,24},{1,5},{5... | collective-permute-start | bytes 73736 | tf_op jit(solution)/shard_map/ppermute | solution.py:364
  22.0 1.2 %collective-permute-start.4 = (bf16[96,128]{1,0:T(8,128)(2,1)S(1)}, bf16[96,128]{1,0:T(8,128)(2,1)S(1)}, u32[]{:S(2)}, u32[]{:S(2)}) collective-permute-start(bf16[96,128]{1,0:T(8,128)(2,1)S(1)} %get-tuple-element.61), channel_id=1, source_target_pairs={{4,8},{8,4},{12,16},{16,12},{20,24},{24,20},{5,9},{9,5},{13,17},{1... | collective-permute-start | bytes 73736 | tf_op jit(solution)/shard_map/ppermute | solution.py:369
  28.2 5.0 %collective-permute-start.8 = (bf16[256,128]{1,0:T(8,128)(2,1)S(1)}, bf16[256,128]{1,0:T(8,128)(2,1)S(1)}, u32[]{:S(2)}, u32[]{:S(2)}) collective-permute-start(bf16[256,128]{1,0:T(8,128)(2,1)S(1)} %get-tuple-element.77.refs_0_), channel_id=1, source_target_pairs={{0,1},{1,0},{2,3},{3,2},{4,6},{5,7},{6,4},{7,5},{8,9},{9,8},{10,11... | collective-permute-start | bytes 196616 | tf_op jit(solution)/shard_map/ppermute | solution.py:378
  29.8 5.4 %collective-permute-start.10 = (bf16[256,128]{1,0:T(8,128)(2,1)S(1)}, bf16[256,128]{1,0:T(8,128)(2,1)S(1)}, u32[]{:S(2)}, u32[]{:S(2)}) collective-permute-start(bf16[256,128]{1,0:T(8,128)(2,1)S(1)} %get-tuple-element.78.refs_0_), channel_id=1, source_target_pairs={{0,1},{1,0},{2,3},{3,2},{4,6},{5,7},{6,4},{7,5},{8,9},{9,8},{10,11... | collective-permute-start | bytes 196616 | tf_op jit(solution)/shard_map/ppermute | solution.py:378
  33.2 5.3 %collective-permute-start.9 = (bf16[256,128]{1,0:T(8,128)(2,1)S(1)}, bf16[256,128]{1,0:T(8,128)(2,1)S(1)}, u32[]{:S(2)}, u32[]{:S(2)}) collective-permute-start(bf16[256,128]{1,0:T(8,128)(2,1)S(1)} %shard_map.120.refs_0_), channel_id=1, source_target_pairs={{0,2},{1,3},{2,0},{3,1},{4,5},{5,4},{6,7},{7,6},{8,10},{9,11},{10,... | collective-permute-start | bytes 196616 | tf_op jit(solution)/shard_map/ppermute | solution.py:378
  35.2 5.2 %collective-permute-start.11 = (bf16[256,128]{1,0:T(8,128)(2,1)S(1)}, bf16[256,128]{1,0:T(8,128)(2,1)S(1)}, u32[]{:S(2)}, u32[]{:S(2)}) collective-permute-start(bf16[256,128]{1,0:T(8,128)(2,1)S(1)} %shard_map.121.refs_2_), channel_id=1, source_target_pairs={{0,2},{1,3},{2,0},{3,1},{4,5},{5,4},{6,7},{7,6},{8,10},{9,11},{10,... | collective-permute-start | bytes 196616 | tf_op jit(solution)/shard_map/ppermute | solution.py:378
  40.5 6.4 %collective-permute-start.17 = (bf16[512,128]{1,0:T(8,128)(2,1)S(1)}, bf16[512,128]{1,0:T(8,128)(2,1)S(1)}, u32[]{:S(2)}, u32[]{:S(2)}) collective-permute-start(bf16[512,128]{1,0:T(8,128)(2,1)S(1)} %shard_map.122.refs_0_), channel_id=1, source_target_pairs={{0,24},{4,28},{8,16},{12,20},{16,8},{20,12},{24,0},{28,4},{1,25},{... | collective-permute-start | bytes 393224 | tf_op jit(solution)/shard_map/ppermute | solution.py:364
  42.5 5.7 %collective-permute-start.15 = (bf16[512,128]{1,0:T(8,128)(2,1)S(1)}, bf16[512,128]{1,0:T(8,128)(2,1)S(1)}, u32[]{:S(2)}, u32[]{:S(2)}) collective-permute-start(bf16[512,128]{1,0:T(8,128)(2,1)S(1)} %shard_map.122.refs_0_), channel_id=1, source_target_pairs={{0,16},{4,20},{8,24},{12,28},{16,0},{20,4},{24,8},{28,12},{1,17},{... | collective-permute-start | bytes 393224 | tf_op jit(solution)/shard_map/ppermute | solution.py:364
  43.7 5.0 %collective-permute-start.13 = (bf16[512,128]{1,0:T(8,128)(2,1)S(1)}, bf16[512,128]{1,0:T(8,128)(2,1)S(1)}, u32[]{:S(2)}, u32[]{:S(2)}) collective-permute-start(bf16[512,128]{1,0:T(8,128)(2,1)S(1)} %shard_map.122.refs_0_), channel_id=1, source_target_pairs={{0,8},{4,12},{8,0},{12,4},{16,24},{20,28},{24,16},{28,20},{1,9},{5... | collective-permute-start | bytes 393224 | tf_op jit(solution)/shard_map/ppermute | solution.py:364
  44.1 5.9 %collective-permute-start.12 = (bf16[512,128]{1,0:T(8,128)(2,1)S(1)}, bf16[512,128]{1,0:T(8,128)(2,1)S(1)}, u32[]{:S(2)}, u32[]{:S(2)}) collective-permute-start(bf16[512,128]{1,0:T(8,128)(2,1)S(1)} %shard_map.122.refs_0_), channel_id=1, source_target_pairs={{0,4},{4,0},{8,12},{12,8},{16,20},{20,16},{24,28},{28,24},{1,5},{5... | collective-permute-start | bytes 393224 | tf_op jit(solution)/shard_map/ppermute | solution.py:364
  46.9 3.1 %collective-permute-start.18 = (bf16[512,128]{1,0:T(8,128)(2,1)S(1)}, bf16[512,128]{1,0:T(8,128)(2,1)S(1)}, u32[]{:S(2)}, u32[]{:S(2)}) collective-permute-start(bf16[512,128]{1,0:T(8,128)(2,1)S(1)} %collective-permute-done.17.refs_3_.refs_6_), channel_id=1, source_target_pairs={{0,4},{4,0},{8,12},{12,8},{16,20},{20,16},{24,28},{28,24},{1,5},{5... | collective-permute-start | bytes 393224 | tf_op jit(solution)/shard_map/ppermute | solution.py:364
  48.2 1.8 %collective-permute-start.16 = (bf16[512,128]{1,0:T(8,128)(2,1)S(1)}, bf16[512,128]{1,0:T(8,128)(2,1)S(1)}, u32[]{:S(2)}, u32[]{:S(2)}) collective-permute-start(bf16[512,128]{1,0:T(8,128)(2,1)S(1)} %collective-permute-done.15.refs_2_.refs_4_), channel_id=1, source_target_pairs={{0,4},{4,0},{8,12},{12,8},{16,20},{20,16},{24,28},{28,24},{1,5},{5... | collective-permute-start | bytes 393224 | tf_op jit(solution)/shard_map/ppermute | solution.py:364
  48.7 1.3 %collective-permute-start.14 = (bf16[512,128]{1,0:T(8,128)(2,1)S(1)}, bf16[512,128]{1,0:T(8,128)(2,1)S(1)}, u32[]{:S(2)}, u32[]{:S(2)}) collective-permute-start(bf16[512,128]{1,0:T(8,128)(2,1)S(1)} %collective-permute-done.13.refs_1_.refs_2_), channel_id=1, source_target_pairs={{0,4},{4,0},{8,12},{12,8},{16,20},{20,16},{24,28},{28,24},{1,5},{5... | collective-permute-start | bytes 393224 | tf_op jit(solution)/shard_map/ppermute | solution.py:364
